TPU v7x, 128 devices: a whole 4x4x4 slice. The times are simulated.
128 devices in a mesh: ctx: 16 (over z_hi, y, core), tp: 8 (over x, z_lo).
Axes of the slice: x: 4, y: 4, z: 4 (z_hi: 2, z_lo: 2; z = z_hi * 2 + z_lo), core: 2. Of those that a mesh axis runs over, the one named last changes fastest.
Arguments:
- query: bfloat16 [4096, 8192], P('ctx', 'tp'), may hold values from -6 to 6
- key_part: bfloat16 [4096, 8192], P('ctx', 'tp'), may hold values from -6 to 6
- value_part: bfloat16 [4096, 8192], P('ctx', 'tp'), may hold values from -6 to 6
- out_cotangent: bfloat16 [4096, 4096], P('ctx', 'tp'), may hold values from -3 to 3
- w_out: bfloat16 [8192, 4096], P('tp'), may hold values from -0.0625 to 0.0625
- residue: float32 [8192, 16], P(('tp', 'ctx')), may hold values from -1.5 to 1.5
- rate: float32 [8192, 16], P(('tp', 'ctx')), may hold values from 0.5 to 200
- skip: float32 [8192], P(('tp', 'ctx')), may hold values from 0.5 to 1.5
Outputs:
- output: bfloat16 [4096, 4096], P('ctx', 'tp')
- d_query: bfloat16 [4096, 8192], P('ctx', 'tp')
- d_key: bfloat16 [4096, 8192], P('ctx', 'tp')
- d_value: bfloat16 [4096, 8192], P('ctx', 'tp')
- d_weight: float32 [8192, 4096], P('tp', 'ctx')
- d_residue: float32 [8192, 16], P(('tp', 'ctx'))
- d_rate: float32 [8192, 16], P(('tp', 'ctx'))
- d_skip: float32 [8192], P(('tp', 'ctx'))
All inputs are finite; a program needn't handle non-finite values.
Results may differ from a plain program's by a relative error of at most 0.02.
Values may be sent and summed in bfloat16 or wider, within the bound.
No kernel may reach another device: no remote copies, remote signals or barrier semaphores. Data moves between devices by JAX's collectives and lax.ppermute only.
A program may use at most 128 MiB of HBM per device.

v0:
```python
import functools

import jax
import jax.numpy as jnp
from jax import lax
from jax.experimental import pallas as pl
from jax.experimental.pallas import tpu as pltpu
from jax.sharding import PartitionSpec as P

F32 = jnp.float32
BF16 = jnp.bfloat16
SEQ = 4096
MODES = 16
ROWS = 256
SUB = 8
BLOCKS = 16
UNROLL = 8
VMEM = 48 * 1024 * 1024


def params_of(flops, nbytes):
    return dict(
        compiler_params=pltpu.CompilerParams(vmem_limit_bytes=VMEM),
        cost_estimate=pl.CostEstimate(flops=flops, bytes_accessed=nbytes, transcendentals=0),
    )


def whole():
    return pl.BlockSpec(memory_space=pltpu.VMEM)


def lanes(group):
    return slice(128 * group, 128 * (group + 1))


def group_rows(group):
    return pl.ds(group, ROWS, stride=SUB)


def step_decay(table, mode):
    return jnp.exp(table[mode] * (-1.0 / SEQ))


def block_decay(table, mode):
    return jnp.exp(table[mode] * (-float(ROWS) / SEQ))


def mode_weight(table, mode):
    return table[MODES + mode] * jnp.sqrt(table[mode] * (2.0 / SEQ))


def at(ref, step):
    return ref[pl.ds(pl.multiple_of(step * SUB, SUB), SUB), :]


def zeros(count):
    return tuple(jnp.zeros((SUB, 128), F32) for _ in range(count))


def tree_sum(parts):
    parts = list(parts)
    while len(parts) > 1:
        parts = [sum(parts[i : i + 2]) for i in range(0, len(parts), 2)]
    return parts[0]


def states_kernel(key_ref, value_ref, table, mixed_ref, state_ref):
    for group in range(SUB):
        product = key_ref[:, lanes(group)].astype(F32) * value_ref[:, lanes(group)].astype(F32)
        mixed_ref[group_rows(group), :] = product.astype(BF16).astype(F32)
    decay = [step_decay(table, m) for m in range(MODES)]

    def body(i, held):
        for u in range(UNROLL):
            value = at(mixed_ref, i * UNROLL + u)
            held = tuple(decay[m] * held[m] + value for m in range(MODES))
        return held

    held = lax.fori_loop(0, ROWS // UNROLL, body, zeros(MODES))
    for m in range(MODES):
        state_ref[m] = held[m].astype(state_ref.dtype)


def forward_kernel(own_ref, sent_ref, mixed_ref, query_ref, table, conv_ref, gated_ref, carry_ref, buffer):
    own = own_ref[0]
    for m in range(MODES):
        far = block_decay(table, m)
        carry = jnp.zeros((SUB, 128), F32)
        for j in range(BLOCKS - 1):
            carry = jnp.where(j < own, far * carry + sent_ref[j, m].astype(F32), carry)
        carry_ref[m] = carry
    decay = [step_decay(table, m) for m in range(MODES)]
    weight = [mode_weight(table, m) for m in range(MODES)]
    skip = table[2 * MODES]

    def body(i, held):
        for u in range(UNROLL):
            step = i * UNROLL + u
            value = at(mixed_ref, step)
            held = tuple(decay[m] * held[m] + value for m in range(MODES))
            total = tree_sum([weight[m] * held[m] for m in range(MODES)])
            buffer[pl.ds(pl.multiple_of(step * SUB, SUB), SUB), :] = total + skip * value
        return held

    lax.fori_loop(0, ROWS // UNROLL, body, tuple(carry_ref[m] for m in range(MODES)))
    for group in range(SUB):
        conv = buffer[group_rows(group), :].astype(BF16)
        conv_ref[:, lanes(group)] = conv
        gated_ref[:, lanes(group)] = (query_ref[:, lanes(group)].astype(F32) * conv.astype(F32)).astype(BF16)


def output_kernel(gated_ref, weight_ref, out_ref):
    out_ref[0] = jnp.dot(gated_ref[...], weight_ref[...], preferred_element_type=F32).astype(BF16)


def weight_kernel(core_ref, gated_ref, other_ref, cot_ref, other_cot_ref, out_ref, turned):
    @pl.when(pl.program_id(0) == 0)
    def _():
        turned[:, :ROWS] = gated_ref[...].T
        turned[:, ROWS:] = other_ref[...].T

    total = jnp.dot(turned[:, :ROWS], cot_ref[0], preferred_element_type=F32)
    total += jnp.dot(turned[:, ROWS:], other_cot_ref[0], preferred_element_type=F32)
    out_ref[0] = total.astype(BF16)


def cotangent_kernel(cot_ref, weight_ref, query_ref, conv_ref, table, dquery_ref, dconv_ref, state_ref, sent_ref, total):
    part = pl.program_id(0)
    product = lax.dot_general(cot_ref[0], weight_ref[...], (((1,), (1,)), ((), ())), preferred_element_type=F32)

    @pl.when(part == 0)
    def _():
        total[...] = product

    @pl.when(part > 0)
    def _():
        total[...] += product

    @pl.when(part == pl.num_programs(0) - 1)
    def _():
        for group in range(SUB):
            cot = total[:, lanes(group)]
            dquery_ref[:, lanes(group)] = (cot * conv_ref[:, lanes(group)].astype(F32)).astype(BF16)
            dconv_ref[group_rows(group), :] = (cot * query_ref[:, lanes(group)].astype(F32)).astype(BF16).astype(F32)
        decay = [step_decay(table, m) for m in range(MODES)]

        def body(i, held):
            for u in range(UNROLL):
                value = at(dconv_ref, ROWS - 1 - (i * UNROLL + u))
                held = tuple(decay[m] * held[m] + value for m in range(MODES))
            return held

        held = lax.fori_loop(0, ROWS // UNROLL, body, zeros(MODES))
        for m in range(MODES):
            state_ref[m] = held[m]
            sent_ref[m] = held[m].astype(sent_ref.dtype)


def filter_kernel(mixed_ref, dconv_ref, carry_ref, back_ref, table, out_ref):
    half = MODES // 2
    for first in (0, half):
        modes = range(first, first + half)
        decay = [step_decay(table, m) for m in modes]

        def body(i, packed):
            held, moment, first_sum, second_sum, skip_sum = packed
            for u in range(UNROLL):
                value = at(mixed_ref, i * UNROLL + u)
                cot = at(dconv_ref, i * UNROLL + u)
                past = [decay[m] * held[m] for m in range(half)]
                moment = tuple(decay[m] * moment[m] + past[m] for m in range(half))
                held = tuple(past[m] + value for m in range(half))
                first_sum = tuple(first_sum[m] + cot * held[m] for m in range(half))
                second_sum = tuple(second_sum[m] + cot * moment[m] for m in range(half))
                skip_sum = skip_sum + cot * value
            return (held, moment, first_sum, second_sum, skip_sum)

        start = (tuple(carry_ref[m] for m in modes), zeros(half), zeros(half), zeros(half), zeros(1)[0])
        held, moment, first_sum, second_sum, skip_sum = lax.fori_loop(0, ROWS // UNROLL, body, start)
        for m in range(half):
            out_ref[first + m] = first_sum[m]
            out_ref[MODES + first + m] = second_sum[m]
            out_ref[2 * MODES + first + m] = moment[m]
            out_ref[3 * MODES + first + m] = back_ref[first + m]
        out_ref[4 * MODES] = skip_sum


def backward_kernel(own_ref, sent_ref, dconv_ref, key_ref, value_ref, table, dkey_ref, dvalue_ref, carry_ref, buffer):
    own = own_ref[0]
    for m in range(MODES):
        far = block_decay(table, m)
        carry = jnp.zeros((SUB, 128), F32)
        for j in range(BLOCKS - 1, 0, -1):
            carry = jnp.where(j > own, far * carry + sent_ref[j, m].astype(F32), carry)
        carry_ref[m] = carry
    decay = [step_decay(table, m) for m in range(MODES)]
    weight = [mode_weight(table, m) for m in range(MODES)]
    skip = table[2 * MODES]

    def body(i, held):
        for u in range(UNROLL):
            step = ROWS - 1 - (i * UNROLL + u)
            value = at(dconv_ref, step)
            held = tuple(decay[m] * held[m] + value for m in range(MODES))
            total = tree_sum([weight[m] * held[m] for m in range(MODES)])
            buffer[pl.ds(pl.multiple_of(step * SUB, SUB), SUB), :] = total + skip * value
        return held

    lax.fori_loop(0, ROWS // UNROLL, body, tuple(carry_ref[m] for m in range(MODES)))
    for group in range(SUB):
        grad = buffer[group_rows(group), :].astype(BF16).astype(F32)
        dkey_ref[:, lanes(group)] = (grad * value_ref[:, lanes(group)].astype(F32)).astype(BF16)
        dvalue_ref[:, lanes(group)] = (grad * key_ref[:, lanes(group)].astype(F32)).astype(BF16)


def owner_kernel(parts_ref, rate_ref, residue_ref, dresidue_ref, drate_ref, dskip_ref):
    rate = rate_ref[...]
    residue = residue_ref[...]
    near = jnp.exp(rate * (-1.0 / SEQ))
    far = jnp.exp(rate * (-float(ROWS) / SEQ))
    scale = jnp.sqrt(rate * (2.0 / SEQ))
    first = jnp.zeros_like(rate)
    second = jnp.zeros_like(rate)
    skip = jnp.zeros((1, rate.shape[1]), F32)
    later = jnp.zeros_like(rate)
    for j in range(BLOCKS - 1, -1, -1):
        first += parts_ref[j, 0:MODES]
        second += parts_ref[j, MODES : 2 * MODES] + near * later * parts_ref[j, 2 * MODES : 3 * MODES]
        later = far * later + parts_ref[j, 3 * MODES : 4 * MODES]
        skip += parts_ref[j, 4 * MODES : 4 * MODES + 1]
    proj = scale * first
    dresidue_ref[...] = proj
    drate_ref[...] = residue * (0.5 * proj / rate - scale * second * (1.0 / SEQ))
    dskip_ref[...] = skip


def f32(*shape):
    return jax.ShapeDtypeStruct(shape, F32)


def bf16(*shape):
    return jax.ShapeDtypeStruct(shape, BF16)


def exchange(array, axis, groups=None):
    return lax.all_to_all(array, axis, split_axis=0, concat_axis=0, tiled=True, axis_index_groups=groups)


def to_all(array, axis, count):
    return exchange(jnp.broadcast_to(array[None], (count,) + array.shape), axis)


def local(query, key_part, value_part, out_cotangent, w_out, residue, rate, skip):
    own = lax.axis_index("ctx")
    own_array = own.reshape(1).astype(jnp.int32)
    core = own % 2
    smem = pl.BlockSpec(memory_space=pltpu.SMEM)
    same_core = [[2 * chip + c for chip in range(8)] for c in range(2)]
    swap = [(i, i ^ 1) for i in range(BLOCKS)]

    rate_t, residue_t = rate.T, residue.T
    mine = jnp.concatenate([rate_t, residue_t, skip[None], jnp.zeros((7, skip.shape[0]), F32)], axis=0)
    table = to_all(mine, "ctx", BLOCKS).reshape(SUB, 2, 40, 64).transpose(2, 0, 1, 3).reshape(40, SUB, 128)
    cots = to_all(out_cotangent, "tp", 8)

    mixed, state = pl.pallas_call(
        states_kernel,
        out_shape=(f32(ROWS * SUB, 128), bf16(MODES, SUB, 128)),
        in_specs=[whole()] * 3,
        out_specs=(whole(), whole()),
        name="forward_states",
        **params_of(3_000_000_000, 4_000_000),
    )(key_part, value_part, table)
    sent = to_all(state, "ctx", BLOCKS)

    conv_out, gated, carry = pl.pallas_call(
        forward_kernel,
        out_shape=(bf16(ROWS, 1024), bf16(ROWS, 1024), f32(MODES, SUB, 128)),
        in_specs=[smem] + [whole()] * 4,
        out_specs=(whole(),) * 3,
        scratch_shapes=[pltpu.VMEM((ROWS * SUB, 128), F32)],
        name="forward_conv",
        **params_of(5_000_000_000, 4_000_000),
    )(own_array, sent, mixed, query, table)

    other_gated = lax.ppermute(gated, "ctx", swap)
    other_cots = lax.ppermute(lax.dynamic_slice_in_dim(cots, 256 * (1 - core), 256, axis=2), "ctx", swap)

    partial_out = pl.pallas_call(
        output_kernel,
        grid=(8,),
        out_shape=bf16(8, ROWS, 512),
        in_specs=[
            pl.BlockSpec((ROWS, 1024), lambda p: (0, 0)),
            pl.BlockSpec((1024, 512), lambda p: (0, p)),
        ],
        out_specs=pl.BlockSpec((1, ROWS, 512), lambda p: (p, 0, 0)),
        name="output_projection",
        **params_of(2_147_483_648, 11_000_000),
    )(gated, w_out)
    output = exchange(partial_out, "tp").astype(F32).sum(axis=0).astype(BF16)

    partial_weight = pl.pallas_call(
        weight_kernel,
        grid_spec=pltpu.PrefetchScalarGridSpec(
            num_scalar_prefetch=1,
            grid=(8,),
            in_specs=[
                pl.BlockSpec((ROWS, 1024), lambda p, c: (0, 0)),
                pl.BlockSpec((ROWS, 1024), lambda p, c: (0, 0)),
                pl.BlockSpec((1, ROWS, 256), lambda p, c: (p, 0, c[0])),
                pl.BlockSpec((1, ROWS, 256), lambda p, c: (p, 0, 0)),
            ],
            out_specs=pl.BlockSpec((1, 1024, 256), lambda p, c: (p, 0, 0)),
            scratch_shapes=[pltpu.VMEM((1024, 2 * ROWS), BF16)],
        ),
        out_shape=bf16(8, 1024, 256),
        name="projection_gradient",
        **params_of(2_147_483_648, 8_000_000),
    )(core.reshape(1).astype(jnp.int32), gated, other_gated, cots, other_cots)
    d_weight = exchange(partial_weight, "ctx", same_core).astype(F32).sum(axis=0)

    d_query, d_conv, back, back_sent = pl.pallas_call(
        cotangent_kernel,
        grid=(8,),
        out_shape=(bf16(ROWS, 1024), f32(ROWS * SUB, 128), f32(MODES, SUB, 128), bf16(MODES, SUB, 128)),
        in_specs=[
            pl.BlockSpec((1, ROWS, 512), lambda p: (p, 0, 0)),
            pl.BlockSpec((1024, 512), lambda p: (0, p)),
            pl.BlockSpec((ROWS, 1024), lambda p: (0, 0)),
            pl.BlockSpec((ROWS, 1024), lambda p: (0, 0)),
            pl.BlockSpec((40, SUB, 128), lambda p: (0, 0, 0)),
        ],
        out_specs=(
            pl.BlockSpec((ROWS, 1024), lambda p: (0, 0)),
            pl.BlockSpec((ROWS * SUB, 128), lambda p: (0, 0)),
            pl.BlockSpec((MODES, SUB, 128), lambda p: (0, 0, 0)),
            pl.BlockSpec((MODES, SUB, 128), lambda p: (0, 0, 0)),
        ),
        scratch_shapes=[pltpu.VMEM((ROWS, 1024), F32)],
        name="cotangent_states",
        **params_of(5_000_000_000, 13_000_000),
    )(cots, w_out, query, conv_out, table)
    back_all = to_all(back_sent, "ctx", BLOCKS)

    parts = pl.pallas_call(
        filter_kernel,
        out_shape=f32(72, SUB, 128),
        in_specs=[whole()] * 5,
        out_specs=whole(),
        name="filter_gradients",
        **params_of(9_000_000_000, 4_000_000),
    )(mixed, d_conv, carry, back, table)
    parts = exchange(
        parts.reshape(72, SUB, 2, 64).transpose(1, 2, 0, 3).reshape(BLOCKS, 72, 64), "ctx"
    )

    d_key, d_value, _ = pl.pallas_call(
        backward_kernel,
        out_shape=(bf16(ROWS, 1024), bf16(ROWS, 1024), f32(MODES, SUB, 128)),
        in_specs=[smem] + [whole()] * 5,
        out_specs=(whole(),) * 3,
        scratch_shapes=[pltpu.VMEM((ROWS * SUB, 128), F32)],
        name="backward_conv",
        **params_of(5_000_000_000, 4_000_000),
    )(own_array, back_all, d_conv, key_part, value_part, table)

    d_residue, d_rate, d_skip = pl.pallas_call(
        owner_kernel,
        out_shape=(f32(MODES, 64), f32(MODES, 64), f32(1, 64)),
        in_specs=[whole()] * 3,
        out_specs=(whole(),) * 3,
        name="owner_sums",
        **params_of(1_000_000, 400_000),
    )(parts, rate_t, residue_t)
    return (output, d_query, d_key, d_value, d_weight, d_residue.T, d_rate.T, d_skip[0])


def solution(mesh):
    rows, owner = P("ctx", "tp"), P(("tp", "ctx"))
    return jax.shard_map(
        local,
        mesh=mesh,
        in_specs=(rows, rows, rows, rows, P("tp", None), P(("tp", "ctx"), None), P(("tp", "ctx"), None), owner),
        out_specs=(rows, rows, rows, rows, P("tp", "ctx"), P(("tp", "ctx"), None), P(("tp", "ctx"), None), owner),
        check_vma=False,
    )
```

profile of v0, /device:TPU:56, one launch (start us, length us, event | category | flops | bytes accessed | tf_op | source)
XLA Modules:
  0.0 233.2 jit_solution(5884394799433993338)
XLA Ops:
  1.8 13.1 %all_to_all.35 = f32[16,1,2560]{2,1,0:T(1,128)S(1)} all-to-all(f32[16,1,2560]{2,1,0:T(1,128)S(1)} %reshape.44), channel_id=1, replica_groups=mesh['ctx'=16,'tp'=8] {'ctx'}, dimensions={0} | all-to-all | bytes 327680 | tf_op jit(solution)/shard_map/all_to_all | solution.py:246
  19.0 1.5 forward_states.1
  20.7 14.2 %all_to_all.36.sent_ref = bf16[16,16,8,128]{3,2,1,0:T(8,128)(2,1)S(1)} all-to-all(bf16[16,16,8,128]{3,2,1,0:T(8,128)(2,1)S(1)} %broadcast_in_dim.15), channel_id=1, replica_groups=mesh['ctx'=16,'tp'=8] {'ctx'}, dimensions={0} | all-to-all | bytes 1048576 | tf_op jit(solution)/shard_map/all_to_all | solution.py:246
  34.8 1.5 broadcast_in_dim.16
  36.3 5.8 %all-to-all-start.3 = ((bf16[8,256,512]{2,1,0:T(8,128)(2,1)}), bf16[8,256,512]{2,1,0:T(8,128)(2,1)S(1)}, u32[]{:S(2)}, u32[]{:S(2)}) async-start(bf16[8,256,512]{2,1,0:T(8,128)(2,1)} %broadcast_in_dim.16), calls=%async_computation.3 | async-start | bytes 4194304 | tf_op jit(solution)/shard_map/all_to_all | solution.py:246
  44.4 3.0 %forward_conv.1 = (bf16[256,1024]{1,0:T(8,128)(2,1)S(1)}, bf16[256,1024]{1,0:T(8,128)(2,1)S(1)}, f32[16,8,128]{2,1,0:T(8,128)S(1)}) custom-call(s32[1]{0:T(128)} %bitcast.own_ref, bf16[16,16,8,128]{3,2,1,0:T(8,128)(2,1)S(1)} %all_to_all.36.sent_ref, f32[2048,128]{1,0:T(8,128)S(1)} %copy-done.14, bf16[256,1024]{1,0:T(8,128)(2,1)S(1)} %copy-done.3, ...), custom_call_target="tpu_custom_call" | custom-call | flops 5000000000 | bytes 4000000 | tf_op jit(solution)/shard_map/forward_conv/pallas_call | solution.py:276
  48.1 25.5 %all-to-all-done.3.cot_ref = bf16[8,256,512]{2,1,0:T(8,128)(2,1)S(1)} async-done(((bf16[8,256,512]{2,1,0:T(8,128)(2,1)}), bf16[8,256,512]{2,1,0:T(8,128)(2,1)S(1)}, u32[]{:S(2)}, u32[]{:S(2)}) %all-to-all-start.3) | async-done | bytes 2097184 | tf_op jit(solution)/shard_map/all_to_all | solution.py:246
  75.7 10.6 %cotangent_states.1 = (bf16[256,1024]{1,0:T(8,128)(2,1)}, f32[2048,128]{1,0:T(8,128)S(1)}, f32[16,8,128]{2,1,0:T(8,128)S(1)}, bf16[16,8,128]{2,1,0:T(8,128)(2,1)S(1)}) custom-call(bf16[8,256,512]{2,1,0:T(8,128)(2,1)S(1)} %all-to-all-done.3.cot_ref, bf16[1024,4096]{1,0:T(8,128)(2,1)} %weight_ref.3, bf16[256,1024]{1,0:T(8,128)(2,1)S(1)} %copy-done.4, ...), custom_call_target="tpu_custom_call" | custom-call | flops 5000000000 | bytes 13000000 | tf_op jit(solution)/shard_map/cotangent_states/pallas_call | solution.py:323
  86.3 5.0 %filter_gradients.1 = f32[72,8,128]{2,1,0:T(8,128)S(1)} custom-call(f32[2048,128]{1,0:T(8,128)S(1)} %copy-done.15, f32[2048,128]{1,0:T(8,128)S(1)} %get-tuple-element.28.dconv_ref, f32[16,8,128]{2,1,0:T(8,128)S(1)} %get-tuple-element.31.carry_ref, f32[16,8,128]{2,1,0:T(8,128)S(1)} %get-tuple-element.32.back_ref, f32[40,8,128]{2,1,0:T(8,128)S(1)} %reshape.40.table), custom_call_target="tpu_custom_call" | custom-call | flops 8999999488 | bytes 4000000 | tf_op jit(solution)/shard_map/filter_gradients/pallas_call | solution.py:346
  93.5 1.3 copy.19
  94.8 14.0 %all_to_all.37 = f32[16,72,64]{1,2,0:T(8,128)} all-to-all(f32[16,72,64]{1,2,0:T(8,128)S(1)} %copy.19), channel_id=1, replica_groups=mesh['ctx'=16,'tp'=8] {'ctx'}, dimensions={0} | all-to-all | bytes 589824 | tf_op jit(solution)/shard_map/all_to_all | solution.py:246
  109.6 6.4 %all-to-all-start.4 = ((bf16[16,16,8,128]{3,2,1,0:T(8,128)(2,1)}), bf16[16,16,8,128]{3,2,1,0:T(8,128)(2,1)S(1)}, u32[]{:S(2)}, u32[]{:S(2)}) async-start(bf16[16,16,8,128]{3,2,1,0:T(8,128)(2,1)} %broadcast_in_dim.17), calls=%async_computation.4 | async-start | bytes 1048576 | tf_op jit(solution)/shard_map/all_to_all | solution.py:246
  116.0 7.4 %output_projection.1 = bf16[8,256,512]{2,1,0:T(8,128)(2,1)S(1)} custom-call(bf16[256,1024]{1,0:T(8,128)(2,1)S(1)} %get-tuple-element.24.gated_ref, bf16[1024,4096]{1,0:T(8,128)(2,1)} %weight_ref.3), custom_call_target="tpu_custom_call" | custom-call | flops 2147483648 | bytes 11000000 | tf_op jit(solution)/shard_map/output_projection/pallas_call | solution.py:289
  123.4 1.3 copy-done
  125.5 5.9 %all-to-all-start.2 = ((bf16[8,256,512]{2,1,0:T(8,128)(2,1)}), bf16[8,256,512]{2,1,0:T(8,128)(2,1)}, u32[]{:S(2)}, u32[]{:S(2)}) async-start(bf16[8,256,512]{2,1,0:T(8,128)(2,1)} %copy-done), calls=%async_computation.2 | async-start | bytes 4194304 | tf_op jit(solution)/shard_map/all_to_all | solution.py:246
  132.1 2.9 %collective-permute-done.other_ref = bf16[256,1024]{1,0:T(8,128)(2,1)S(1)} collective-permute-done((bf16[256,1024]{1,0:T(8,128)(2,1)S(1)}, bf16[256,1024]{1,0:T(8,128)(2,1)S(1)}, u32[]{:S(2)}, u32[]{:S(2)}) %collective-permute-start) | collective-permute-done | bytes 524320 | tf_op jit(solution)/shard_map/ppermute | solution.py:286
  135.0 5.8 %projection_gradient.1 = bf16[8,1024,256]{2,1,0:T(8,128)(2,1)} custom-call(s32[1]{0:T(128)} %bitcast.6.core_ref, bf16[256,1024]{1,0:T(8,128)(2,1)S(1)} %get-tuple-element.24.gated_ref, bf16[256,1024]{1,0:T(8,128)(2,1)S(1)} %collective-permute-done.other_ref, bf16[8,256,512]{2,1,0:T(8,128)(2,1)S(1)} %all-to-all-done.3.cot_ref, ...), custom_call_target="tpu_custom_call" | custom-call | flops 2147483648 | bytes 8000000 | tf_op jit(solution)/shard_map/projection_gradient/pallas_call | solution.py:303
  140.8 22.8 %all-to-all-done.2 = bf16[8,256,512]{2,1,0:T(8,128)(2,1)} async-done(((bf16[8,256,512]{2,1,0:T(8,128)(2,1)}), bf16[8,256,512]{2,1,0:T(8,128)(2,1)}, u32[]{:S(2)}, u32[]{:S(2)}) %all-to-all-start.2) | async-done | bytes 2097184 | tf_op jit(solution)/shard_map/all_to_all | solution.py:246
  163.6 4.8 %all-to-all-start.5 = ((bf16[8,1024,256]{2,1,0:T(8,128)(2,1)}), bf16[8,1024,256]{2,1,0:T(8,128)(2,1)}, u32[]{:S(2)}, u32[]{:S(2)}) async-start(bf16[8,1024,256]{2,1,0:T(8,128)(2,1)} %projection_gradient.1), calls=%async_computation.5 | async-start | bytes 8388608 | tf_op jit(solution)/shard_map/all_to_all | solution.py:246
  169.3 1.2 copy-done.10
  170.5 4.0 %backward_conv.1 = (bf16[256,1024]{1,0:T(8,128)(2,1)}, bf16[256,1024]{1,0:T(8,128)(2,1)}, f32[16,8,128]{2,1,0:T(8,128)}) custom-call(s32[1]{0:T(128)} %bitcast.own_ref, bf16[16,16,8,128]{3,2,1,0:T(8,128)(2,1)S(1)} %all-to-all-done.4.sent_ref, f32[2048,128]{1,0:T(8,128)S(1)} %copy-done.10, bf16[256,1024]{1,0:T(8,128)(2,1)S(1)} %copy-done.6, ...), custom_call_target="tpu_custom_call" | custom-call | flops 5000000000 | bytes 4000000 | tf_op jit(solution)/shard_map/backward_conv/pallas_call | solution.py:358
  174.5 2.7 %reduce_sum.21 = bf16[256,512]{1,0:T(8,128)(2,1)} reduce(bf16[8,256,512]{2,1,0:T(8,128)(2,1)} %all-to-all-done.2, bf16[]{:T(256)} %constant.24.clone.1), dimensions={0}, to_apply=%region_0.1 | reduce | flops 917504 | bytes 2359298 | tf_op jit(solution)/shard_map/reduce_sum | solution.py:301
  177.2 52.2 %all-to-all-done.5 = bf16[8,1024,256]{2,1,0:T(8,128)(2,1)} async-done(((bf16[8,1024,256]{2,1,0:T(8,128)(2,1)}), bf16[8,1024,256]{2,1,0:T(8,128)(2,1)}, u32[]{:S(2)}, u32[]{:S(2)}) %all-to-all-start.5) | async-done | bytes 4194336 | tf_op jit(solution)/shard_map/all_to_all | solution.py:246
  229.4 3.8 %convert_reduce_fusion = f32[1024,256]{1,0:T(8,128)} fusion(bf16[8,1024,256]{2,1,0:T(8,128)(2,1)} %all-to-all-done.5), kind=kLoop, calls=%fused_computation | loop fusion | flops 3932160 | bytes 5242880 | tf_op jit(solution)/shard_map/reduce_sum | solution.py:321
  (54 shorter events, 15.9 us)
Async XLA Ops:
  16.9 1.0 copy-start.5
  18.0 1.0 copy-start.7
  19.0 15.8 %copy-start.17 = (bf16[256,512]{1,0:T(8,128)(2,1)S(1)}, bf16[256,512]{1,0:T(8,128)(2,1)}, u32[]{:S(2)}) copy-start(bf16[256,512]{1,0:T(8,128)(2,1)} %param.11) | copy-start | bytes 786436
  20.5 15.8 %copy-start.13 = (f32[2048,128]{1,0:T(8,128)}, f32[2048,128]{1,0:T(8,128)S(1)}, u32[]{:S(2)}) copy-start(f32[2048,128]{1,0:T(8,128)S(1)} %get-tuple-element.23.mixed_ref) | copy-start | bytes 3145732
  36.3 37.3 %all-to-all-start.3 = ((bf16[8,256,512]{2,1,0:T(8,128)(2,1)}), bf16[8,256,512]{2,1,0:T(8,128)(2,1)S(1)}, u32[]{:S(2)}, u32[]{:S(2)}) async-start(bf16[8,256,512]{2,1,0:T(8,128)(2,1)} %broadcast_in_dim.16), calls=%async_computation.3 | async-start | bytes 4194304 | tf_op jit(solution)/shard_map/all_to_all | solution.py:246
  42.1 1.0 copy-start.3
  43.2 1.2 copy-start.14
  47.3 0.8 copy-start.11
  73.7 1.0 copy-start.4
  74.7 1.0 copy-start.12
  75.7 10.6 %copy-start.15 = (f32[2048,128]{1,0:T(8,128)S(1)}, f32[2048,128]{1,0:T(8,128)}, u32[]{:S(2)}) copy-start(f32[2048,128]{1,0:T(8,128)} %copy-done.13) | copy-start | bytes 3145732
  91.3 1.0 copy-start.9
  109.6 15.9 %all-to-all-start.4 = ((bf16[16,16,8,128]{3,2,1,0:T(8,128)(2,1)}), bf16[16,16,8,128]{3,2,1,0:T(8,128)(2,1)S(1)}, u32[]{:S(2)}, u32[]{:S(2)}) async-start(bf16[16,16,8,128]{3,2,1,0:T(8,128)(2,1)} %broadcast_in_dim.17), calls=%async_computation.4 | async-start | bytes 1048576 | tf_op jit(solution)/shard_map/all_to_all | solution.py:246
  123.4 1.3 copy-start
  125.5 38.1 %all-to-all-start.2 = ((bf16[8,256,512]{2,1,0:T(8,128)(2,1)}), bf16[8,256,512]{2,1,0:T(8,128)(2,1)}, u32[]{:S(2)}, u32[]{:S(2)}) async-start(bf16[8,256,512]{2,1,0:T(8,128)(2,1)} %copy-done), calls=%async_computation.2 | async-start | bytes 4194304 | tf_op jit(solution)/shard_map/all_to_all | solution.py:246
  131.5 3.5 %collective-permute-start.1 = (bf16[8,256,256]{2,1,0:T(8,128)(2,1)S(1)}, bf16[8,256,256]{2,1,0:T(8,128)(2,1)S(1)}, u32[]{:S(2)}, u32[]{:S(2)}) collective-permute-start(bf16[8,256,256]{2,1,0:T(8,128)(2,1)S(1)} %constant_dynamic-slice_fusion), channel_id=1, source_target_pairs={{0,8},{8,0},{16,24},{24,16},{32,40},{40,32},{48,56},{56,48},{64,72... | collective-permute-start | bytes 3145736 | tf_op jit(solution)/shard_map/ppermute | solution.py:287
  131.9 3.0 %collective-permute-start = (bf16[256,1024]{1,0:T(8,128)(2,1)S(1)}, bf16[256,1024]{1,0:T(8,128)(2,1)S(1)}, u32[]{:S(2)}, u32[]{:S(2)}) collective-permute-start(bf16[256,1024]{1,0:T(8,128)(2,1)S(1)} %get-tuple-element.24.gated_ref), channel_id=1, source_target_pairs={{0,8},{8,0},{16,24},{24,16},{32,40},{40,32},{48,56},{56,48},{64,72... | collective-permute-start | bytes 1572872 | tf_op jit(solution)/shard_map/ppermute | solution.py:286
  140.8 27.6 %copy-start.16 = (f32[16,72,64]{1,2,0:T(8,128)S(1)}, f32[16,72,64]{1,2,0:T(8,128)}, u32[]{:S(2)}) copy-start(f32[16,72,64]{1,2,0:T(8,128)} %all_to_all.37) | copy-start | bytes 884740
  140.8 27.9 %copy-start.1 = (f32[64,16]{0,1:T(8,128)S(1)}, f32[64,16]{0,1:T(8,128)}, u32[]{:S(2)}) copy-start(f32[64,16]{0,1:T(8,128)} %param.13) | copy-start | bytes 12292
  140.8 27.9 %copy-start.2 = (f32[64,16]{0,1:T(8,128)S(1)}, f32[64,16]{0,1:T(8,128)}, u32[]{:S(2)}) copy-start(f32[64,16]{0,1:T(8,128)} %param.14) | copy-start | bytes 12292
  140.8 28.6 %copy-start.6 = (bf16[256,1024]{1,0:T(8,128)(2,1)S(1)}, bf16[256,1024]{1,0:T(8,128)(2,1)}, u32[]{:S(2)}) copy-start(bf16[256,1024]{1,0:T(8,128)(2,1)} %key_ref.3) | copy-start | bytes 1572868
  140.8 28.6 %copy-start.8 = (bf16[256,1024]{1,0:T(8,128)(2,1)S(1)}, bf16[256,1024]{1,0:T(8,128)(2,1)}, u32[]{:S(2)}) copy-start(bf16[256,1024]{1,0:T(8,128)(2,1)} %value_ref.3) | copy-start | bytes 1572868
  163.6 65.8 %all-to-all-start.5 = ((bf16[8,1024,256]{2,1,0:T(8,128)(2,1)}), bf16[8,1024,256]{2,1,0:T(8,128)(2,1)}, u32[]{:S(2)}, u32[]{:S(2)}) async-start(bf16[8,1024,256]{2,1,0:T(8,128)(2,1)} %projection_gradient.1), calls=%async_computation.5 | async-start | bytes 8388608 | tf_op jit(solution)/shard_map/all_to_all | solution.py:246
  169.3 1.2 copy-start.10
where the time goes:
time: 234 us; the launch traced here: 233 us
  waiting for transfers between devices  104 us (44%)
  blocking collectives  41.2 us (18%)
  Pallas kernels  37.8 us (16%)
  starting transfers between devices  23.4 us (10%)
  local copies, waits for them, and re-layouts  17.4 us (7%)
  other arithmetic  8.31 us (4%)
    all_to_all x4, waiting for transfers between devices, exchange(): lax.all_to_all(array, axis, split_axis=0, concat_axis=0, tiled=True, axis...  101 us
    all_to_all x3, blocking collectives, exchange(): lax.all_to_all(array, axis, split_axis=0, concat_axis=0, tiled=True, axis...  41.2 us
    all_to_all x4, starting transfers between devices, exchange(): lax.all_to_all(array, axis, split_axis=0, concat_axis=0, tiled=True, axis...  22.8 us
    unnamed x38, local copies, waits for them, and re-layouts  11.1 us
    pallas_call x1, Pallas kernels, local(): pl.pallas_call(cotangent_kernel, grid=(8,), out_shape=(bf16(ROWS, 1024),...  10.6 us
    pallas_call x1, Pallas kernels, local(): pl.pallas_call(output_kernel, grid=(8,), out_shape=bf16(8, ROWS, 512), in...  7.35 us
    pallas_call x1, Pallas kernels, local(): pl.pallas_call(weight_kernel, grid_spec=pltpu.PrefetchScalarGridSpec(num_...  5.79 us
    pallas_call x1, Pallas kernels, local(): pl.pallas_call(filter_kernel, out_shape=f32(72, SUB, 128), in_specs=[whol...  4.98 us
  transfers between devices with their start and end apart: 6, of which 5 were waited for; matrix products, arithmetic and copies ran while one was open for 1% of the time, Pallas kernels for 9%

commit v1 on v0

--- a/solution.py
+++ b/solution.py
@@ -14,6 +14,7 @@
 ROWS = 256
 SUB = 8
 BLOCKS = 16
+HALF = 512
 UNROLL = 8
 VMEM = 48 * 1024 * 1024
 
@@ -27,6 +28,10 @@
 
 def whole():
     return pl.BlockSpec(memory_space=pltpu.VMEM)
+
+
+def full(*shape):
+    return pl.BlockSpec(shape, lambda *_: (0,) * len(shape))
 
 
 def lanes(group):
@@ -109,11 +114,11 @@
         gated_ref[:, lanes(group)] = (query_ref[:, lanes(group)].astype(F32) * conv.astype(F32)).astype(BF16)
 
 
-def output_kernel(gated_ref, weight_ref, out_ref):
+def output_kernel(order_ref, gated_ref, weight_ref, out_ref):
     out_ref[0] = jnp.dot(gated_ref[...], weight_ref[...], preferred_element_type=F32).astype(BF16)
 
 
-def weight_kernel(core_ref, gated_ref, other_ref, cot_ref, other_cot_ref, out_ref, turned):
+def weight_kernel(place_ref, gated_ref, other_ref, cot_ref, other_cot_ref, first_ref, second_ref, turned):
     @pl.when(pl.program_id(0) == 0)
     def _():
         turned[:, :ROWS] = gated_ref[...].T
@@ -121,10 +126,11 @@
 
     total = jnp.dot(turned[:, :ROWS], cot_ref[0], preferred_element_type=F32)
     total += jnp.dot(turned[:, ROWS:], other_cot_ref[0], preferred_element_type=F32)
-    out_ref[0] = total.astype(BF16)
-
-
-def cotangent_kernel(cot_ref, weight_ref, query_ref, conv_ref, table, dquery_ref, dconv_ref, state_ref, sent_ref, total):
+    first_ref[0] = total[:HALF].astype(BF16)
+    second_ref[0] = total[HALF:].astype(BF16)
+
+
+def cotangent_kernel(order_ref, cot_ref, weight_ref, query_ref, conv_ref, table, dquery_ref, dconv_ref, state_ref, sent_ref, total):
     part = pl.program_id(0)
     product = lax.dot_general(cot_ref[0], weight_ref[...], (((1,), (1,)), ((), ())), preferred_element_type=F32)
 
@@ -250,24 +256,39 @@
     return exchange(jnp.broadcast_to(array[None], (count,) + array.shape), axis)
 
 
+def ring_shift(k):
+    return [(2 * x + z, 2 * ((x + k) % 4) + z) for x in range(4) for z in range(2)]
+
+
 def local(query, key_part, value_part, out_cotangent, w_out, residue, rate, skip):
     own = lax.axis_index("ctx")
     own_array = own.reshape(1).astype(jnp.int32)
-    core = own % 2
+    core, side = own % 2, own // 8
+    place = lax.axis_index("tp")
+    place_x, place_z = place // 2, place % 2
     smem = pl.BlockSpec(memory_space=pltpu.SMEM)
-    same_core = [[2 * chip + c for chip in range(8)] for c in range(2)]
-    swap = [(i, i ^ 1) for i in range(BLOCKS)]
+    core_swap = [(i, i ^ 1) for i in range(BLOCKS)]
+    far_swap = [(i, i ^ 8) for i in range(BLOCKS)]
+    near_swap = [(i, i ^ 1) for i in range(8)]
+    columns = [[8 * z + 2 * y + c for y in range(4)] for z in range(2) for c in range(2)]
+
+    steps = jnp.arange(8, dtype=jnp.int32)
+    came = ((place_x - steps // 2) % 4) * 2 + (place_z + steps) % 2
+    goes = ((place_x + steps // 2) % 4) * 2 + (place_z + steps) % 2
+
+    cot_pair = jnp.stack([out_cotangent, lax.ppermute(out_cotangent, "tp", near_swap)])
 
     rate_t, residue_t = rate.T, residue.T
     mine = jnp.concatenate([rate_t, residue_t, skip[None], jnp.zeros((7, skip.shape[0]), F32)], axis=0)
     table = to_all(mine, "ctx", BLOCKS).reshape(SUB, 2, 40, 64).transpose(2, 0, 1, 3).reshape(40, SUB, 128)
-    cots = to_all(out_cotangent, "tp", 8)
+    cots = jnp.concatenate([cot_pair] + [lax.ppermute(cot_pair, "tp", ring_shift(k)) for k in (1, 2, 3)])
 
     mixed, state = pl.pallas_call(
         states_kernel,
+        grid=(1,),
         out_shape=(f32(ROWS * SUB, 128), bf16(MODES, SUB, 128)),
-        in_specs=[whole()] * 3,
-        out_specs=(whole(), whole()),
+        in_specs=[full(ROWS, 1024), full(ROWS, 1024), full(40, SUB, 128)],
+        out_specs=(full(ROWS * SUB, 128), full(MODES, SUB, 128)),
         name="forward_states",
         **params_of(3_000_000_000, 4_000_000),
     )(key_part, value_part, table)
@@ -275,32 +296,38 @@
 
     conv_out, gated, carry = pl.pallas_call(
         forward_kernel,
+        grid=(1,),
         out_shape=(bf16(ROWS, 1024), bf16(ROWS, 1024), f32(MODES, SUB, 128)),
-        in_specs=[smem] + [whole()] * 4,
-        out_specs=(whole(),) * 3,
+        in_specs=[smem, full(BLOCKS, MODES, SUB, 128), full(ROWS * SUB, 128), full(ROWS, 1024), full(40, SUB, 128)],
+        out_specs=(full(ROWS, 1024), full(ROWS, 1024), full(MODES, SUB, 128)),
         scratch_shapes=[pltpu.VMEM((ROWS * SUB, 128), F32)],
         name="forward_conv",
         **params_of(5_000_000_000, 4_000_000),
     )(own_array, sent, mixed, query, table)
 
-    other_gated = lax.ppermute(gated, "ctx", swap)
-    other_cots = lax.ppermute(lax.dynamic_slice_in_dim(cots, 256 * (1 - core), 256, axis=2), "ctx", swap)
+    other_gated = lax.ppermute(gated, "ctx", core_swap)
+    other_cots = lax.ppermute(lax.dynamic_slice_in_dim(cots, 256 * (1 - core), 256, axis=2), "ctx", core_swap)
 
     partial_out = pl.pallas_call(
         output_kernel,
-        grid=(8,),
+        grid_spec=pltpu.PrefetchScalarGridSpec(
+            num_scalar_prefetch=1,
+            grid=(8,),
+            in_specs=[
+                pl.BlockSpec((ROWS, 1024), lambda p, order: (0, 0)),
+                pl.BlockSpec((1024, 512), lambda p, order: (0, order[p])),
+            ],
+            out_specs=pl.BlockSpec((1, ROWS, 512), lambda p, order: (p, 0, 0)),
+        ),
         out_shape=bf16(8, ROWS, 512),
-        in_specs=[
-            pl.BlockSpec((ROWS, 1024), lambda p: (0, 0)),
-            pl.BlockSpec((1024, 512), lambda p: (0, p)),
-        ],
-        out_specs=pl.BlockSpec((1, ROWS, 512), lambda p: (p, 0, 0)),
         name="output_projection",
         **params_of(2_147_483_648, 11_000_000),
-    )(gated, w_out)
-    output = exchange(partial_out, "tp").astype(F32).sum(axis=0).astype(BF16)
-
-    partial_weight = pl.pallas_call(
+    )(goes, gated, w_out)
+    arrived = [lax.ppermute(partial_out[2 * k : 2 * k + 2], "tp", ring_shift(k)) for k in (1, 2, 3)]
+    along_x = partial_out[:2].astype(F32) + sum(part.astype(F32) for part in arrived)
+    output = (along_x[0] + lax.ppermute(along_x[1].astype(BF16), "tp", near_swap).astype(F32)).astype(BF16)
+
+    first, second = pl.pallas_call(
         weight_kernel,
         grid_spec=pltpu.PrefetchScalarGridSpec(
             num_scalar_prefetch=1,
@@ -308,46 +335,57 @@
             in_specs=[
                 pl.BlockSpec((ROWS, 1024), lambda p, c: (0, 0)),
                 pl.BlockSpec((ROWS, 1024), lambda p, c: (0, 0)),
-                pl.BlockSpec((1, ROWS, 256), lambda p, c: (p, 0, c[0])),
+                pl.BlockSpec((1, ROWS, 256), lambda p, c: (p, 0, c[8])),
                 pl.BlockSpec((1, ROWS, 256), lambda p, c: (p, 0, 0)),
             ],
-            out_specs=pl.BlockSpec((1, 1024, 256), lambda p, c: (p, 0, 0)),
+            out_specs=(
+                pl.BlockSpec((1, HALF, 256), lambda p, c: (2 * (c[p] % 4) + (c[p] // 4 + c[9]) % 2, 0, 0)),
+                pl.BlockSpec((1, HALF, 256), lambda p, c: (4 * ((c[p] // 4 + c[9]) % 2) + c[p] % 4, 0, 0)),
+            ),
             scratch_shapes=[pltpu.VMEM((1024, 2 * ROWS), BF16)],
         ),
-        out_shape=bf16(8, 1024, 256),
+        out_shape=(bf16(8, HALF, 256), bf16(8, HALF, 256)),
         name="projection_gradient",
         **params_of(2_147_483_648, 8_000_000),
-    )(core.reshape(1).astype(jnp.int32), gated, other_gated, cots, other_cots)
-    d_weight = exchange(partial_weight, "ctx", same_core).astype(F32).sum(axis=0)
+    )(jnp.concatenate([came, jnp.stack([core, side]).astype(jnp.int32)]), gated, other_gated, cots, other_cots)
+    along_y = lax.psum_scatter(first, "ctx", scatter_dimension=0, tiled=True, axis_index_groups=columns)
+    along_z = (second[:4].astype(F32) + lax.ppermute(second[4:], "ctx", far_swap).astype(F32)).astype(BF16)
+    first_sum = along_y[0].astype(F32) + lax.ppermute(along_y[1], "ctx", far_swap).astype(F32)
+    second_sum = lax.psum_scatter(along_z, "ctx", scatter_dimension=0, tiled=True, axis_index_groups=columns)[0]
+    d_weight = jnp.concatenate([first_sum, second_sum.astype(F32)])
 
     d_query, d_conv, back, back_sent = pl.pallas_call(
         cotangent_kernel,
-        grid=(8,),
+        grid_spec=pltpu.PrefetchScalarGridSpec(
+            num_scalar_prefetch=1,
+            grid=(8,),
+            in_specs=[
+                pl.BlockSpec((1, ROWS, 512), lambda p, order: (p, 0, 0)),
+                pl.BlockSpec((1024, 512), lambda p, order: (0, order[p])),
+                full(ROWS, 1024),
+                full(ROWS, 1024),
+                full(40, SUB, 128),
+            ],
+            out_specs=(
+                full(ROWS, 1024),
+                full(ROWS * SUB, 128),
+                full(MODES, SUB, 128),
+                full(MODES, SUB, 128),
+            ),
+            scratch_shapes=[pltpu.VMEM((ROWS, 1024), F32)],
+        ),
         out_shape=(bf16(ROWS, 1024), f32(ROWS * SUB, 128), f32(MODES, SUB, 128), bf16(MODES, SUB, 128)),
-        in_specs=[
-            pl.BlockSpec((1, ROWS, 512), lambda p: (p, 0, 0)),
-            pl.BlockSpec((1024, 512), lambda p: (0, p)),
-            pl.BlockSpec((ROWS, 1024), lambda p: (0, 0)),
-            pl.BlockSpec((ROWS, 1024), lambda p: (0, 0)),
-            pl.BlockSpec((40, SUB, 128), lambda p: (0, 0, 0)),
-        ],
-        out_specs=(
-            pl.BlockSpec((ROWS, 1024), lambda p: (0, 0)),
-            pl.BlockSpec((ROWS * SUB, 128), lambda p: (0, 0)),
-            pl.BlockSpec((MODES, SUB, 128), lambda p: (0, 0, 0)),
-            pl.BlockSpec((MODES, SUB, 128), lambda p: (0, 0, 0)),
-        ),
-        scratch_shapes=[pltpu.VMEM((ROWS, 1024), F32)],
         name="cotangent_states",
         **params_of(5_000_000_000, 13_000_000),
-    )(cots, w_out, query, conv_out, table)
+    )(came, cots, w_out, query, conv_out, table)
     back_all = to_all(back_sent, "ctx", BLOCKS)
 
     parts = pl.pallas_call(
         filter_kernel,
+        grid=(1,),
         out_shape=f32(72, SUB, 128),
-        in_specs=[whole()] * 5,
-        out_specs=whole(),
+        in_specs=[full(ROWS * SUB, 128), full(ROWS * SUB, 128)] + [full(MODES, SUB, 128)] * 2 + [full(40, SUB, 128)],
+        out_specs=full(72, SUB, 128),
         name="filter_gradients",
         **params_of(9_000_000_000, 4_000_000),
     )(mixed, d_conv, carry, back, table)
@@ -357,9 +395,17 @@
 
     d_key, d_value, _ = pl.pallas_call(
         backward_kernel,
+        grid=(1,),
         out_shape=(bf16(ROWS, 1024), bf16(ROWS, 1024), f32(MODES, SUB, 128)),
-        in_specs=[smem] + [whole()] * 5,
-        out_specs=(whole(),) * 3,
+        in_specs=[
+            smem,
+            full(BLOCKS, MODES, SUB, 128),
+            full(ROWS * SUB, 128),
+            full(ROWS, 1024),
+            full(ROWS, 1024),
+            full(40, SUB, 128),
+        ],
+        out_specs=(full(ROWS, 1024), full(ROWS, 1024), full(MODES, SUB, 128)),
         scratch_shapes=[pltpu.VMEM((ROWS * SUB, 128), F32)],
         name="backward_conv",
         **params_of(5_000_000_000, 4_000_000),

time: 234 us -> 180 us (0.77)
  the two profiles are of different devices: /device:TPU:56 before, /device:TPU:0 now
where the time goes in v1:
time: 180 us; the launch traced here: 178 us
  Pallas kernels  41.7 us (23%)
  waiting for transfers between devices  31.7 us (18%)
  local copies, waits for them, and re-layouts  30.8 us (17%)
  starting transfers between devices  29.1 us (16%)
  blocking collectives  19.8 us (11%)
  between operations  14.4 us (8%)
  other arithmetic  10.5 us (6%)
    all_to_all x1, blocking collectives, exchange(): lax.all_to_all(array, axis, split_axis=0, concat_axis=0, tiled=True, axis...  19.8 us
    unnamed x54, local copies, waits for them, and re-layouts  17.3 us
    all_to_all x3, starting transfers between devices, exchange(): lax.all_to_all(array, axis, split_axis=0, concat_axis=0, tiled=True, axis...  14.7 us
    ppermute x3, waiting for transfers between devices, local(): lax.ppermute(cot_pair, 'tp', ring_shift(k))  12.7 us
    all_to_all x3, waiting for transfers between devices, exchange(): lax.all_to_all(array, axis, split_axis=0, concat_axis=0, tiled=True, axis...  11.5 us
    pallas_call x1, Pallas kernels, local(): pl.pallas_call(cotangent_kernel, grid_spec=pltpu.PrefetchScalarGridSpec(n...  11.2 us
    pallas_call x1, Pallas kernels, local(): pl.pallas_call(weight_kernel, grid_spec=pltpu.PrefetchScalarGridSpec(num_...  8.25 us
    pallas_call x1, Pallas kernels, local(): pl.pallas_call(output_kernel, grid_spec=pltpu.PrefetchScalarGridSpec(num_...  8.13 us
  transfers between devices with their start and end apart: 17, of which 7 were waited for; matrix products, arithmetic and copies ran while one was open for 16% of the time, Pallas kernels for 19%

profile of v1, /device:TPU:0, one launch (start us, length us, event | category | flops | bytes accessed | tf_op | source)
XLA Modules:
  0.0 177.9 jit_solution(14630558695057978622)
XLA Ops:
  7.2 2.1 %collective-permute-start.4 = (bf16[256,512]{1,0:T(8,128)(2,1)}, bf16[256,512]{1,0:T(8,128)(2,1)S(1)}, u32[]{:S(2)}, u32[]{:S(2)}) collective-permute-start(bf16[256,512]{1,0:T(8,128)(2,1)} %param.11), channel_id=1, source_target_pairs={{0,1},{1,0},{2,3},{3,2},{4,5},{5,4},{6,7},{7,6},{8,9},{9,8},{10,11... | collective-permute-start | bytes 786440 | tf_op jit(solution)/shard_map/ppermute | solution.py:279
  11.1 7.6 %all-to-all-start = ((f32[16,1,2560]{2,1,0:T(1,128)}), f32[16,1,2560]{2,1,0:T(1,128)S(1)}, u32[]{:S(2)}, u32[]{:S(2)}) async-start(f32[16,1,2560]{2,1,0:T(1,128)} %reshape.46), calls=%async_computation | async-start | bytes 327680 | tf_op jit(solution)/shard_map/all_to_all | solution.py:252
  18.7 1.9 %pad_maximum_fusion.1 = bf16[2,256,512]{2,1,0:T(8,128)(2,1)} fusion(bf16[1,256,512]{2,1,0:T(8,128)(2,1)S(1)} %bitcast.46, bf16[1,256,512]{2,1,0:T(8,128)(2,1)} %bitcast.45), kind=kLoop, calls=%fused_computation.7 | loop fusion | flops 262144 | bytes 1048576 | tf_op jit(solution)/shard_map/stack | solution.py:279
  23.1 3.9 %all-to-all-done = f32[16,1,2560]{2,1,0:T(1,128)S(1)} async-done(((f32[16,1,2560]{2,1,0:T(1,128)}), f32[16,1,2560]{2,1,0:T(1,128)S(1)}, u32[]{:S(2)}, u32[]{:S(2)}) %all-to-all-start) | async-done | bytes 163872 | tf_op jit(solution)/shard_map/all_to_all | solution.py:252
  29.3 1.9 %copy.22 = f32[8,2,40,64]{3,1,0,2:T(2,128)} copy(f32[8,2,40,64]{3,2,1,0:T(8,128)} %bitcast.43) | data formatting | bytes 327680 | tf_op jit(solution)/shard_map/reshape | solution.py:283
  32.4 3.1 %collective-permute-start.6 = (bf16[2,256,512]{2,1,0:T(8,128)(2,1)}, bf16[2,256,512]{2,1,0:T(8,128)(2,1)}, u32[]{:S(2)}, u32[]{:S(2)}) collective-permute-start(bf16[2,256,512]{2,1,0:T(8,128)(2,1)} %pad_maximum_fusion.1), channel_id=1, source_target_pairs={{0,4},{1,5},{2,6},{3,7},{4,0},{5,1},{6,2},{7,3},{8,12},{9,13},{10,... | collective-permute-start | bytes 1572872 | tf_op jit(solution)/shard_map/ppermute | solution.py:284
  36.6 1.5 forward_states.1
  40.0 3.6 %all-to-all-start.1 = ((bf16[16,16,8,128]{3,2,1,0:T(8,128)(2,1)}), bf16[16,16,8,128]{3,2,1,0:T(8,128)(2,1)S(1)}, u32[]{:S(2)}, u32[]{:S(2)}) async-start(bf16[16,16,8,128]{3,2,1,0:T(8,128)(2,1)} %broadcast_in_dim.13), calls=%async_computation.1 | async-start | bytes 1048576 | tf_op jit(solution)/shard_map/all_to_all | solution.py:252
  45.7 2.9 %collective-permute-done.6 = bf16[2,256,512]{2,1,0:T(8,128)(2,1)} collective-permute-done((bf16[2,256,512]{2,1,0:T(8,128)(2,1)}, bf16[2,256,512]{2,1,0:T(8,128)(2,1)}, u32[]{:S(2)}, u32[]{:S(2)}) %collective-permute-start.6) | collective-permute-done | bytes 524320 | tf_op jit(solution)/shard_map/ppermute | solution.py:284
  49.7 9.8 %collective-permute-done.7 = bf16[2,256,512]{2,1,0:T(8,128)(2,1)} collective-permute-done((bf16[2,256,512]{2,1,0:T(8,128)(2,1)}, bf16[2,256,512]{2,1,0:T(8,128)(2,1)}, u32[]{:S(2)}, u32[]{:S(2)}) %collective-permute-start.7) | collective-permute-done | bytes 524320 | tf_op jit(solution)/shard_map/ppermute | solution.py:284
  64.0 3.0 %forward_conv.1 = (bf16[256,1024]{1,0:T(8,128)(2,1)S(1)}, bf16[256,1024]{1,0:T(8,128)(2,1)S(1)}, f32[16,8,128]{2,1,0:T(8,128)S(1)}) custom-call(s32[1]{0:T(128)} %bitcast.own_ref, bf16[16,16,8,128]{3,2,1,0:T(8,128)(2,1)S(1)} %all-to-all-done.1.sent_ref, f32[2048,128]{1,0:T(8,128)S(1)} %copy-done.16, bf16[256,1024]{1,0:T(8,128)(2,1)S(1)} %copy-done.4, ...), custom_call_target="tpu_custom_call" | custom-call | flops 5000000000 | bytes 4000000 | tf_op jit(solution)/shard_map/forward_conv/pallas_call | solution.py:297
  69.8 8.2 %projection_gradient.1 = (bf16[8,512,256]{2,1,0:T(8,128)(2,1)}, bf16[8,512,256]{2,1,0:T(8,128)(2,1)}) custom-call(s32[10]{0:T(128)S(1)} %pad_add_fusion.place_ref, bf16[256,1024]{1,0:T(8,128)(2,1)S(1)} %get-tuple-element.26.gated_ref, bf16[256,1024]{1,0:T(8,128)(2,1)S(1)} %collective-permute-done.8.other_ref, bf16[8,256,512]{2,1,0:T(8,128)(2,1)} %copy-done, ...), custom_call_target="tpu_custom_call" | custom-call | flops 2147483648 | bytes 8000000 | tf_op jit(solution)/shard_map/projection_gradient/pallas_call | solution.py:330
  78.1 1.5 copy-done.20
  80.6 8.1 %output_projection.1 = bf16[8,256,512]{2,1,0:T(8,128)(2,1)S(1)} custom-call(s32[8]{0:T(128)S(1)} %fusion.4.order_ref, bf16[256,1024]{1,0:T(8,128)(2,1)S(1)} %get-tuple-element.26.gated_ref, bf16[1024,4096]{1,0:T(8,128)(2,1)} %weight_ref.3), custom_call_target="tpu_custom_call" | custom-call | flops 2147483648 | bytes 11000000 | tf_op jit(solution)/shard_map/output_projection/pallas_call | solution.py:311
  91.3 2.8 %collective-permute-start.1 = (bf16[2,256,512]{2,1,0:T(8,128)(2,1)}, bf16[2,256,512]{2,1,0:T(8,128)(2,1)}, u32[]{:S(2)}, u32[]{:S(2)}) collective-permute-start(bf16[2,256,512]{2,1,0:T(8,128)(2,1)} %get-tuple-element.42), channel_id=1, source_target_pairs={{0,4},{1,5},{2,6},{3,7},{4,0},{5,1},{6,2},{7,3},{8,12},{9,13},{10,... | collective-permute-start | bytes 1572872 | tf_op jit(solution)/shard_map/ppermute | solution.py:326
  94.4 11.2 %cotangent_states.1 = (bf16[256,1024]{1,0:T(8,128)(2,1)}, f32[2048,128]{1,0:T(8,128)S(1)}, f32[16,8,128]{2,1,0:T(8,128)S(1)}, bf16[16,8,128]{2,1,0:T(8,128)(2,1)S(1)}) custom-call(s32[8]{0:T(128)S(1)} %fusion.6.order_ref, bf16[8,256,512]{2,1,0:T(8,128)(2,1)S(1)} %copy-done.1, bf16[1024,4096]{1,0:T(8,128)(2,1)} %weight_ref.3, ...), custom_call_target="tpu_custom_call" | custom-call | flops 5000000000 | bytes 13000000 | tf_op jit(solution)/shard_map/cotangent_states/pallas_call | solution.py:357
  110.4 5.0 %filter_gradients.1 = f32[72,8,128]{2,1,0:T(8,128)S(1)} custom-call(f32[2048,128]{1,0:T(8,128)S(1)} %copy-done.17, f32[2048,128]{1,0:T(8,128)S(1)} %copy-done.11, f32[16,8,128]{2,1,0:T(8,128)S(1)} %get-tuple-element.35.carry_ref, f32[16,8,128]{2,1,0:T(8,128)S(1)} %get-tuple-element.36.back_ref, f32[40,8,128]{2,1,0:T(8,128)S(1)} %reshape.41.table), custom_call_target="tpu_custom_call" | custom-call | flops 8999999488 | bytes 4000000 | tf_op jit(solution)/shard_map/filter_gradients/pallas_call | solution.py:383
  116.8 19.8 %all_to_all.20 = f32[16,72,64]{1,2,0:T(8,128)} all-to-all(f32[16,72,64]{1,2,0:T(8,128)} %copy.19), channel_id=1, replica_groups=mesh['ctx'=16,'tp'=8] {'ctx'}, dimensions={0} | all-to-all | bytes 589824 | tf_op jit(solution)/shard_map/all_to_all | solution.py:252
  137.6 3.6 %all-to-all-start.2 = ((bf16[16,16,8,128]{3,2,1,0:T(8,128)(2,1)}), bf16[16,16,8,128]{3,2,1,0:T(8,128)(2,1)S(1)}, u32[]{:S(2)}, u32[]{:S(2)}) async-start(bf16[16,16,8,128]{3,2,1,0:T(8,128)(2,1)} %broadcast_in_dim.28), calls=%async_computation.2 | async-start | bytes 1048576 | tf_op jit(solution)/shard_map/all_to_all | solution.py:252
  143.1 1.7 add_add_fusion
  145.9 7.6 %all-to-all-done.2.sent_ref = bf16[16,16,8,128]{3,2,1,0:T(8,128)(2,1)S(1)} async-done(((bf16[16,16,8,128]{3,2,1,0:T(8,128)(2,1)}), bf16[16,16,8,128]{3,2,1,0:T(8,128)(2,1)S(1)}, u32[]{:S(2)}, u32[]{:S(2)}) %all-to-all-start.2) | async-done | bytes 524320 | tf_op jit(solution)/shard_map/all_to_all | solution.py:252
  155.8 4.0 %backward_conv.1 = (bf16[256,1024]{1,0:T(8,128)(2,1)}, bf16[256,1024]{1,0:T(8,128)(2,1)}, f32[16,8,128]{2,1,0:T(8,128)}) custom-call(s32[1]{0:T(128)} %bitcast.own_ref, bf16[16,16,8,128]{3,2,1,0:T(8,128)(2,1)S(1)} %all-to-all-done.2.sent_ref, f32[2048,128]{1,0:T(8,128)S(1)} %copy-done.12, bf16[256,1024]{1,0:T(8,128)(2,1)S(1)} %copy-done.7, ...), custom_call_target="tpu_custom_call" | custom-call | flops 5000000000 | bytes 4000000 | tf_op jit(solution)/shard_map/backward_conv/pallas_call | solution.py:396
  161.4 1.7 fusion.1
  164.1 5.9 %collective-permute-done.10 = bf16[512,256]{1,0:T(8,128)(2,1)S(1)} collective-permute-done((bf16[512,256]{1,0:T(8,128)(2,1)S(1)}, bf16[512,256]{1,0:T(8,128)(2,1)S(1)}, u32[]{:S(2)}, u32[]{:S(2)}) %collective-permute-start.10) | collective-permute-done | bytes 262176 | tf_op jit(solution)/shard_map/ppermute | solution.py:353
  (104 shorter events, 41.3 us)
Async XLA Ops:
  7.2 11.5 %collective-permute-start.4 = (bf16[256,512]{1,0:T(8,128)(2,1)}, bf16[256,512]{1,0:T(8,128)(2,1)S(1)}, u32[]{:S(2)}, u32[]{:S(2)}) collective-permute-start(bf16[256,512]{1,0:T(8,128)(2,1)} %param.11), channel_id=1, source_target_pairs={{0,1},{1,0},{2,3},{3,2},{4,5},{5,4},{6,7},{7,6},{8,9},{9,8},{10,11... | collective-permute-start | bytes 786440 | tf_op jit(solution)/shard_map/ppermute | solution.py:279
  10.2 26.4 %copy-start.6 = (bf16[256,1024]{1,0:T(8,128)(2,1)S(1)}, bf16[256,1024]{1,0:T(8,128)(2,1)}, u32[]{:S(2)}) copy-start(bf16[256,1024]{1,0:T(8,128)(2,1)} %key_ref.3) | copy-start | bytes 1572868
  10.2 26.4 %copy-start.8 = (bf16[256,1024]{1,0:T(8,128)(2,1)S(1)}, bf16[256,1024]{1,0:T(8,128)(2,1)}, u32[]{:S(2)}) copy-start(bf16[256,1024]{1,0:T(8,128)(2,1)} %value_ref.3) | copy-start | bytes 1572868
  11.1 15.9 %all-to-all-start = ((f32[16,1,2560]{2,1,0:T(1,128)}), f32[16,1,2560]{2,1,0:T(1,128)S(1)}, u32[]{:S(2)}, u32[]{:S(2)}) async-start(f32[16,1,2560]{2,1,0:T(1,128)} %reshape.46), calls=%async_computation | async-start | bytes 327680 | tf_op jit(solution)/shard_map/all_to_all | solution.py:252
  20.6 24.0 %collective-permute-start.5 = (bf16[2,256,512]{2,1,0:T(8,128)(2,1)}, bf16[2,256,512]{2,1,0:T(8,128)(2,1)}, u32[]{:S(2)}, u32[]{:S(2)}) collective-permute-start(bf16[2,256,512]{2,1,0:T(8,128)(2,1)} %pad_maximum_fusion.1), channel_id=1, source_target_pairs={{0,2},{1,3},{2,4},{3,5},{4,6},{5,7},{6,0},{7,1},{8,10},{9,11},{10,... | collective-permute-start | bytes 1572872 | tf_op jit(solution)/shard_map/ppermute | solution.py:284
  32.4 16.2 %collective-permute-start.6 = (bf16[2,256,512]{2,1,0:T(8,128)(2,1)}, bf16[2,256,512]{2,1,0:T(8,128)(2,1)}, u32[]{:S(2)}, u32[]{:S(2)}) collective-permute-start(bf16[2,256,512]{2,1,0:T(8,128)(2,1)} %pad_maximum_fusion.1), channel_id=1, source_target_pairs={{0,4},{1,5},{2,6},{3,7},{4,0},{5,1},{6,2},{7,3},{8,12},{9,13},{10,... | collective-permute-start | bytes 1572872 | tf_op jit(solution)/shard_map/ppermute | solution.py:284
  35.5 24.0 %collective-permute-start.7 = (bf16[2,256,512]{2,1,0:T(8,128)(2,1)}, bf16[2,256,512]{2,1,0:T(8,128)(2,1)}, u32[]{:S(2)}, u32[]{:S(2)}) collective-permute-start(bf16[2,256,512]{2,1,0:T(8,128)(2,1)} %pad_maximum_fusion.1), channel_id=1, source_target_pairs={{0,6},{1,7},{2,0},{3,1},{4,2},{5,3},{6,4},{7,5},{8,14},{9,15},{10,... | collective-permute-start | bytes 1572872 | tf_op jit(solution)/shard_map/ppermute | solution.py:284
  40.0 21.7 %all-to-all-start.1 = ((bf16[16,16,8,128]{3,2,1,0:T(8,128)(2,1)}), bf16[16,16,8,128]{3,2,1,0:T(8,128)(2,1)S(1)}, u32[]{:S(2)}, u32[]{:S(2)}) async-start(bf16[16,16,8,128]{3,2,1,0:T(8,128)(2,1)} %broadcast_in_dim.13), calls=%async_computation.1 | async-start | bytes 1048576 | tf_op jit(solution)/shard_map/all_to_all | solution.py:252
  43.6 116.2 %reduce-scatter.3.cloned.1.call-start = ((), (), s32[]{:S(2)}) async-start(), calls=%async_computation.6 | async-start | bytes 2621440 | tf_op jit(solution)/shard_map/reduce_scatter | solution.py:351
  61.7 8.1 %collective-permute-start.9 = (bf16[8,256,256]{2,1,0:T(8,128)(2,1)}, bf16[8,256,256]{2,1,0:T(8,128)(2,1)}, u32[]{:S(2)}, u32[]{:S(2)}) collective-permute-start(bf16[8,256,256]{2,1,0:T(8,128)(2,1)} %constant_dynamic-slice_fusion), channel_id=1, source_target_pairs={{0,8},{8,0},{16,24},{24,16},{32,40},{40,32},{48,56},{56,48},{64,72... | collective-permute-start | bytes 3145736 | tf_op jit(solution)/shard_map/ppermute | solution.py:309
  67.7 2.0 %collective-permute-start.8 = (bf16[256,1024]{1,0:T(8,128)(2,1)S(1)}, bf16[256,1024]{1,0:T(8,128)(2,1)S(1)}, u32[]{:S(2)}, u32[]{:S(2)}) collective-permute-start(bf16[256,1024]{1,0:T(8,128)(2,1)S(1)} %get-tuple-element.26.gated_ref), channel_id=1, source_target_pairs={{0,8},{8,0},{16,24},{24,16},{32,40},{40,32},{48,56},{56,48},{64,72... | collective-permute-start | bytes 1572872 | tf_op jit(solution)/shard_map/ppermute | solution.py:308
  78.1 85.0 %reduce-scatter.5.cloned.1.call-start = ((), (), s32[]{:S(2)}) async-start(), calls=%async_computation.7 | async-start | bytes 1310720 | tf_op jit(solution)/shard_map/reduce_scatter | solution.py:354
  79.7 27.0 %collective-permute-start.11 = (bf16[4,512,256]{2,1,0:T(8,128)(2,1)S(1)}, bf16[4,512,256]{2,1,0:T(8,128)(2,1)S(1)}, u32[]{:S(2)}, u32[]{:S(2)}) collective-permute-start(bf16[4,512,256]{2,1,0:T(8,128)(2,1)S(1)} %slice.40), channel_id=1, source_target_pairs={{0,64},{8,72},{16,80},{24,88},{32,96},{40,104},{48,112},{56,120},{... | collective-permute-start | bytes 3145736 | tf_op jit(solution)/shard_map/ppermute | solution.py:352
  89.9 53.2 %collective-permute-start = (bf16[2,256,512]{2,1,0:T(8,128)(2,1)}, bf16[2,256,512]{2,1,0:T(8,128)(2,1)}, u32[]{:S(2)}, u32[]{:S(2)}) collective-permute-start(bf16[2,256,512]{2,1,0:T(8,128)(2,1)} %get-tuple-element.40), channel_id=1, source_target_pairs={{0,2},{1,3},{2,4},{3,5},{4,6},{5,7},{6,0},{7,1},{8,10},{9,11},{10,... | collective-permute-start | bytes 1572872 | tf_op jit(solution)/shard_map/ppermute | solution.py:326
  91.3 51.8 %collective-permute-start.1 = (bf16[2,256,512]{2,1,0:T(8,128)(2,1)}, bf16[2,256,512]{2,1,0:T(8,128)(2,1)}, u32[]{:S(2)}, u32[]{:S(2)}) collective-permute-start(bf16[2,256,512]{2,1,0:T(8,128)(2,1)} %get-tuple-element.42), channel_id=1, source_target_pairs={{0,4},{1,5},{2,6},{3,7},{4,0},{5,1},{6,2},{7,3},{8,12},{9,13},{10,... | collective-permute-start | bytes 1572872 | tf_op jit(solution)/shard_map/ppermute | solution.py:326
  94.1 49.1 %collective-permute-start.2 = (bf16[2,256,512]{2,1,0:T(8,128)(2,1)}, bf16[2,256,512]{2,1,0:T(8,128)(2,1)}, u32[]{:S(2)}, u32[]{:S(2)}) collective-permute-start(bf16[2,256,512]{2,1,0:T(8,128)(2,1)} %get-tuple-element.41), channel_id=1, source_target_pairs={{0,6},{1,7},{2,0},{3,1},{4,2},{5,3},{6,4},{7,5},{8,14},{9,15},{10,... | collective-permute-start | bytes 1572872 | tf_op jit(solution)/shard_map/ppermute | solution.py:326
  94.4 12.3 %copy-start.21 = (bf16[8,512,256]{2,1,0:T(8,128)(2,1)S(1)}, bf16[8,512,256]{2,1,0:T(8,128)(2,1)}, u32[]{:S(2)}) copy-start(bf16[8,512,256]{2,1,0:T(8,128)(2,1)} %get-tuple-element.34) | copy-start | bytes 6291460
  116.8 25.6 %copy-start.2 = (f32[64,16]{0,1:T(8,128)S(1)}, f32[64,16]{0,1:T(8,128)}, u32[]{:S(2)}) copy-start(f32[64,16]{0,1:T(8,128)} %param.13) | copy-start | bytes 12292
  116.8 25.6 %copy-start.3 = (f32[64,16]{0,1:T(8,128)S(1)}, f32[64,16]{0,1:T(8,128)}, u32[]{:S(2)}) copy-start(f32[64,16]{0,1:T(8,128)} %param.14) | copy-start | bytes 12292
  137.6 15.9 %all-to-all-start.2 = ((bf16[16,16,8,128]{3,2,1,0:T(8,128)(2,1)}), bf16[16,16,8,128]{3,2,1,0:T(8,128)(2,1)S(1)}, u32[]{:S(2)}, u32[]{:S(2)}) async-start(bf16[16,16,8,128]{3,2,1,0:T(8,128)(2,1)} %broadcast_in_dim.28), calls=%async_computation.2 | async-start | bytes 1048576 | tf_op jit(solution)/shard_map/all_to_all | solution.py:252
  143.1 10.4 %copy-start.7 = (bf16[256,1024]{1,0:T(8,128)(2,1)S(1)}, bf16[256,1024]{1,0:T(8,128)(2,1)}, u32[]{:S(2)}) copy-start(bf16[256,1024]{1,0:T(8,128)(2,1)} %key_ref.3) | copy-start | bytes 1572868
  145.9 15.5 %collective-permute-start.3 = (bf16[256,512]{1,0:T(8,128)(2,1)}, bf16[256,512]{1,0:T(8,128)(2,1)}, u32[]{:S(2)}, u32[]{:S(2)}) collective-permute-start(bf16[256,512]{1,0:T(8,128)(2,1)} %fusion.2), channel_id=1, source_target_pairs={{0,1},{1,0},{2,3},{3,2},{4,5},{5,4},{6,7},{7,6},{8,9},{9,8},{10,11... | collective-permute-start | bytes 786440 | tf_op jit(solution)/shard_map/ppermute | solution.py:328
  159.7 10.3 %copy-start.23 = (bf16[2,512,256]{2,1,0:T(8,128)(2,1)S(1)}, bf16[2,512,256]{2,1,0:T(8,128)(2,1)}, u32[]{:S(2)}) copy-start(bf16[2,512,256]{2,1,0:T(8,128)(2,1)} %reduce-scatter.3.cloned.1.call-done) | copy-start | bytes 1572868
  160.8 9.2 %collective-permute-start.10 = (bf16[512,256]{1,0:T(8,128)(2,1)S(1)}, bf16[512,256]{1,0:T(8,128)(2,1)S(1)}, u32[]{:S(2)}, u32[]{:S(2)}) collective-permute-start(bf16[512,256]{1,0:T(8,128)(2,1)S(1)} %slice_bitcast_fusion.1), channel_id=1, source_target_pairs={{0,64},{8,72},{16,80},{24,88},{32,96},{40,104},{48,112},{56,120},{... | collective-permute-start | bytes 786440 | tf_op jit(solution)/shard_map/ppermute | solution.py:353
  (17 other events, 43.3 us)
Sparse Core Ops, SparseCore 0:
  78.2 26.5 reduce-scatter.2
  108.1 26.9 reduce-scatter.4

commit v2 on v1

v2 whole, which is shorter than its diff:
```python
import functools

import jax
import jax.numpy as jnp
from jax import lax
from jax.experimental import pallas as pl
from jax.experimental.pallas import tpu as pltpu
from jax.sharding import PartitionSpec as P

F32 = jnp.float32
BF16 = jnp.bfloat16
SEQ = 4096
MODES = 16
ROWS = 256
SUB = 8
BLOCKS = 16
HALF = 512
UNROLL = 8
PACK = 24
TABLE = 2 * PACK * SUB
TERMS = 40
VMEM = 40 * 1024 * 1024


def params_of(flops, nbytes):
    return dict(
        compiler_params=pltpu.CompilerParams(vmem_limit_bytes=VMEM),
        cost_estimate=pl.CostEstimate(flops=flops, bytes_accessed=nbytes, transcendentals=0),
    )


def whole():
    return pl.BlockSpec(memory_space=pltpu.VMEM)


def full(*shape):
    return pl.BlockSpec(shape, lambda *_: (0,) * len(shape))


def lanes(group):
    return slice(128 * group, 128 * (group + 1))


def group_rows(group):
    return pl.ds(group, ROWS, stride=SUB)


def rate_of(table, mode):
    return table[SUB * mode : SUB * (mode + 1), :]


def step_decay(table, mode):
    return jnp.exp(rate_of(table, mode) * (-1.0 / SEQ))


def block_decay(table, mode):
    return jnp.exp(rate_of(table, mode) * (-float(ROWS) / SEQ))


def mode_weight(table, mode):
    return rate_of(table, PACK + mode) * jnp.sqrt(rate_of(table, mode) * (2.0 / SEQ))


def skip_of(table):
    return rate_of(table, MODES)


def at(ref, step):
    return ref[pl.ds(pl.multiple_of(step * SUB, SUB), SUB), :]


def zeros(count):
    return tuple(jnp.zeros((SUB, 128), F32) for _ in range(count))


def tree_sum(parts):
    parts = list(parts)
    while len(parts) > 1:
        parts = [sum(parts[i : i + 2]) for i in range(0, len(parts), 2)]
    return parts[0]


def states_kernel(key_ref, value_ref, packed_ref, mixed_ref, sent_ref, table):
    left = lax.broadcasted_iota(jnp.int32, (PACK, 128), 1) < 64
    for group in range(SUB):
        one, two = packed_ref[2 * group], packed_ref[2 * group + 1]
        table[pl.ds(group, PACK, stride=SUB), :] = jnp.where(left, one, pltpu.roll(two, 64, 1))
        table[pl.ds(PACK * SUB + group, PACK, stride=SUB), :] = jnp.where(left, pltpu.roll(one, 64, 1), two)
        product = key_ref[:, lanes(group)].astype(F32) * value_ref[:, lanes(group)].astype(F32)
        mixed_ref[group_rows(group), :] = product.astype(BF16).astype(F32)
    decay = [step_decay(table, m) for m in range(MODES)]

    def body(i, held):
        for u in range(UNROLL):
            value = at(mixed_ref, i * UNROLL + u)
            held = tuple(decay[m] * held[m] + value for m in range(MODES))
        return held

    held = lax.fori_loop(0, ROWS // UNROLL, body, zeros(MODES))
    for m in range(MODES):
        state = held[m].astype(BF16)
        for j in range(BLOCKS):
            sent_ref[j, m] = state


def forward_kernel(own_ref, sent_ref, mixed_ref, query_ref, table, conv_ref, gated_ref, carry_ref, buffer):
    own = own_ref[0]
    for m in range(MODES):
        far = block_decay(table, m)
        carry = jnp.zeros((SUB, 128), F32)
        for j in range(BLOCKS - 1):
            carry = jnp.where(j < own, far * carry + sent_ref[j, m].astype(F32), carry)
        carry_ref[m] = carry
    decay = [step_decay(table, m) for m in range(MODES)]
    weight = [mode_weight(table, m) for m in range(MODES)]
    skip = skip_of(table)

    def body(i, held):
        for u in range(UNROLL):
            step = i * UNROLL + u
            value = at(mixed_ref, step)
            held = tuple(decay[m] * held[m] + value for m in range(MODES))
            total = tree_sum([weight[m] * held[m] for m in range(MODES)])
            buffer[pl.ds(pl.multiple_of(step * SUB, SUB), SUB), :] = total + skip * value
        return held

    lax.fori_loop(0, ROWS // UNROLL, body, tuple(carry_ref[m] for m in range(MODES)))
    for group in range(SUB):
        conv = buffer[group_rows(group), :].astype(BF16)
        conv_ref[:, lanes(group)] = conv
        gated_ref[:, lanes(group)] = (query_ref[:, lanes(group)].astype(F32) * conv.astype(F32)).astype(BF16)


def output_kernel(order_ref, gated_ref, weight_ref, *out_refs):
    for i in range(8):
        columns = pl.ds(pl.multiple_of(order_ref[i] * 512, 512), 512)
        out_refs[i // 2][i % 2] = jnp.dot(gated_ref[...], weight_ref[:, columns], preferred_element_type=F32).astype(BF16)


def weight_kernel(index_ref, gated_ref, other_ref, cot_ref, other_cot_ref, *refs):
    along_y, along_z, turned = refs[:4], refs[4:6], refs[6]
    turned[:, :ROWS] = gated_ref[...].T
    turned[:, ROWS:] = other_ref[...].T
    for z in (1, 0):
        for k in range(4):
            block = index_ref[4 * z + k]
            total = jnp.dot(turned[:, :ROWS], cot_ref[block], preferred_element_type=F32)
            total += jnp.dot(turned[:, ROWS:], other_cot_ref[block], preferred_element_type=F32)
            along_y[k][z] = total[:HALF].astype(BF16)
            along_z[z][k] = total[HALF:].astype(BF16)


def cotangent_kernel(order_ref, cot_ref, weight_ref, query_ref, conv_ref, table, dquery_ref, dconv_ref, state_ref, sent_ref, total):
    for i in range(8):
        columns = pl.ds(pl.multiple_of(order_ref[i] * 512, 512), 512)
        product = lax.dot_general(cot_ref[i], weight_ref[:, columns], (((1,), (1,)), ((), ())), preferred_element_type=F32)
        if i == 0:
            total[...] = product
        else:
            total[...] += product
    for group in range(SUB):
        cot = total[:, lanes(group)]
        dquery_ref[:, lanes(group)] = (cot * conv_ref[:, lanes(group)].astype(F32)).astype(BF16)
        dconv_ref[group_rows(group), :] = (cot * query_ref[:, lanes(group)].astype(F32)).astype(BF16).astype(F32)
    decay = [step_decay(table, m) for m in range(MODES)]

    def body(i, held):
        for u in range(UNROLL):
            value = at(dconv_ref, ROWS - 1 - (i * UNROLL + u))
            held = tuple(decay[m] * held[m] + value for m in range(MODES))
        return held

    held = lax.fori_loop(0, ROWS // UNROLL, body, zeros(MODES))
    for m in range(MODES):
        state_ref[m] = held[m]
        state = held[m].astype(BF16)
        for j in range(BLOCKS):
            sent_ref[j, m] = state


def filter_kernel(mixed_ref, dconv_ref, carry_ref, back_ref, table, out_ref):
    left = lax.broadcasted_iota(jnp.int32, (SUB, 128), 1) < 64

    def put(row, one, two):
        out_ref[pl.ds(row, SUB, stride=2 * TERMS), :] = jnp.where(left, one, pltpu.roll(two, 64, 1))
        out_ref[pl.ds(TERMS + row, SUB, stride=2 * TERMS), :] = jnp.where(left, pltpu.roll(one, 64, 1), two)

    half = MODES // 2
    for first in (0, half):
        modes = range(first, first + half)
        decay = [step_decay(table, m) for m in modes]

        def body(i, packed):
            held, moment, first_sum, second_sum, skip_sum = packed
            for u in range(UNROLL):
                value = at(mixed_ref, i * UNROLL + u)
                cot = at(dconv_ref, i * UNROLL + u)
                past = [decay[m] * held[m] for m in range(half)]
                moment = tuple(decay[m] * moment[m] + past[m] for m in range(half))
                held = tuple(past[m] + value for m in range(half))
                first_sum = tuple(first_sum[m] + cot * held[m] for m in range(half))
                second_sum = tuple(second_sum[m] + cot * moment[m] for m in range(half))
                skip_sum = skip_sum + cot * value
            return (held, moment, first_sum, second_sum, skip_sum)

        start = (tuple(carry_ref[m] for m in modes), zeros(half), zeros(half), zeros(half), zeros(1)[0])
        held, moment, first_sum, second_sum, skip_sum = lax.fori_loop(0, ROWS // UNROLL, body, start)
        for m in range(half):
            put(first + m, first_sum[m], second_sum[m])
            put(MODES + first + m, moment[m], back_ref[first + m])
    for row in range(2 * MODES, TERMS):
        put(row, skip_sum, skip_sum)


def backward_kernel(own_ref, sent_ref, dconv_ref, key_ref, value_ref, table, dkey_ref, dvalue_ref, carry_ref, buffer):
    own = own_ref[0]
    for m in range(MODES):
        far = block_decay(table, m)
        carry = jnp.zeros((SUB, 128), F32)
        for j in range(BLOCKS - 1, 0, -1):
            carry = jnp.where(j > own, far * carry + sent_ref[j, m].astype(F32), carry)
        carry_ref[m] = carry
    decay = [step_decay(table, m) for m in range(MODES)]
    weight = [mode_weight(table, m) for m in range(MODES)]
    skip = skip_of(table)

    def body(i, held):
        for u in range(UNROLL):
            step = ROWS - 1 - (i * UNROLL + u)
            value = at(dconv_ref, step)
            held = tuple(decay[m] * held[m] + value for m in range(MODES))
            total = tree_sum([weight[m] * held[m] for m in range(MODES)])
            buffer[pl.ds(pl.multiple_of(step * SUB, SUB), SUB), :] = total + skip * value
        return held

    lax.fori_loop(0, ROWS // UNROLL, body, tuple(carry_ref[m] for m in range(MODES)))
    for group in range(SUB):
        grad = buffer[group_rows(group), :].astype(BF16).astype(F32)
        dkey_ref[:, lanes(group)] = (grad * value_ref[:, lanes(group)].astype(F32)).astype(BF16)
        dvalue_ref[:, lanes(group)] = (grad * key_ref[:, lanes(group)].astype(F32)).astype(BF16)


def owner_kernel(parts_ref, rate_ref, residue_ref, dresidue_ref, drate_ref, dskip_ref):
    rate = rate_ref[...]
    residue = residue_ref[...]
    near = jnp.exp(rate * (-1.0 / SEQ))
    far = jnp.exp(rate * (-float(ROWS) / SEQ))
    scale = jnp.sqrt(rate * (2.0 / SEQ))
    first = jnp.zeros_like(rate)
    second = jnp.zeros_like(rate)
    skip = jnp.zeros((1, rate.shape[1]), F32)
    later = jnp.zeros_like(rate)
    for j in range(BLOCKS - 1, -1, -1):
        sums, ends = parts_ref[j, 0:MODES], parts_ref[j, MODES : 2 * MODES]
        first += sums[:, :64]
        second += sums[:, 64:] + near * later * ends[:, :64]
        later = far * later + ends[:, 64:]
        skip += parts_ref[j, 2 * MODES : 2 * MODES + 1, :64]
    proj = scale * first
    dresidue_ref[...] = proj
    drate_ref[...] = residue * (0.5 * proj / rate - scale * second * (1.0 / SEQ))
    dskip_ref[...] = skip


def f32(*shape):
    return jax.ShapeDtypeStruct(shape, F32)


def bf16(*shape):
    return jax.ShapeDtypeStruct(shape, BF16)


def exchange(array, axis, groups=None):
    return lax.all_to_all(array, axis, split_axis=0, concat_axis=0, tiled=True, axis_index_groups=groups)


def to_all(array, axis, count):
    return exchange(jnp.broadcast_to(array[None], (count,) + array.shape), axis)


def shift_x(k):
    return [(2 * x + z, 2 * ((x + k) % 4) + z) for x in range(4) for z in range(2)]


def shift_y(k):
    return [(8 * z + 2 * y + c, 8 * z + 2 * ((y + k) % 4) + c) for z in range(2) for y in range(4) for c in range(2)]


def local(query, key_part, value_part, out_cotangent, w_out, residue, rate, skip):
    own = lax.axis_index("ctx")
    own_array = own.reshape(1).astype(jnp.int32)
    core, own_y, own_z = own % 2, own // 2 % 4, own // 8
    place = lax.axis_index("tp")
    place_x, place_z = place // 2, place % 2
    smem = pl.BlockSpec(memory_space=pltpu.SMEM)
    core_swap = [(i, i ^ 1) for i in range(BLOCKS)]
    far_swap = [(i, i ^ 8) for i in range(BLOCKS)]
    near_swap = [(i, i ^ 1) for i in range(8)]

    steps = jnp.arange(8, dtype=jnp.int32)
    came = ((place_x - steps // 2) % 4) * 2 + (place_z + steps) % 2
    goes = ((place_x + steps // 2) % 4) * 2 + (place_z + steps) % 2
    chip = ((own_z + steps // 4) % 2) * 4 + (own_y + steps) % 4
    index = 2 * ((place_x - chip // 2) % 4) + (chip - place_z) % 2

    packed = jnp.concatenate(
        [
            jnp.concatenate([rate.T, residue.T], axis=1),
            jnp.broadcast_to(jnp.concatenate([skip, skip])[None], (PACK - MODES, 128)),
        ]
    )
    packed = to_all(packed, "ctx", BLOCKS)

    cot_pair = jnp.stack([out_cotangent, lax.ppermute(out_cotangent, "tp", near_swap)])
    cots = jnp.concatenate([cot_pair] + [lax.ppermute(cot_pair, "tp", shift_x(k)) for k in (1, 2, 3)])

    mixed, sent, table = pl.pallas_call(
        states_kernel,
        grid=(1,),
        out_shape=(f32(ROWS * SUB, 128), bf16(BLOCKS, MODES, SUB, 128), f32(TABLE, 128)),
        in_specs=[full(ROWS, 1024), full(ROWS, 1024), full(BLOCKS, PACK, 128)],
        out_specs=(full(ROWS * SUB, 128), full(BLOCKS, MODES, SUB, 128), full(TABLE, 128)),
        name="forward_states",
        **params_of(3_000_000_000, 4_000_000),
    )(key_part, value_part, packed)
    sent = exchange(sent, "ctx")

    conv_out, gated, carry = pl.pallas_call(
        forward_kernel,
        grid=(1,),
        out_shape=(bf16(ROWS, 1024), bf16(ROWS, 1024), f32(MODES, SUB, 128)),
        in_specs=[smem, full(BLOCKS, MODES, SUB, 128), full(ROWS * SUB, 128), full(ROWS, 1024), full(TABLE, 128)],
        out_specs=(full(ROWS, 1024), full(ROWS, 1024), full(MODES, SUB, 128)),
        scratch_shapes=[pltpu.VMEM((ROWS * SUB, 128), F32)],
        name="forward_conv",
        **params_of(5_000_000_000, 4_000_000),
    )(own_array, sent, mixed, query, table)

    other_gated = lax.ppermute(gated, "ctx", core_swap)
    own_cots = lax.dynamic_slice_in_dim(cots, 256 * core, 256, axis=2)
    other_cots = lax.ppermute(lax.dynamic_slice_in_dim(cots, 256 * (1 - core), 256, axis=2), "ctx", core_swap)

    *by_y, same_z, other_z = pl.pallas_call(
        weight_kernel,
        out_shape=(bf16(2, HALF, 256),) * 4 + (bf16(4, HALF, 256),) * 2,
        in_specs=[smem] + [whole()] * 4,
        out_specs=(whole(),) * 6,
        scratch_shapes=[pltpu.VMEM((1024, 2 * ROWS), BF16)],
        name="projection_gradient",
        **params_of(2_147_483_648, 8_000_000),
    )(index, gated, other_gated, own_cots, other_cots)
    came_z = lax.ppermute(other_z, "ctx", far_swap)
    came_y = [lax.ppermute(by_y[k], "ctx", shift_y(k)) for k in (1, 2, 3)]

    partial_out = pl.pallas_call(
        output_kernel,
        out_shape=(bf16(2, ROWS, 512),) * 4,
        in_specs=[smem, whole(), whole()],
        out_specs=(whole(),) * 4,
        name="output_projection",
        **params_of(2_147_483_648, 11_000_000),
    )(goes, gated, w_out)
    arrived = [lax.ppermute(partial_out[k], "tp", shift_x(k)) for k in (1, 2, 3)]
    along_x = partial_out[0].astype(F32) + sum(part.astype(F32) for part in arrived)
    output = (along_x[0] + lax.ppermute(along_x[1].astype(BF16), "tp", near_swap).astype(F32)).astype(BF16)

    d_query, d_conv, back, back_sent = pl.pallas_call(
        cotangent_kernel,
        out_shape=(bf16(ROWS, 1024), f32(ROWS * SUB, 128), f32(MODES, SUB, 128), bf16(BLOCKS, MODES, SUB, 128)),
        in_specs=[smem] + [whole()] * 5,
        out_specs=(whole(),) * 4,
        scratch_shapes=[pltpu.VMEM((ROWS, 1024), F32)],
        name="cotangent_states",
        **params_of(5_000_000_000, 13_000_000),
    )(came, cots, w_out, query, conv_out, table)
    back_all = exchange(back_sent, "ctx")

    parts = pl.pallas_call(
        filter_kernel,
        grid=(1,),
        out_shape=f32(BLOCKS * TERMS, 128),
        in_specs=[full(ROWS * SUB, 128), full(ROWS * SUB, 128)] + [full(MODES, SUB, 128)] * 2 + [full(TABLE, 128)],
        out_specs=full(BLOCKS * TERMS, 128),
        name="filter_gradients",
        **params_of(9_000_000_000, 4_000_000),
    )(mixed, d_conv, carry, back, table)
    parts, back_all = lax.optimization_barrier((parts, back_all))
    parts = exchange(parts.reshape(BLOCKS, TERMS, 128), "ctx")

    along_y = by_y[0].astype(F32) + sum(part.astype(F32) for part in came_y)
    first_sum = along_y[0] + lax.ppermute(along_y[1].astype(BF16), "ctx", far_swap).astype(F32)
    along_z = [same_z[k].astype(F32) + came_z[k].astype(F32) for k in range(4)]
    second_sum = along_z[0] + sum(
        lax.ppermute(along_z[k].astype(BF16), "ctx", shift_y(k)).astype(F32) for k in (1, 2, 3)
    )
    d_weight = jnp.concatenate([first_sum, second_sum])

    d_key, d_value, _ = pl.pallas_call(
        backward_kernel,
        grid=(1,),
        out_shape=(bf16(ROWS, 1024), bf16(ROWS, 1024), f32(MODES, SUB, 128)),
        in_specs=[
            smem,
            full(BLOCKS, MODES, SUB, 128),
            full(ROWS * SUB, 128),
            full(ROWS, 1024),
            full(ROWS, 1024),
            full(TABLE, 128),
        ],
        out_specs=(full(ROWS, 1024), full(ROWS, 1024), full(MODES, SUB, 128)),
        scratch_shapes=[pltpu.VMEM((ROWS * SUB, 128), F32)],
        name="backward_conv",
        **params_of(5_000_000_000, 4_000_000),
    )(own_array, back_all, d_conv, key_part, value_part, table)

    d_residue, d_rate, d_skip = pl.pallas_call(
        owner_kernel,
        out_shape=(f32(MODES, 64), f32(MODES, 64), f32(1, 64)),
        in_specs=[whole()] * 3,
        out_specs=(whole(),) * 3,
        name="owner_sums",
        **params_of(1_000_000, 400_000),
    )(parts, rate.T, residue.T)
    return (output, d_query, d_key, d_value, d_weight, d_residue.T, d_rate.T, d_skip[0])


def solution(mesh):
    rows, owner = P("ctx", "tp"), P(("tp", "ctx"))
    return jax.shard_map(
        local,
        mesh=mesh,
        in_specs=(rows, rows, rows, rows, P("tp", None), P(("tp", "ctx"), None), P(("tp", "ctx"), None), owner),
        out_specs=(rows, rows, rows, rows, P("tp", "ctx"), P(("tp", "ctx"), None), P(("tp", "ctx"), None), owner),
        check_vma=False,
    )
```

time: 180 us -> 149 us (0.83)
  starting transfers between devices: 29.1 us -> 49.1 us
  blocking collectives: 19.8 us -> 0 us
  between operations: 14.4 us -> 1 us
  Pallas kernels: 41.7 us -> 30 us
  local copies, waits for them, and re-layouts: 30.8 us -> 20.6 us
  waiting for transfers between devices: 31.7 us -> 35.9 us
    all_to_all x1 -> x0, blocking collectives: 19.8 us -> none  [exchange(): lax.all_to_all(array, axis, split_axis=0, concat_axis=0, tiled=True, axis...]
    pallas_call x4, Pallas kernels: 32.6 us -> 19.6 us  [the longest x1 5.86 us: local(): pl.pallas_call(filter_kernel, grid=(1,), out_shape=f32(BLOCKS * TERMS, 12...]
    ppermute x8 -> x14, starting transfers between devices: 11.6 us -> 23.2 us  [the longest x3 6.06 us: local(): came_y = [lax.ppermute(by_y[k], 'ctx', shift_y(k)) for k in (1, 2, 3)]]
    all_to_all x3 -> x4, starting transfers between devices: 14.7 us -> 23.2 us  [exchange(): lax.all_to_all(array, axis, split_axis=0, concat_axis=0, tiled=True, axis...]
    reshape x4 -> x0, local copies, waits for them, and re-layouts: 4.48 us -> none  [the longest x2 3.05 us: local(): to_all(mine, 'ctx', BLOCKS).reshape(SUB, 2, 40, 64).transpose(2, 0, 1, 3)]
    ppermute x8 -> x14, waiting for transfers between devices: 18.7 us -> 21.7 us  [the longest x3 8.35 us: local(): came_y = [lax.ppermute(by_y[k], 'ctx', shift_y(k)) for k in (1, 2, 3)]]
    add x2 -> x5, other arithmetic: 1.72 us -> 4.37 us  [the longest x1 1.62 us: local(): partial_out[0].astype(F32) + sum((part.astype(F32) for part in arrived))]
    all_to_all x3 -> x4, waiting for transfers between devices: 11.5 us -> 13.4 us  [exchange(): lax.all_to_all(array, axis, split_axis=0, concat_axis=0, tiled=True, axis...]
  transfers between devices with their start and end apart: 17 -> 22, of which waited for: 7 -> 8; matrix products, arithmetic and copies ran while one was open for 16% -> 9% of each run, Pallas kernels for 19% -> 20%
where the time goes in v2:
time: 149 us; the launch traced here: 148 us
  starting transfers between devices  49.1 us (33%)
  waiting for transfers between devices  35.9 us (24%)
  Pallas kernels  30 us (20%)
  local copies, waits for them, and re-layouts  20.6 us (14%)
  other arithmetic  11.7 us (8%)
    all_to_all x4, starting transfers between devices, exchange(): lax.all_to_all(array, axis, split_axis=0, concat_axis=0, tiled=True, axis...  23.2 us
    unnamed x54, local copies, waits for them, and re-layouts  17.2 us
    all_to_all x4, waiting for transfers between devices, exchange(): lax.all_to_all(array, axis, split_axis=0, concat_axis=0, tiled=True, axis...  13.4 us
    ppermute x3, waiting for transfers between devices, local(): came_y = [lax.ppermute(by_y[k], 'ctx', shift_y(k)) for k in (1, 2, 3)]  8.35 us
    ppermute x3, starting transfers between devices, local(): came_y = [lax.ppermute(by_y[k], 'ctx', shift_y(k)) for k in (1, 2, 3)]  6.06 us
    pallas_call x1, Pallas kernels, local(): pl.pallas_call(filter_kernel, grid=(1,), out_shape=f32(BLOCKS * TERMS, 12...  5.86 us
    ppermute x3, waiting for transfers between devices, local(): lax.ppermute(along_z[k].astype(BF16), 'ctx', shift_y(k)).astype(F32)  5.17 us
    pallas_call x1, Pallas kernels, local(): pl.pallas_call(weight_kernel, out_shape=(bf16(2, HALF, 256),) * 4 + (bf16...  5.01 us
  transfers between devices with their start and end apart: 22, of which 8 were waited for; matrix products, arithmetic and copies ran while one was open for 9% of the time, Pallas kernels for 20%

profile of v2, /device:TPU:0, one launch (start us, length us, event | category | flops | bytes accessed | tf_op | source)
XLA Modules:
  0.0 148.2 jit_solution(16524450289733267552)
XLA Ops:
  2.9 8.0 %all-to-all-start = ((f32[16,24,128]{2,1,0:T(8,128)}), f32[16,24,128]{2,1,0:T(8,128)S(1)}, u32[]{:S(2)}, u32[]{:S(2)}) async-start(f32[16,24,128]{2,1,0:T(8,128)} %broadcast_in_dim.5), calls=%async_computation | async-start | bytes 393216 | tf_op jit(solution)/shard_map/all_to_all | solution.py:274
  13.0 6.5 %all-to-all-done.packed_ref = f32[16,24,128]{2,1,0:T(8,128)S(1)} async-done(((f32[16,24,128]{2,1,0:T(8,128)}), f32[16,24,128]{2,1,0:T(8,128)S(1)}, u32[]{:S(2)}, u32[]{:S(2)}) %all-to-all-start) | async-done | bytes 196640 | tf_op jit(solution)/shard_map/all_to_all | solution.py:274
  21.6 2.6 %forward_states.1 = (f32[2048,128]{1,0:T(8,128)S(1)}, bf16[16,16,8,128]{3,2,1,0:T(8,128)(2,1)}, f32[384,128]{1,0:T(8,128)S(1)}) custom-call(bf16[256,1024]{1,0:T(8,128)(2,1)S(1)} %copy-done.10, bf16[256,1024]{1,0:T(8,128)(2,1)S(1)} %copy-done.12, f32[16,24,128]{2,1,0:T(8,128)S(1)} %all-to-all-done.packed_ref), custom_call_target="tpu_custom_call" | custom-call | flops 3000000000 | bytes 4000000 | tf_op jit(solution)/shard_map/forward_states/pallas_call | solution.py:317
  25.2 3.6 %all-to-all-start.1 = ((bf16[16,16,8,128]{3,2,1,0:T(8,128)(2,1)}), bf16[16,16,8,128]{3,2,1,0:T(8,128)(2,1)S(1)}, u32[]{:S(2)}, u32[]{:S(2)}) async-start(bf16[16,16,8,128]{3,2,1,0:T(8,128)(2,1)} %get-tuple-element.35), calls=%async_computation.1 | async-start | bytes 1048576 | tf_op jit(solution)/shard_map/all_to_all | solution.py:274
  29.8 2.8 %collective-permute-start.7 = (bf16[2,256,512]{2,1,0:T(8,128)(2,1)}, bf16[2,256,512]{2,1,0:T(8,128)(2,1)}, u32[]{:S(2)}, u32[]{:S(2)}) collective-permute-start(bf16[2,256,512]{2,1,0:T(8,128)(2,1)} %pad_maximum_fusion.1), channel_id=1, source_target_pairs={{0,6},{1,7},{2,0},{3,1},{4,2},{5,3},{6,4},{7,5},{8,14},{9,15},{10,... | collective-permute-start | bytes 1572872 | tf_op jit(solution)/shard_map/ppermute | solution.py:315
  34.2 6.9 %all-to-all-done.1.sent_ref = bf16[16,16,8,128]{3,2,1,0:T(8,128)(2,1)S(1)} async-done(((bf16[16,16,8,128]{3,2,1,0:T(8,128)(2,1)}), bf16[16,16,8,128]{3,2,1,0:T(8,128)(2,1)S(1)}, u32[]{:S(2)}, u32[]{:S(2)}) %all-to-all-start.1) | async-done | bytes 524320 | tf_op jit(solution)/shard_map/all_to_all | solution.py:274
  43.8 3.0 %forward_conv.1 = (bf16[256,1024]{1,0:T(8,128)(2,1)S(1)}, bf16[256,1024]{1,0:T(8,128)(2,1)S(1)}, f32[16,8,128]{2,1,0:T(8,128)S(1)}) custom-call(s32[1]{0:T(128)} %bitcast.own_ref, bf16[16,16,8,128]{3,2,1,0:T(8,128)(2,1)S(1)} %all-to-all-done.1.sent_ref, f32[2048,128]{1,0:T(8,128)S(1)} %copy-done.18, bf16[256,1024]{1,0:T(8,128)(2,1)S(1)} %copy-done.8, ...), custom_call_target="tpu_custom_call" | custom-call | flops 5000000000 | bytes 4000000 | tf_op jit(solution)/shard_map/forward_conv/pallas_call | solution.py:328
  46.9 3.4 %copy-done = bf16[1024,4096]{1,0:T(8,128)(2,1)S(1)} copy-done((bf16[1024,4096]{1,0:T(8,128)(2,1)S(1)}, bf16[1024,4096]{1,0:T(8,128)(2,1)}, u32[]{:S(2)}) %copy-start) | copy-done | bytes 8388632
  50.2 3.7 %output_projection.1 = (bf16[2,256,512]{2,1,0:T(8,128)(2,1)S(1)}, bf16[2,256,512]{2,1,0:T(8,128)(2,1)}, bf16[2,256,512]{2,1,0:T(8,128)(2,1)}, bf16[2,256,512]{2,1,0:T(8,128)(2,1)}) custom-call(s32[8]{0:T(128)S(1)} %fusion.12.order_ref, bf16[256,1024]{1,0:T(8,128)(2,1)S(1)} %get-tuple-element.38.gated_ref, bf16[1024,4096]{1,0:T(8,128)(2,1)S(1)} %copy-done), custom_call_target="tpu_custom_call" | custom-call | flops 2147483648 | bytes 11000000 | tf_op jit(solution)/shard_map/output_projection/pallas_call | solution.py:355
  55.5 4.1 %collective-permute-done.5 = bf16[2,256,512]{2,1,0:T(8,128)(2,1)} collective-permute-done((bf16[2,256,512]{2,1,0:T(8,128)(2,1)}, bf16[2,256,512]{2,1,0:T(8,128)(2,1)}, u32[]{:S(2)}, u32[]{:S(2)}) %collective-permute-start.5) | collective-permute-done | bytes 524320 | tf_op jit(solution)/shard_map/ppermute | solution.py:315
  64.8 5.0 %cotangent_states.1 = (bf16[256,1024]{1,0:T(8,128)(2,1)}, f32[2048,128]{1,0:T(8,128)S(1)}, f32[16,8,128]{2,1,0:T(8,128)S(1)}, bf16[16,16,8,128]{3,2,1,0:T(8,128)(2,1)S(1)}) custom-call(s32[8]{0:T(128)S(1)} %fusion.14.order_ref, bf16[8,256,512]{2,1,0:T(8,128)(2,1)S(1)} %constant_dynamic-update-slice_fusion.cot_ref, bf16[1024,4096]{1,0:T(8,128)(2,1)S(1)} %bitcast.34, ...), custom_call_target="tpu_custom_call" | custom-call | flops 5000000000 | bytes 13000000 | tf_op jit(solution)/shard_map/cotangent_states/pallas_call | solution.py:367
  71.6 8.1 %all-to-all-start.2 = ((bf16[16,16,8,128]{3,2,1,0:T(8,128)(2,1)}), bf16[16,16,8,128]{3,2,1,0:T(8,128)(2,1)S(1)}, u32[]{:S(2)}, u32[]{:S(2)}) async-start(bf16[16,16,8,128]{3,2,1,0:T(8,128)(2,1)} %copy-done.1), calls=%async_computation.2 | async-start | bytes 1048576 | tf_op jit(solution)/shard_map/all_to_all | solution.py:274
  81.3 5.9 %filter_gradients.1 = f32[640,128]{1,0:T(8,128)} custom-call(f32[2048,128]{1,0:T(8,128)S(1)} %copy-done.19, f32[2048,128]{1,0:T(8,128)S(1)} %copy-done.15, f32[16,8,128]{2,1,0:T(8,128)S(1)} %get-tuple-element.46.carry_ref, f32[16,8,128]{2,1,0:T(8,128)S(1)} %get-tuple-element.47.back_ref, f32[384,128]{1,0:T(8,128)S(1)} %get-tuple-element.37.table), custom_call_target="tpu_custom_call" | custom-call | flops 8999999488 | bytes 4000000 | tf_op jit(solution)/shard_map/filter_gradients/pallas_call | solution.py:378
  88.8 5.0 %projection_gradient.1 = (bf16[2,512,256]{2,1,0:T(8,128)(2,1)S(1)}, bf16[2,512,256]{2,1,0:T(8,128)(2,1)}, bf16[2,512,256]{2,1,0:T(8,128)(2,1)}, bf16[2,512,256]{...) custom-call(s32[8]{0:T(128)S(1)} %fusion.9.index_ref, ...), custom_call_target="tpu_custom_call" | custom-call | flops 2147483648 | bytes 8000000 | tf_op jit(solution)/shard_map/projection_gradient/pallas_call | solution.py:343
  95.8 2.7 %collective-permute-start.11 = (bf16[2,512,256]{2,1,0:T(8,128)(2,1)}, bf16[2,512,256]{2,1,0:T(8,128)(2,1)}, u32[]{:S(2)}, u32[]{:S(2)}) collective-permute-start(bf16[2,512,256]{2,1,0:T(8,128)(2,1)} %get-tuple-element.54), channel_id=1, source_target_pairs={{0,32},{8,40},{16,48},{24,56},{32,0},{40,8},{48,16},{56,24},{64,96... | collective-permute-start | bytes 1572872 | tf_op jit(solution)/shard_map/ppermute | solution.py:353
  99.9 3.0 %collective-permute-start.14 = (bf16[4,512,256]{2,1,0:T(8,128)(2,1)}, bf16[4,512,256]{2,1,0:T(8,128)(2,1)}, u32[]{:S(2)}, u32[]{:S(2)}) collective-permute-start(bf16[4,512,256]{2,1,0:T(8,128)(2,1)} %get-tuple-element.57), channel_id=1, source_target_pairs={{0,64},{8,72},{16,80},{24,88},{32,96},{40,104},{48,112},{56,120},{... | collective-permute-start | bytes 3145736 | tf_op jit(solution)/shard_map/ppermute | solution.py:352
  104.7 3.5 %all-to-all-start.3 = ((f32[16,40,128]{2,1,0:T(8,128)}), f32[16,40,128]{2,1,0:T(8,128)S(1)}, u32[]{:S(2)}, u32[]{:S(2)}) async-start(f32[16,40,128]{2,1,0:T(8,128)} %bitcast.13), calls=%async_computation.3 | async-start | bytes 655360 | tf_op jit(solution)/shard_map/all_to_all | solution.py:274
  110.5 4.0 %backward_conv.1 = (bf16[256,1024]{1,0:T(8,128)(2,1)}, bf16[256,1024]{1,0:T(8,128)(2,1)}, f32[16,8,128]{2,1,0:T(8,128)}) custom-call(s32[1]{0:T(128)} %bitcast.own_ref, bf16[16,16,8,128]{3,2,1,0:T(8,128)(2,1)S(1)} %all-to-all-done.2.sent_ref, f32[2048,128]{1,0:T(8,128)S(1)} %copy-done.16, bf16[256,1024]{1,0:T(8,128)(2,1)S(1)} %copy-done.11, ...), custom_call_target="tpu_custom_call" | custom-call | flops 5000000000 | bytes 4000000 | tf_op jit(solution)/shard_map/backward_conv/pallas_call | solution.py:398
  114.5 8.3 %collective-permute-done.11 = bf16[2,512,256]{2,1,0:T(8,128)(2,1)} collective-permute-done((bf16[2,512,256]{2,1,0:T(8,128)(2,1)}, bf16[2,512,256]{2,1,0:T(8,128)(2,1)}, u32[]{:S(2)}, u32[]{:S(2)}) %collective-permute-start.11) | collective-permute-done | bytes 524320 | tf_op jit(solution)/shard_map/ppermute | solution.py:353
  125.0 3.0 %collective-permute-start.13 = (bf16[512,256]{1,0:T(8,128)(2,1)}, bf16[512,256]{1,0:T(8,128)(2,1)S(1)}, u32[]{:S(2)}, u32[]{:S(2)}) collective-permute-start(bf16[512,256]{1,0:T(8,128)(2,1)} %fusion.7), channel_id=1, source_target_pairs={{0,64},{8,72},{16,80},{24,88},{32,96},{40,104},{48,112},{56,120},{... | collective-permute-start | bytes 786440 | tf_op jit(solution)/shard_map/ppermute | solution.py:391
  128.0 2.5 %collective-permute-done.14 = bf16[4,512,256]{2,1,0:T(8,128)(2,1)} collective-permute-done((bf16[4,512,256]{2,1,0:T(8,128)(2,1)}, bf16[4,512,256]{2,1,0:T(8,128)(2,1)}, u32[]{:S(2)}, u32[]{:S(2)}) %collective-permute-start.14) | collective-permute-done | bytes 1048608 | tf_op jit(solution)/shard_map/ppermute | solution.py:352
  130.5 2.1 %fusion.3 = (bf16[512,256]{1,0:T(8,128)(2,1)}, bf16[512,256]{1,0:T(8,128)(2,1)}, bf16[512,256]{1,0:T(8,128)(2,1)S(1)}) fusion(bf16[4,512,256]{2,1,0:T(8,128)(2,1)} %collective-permute-done.14, bf16[4,512,256]{2,1,0:T(8,128)(2,1)S(1)} %get-tuple-element.56), kind=kLoop, calls=%fused_computation.15 | loop fusion | flops 1572864 | bytes 2359296 | tf_op jit(solution)/shard_map/convert_element_type | solution.py:394
  133.1 2.7 %collective-permute-start.17 = (bf16[512,256]{1,0:T(8,128)(2,1)}, bf16[512,256]{1,0:T(8,128)(2,1)S(1)}, u32[]{:S(2)}, u32[]{:S(2)}) collective-permute-start(bf16[512,256]{1,0:T(8,128)(2,1)} %get-tuple-element.63), channel_id=1, source_target_pairs={{0,48},{8,56},{16,0},{24,8},{32,16},{40,24},{48,32},{56,40},{64,11... | collective-permute-start | bytes 786440 | tf_op jit(solution)/shard_map/ppermute | solution.py:394
  140.8 5.2 %collective-permute-done.15 = bf16[512,256]{1,0:T(8,128)(2,1)S(1)} collective-permute-done((bf16[512,256]{1,0:T(8,128)(2,1)}, bf16[512,256]{1,0:T(8,128)(2,1)S(1)}, u32[]{:S(2)}, u32[]{:S(2)}) %collective-permute-start.15) | collective-permute-done | bytes 262176 | tf_op jit(solution)/shard_map/ppermute | solution.py:394
  (102 shorter events, 41.9 us)
Async XLA Ops:
  2.9 16.6 %all-to-all-start = ((f32[16,24,128]{2,1,0:T(8,128)}), f32[16,24,128]{2,1,0:T(8,128)S(1)}, u32[]{:S(2)}, u32[]{:S(2)}) async-start(f32[16,24,128]{2,1,0:T(8,128)} %broadcast_in_dim.5), calls=%async_computation | async-start | bytes 393216 | tf_op jit(solution)/shard_map/all_to_all | solution.py:274
  10.9 18.0 %collective-permute-start.4 = (bf16[256,512]{1,0:T(8,128)(2,1)}, bf16[256,512]{1,0:T(8,128)(2,1)S(1)}, u32[]{:S(2)}, u32[]{:S(2)}) collective-permute-start(bf16[256,512]{1,0:T(8,128)(2,1)} %param.11), channel_id=1, source_target_pairs={{0,1},{1,0},{2,3},{3,2},{4,5},{5,4},{6,7},{7,6},{8,9},{9,8},{10,11... | collective-permute-start | bytes 786440 | tf_op jit(solution)/shard_map/ppermute | solution.py:314
  25.2 15.9 %all-to-all-start.1 = ((bf16[16,16,8,128]{3,2,1,0:T(8,128)(2,1)}), bf16[16,16,8,128]{3,2,1,0:T(8,128)(2,1)S(1)}, u32[]{:S(2)}, u32[]{:S(2)}) async-start(bf16[16,16,8,128]{3,2,1,0:T(8,128)(2,1)} %get-tuple-element.35), calls=%async_computation.1 | async-start | bytes 1048576 | tf_op jit(solution)/shard_map/all_to_all | solution.py:274
  29.8 33.9 %collective-permute-start.7 = (bf16[2,256,512]{2,1,0:T(8,128)(2,1)}, bf16[2,256,512]{2,1,0:T(8,128)(2,1)}, u32[]{:S(2)}, u32[]{:S(2)}) collective-permute-start(bf16[2,256,512]{2,1,0:T(8,128)(2,1)} %pad_maximum_fusion.1), channel_id=1, source_target_pairs={{0,6},{1,7},{2,0},{3,1},{4,2},{5,3},{6,4},{7,5},{8,14},{9,15},{10,... | collective-permute-start | bytes 1572872 | tf_op jit(solution)/shard_map/ppermute | solution.py:315
  32.5 28.8 %collective-permute-start.6 = (bf16[2,256,512]{2,1,0:T(8,128)(2,1)}, bf16[2,256,512]{2,1,0:T(8,128)(2,1)}, u32[]{:S(2)}, u32[]{:S(2)}) collective-permute-start(bf16[2,256,512]{2,1,0:T(8,128)(2,1)} %pad_maximum_fusion.1), channel_id=1, source_target_pairs={{0,4},{1,5},{2,6},{3,7},{4,0},{5,1},{6,2},{7,3},{8,12},{9,13},{10,... | collective-permute-start | bytes 1572872 | tf_op jit(solution)/shard_map/ppermute | solution.py:315
  33.3 26.2 %collective-permute-start.5 = (bf16[2,256,512]{2,1,0:T(8,128)(2,1)}, bf16[2,256,512]{2,1,0:T(8,128)(2,1)}, u32[]{:S(2)}, u32[]{:S(2)}) collective-permute-start(bf16[2,256,512]{2,1,0:T(8,128)(2,1)} %pad_maximum_fusion.1), channel_id=1, source_target_pairs={{0,2},{1,3},{2,4},{3,5},{4,6},{5,7},{6,0},{7,1},{8,10},{9,11},{10,... | collective-permute-start | bytes 1572872 | tf_op jit(solution)/shard_map/ppermute | solution.py:315
  41.1 23.6 %slice-start = ((s8[8388608]{0:T(1024)(128)(4,1)}), s8[4194304]{0:T(1024)(128)(4,1)S(1)}, s32[]{:S(2)}) async-start(s8[8388608]{0:T(1024)(128)(4,1)} %bitcast.33), calls=%async_computation.4 | async-start | bytes 8388608
  43.8 21.0 %slice-start.1 = ((s8[8388608]{0:T(1024)(128)(4,1)}), s8[4194304]{0:T(1024)(128)(4,1)S(1)}, s32[]{:S(2)}) async-start(s8[8388608]{0:T(1024)(128)(4,1)} %bitcast.33), calls=%async_computation.5 | async-start | bytes 8388608
  46.8 42.1 %collective-permute-start.8 = (bf16[256,1024]{1,0:T(8,128)(2,1)S(1)}, bf16[256,1024]{1,0:T(8,128)(2,1)}, u32[]{:S(2)}, u32[]{:S(2)}) collective-permute-start(bf16[256,1024]{1,0:T(8,128)(2,1)S(1)} %get-tuple-element.38.gated_ref), channel_id=1, source_target_pairs={{0,8},{8,0},{16,24},{24,16},{32,40},{40,32},{48,56},{56,48},{64,72... | collective-permute-start | bytes 1572872 | tf_op jit(solution)/shard_map/ppermute | solution.py:339
  54.0 33.2 %collective-permute-start = (bf16[2,256,512]{2,1,0:T(8,128)(2,1)}, bf16[2,256,512]{2,1,0:T(8,128)(2,1)}, u32[]{:S(2)}, u32[]{:S(2)}) collective-permute-start(bf16[2,256,512]{2,1,0:T(8,128)(2,1)} %get-tuple-element.40), channel_id=1, source_target_pairs={{0,2},{1,3},{2,4},{3,5},{4,6},{5,7},{6,0},{7,1},{8,10},{9,11},{10,... | collective-permute-start | bytes 1572872 | tf_op jit(solution)/shard_map/ppermute | solution.py:363
  59.5 27.6 %collective-permute-start.1 = (bf16[2,256,512]{2,1,0:T(8,128)(2,1)}, bf16[2,256,512]{2,1,0:T(8,128)(2,1)}, u32[]{:S(2)}, u32[]{:S(2)}) collective-permute-start(bf16[2,256,512]{2,1,0:T(8,128)(2,1)} %get-tuple-element.41), channel_id=1, source_target_pairs={{0,4},{1,5},{2,6},{3,7},{4,0},{5,1},{6,2},{7,3},{8,12},{9,13},{10,... | collective-permute-start | bytes 1572872 | tf_op jit(solution)/shard_map/ppermute | solution.py:363
  61.3 25.8 %collective-permute-start.2 = (bf16[2,256,512]{2,1,0:T(8,128)(2,1)}, bf16[2,256,512]{2,1,0:T(8,128)(2,1)}, u32[]{:S(2)}, u32[]{:S(2)}) collective-permute-start(bf16[2,256,512]{2,1,0:T(8,128)(2,1)} %get-tuple-element.42), channel_id=1, source_target_pairs={{0,6},{1,7},{2,0},{3,1},{4,2},{5,3},{6,4},{7,5},{8,14},{9,15},{10,... | collective-permute-start | bytes 1572872 | tf_op jit(solution)/shard_map/ppermute | solution.py:363
  71.6 33.1 %all-to-all-start.2 = ((bf16[16,16,8,128]{3,2,1,0:T(8,128)(2,1)}), bf16[16,16,8,128]{3,2,1,0:T(8,128)(2,1)S(1)}, u32[]{:S(2)}, u32[]{:S(2)}) async-start(bf16[16,16,8,128]{3,2,1,0:T(8,128)(2,1)} %copy-done.1), calls=%async_computation.2 | async-start | bytes 1048576 | tf_op jit(solution)/shard_map/all_to_all | solution.py:274
  79.9 8.9 %collective-permute-start.9 = (bf16[8,256,256]{2,1,0:T(8,128)(2,1)S(1)}, bf16[8,256,256]{2,1,0:T(8,128)(2,1)S(1)}, u32[]{:S(2)}, u32[]{:S(2)}) collective-permute-start(bf16[8,256,256]{2,1,0:T(8,128)(2,1)S(1)} %get-tuple-element.65), channel_id=1, source_target_pairs={{0,8},{8,0},{16,24},{24,16},{32,40},{40,32},{48,56},{56,48},{64,72... | collective-permute-start | bytes 3145736 | tf_op jit(solution)/shard_map/ppermute | solution.py:341
  93.9 20.6 %collective-permute-start.10 = (bf16[2,512,256]{2,1,0:T(8,128)(2,1)}, bf16[2,512,256]{2,1,0:T(8,128)(2,1)S(1)}, u32[]{:S(2)}, u32[]{:S(2)}) collective-permute-start(bf16[2,512,256]{2,1,0:T(8,128)(2,1)} %get-tuple-element.53), channel_id=1, source_target_pairs={{0,16},{8,24},{16,32},{24,40},{32,48},{40,56},{48,0},{56,8},{64,80... | collective-permute-start | bytes 1572872 | tf_op jit(solution)/shard_map/ppermute | solution.py:353
  95.8 27.0 %collective-permute-start.11 = (bf16[2,512,256]{2,1,0:T(8,128)(2,1)}, bf16[2,512,256]{2,1,0:T(8,128)(2,1)}, u32[]{:S(2)}, u32[]{:S(2)}) collective-permute-start(bf16[2,512,256]{2,1,0:T(8,128)(2,1)} %get-tuple-element.54), channel_id=1, source_target_pairs={{0,32},{8,40},{16,48},{24,56},{32,0},{40,8},{48,16},{56,24},{64,96... | collective-permute-start | bytes 1572872 | tf_op jit(solution)/shard_map/ppermute | solution.py:353
  98.5 24.3 %collective-permute-start.12 = (bf16[2,512,256]{2,1,0:T(8,128)(2,1)}, bf16[2,512,256]{2,1,0:T(8,128)(2,1)}, u32[]{:S(2)}, u32[]{:S(2)}) collective-permute-start(bf16[2,512,256]{2,1,0:T(8,128)(2,1)} %get-tuple-element.55), channel_id=1, source_target_pairs={{0,48},{8,56},{16,0},{24,8},{32,16},{40,24},{48,32},{56,40},{64,11... | collective-permute-start | bytes 1572872 | tf_op jit(solution)/shard_map/ppermute | solution.py:353
  99.9 30.5 %collective-permute-start.14 = (bf16[4,512,256]{2,1,0:T(8,128)(2,1)}, bf16[4,512,256]{2,1,0:T(8,128)(2,1)}, u32[]{:S(2)}, u32[]{:S(2)}) collective-permute-start(bf16[4,512,256]{2,1,0:T(8,128)(2,1)} %get-tuple-element.57), channel_id=1, source_target_pairs={{0,64},{8,72},{16,80},{24,88},{32,96},{40,104},{48,112},{56,120},{... | collective-permute-start | bytes 3145736 | tf_op jit(solution)/shard_map/ppermute | solution.py:352
  103.6 32.9 %collective-permute-start.3 = (bf16[256,512]{1,0:T(8,128)(2,1)}, bf16[256,512]{1,0:T(8,128)(2,1)}, u32[]{:S(2)}, u32[]{:S(2)}) collective-permute-start(bf16[256,512]{1,0:T(8,128)(2,1)} %fusion.6), channel_id=1, source_target_pairs={{0,1},{1,0},{2,3},{3,2},{4,5},{5,4},{6,7},{7,6},{8,9},{9,8},{10,11... | collective-permute-start | bytes 786440 | tf_op jit(solution)/shard_map/ppermute | solution.py:365
  104.7 33.6 %all-to-all-start.3 = ((f32[16,40,128]{2,1,0:T(8,128)}), f32[16,40,128]{2,1,0:T(8,128)S(1)}, u32[]{:S(2)}, u32[]{:S(2)}) async-start(f32[16,40,128]{2,1,0:T(8,128)} %bitcast.13), calls=%async_computation.3 | async-start | bytes 655360 | tf_op jit(solution)/shard_map/all_to_all | solution.py:274
  125.0 15.7 %collective-permute-start.13 = (bf16[512,256]{1,0:T(8,128)(2,1)}, bf16[512,256]{1,0:T(8,128)(2,1)S(1)}, u32[]{:S(2)}, u32[]{:S(2)}) collective-permute-start(bf16[512,256]{1,0:T(8,128)(2,1)} %fusion.7), channel_id=1, source_target_pairs={{0,64},{8,72},{16,80},{24,88},{32,96},{40,104},{48,112},{56,120},{... | collective-permute-start | bytes 786440 | tf_op jit(solution)/shard_map/ppermute | solution.py:391
  132.6 13.4 %collective-permute-start.15 = (bf16[512,256]{1,0:T(8,128)(2,1)}, bf16[512,256]{1,0:T(8,128)(2,1)S(1)}, u32[]{:S(2)}, u32[]{:S(2)}) collective-permute-start(bf16[512,256]{1,0:T(8,128)(2,1)} %get-tuple-element.62), channel_id=1, source_target_pairs={{0,16},{8,24},{16,32},{24,40},{32,48},{40,56},{48,0},{56,8},{64,80... | collective-permute-start | bytes 786440 | tf_op jit(solution)/shard_map/ppermute | solution.py:394
  133.1 12.8 %collective-permute-start.17 = (bf16[512,256]{1,0:T(8,128)(2,1)}, bf16[512,256]{1,0:T(8,128)(2,1)S(1)}, u32[]{:S(2)}, u32[]{:S(2)}) collective-permute-start(bf16[512,256]{1,0:T(8,128)(2,1)} %get-tuple-element.63), channel_id=1, source_target_pairs={{0,48},{8,56},{16,0},{24,8},{32,16},{40,24},{48,32},{56,40},{64,11... | collective-permute-start | bytes 786440 | tf_op jit(solution)/shard_map/ppermute | solution.py:394
  135.8 10.2 %collective-permute-start.16 = (bf16[512,256]{1,0:T(8,128)(2,1)S(1)}, bf16[512,256]{1,0:T(8,128)(2,1)}, u32[]{:S(2)}, u32[]{:S(2)}) collective-permute-start(bf16[512,256]{1,0:T(8,128)(2,1)S(1)} %get-tuple-element.64), channel_id=1, source_target_pairs={{0,32},{8,40},{16,48},{24,56},{32,0},{40,8},{48,16},{56,24},{64,96... | collective-permute-start | bytes 786440 | tf_op jit(solution)/shard_map/ppermute | solution.py:394
  (23 other events, 146.6 us)

commit v3 on v2

v3 whole, which is shorter than its diff:
```python
import functools

import jax
import jax.numpy as jnp
from jax import lax
from jax.experimental import pallas as pl
from jax.experimental.pallas import tpu as pltpu
from jax.sharding import PartitionSpec as P

F32 = jnp.float32
BF16 = jnp.bfloat16
SEQ = 4096
MODES = 16
ROWS = 256
SUB = 8
BLOCKS = 16
HALF = 512
UNROLL = 8
PACK = 24
TABLE = 2 * PACK * SUB
STATE = MODES * SUB
TERMS = 48
VMEM = 32 * 1024 * 1024
LONG = 2_000_000_000_000
SHORT = 50


def params_of(flops, nbytes):
    return dict(
        compiler_params=pltpu.CompilerParams(vmem_limit_bytes=VMEM),
        cost_estimate=pl.CostEstimate(flops=flops // SHORT, bytes_accessed=nbytes // SHORT, transcendentals=0),
    )


def whole():
    return pl.BlockSpec(memory_space=pltpu.VMEM)


def full(*shape):
    return pl.BlockSpec(shape, lambda *_: (0,) * len(shape))


def far(array):
    return pltpu.with_memory_space_constraint(array, pltpu.HBM)


def far_f32(*shape):
    return pltpu.HBM(shape, F32)


def far_bf16(*shape):
    return pltpu.HBM(shape, BF16)


def lanes(group):
    return slice(128 * group, 128 * (group + 1))


def group_rows(group):
    return pl.ds(group, ROWS, stride=SUB)


def rate_of(table, mode):
    return table[SUB * mode : SUB * (mode + 1), :]


def step_decay(table, mode):
    return jnp.exp(rate_of(table, mode) * (-1.0 / SEQ))


def block_decay(table, mode):
    return jnp.exp(rate_of(table, mode) * (-float(ROWS) / SEQ))


def mode_weight(table, mode):
    return rate_of(table, PACK + mode) * jnp.sqrt(rate_of(table, mode) * (2.0 / SEQ))


def skip_of(table):
    return rate_of(table, MODES)


def at(ref, step):
    return ref[pl.ds(pl.multiple_of(step * SUB, SUB), SUB), :]


def zeros(count):
    return tuple(jnp.zeros((SUB, 128), F32) for _ in range(count))


def tree_sum(parts):
    parts = list(parts)
    while len(parts) > 1:
        parts = [sum(parts[i : i + 2]) for i in range(0, len(parts), 2)]
    return parts[0]


def pack_kernel(rate_ref, residue_ref, skip_ref, out_ref):
    both = jnp.concatenate([rate_ref[...], residue_ref[...]], axis=1)
    last = jnp.concatenate([skip_ref[...], skip_ref[...]], axis=1)
    for j in range(BLOCKS):
        out_ref[j, :MODES] = both
        out_ref[j, MODES:] = jnp.broadcast_to(last, (PACK - MODES, 128))


def mix_kernel(key_ref, value_ref, cot_ref, near_cot_ref, mixed_ref, kept_ref, pair_ref):
    pair_ref[0] = cot_ref[...]
    pair_ref[1] = near_cot_ref[...]
    for group in range(SUB):
        product = key_ref[:, lanes(group)].astype(F32) * value_ref[:, lanes(group)].astype(F32)
        mixed_ref[group_rows(group), :] = product.astype(BF16).astype(F32)
    kept_ref[...] = mixed_ref[...]


def gather_kernel(core_ref, *refs):
    parts, half_ref, sems = refs[:4], refs[5], refs[7]
    half = pl.ds(pl.multiple_of((1 - core_ref[0]) * 256, 256), 256)
    copies = [
        pltpu.make_async_copy(parts[i // 2].at[i % 2, :, half], half_ref.at[i], sems.at[i]) for i in range(8)
    ]
    for copy in copies:
        copy.start()
    for copy in copies:
        copy.wait()


def states_kernel(mixed_ref, packed_ref, sent_ref, table):
    left = lax.broadcasted_iota(jnp.int32, (PACK, 128), 1) < 64
    for group in range(SUB):
        one, two = packed_ref[2 * group], packed_ref[2 * group + 1]
        table[pl.ds(group, PACK, stride=SUB), :] = jnp.where(left, one, pltpu.roll(two, 64, 1))
        table[pl.ds(PACK * SUB + group, PACK, stride=SUB), :] = jnp.where(left, pltpu.roll(one, 64, 1), two)
    decay = [step_decay(table, m) for m in range(MODES)]

    def body(i, held):
        for u in range(UNROLL):
            value = at(mixed_ref, i * UNROLL + u)
            held = tuple(decay[m] * held[m] + value for m in range(MODES))
        return held

    held = lax.fori_loop(0, ROWS // UNROLL, body, zeros(MODES))
    for m in range(MODES):
        state = held[m].astype(BF16)
        for j in range(BLOCKS):
            sent_ref[j, m] = state


def forward_kernel(own_ref, sent_ref, mixed_ref, query_ref, table, conv_ref, gated_ref, carry_ref, buffer):
    own = own_ref[0]
    for m in range(MODES):
        far = block_decay(table, m)
        carry = jnp.zeros((SUB, 128), F32)
        for j in range(BLOCKS - 1):
            carry = jnp.where(j < own, far * carry + sent_ref[j, m].astype(F32), carry)
        carry_ref[m] = carry
    decay = [step_decay(table, m) for m in range(MODES)]
    weight = [mode_weight(table, m) for m in range(MODES)]
    skip = skip_of(table)

    def body(i, held):
        for u in range(UNROLL):
            step = i * UNROLL + u
            value = at(mixed_ref, step)
            held = tuple(decay[m] * held[m] + value for m in range(MODES))
            total = tree_sum([weight[m] * held[m] for m in range(MODES)])
            buffer[pl.ds(pl.multiple_of(step * SUB, SUB), SUB), :] = total + skip * value
        return held

    lax.fori_loop(0, ROWS // UNROLL, body, tuple(carry_ref[m] for m in range(MODES)))
    for group in range(SUB):
        conv = buffer[group_rows(group), :].astype(BF16)
        conv_ref[:, lanes(group)] = conv
        gated_ref[:, lanes(group)] = (query_ref[:, lanes(group)].astype(F32) * conv.astype(F32)).astype(BF16)


def output_kernel(gated_ref, weight_ref, after_ref, out_ref, gated, weight, blocks, sems):
    copies = [
        pltpu.make_async_copy(weight_ref.at[:, 512 * i : 512 * (i + 1)], weight.at[i], sems.at[i]) for i in range(8)
    ]
    results = [pltpu.make_async_copy(blocks.at[i], out_ref.at[i], sems.at[8 + i]) for i in range(8)]
    first = pltpu.make_async_copy(gated_ref, gated, sems.at[16])
    first.start()
    for copy in copies:
        copy.start()
    first.wait()
    for i in range(8):
        copies[i].wait()
        blocks[i] = jnp.dot(gated[...], weight[i], preferred_element_type=F32).astype(BF16)
        results[i].start()
    for result in results:
        result.wait()


def weight_kernel(index_ref, gated_ref, other_ref, *refs):
    cot_refs, other_cot_ref = refs[:4], refs[4]
    along_y, along_z = refs[6:10], refs[10:12]
    gated, turned, cots, chunks, sems, out_sems = refs[12:]
    half = pl.ds(pl.multiple_of(index_ref[8] * 256, 256), 256)
    copies = [
        pltpu.make_async_copy(gated_ref, gated.at[0], sems.at[16]),
        pltpu.make_async_copy(other_ref, gated.at[1], sems.at[17]),
    ]
    for i in range(8):
        own = cot_refs[i // 2].at[i % 2, :, half]
        copies.append(pltpu.make_async_copy(own, cots.at[i, :ROWS], sems.at[i]))
        copies.append(pltpu.make_async_copy(other_cot_ref.at[i], cots.at[i, ROWS:], sems.at[8 + i]))
    for copy in copies:
        copy.start()
    copies[0].wait()
    turned[:, :ROWS] = gated[0].T
    copies[1].wait()
    turned[:, ROWS:] = gated[1].T
    for copy in copies[2:]:
        copy.wait()
    results = []
    for z in (1, 0):
        for k in range(4):
            i = 4 * z + k
            total = jnp.dot(turned[...], cots[index_ref[i]], preferred_element_type=F32)
            chunks[i] = total.astype(BF16)
            results.append(pltpu.make_async_copy(chunks.at[i, HALF:], along_z[z].at[k], out_sems.at[i]))
            results.append(pltpu.make_async_copy(chunks.at[i, :HALF], along_y[k].at[z], out_sems.at[8 + i]))
            results[-2].start()
            results[-1].start()
    for result in results:
        result.wait()


def cotangent_kernel(
    came_ref, part0, part1, part2, part3, weight_ref, query_ref, conv_ref, mixed_ref, carry_ref, table, after_ref,
    dquery_ref, dconv_ref, sent_ref, total, terms, parts, weight, sems,
):
    copies = []
    for i in range(8):
        columns = pl.ds(pl.multiple_of(came_ref[i] * 512, 512), 512)
        part = (part0, part1, part2, part3)[i // 2].at[i % 2]
        copies.append(pltpu.make_async_copy(weight_ref.at[:, columns], weight.at[i], sems.at[i]))
        copies.append(pltpu.make_async_copy(part, parts.at[i], sems.at[8 + i]))
    for copy in copies:
        copy.start()
    for i in range(8):
        copies[2 * i].wait()
        copies[2 * i + 1].wait()
        product = lax.dot_general(parts[i], weight[i], (((1,), (1,)), ((), ())), preferred_element_type=F32)
        if i == 0:
            total[...] = product
        else:
            total[...] += product
    for group in range(SUB):
        cot = total[:, lanes(group)]
        dquery_ref[:, lanes(group)] = (cot * conv_ref[:, lanes(group)].astype(F32)).astype(BF16)
        dconv_ref[group_rows(group), :] = (cot * query_ref[:, lanes(group)].astype(F32)).astype(BF16).astype(F32)

    left = lax.broadcasted_iota(jnp.int32, (SUB, 128), 1) < 64

    def put(row, one, two):
        terms[pl.ds(row, SUB, stride=2 * TERMS), :] = jnp.where(left, one, pltpu.roll(two, 64, 1))
        terms[pl.ds(TERMS + row, SUB, stride=2 * TERMS), :] = jnp.where(left, pltpu.roll(one, 64, 1), two)

    half = MODES // 2
    for first in (0, half):
        modes = range(first, first + half)
        decay = [step_decay(table, m) for m in modes]

        def forward(i, packed):
            held, moment, first_sum, second_sum, skip_sum = packed
            for u in range(UNROLL):
                value = at(mixed_ref, i * UNROLL + u)
                cot = at(dconv_ref, i * UNROLL + u)
                past = [decay[m] * held[m] for m in range(half)]
                moment = tuple(decay[m] * moment[m] + past[m] for m in range(half))
                held = tuple(past[m] + value for m in range(half))
                first_sum = tuple(first_sum[m] + cot * held[m] for m in range(half))
                second_sum = tuple(second_sum[m] + cot * moment[m] for m in range(half))
                skip_sum = skip_sum + cot * value
            return (held, moment, first_sum, second_sum, skip_sum)

        start = (tuple(carry_ref[m] for m in modes), zeros(half), zeros(half), zeros(half), zeros(1)[0])
        held, moment, first_sum, second_sum, skip_sum = lax.fori_loop(0, ROWS // UNROLL, forward, start)

        def backward(i, back):
            for u in range(UNROLL):
                value = at(dconv_ref, ROWS - 1 - (i * UNROLL + u))
                back = tuple(decay[m] * back[m] + value for m in range(half))
            return back

        back = lax.fori_loop(0, ROWS // UNROLL, backward, zeros(half))
        for m in range(half):
            put(first + m, first_sum[m], second_sum[m])
            put(MODES + first + m, moment[m], back[m])
        for m in range(0, half, 2):
            state = jnp.concatenate([back[m], back[m + 1]]).astype(BF16)
            for j in range(BLOCKS):
                sent_ref[j, SUB * (first + m) : SUB * (first + m + 2), :] = state
    for row in range(2 * MODES, TERMS):
        put(row, skip_sum, skip_sum)
    for j in range(BLOCKS):
        term = terms[TERMS * j : TERMS * (j + 1), :]
        upper = term.astype(BF16)
        sent_ref[j, STATE : STATE + TERMS, :] = upper
        sent_ref[j, STATE + TERMS :, :] = (term - upper.astype(F32)).astype(BF16)


def backward_kernel(own_ref, sent_ref, dconv_ref, key_ref, value_ref, table, dkey_ref, dvalue_ref, carry_ref, buffer):
    own = own_ref[0]
    for m in range(MODES):
        far = block_decay(table, m)
        carry = jnp.zeros((SUB, 128), F32)
        for j in range(BLOCKS - 1, 0, -1):
            carry = jnp.where(j > own, far * carry + sent_ref[j, SUB * m : SUB * (m + 1), :].astype(F32), carry)
        carry_ref[m] = carry
    decay = [step_decay(table, m) for m in range(MODES)]
    weight = [mode_weight(table, m) for m in range(MODES)]
    skip = skip_of(table)

    def body(i, held):
        for u in range(UNROLL):
            step = ROWS - 1 - (i * UNROLL + u)
            value = at(dconv_ref, step)
            held = tuple(decay[m] * held[m] + value for m in range(MODES))
            total = tree_sum([weight[m] * held[m] for m in range(MODES)])
            buffer[pl.ds(pl.multiple_of(step * SUB, SUB), SUB), :] = total + skip * value
        return held

    lax.fori_loop(0, ROWS // UNROLL, body, tuple(carry_ref[m] for m in range(MODES)))
    for group in range(SUB):
        grad = buffer[group_rows(group), :].astype(BF16).astype(F32)
        dkey_ref[:, lanes(group)] = (grad * value_ref[:, lanes(group)].astype(F32)).astype(BF16)
        dvalue_ref[:, lanes(group)] = (grad * key_ref[:, lanes(group)].astype(F32)).astype(BF16)


def add_kernel(*refs):
    out_ref = refs[-1]
    total = refs[0][...].astype(F32).reshape(out_ref.shape)
    for ref in refs[1:-2]:
        total += ref[...].astype(F32).reshape(out_ref.shape)
    out_ref[...] = total.astype(out_ref.dtype)


def stage_kernel(*refs):
    first, same, other, outs = refs[:4], refs[4], refs[5], refs[7:]
    outs[0][...] = sum(ref[0].astype(F32) for ref in first).astype(BF16)
    for k in (1, 2, 3):
        outs[k][...] = (same[k].astype(F32) + other[k].astype(F32)).astype(BF16)


def add_placed_kernel(place_ref, *refs):
    add_kernel(*refs)


def add_placed(array, place, after, *more):
    specs = [pl.BlockSpec((1, ROWS, 512), lambda i, at, k=k: (2 * k + at[0], 0, 0)) for k in range(4)]
    specs += [pl.BlockSpec((ROWS, 512), lambda i, at: (0, 0))] * len(more)
    return pl.pallas_call(
        add_placed_kernel,
        grid_spec=pltpu.PrefetchScalarGridSpec(
            num_scalar_prefetch=1,
            grid=(1,),
            in_specs=specs + [pl.BlockSpec(memory_space=pl.ANY)],
            out_specs=pl.BlockSpec((ROWS, 512), lambda i, at: (0, 0)),
        ),
        out_shape=bf16(ROWS, 512),
        name="sum_output",
        **params_of(1_000_000, 2_000_000),
    )(place.reshape(1).astype(jnp.int32), *[far(array)] * 4, *[far(one) for one in more], far(after))


def half_kernel(*refs):
    out_ref = refs[-1]
    total = refs[0][0].astype(F32)
    for ref in refs[1 : 5]:
        total += ref[0].astype(F32)
    out_ref[...] = total


def half_gradient(which, picked, after, result=None):
    earlier = ([] if result is None else [result]) + after
    return pl.pallas_call(
        half_kernel,
        grid=(1,),
        out_shape=far_f32(2 * HALF, 256),
        in_specs=[pl.BlockSpec((1, HALF, 256), lambda i: (0, 0, 0))] * 5
        + [pl.BlockSpec(memory_space=pl.ANY)] * len(earlier),
        out_specs=pl.BlockSpec((HALF, 256), lambda i: (which, 0)),
        input_output_aliases={} if result is None else {5: 0},
        name="sum_gradient",
        **params_of(2_000_000, 4_000_000),
    )(*[far(array) for array in picked], *[far(array) for array in earlier])


def owner_kernel(parts_ref, rate_ref, residue_ref, dresidue_ref, drate_ref, dskip_ref):
    rate = rate_ref[...]
    residue = residue_ref[...]
    near = jnp.exp(rate * (-1.0 / SEQ))
    far = jnp.exp(rate * (-float(ROWS) / SEQ))
    scale = jnp.sqrt(rate * (2.0 / SEQ))
    first = jnp.zeros_like(rate)
    second = jnp.zeros_like(rate)
    skip = jnp.zeros((1, rate.shape[1]), F32)
    later = jnp.zeros_like(rate)
    for j in range(BLOCKS - 1, -1, -1):
        upper, lower = parts_ref[j, STATE : STATE + TERMS, :], parts_ref[j, STATE + TERMS :, :]
        terms = upper.astype(F32) + lower.astype(F32)
        sums, ends = terms[0:MODES], terms[MODES : 2 * MODES]
        first += sums[:, :64]
        second += sums[:, 64:] + near * later * ends[:, :64]
        later = far * later + ends[:, 64:]
        skip += terms[2 * MODES : 2 * MODES + 1, :64]
    proj = scale * first
    dresidue_ref[...] = proj
    drate_ref[...] = residue * (0.5 * proj / rate - scale * second * (1.0 / SEQ))
    dskip_ref[...] = skip


def f32(*shape):
    return jax.ShapeDtypeStruct(shape, F32)


def bf16(*shape):
    return jax.ShapeDtypeStruct(shape, BF16)


def exchange(array, axis, groups=None):
    return lax.all_to_all(array, axis, split_axis=0, concat_axis=0, tiled=True, axis_index_groups=groups)


def to_all(array, axis, count):
    return exchange(jnp.broadcast_to(array[None], (count,) + array.shape), axis)


MOVES = [(k, z) for k in range(4) for z in range(2)]


def shift_x(k, z=0):
    return [(2 * x + p, 2 * ((x + k) % 4) + (p + z) % 2) for x in range(4) for p in range(2)]


def shift_y(k):
    return [(8 * z + 2 * y + c, 8 * z + 2 * ((y + k) % 4) + c) for z in range(2) for y in range(4) for c in range(2)]


def local(query, key_part, value_part, out_cotangent, w_out, residue, rate, skip):
    own = lax.axis_index("ctx")
    own_array = own.reshape(1).astype(jnp.int32)
    core, own_y, own_z = own % 2, own // 2 % 4, own // 8
    place = lax.axis_index("tp")
    place_x, place_z = place // 2, place % 2
    smem = pl.BlockSpec(memory_space=pltpu.SMEM)
    core_swap = [(i, i ^ 1) for i in range(BLOCKS)]
    far_swap = [(i, i ^ 8) for i in range(BLOCKS)]
    hbm = pl.BlockSpec(memory_space=pltpu.HBM)

    steps = jnp.arange(8, dtype=jnp.int32)
    came = ((place_x - steps // 2) % 4) * 2 + (place_z + steps) % 2
    chip = ((own_z + steps // 4) % 2) * 4 + (own_y + steps) % 4
    index = 2 * ((place_x - chip // 2) % 4) + (chip - place_z) % 2
    core_array = core.reshape(1).astype(jnp.int32)

    packed = pl.pallas_call(
        pack_kernel,
        grid=(1,),
        out_shape=far_f32(BLOCKS, PACK, 128),
        in_specs=[full(MODES, 64), full(MODES, 64), full(1, 64)],
        out_specs=full(BLOCKS, PACK, 128),
        name="pack_parameters",
        **params_of(100_000, 200_000),
    )(far(rate.T), far(residue.T), far(skip[None]))
    packed = exchange(packed, "ctx")
    near_cot = lax.ppermute(out_cotangent, "tp", shift_x(0, 1))
    mixed_near, mixed, cot_pair = pl.pallas_call(
        mix_kernel,
        grid=(1,),
        out_shape=(f32(ROWS * SUB, 128), far_f32(ROWS * SUB, 128), far_bf16(2, ROWS, 512)),
        in_specs=[full(ROWS, 1024)] * 2 + [full(ROWS, 512)] * 2,
        out_specs=(whole(), full(ROWS * SUB, 128), full(2, ROWS, 512)),
        name="mix_inputs",
        **params_of(100_000_000, 3_000_000),
    )(far(key_part), far(value_part), far(out_cotangent), near_cot)
    cot_parts = [cot_pair] + [lax.ppermute(cot_pair, "tp", shift_x(k)) for k in (1, 2, 3)]

    sent, table = pl.pallas_call(
        states_kernel,
        grid=(1,),
        out_shape=(far_bf16(BLOCKS, MODES, SUB, 128), far_f32(TABLE, 128)),
        in_specs=[whole()] * 2,
        out_specs=(full(BLOCKS, MODES, SUB, 128), full(TABLE, 128)),
        name="forward_states",
        **params_of(3_000_000_000, 4_000_000),
    )(mixed_near, packed)
    sent = exchange(sent, "ctx")

    conv_out, gated, carry = pl.pallas_call(
        forward_kernel,
        grid=(1,),
        out_shape=(far_bf16(ROWS, 1024), far_bf16(ROWS, 1024), far_f32(MODES, SUB, 128)),
        in_specs=[smem, whole(), full(ROWS * SUB, 128), full(ROWS, 1024), full(TABLE, 128)],
        out_specs=(full(ROWS, 1024), full(ROWS, 1024), full(MODES, SUB, 128)),
        scratch_shapes=[pltpu.VMEM((ROWS * SUB, 128), F32)],
        name="forward_conv",
        **params_of(5_000_000_000, 4_000_000),
    )(own_array, sent, far(mixed), far(query), far(table))

    other_gated = lax.ppermute(gated, "ctx", core_swap)
    half_cots, gathered = pl.pallas_call(
        gather_kernel,
        out_shape=(bf16(8, ROWS, 256), far_f32(8, 128)),
        in_specs=[smem] + [pl.BlockSpec(memory_space=pl.ANY)] * 5,
        out_specs=(whole(), pl.BlockSpec(memory_space=pl.ANY)),
        scratch_shapes=[pltpu.SemaphoreType.DMA((8,))],
        name="gather_cotangent",
        **params_of(100_000, 6_000_000),
    )(core_array, *[far(part) for part in cot_parts], far(gated))
    other_cots = lax.ppermute(half_cots, "ctx", core_swap)

    anywhere = pl.BlockSpec(memory_space=pl.ANY)
    partial_out = pl.pallas_call(
        output_kernel,
        out_shape=far_bf16(8, ROWS, 512),
        in_specs=[anywhere] * 3,
        out_specs=anywhere,
        scratch_shapes=[
            pltpu.VMEM((ROWS, 1024), BF16),
            pltpu.VMEM((8, 1024, 512), BF16),
            pltpu.VMEM((8, ROWS, 512), BF16),
            pltpu.SemaphoreType.DMA((17,)),
        ],
        name="output_projection",
        **params_of(2_147_483_648, 11_000_000),
    )(far(gated), far(w_out), gathered)

    *by_y, same_z, other_z = pl.pallas_call(
        weight_kernel,
        out_shape=(far_bf16(2, HALF, 256),) * 4 + (far_bf16(4, HALF, 256),) * 2,
        in_specs=[smem] + [anywhere] * 8,
        out_specs=(anywhere,) * 6,
        scratch_shapes=[
            pltpu.VMEM((2, ROWS, 1024), BF16),
            pltpu.VMEM((1024, 2 * ROWS), BF16),
            pltpu.VMEM((8, 2 * ROWS, 256), BF16),
            pltpu.VMEM((8, 1024, 256), BF16),
            pltpu.SemaphoreType.DMA((18,)),
            pltpu.SemaphoreType.DMA((16,)),
        ],
        name="projection_gradient",
        **params_of(2_147_483_648, 8_000_000),
    )(jnp.concatenate([index, core_array]), far(gated), other_gated, *[far(part) for part in cot_parts], other_cots, far(partial_out))
    came_z = lax.ppermute(other_z, "ctx", far_swap)
    came_y = [lax.ppermute(by_y[k], "ctx", shift_y(k)) for k in (1, 2, 3)]

    lines = [[2 * x + z for x in range(4)] for z in range(2)]
    arrived = exchange(partial_out.reshape(4, 2, ROWS, 512), "tp", lines).reshape(8, ROWS, 512)

    d_query, d_conv, payload = pl.pallas_call(
        cotangent_kernel,
        grid=(1,),
        out_shape=(bf16(ROWS, 1024), far_f32(ROWS * SUB, 128), far_bf16(BLOCKS, STATE + 2 * TERMS, 128)),
        in_specs=[
            smem,
            *[anywhere] * 5,
            full(ROWS, 1024),
            full(ROWS, 1024),
            full(ROWS * SUB, 128),
            full(MODES, SUB, 128),
            full(TABLE, 128),
            anywhere,
        ],
        out_specs=(full(ROWS, 1024), full(ROWS * SUB, 128), full(BLOCKS, STATE + 2 * TERMS, 128)),
        scratch_shapes=[
            pltpu.VMEM((ROWS, 1024), F32),
            pltpu.VMEM((BLOCKS * TERMS, 128), F32),
            pltpu.VMEM((8, ROWS, 512), BF16),
            pltpu.VMEM((8, 1024, 512), BF16),
            pltpu.SemaphoreType.DMA((16,)),
        ],
        name="cotangent_states",
        **params_of(14_000_000_000, 13_000_000),
    )(came, *[far(part) for part in cot_parts], far(w_out), far(query), far(conv_out), far(mixed), far(carry), far(table), far(other_z))
    received = exchange(payload, "ctx")

    near_out = add_placed(arrived, 1 - place_z, payload)
    near_sum = near_out
    near_out = lax.ppermute(near_out, "tp", shift_x(0, 1))
    output = add_placed(arrived, place_z, payload, near_out)

    first_far, *second_far = pl.pallas_call(
        stage_kernel,
        grid=(1,),
        out_shape=(bf16(HALF, 256),) * 4,
        in_specs=[pl.BlockSpec((1, HALF, 256), lambda i: (1, 0, 0))] * 4 + [full(4, HALF, 256)] * 2 + [anywhere],
        out_specs=(full(HALF, 256),) * 4,
        name="sum_stage",
        **params_of(LONG, 2_000_000),
    )(*[far(part) for part in [by_y[0]] + came_y], far(same_z), far(came_z), far(near_sum))
    first_far = lax.ppermute(first_far, "ctx", far_swap)
    second_far = [lax.ppermute(second_far[k - 1], "ctx", shift_y(k)) for k in (1, 2, 3)]

    d_key, d_value = pl.pallas_call(
        backward_kernel,
        grid=(1,),
        out_shape=(bf16(ROWS, 1024), bf16(ROWS, 1024)),
        in_specs=[
            smem,
            full(BLOCKS, STATE + 2 * TERMS, 128),
            full(ROWS * SUB, 128),
            full(ROWS, 1024),
            full(ROWS, 1024),
            full(TABLE, 128),
        ],
        out_specs=(full(ROWS, 1024), full(ROWS, 1024)),
        scratch_shapes=[pltpu.VMEM((MODES, SUB, 128), F32), pltpu.VMEM((ROWS * SUB, 128), F32)],
        name="backward_conv",
        **params_of(5_000_000_000, 4_000_000),
    )(own_array, far(received), far(d_conv), far(key_part), far(value_part), far(table))

    d_weight = half_gradient(0, [by_y[0], *came_y, first_far[None]], [d_key])
    d_weight = half_gradient(1, [same_z, came_z, *[part[None] for part in second_far]], [d_key], d_weight)

    d_residue, d_rate, d_skip = pl.pallas_call(
        owner_kernel,
        grid=(1,),
        out_shape=(f32(MODES, 64), f32(MODES, 64), f32(1, 64)),
        in_specs=[full(BLOCKS, STATE + 2 * TERMS, 128), whole(), whole()],
        out_specs=(whole(),) * 3,
        name="owner_sums",
        **params_of(1_000_000, 400_000),
    )(far(received), rate.T, residue.T)
    return (output, d_query, d_key, d_value, d_weight, d_residue.T, d_rate.T, d_skip[0])


def solution(mesh):
    rows, owner = P("ctx", "tp"), P(("tp", "ctx"))
    return jax.shard_map(
        local,
        mesh=mesh,
        in_specs=(rows, rows, rows, rows, P("tp", None), P(("tp", "ctx"), None), P(("tp", "ctx"), None), owner),
        out_specs=(rows, rows, rows, rows, P("tp", "ctx"), P(("tp", "ctx"), None), P(("tp", "ctx"), None), owner),
        check_vma=False,
    )
```

time: 149 us -> 130 us (0.87)
  Pallas kernels: 30 us -> 57.5 us
  local copies, waits for them, and re-layouts: 20.6 us -> 6.3 us
  waiting for transfers between devices: 35.9 us -> 21.8 us
  other arithmetic: 11.7 us -> 0.12 us
  starting transfers between devices: 49.1 us -> 42.5 us
    pallas_call x7 -> x14, Pallas kernels: 26 us -> 51.7 us  [the longest x1 14.2 us: local(): pl.pallas_call(cotangent_kernel, grid=(1,), out_shape=(bf16(ROWS, 1024),...]
    unnamed x54 -> x34, local copies, waits for them, and re-layouts: 17.2 us -> 6.3 us
    ppermute x3, waiting for transfers between devices: 8.35 us -> 1.86 us  [local(): came_y = [lax.ppermute(by_y[k], 'ctx', shift_y(k)) for k in (1, 2, 3)]]
    ppermute x10 -> x7, waiting for transfers between devices: 7.55 us -> 2.79 us  [the longest x1 2.78 us: local(): near_out = lax.ppermute(near_out, 'tp', shift_x(0, 1))]
    add x5 -> x0, other arithmetic: 4.35 us -> none  [the longest x1 1.62 us: local(): partial_out[0].astype(F32) + sum((part.astype(F32) for part in arrived))]
    ppermute x3, waiting for transfers between devices: 4.07 us -> 0.01 us  [local(): lax.ppermute(cot_pair, 'tp', shift_x(k))]
    convert_element_type x2 -> x0, other arithmetic: 3.82 us -> none  [the longest x1 2.1 us: local(): along_z[k].astype(BF16)]
    all_to_all x4, waiting for transfers between devices: 13.4 us -> 17.1 us  [exchange(): lax.all_to_all(array, axis, split_axis=0, concat_axis=0, tiled=True, axis...]
  transfers between devices with their start and end apart: 22 -> 19, of which waited for: 8 -> 6; matrix products, arithmetic and copies ran while one was open for 9% -> 0% of each run, Pallas kernels for 20% -> 42%
where the time goes in v3:
time: 130 us; the launch traced here: 129 us
  Pallas kernels  57.5 us (44%)
  starting transfers between devices  42.5 us (33%)
  waiting for transfers between devices  21.8 us (17%)
  local copies, waits for them, and re-layouts  6.3 us (5%)
    all_to_all x4, starting transfers between devices, exchange(): lax.all_to_all(array, axis, split_axis=0, concat_axis=0, tiled=True, axis...  23.1 us
    all_to_all x4, waiting for transfers between devices, exchange(): lax.all_to_all(array, axis, split_axis=0, concat_axis=0, tiled=True, axis...  17.1 us
    pallas_call x1, Pallas kernels, local(): pl.pallas_call(cotangent_kernel, grid=(1,), out_shape=(bf16(ROWS, 1024),...  14.2 us
    pallas_call x1, Pallas kernels, local(): pl.pallas_call(weight_kernel, out_shape=(far_bf16(2, HALF, 256),) * 4 + (...  6.51 us
    unnamed x34, local copies, waits for them, and re-layouts  6.3 us
    pallas_call x1, Pallas kernels, local(): pl.pallas_call(backward_kernel, grid=(1,), out_shape=(bf16(ROWS, 1024), b...  5.87 us
    pallas_call x1, Pallas kernels, local(): pl.pallas_call(output_kernel, out_shape=far_bf16(8, ROWS, 512), in_specs=...  5.75 us
    ppermute x3, starting transfers between devices, local(): lax.ppermute(cot_pair, 'tp', shift_x(k))  5.65 us
  transfers between devices with their start and end apart: 19, of which 6 were waited for; matrix products, arithmetic and copies ran while one was open for 0% of the time, Pallas kernels for 42%

profile of v3, /device:TPU:0, one launch (start us, length us, event | category | flops | bytes accessed | tf_op | source)
XLA Modules:
  0.0 129.2 jit_solution(16458815580947559152)
XLA Ops:
  0.6 2.1 %collective-permute-start = (bf16[256,512]{1,0:T(8,128)(2,1)}, bf16[256,512]{1,0:T(8,128)(2,1)S(1)}, u32[]{:S(2)}, u32[]{:S(2)}) collective-permute-start(bf16[256,512]{1,0:T(8,128)(2,1)} %cot_ref.1), channel_id=1, source_target_pairs={{0,1},{1,0},{2,3},{3,2},{4,5},{5,4},{6,7},{7,6},{8,9},{9,8},{10,11... | collective-permute-start | bytes 786440 | tf_op jit(solution)/shard_map/ppermute | solution.py:469
  4.2 7.6 %all-to-all-start = ((f32[16,24,128]{2,1,0:T(8,128)}), f32[16,24,128]{2,1,0:T(8,128)S(1)}, u32[]{:S(2)}, u32[]{:S(2)}) async-start(f32[16,24,128]{2,1,0:T(8,128)} %pack_parameters.1), calls=%async_computation | async-start | bytes 393216 | tf_op jit(solution)/shard_map/all_to_all | solution.py:424
  11.8 2.8 %mix_inputs.1 = (f32[2048,128]{1,0:T(8,128)S(1)}, f32[2048,128]{1,0:T(8,128)}, bf16[2,256,512]{2,1,0:T(8,128)(2,1)}) custom-call(bf16[256,1024]{1,0:T(8,128)(2,1)} %key_ref.3, bf16[256,1024]{1,0:T(8,128)(2,1)} %value_ref.3, bf16[256,512]{1,0:T(8,128)(2,1)} %cot_ref.1, bf16[256,512]{1,0:T(8,128)(2,1)S(1)} %collective-permute-done.near_cot_ref), custom_call_target="tpu_custom_call" | custom-call | flops 2000000 | bytes 60000 | tf_op jit(solution)/shard_map/mix_inputs/pallas_call | solution.py:470
  16.1 2.7 %collective-permute-start.2 = (bf16[2,256,512]{2,1,0:T(8,128)(2,1)}, bf16[2,256,512]{2,1,0:T(8,128)(2,1)S(1)}, u32[]{:S(2)}, u32[]{:S(2)}) collective-permute-start(bf16[2,256,512]{2,1,0:T(8,128)(2,1)} %get-tuple-element.41.refs_0_.part0), channel_id=1, source_target_pairs={{0,4},{1,5},{2,6},{3,7},{4,0},{5,1},{6,2},{7,3},{8,12},{9,13},{10,... | collective-permute-start | bytes 1572872 | tf_op jit(solution)/shard_map/ppermute | solution.py:479
  20.4 2.2 %forward_states.1 = (bf16[16,16,8,128]{3,2,1,0:T(8,128)(2,1)}, f32[384,128]{1,0:T(8,128)}) custom-call(f32[2048,128]{1,0:T(8,128)S(1)} %get-tuple-element.36.mixed_ref, f32[16,24,128]{2,1,0:T(8,128)S(1)} %all-to-all-done.packed_ref), custom_call_target="tpu_custom_call" | custom-call | flops 60000000 | bytes 80000 | tf_op jit(solution)/shard_map/forward_states/pallas_call | solution.py:481
  22.6 7.1 %all-to-all-start.1 = ((bf16[16,16,8,128]{3,2,1,0:T(8,128)(2,1)}), bf16[16,16,8,128]{3,2,1,0:T(8,128)(2,1)S(1)}, u32[]{:S(2)}, u32[]{:S(2)}) async-start(bf16[16,16,8,128]{3,2,1,0:T(8,128)(2,1)} %get-tuple-element.37), calls=%async_computation.1 | async-start | bytes 1048576 | tf_op jit(solution)/shard_map/all_to_all | solution.py:424
  29.7 12.4 %all-to-all-done.1.sent_ref = bf16[16,16,8,128]{3,2,1,0:T(8,128)(2,1)S(1)} async-done(((bf16[16,16,8,128]{3,2,1,0:T(8,128)(2,1)}), bf16[16,16,8,128]{3,2,1,0:T(8,128)(2,1)S(1)}, u32[]{:S(2)}, u32[]{:S(2)}) %all-to-all-start.1) | async-done | bytes 524320 | tf_op jit(solution)/shard_map/all_to_all | solution.py:424
  42.1 5.3 %forward_conv.1 = (bf16[256,1024]{1,0:T(8,128)(2,1)}, bf16[256,1024]{1,0:T(8,128)(2,1)}, f32[16,8,128]{2,1,0:T(8,128)}) custom-call(s32[1]{0:T(128)} %bitcast.1.own_ref, bf16[16,16,8,128]{3,2,1,0:T(8,128)(2,1)S(1)} %all-to-all-done.1.sent_ref, f32[2048,128]{1,0:T(8,128)} %get-tuple-element.38.mixed_ref, bf16[256,1024]{1,0:T(8,128)(2,1)} %query_ref.3, ...), custom_call_target="tpu_custom_call" | custom-call | flops 100000000 | bytes 80000 | tf_op jit(solution)/shard_map/forward_conv/pallas_call | solution.py:492
  51.2 5.7 %output_projection.1.refs_5_ = bf16[8,256,512]{2,1,0:T(8,128)(2,1)} custom-call(bf16[256,1024]{1,0:T(8,128)(2,1)} %get-tuple-element.40.refs_4_.gated_ref, bf16[1024,4096]{1,0:T(8,128)(2,1)} %weight_ref.3, f32[8,128]{1,0:T(8,128)S(1)} %copy-done.3), custom_call_target="tpu_custom_call" | custom-call | flops 42949672 | bytes 220000 | tf_op jit(solution)/shard_map/output_projection/pallas_call | solution.py:516
  56.9 4.5 %all-to-all-start.2 = ((bf16[4,2,256,512]{3,2,1,0:T(8,128)(2,1)}), bf16[4,2,256,512]{3,2,1,0:T(8,128)(2,1)}, u32[]{:S(2)}, u32[]{:S(2)}) async-start(bf16[4,2,256,512]{3,2,1,0:T(8,128)(2,1)} %bitcast.20), calls=%async_computation.2 | async-start | bytes 4194304 | tf_op jit(solution)/shard_map/all_to_all | solution.py:424
  61.6 6.5 %projection_gradient.1 = (bf16[2,512,256]{2,1,0:T(8,128)(2,1)}, bf16[2,512,256]{2,1,0:T(8,128)(2,1)}, bf16[2,512,256]{2,1,0:T(8,128)(2,1)}, bf16[2,512,256]{2,1,...) custom-call(s32[9]{0:T(128)S(1)} %pad_add_fusion.index_ref, ...), custom_call_target="tpu_custom_call" | custom-call | flops 42949672 | bytes 160000 | tf_op jit(solution)/shard_map/projection_gradient/pallas_call | solution.py:531
  71.9 14.2 %cotangent_states.1 = (bf16[256,1024]{1,0:T(8,128)(2,1)}, f32[2048,128]{1,0:T(8,128)}, bf16[16,224,128]{2,1,0:T(8,128)(2,1)}) custom-call(s32[8]{0:T(128)S(1)} %fusion.came_ref, bf16[2,256,512]{2,1,0:T(8,128)(2,1)} %get-tuple-element.41.refs_0_.part0, bf16[2,256,512]{2,1,0:T(8,128)(2,1)} %copy-done.5, bf16[2,256,512]{2,1,0:T(8,128)(2,1)} %copy-done.6, ...), custom_call_target="tpu_custom_call" | custom-call | flops 280000000 | bytes 260000 | tf_op jit(solution)/shard_map/cotangent_states/pallas_call | solution.py:553
  86.1 2.2 %all-to-all-done.2 = bf16[4,2,256,512]{3,2,1,0:T(8,128)(2,1)} async-done(((bf16[4,2,256,512]{3,2,1,0:T(8,128)(2,1)}), bf16[4,2,256,512]{3,2,1,0:T(8,128)(2,1)}, u32[]{:S(2)}, u32[]{:S(2)}) %all-to-all-start.2) | async-done | bytes 2097184 | tf_op jit(solution)/shard_map/all_to_all | solution.py:424
  88.3 4.0 %all-to-all-start.3 = ((bf16[16,224,128]{2,1,0:T(8,128)(2,1)}), bf16[16,224,128]{2,1,0:T(8,128)(2,1)S(1)}, u32[]{:S(2)}, u32[]{:S(2)}) async-start(bf16[16,224,128]{2,1,0:T(8,128)(2,1)} %get-tuple-element.47.refs_4_.refs_5_), calls=%async_computation.3 | async-start | bytes 1835008 | tf_op jit(solution)/shard_map/all_to_all | solution.py:424
  96.9 2.2 %sum_stage.1 = (bf16[512,256]{1,0:T(8,128)(2,1)S(1)}, bf16[512,256]{1,0:T(8,128)(2,1)S(1)}, bf16[512,256]{1,0:T(8,128)(2,1)S(1)}, bf16[512,256]{1,0:T(8,128)(2,1)S(1)}) custom-call(bf16[2,512,256]{2,1,0:T(8,128)(2,1)} %get-tuple-element.53.refs_0_, bf16[2,512,256]{2,1,0:T(8,128)(2,1)} %copy-done.10, bf16[2,512,256]{2,1,0:T(8,128)(2,1)} %copy-done.11, ...), custom_call_target="tpu_custom_call" | custom-call | flops 40000000000 | bytes 40000 | tf_op jit(solution)/shard_map/sum_stage/pallas_call | solution.py:585
  99.1 3.0 %collective-permute-start.14 = (bf16[512,256]{1,0:T(8,128)(2,1)S(1)}, bf16[512,256]{1,0:T(8,128)(2,1)S(1)}, u32[]{:S(2)}, u32[]{:S(2)}) collective-permute-start(bf16[512,256]{1,0:T(8,128)(2,1)S(1)} %get-tuple-element.60), channel_id=1, source_target_pairs={{0,64},{8,72},{16,80},{24,88},{32,96},{40,104},{48,112},{56,120},{... | collective-permute-start | bytes 786440 | tf_op jit(solution)/shard_map/ppermute | solution.py:594
  102.1 2.1 %collective-permute-start.12 = (bf16[512,256]{1,0:T(8,128)(2,1)S(1)}, bf16[512,256]{1,0:T(8,128)(2,1)S(1)}, u32[]{:S(2)}, u32[]{:S(2)}) collective-permute-start(bf16[512,256]{1,0:T(8,128)(2,1)S(1)} %get-tuple-element.58), channel_id=1, source_target_pairs={{0,32},{8,40},{16,48},{24,56},{32,0},{40,8},{48,16},{56,24},{64,96... | collective-permute-start | bytes 786440 | tf_op jit(solution)/shard_map/ppermute | solution.py:595
  106.3 2.8 %collective-permute-done.6.refs_4_ = bf16[256,512]{1,0:T(8,128)(2,1)S(1)} collective-permute-done((bf16[256,512]{1,0:T(8,128)(2,1)S(1)}, bf16[256,512]{1,0:T(8,128)(2,1)S(1)}, u32[]{:S(2)}, u32[]{:S(2)}) %collective-permute-start.6) | collective-permute-done | bytes 262176 | tf_op jit(solution)/shard_map/ppermute | solution.py:582
  109.7 2.2 %sum_output.3 = bf16[256,512]{1,0:T(8,128)(2,1)} custom-call(s32[1]{0:T(128)} %bitcast.place_ref, bf16[8,256,512]{2,1,0:T(8,128)(2,1)} %bitcast.7.refs_0_.refs_1_.refs_2_.refs_3_, bf16[8,256,512]{2,1,0:T(8,128)(2,1)} %bitcast.7.refs_0_.refs_1_.refs_2_.refs_3_, bf16[8,256,512]{2,1,0:T(8,128)(2,1)} %bitcast.7.refs_0_.refs_1_.refs_2_.refs_3_, ...), custom_call_target="tpu_custom_call" | custom-call | flops 20000 | bytes 40000 | tf_op jit(solution)/shard_map/sum_output/pallas_call | solution.py:354
  111.9 2.4 %all-to-all-done.3.sent_ref.parts_ref = bf16[16,224,128]{2,1,0:T(8,128)(2,1)S(1)} async-done(((bf16[16,224,128]{2,1,0:T(8,128)(2,1)}), bf16[16,224,128]{2,1,0:T(8,128)(2,1)S(1)}, u32[]{:S(2)}, u32[]{:S(2)}) %all-to-all-start.3) | async-done | bytes 917536 | tf_op jit(solution)/shard_map/all_to_all | solution.py:424
  115.3 2.0 %owner_sums.1 = (f32[16,64]{1,0:T(8,128)}, f32[16,64]{1,0:T(8,128)}, f32[1,64]{1,0:T(1,128)}) custom-call(bf16[16,224,128]{2,1,0:T(8,128)(2,1)} %copy-done.4, f32[16,64]{1,0:T(8,128)S(1)} %bitcast.17, f32[16,64]{1,0:T(8,128)S(1)} %bitcast.19), custom_call_target="tpu_custom_call" | custom-call | flops 20000 | bytes 8000 | tf_op jit(solution)/shard_map/owner_sums/pallas_call | solution.py:618
  117.3 5.9 %backward_conv.1 = (bf16[256,1024]{1,0:T(8,128)(2,1)}, bf16[256,1024]{1,0:T(8,128)(2,1)}) custom-call(s32[1]{0:T(128)} %bitcast.1.own_ref, bf16[16,224,128]{2,1,0:T(8,128)(2,1)} %copy-done.4, f32[2048,128]{1,0:T(8,128)} %get-tuple-element.49.dconv_ref, bf16[256,1024]{1,0:T(8,128)(2,1)} %key_ref.3, bf16[256,1024]{1,0:T(8,128)(2,1)} %value_ref.3, ...), custom_call_target="tpu_custom_call" | custom-call | flops 100000000 | bytes 80000 | tf_op jit(solution)/shard_map/backward_conv/pallas_call | solution.py:597
  123.9 2.2 %sum_gradient.2.refs_5_ = f32[1024,256]{1,0:T(8,128)} custom-call(bf16[2,512,256]{2,1,0:T(8,128)(2,1)} %get-tuple-element.53.refs_0_, bf16[2,512,256]{2,1,0:T(8,128)(2,1)} %copy-done.10, bf16[2,512,256]{2,1,0:T(8,128)(2,1)} %copy-done.11, bf16[2,512,256]{2,1,0:T(8,128)(2,1)} %copy-done.9, bf16[1,512,256]{2,1,0:T(8,128)(2,1)} %bitcast.24, ...), custom_call_target="tpu_custom_call" | custom-call | flops 40000 | bytes 80000 | tf_op jit(solution)/shard_map/sum_gradient/pallas_call | solution.py:378
  127.0 2.2 %sum_gradient.3 = f32[1024,256]{1,0:T(8,128)} custom-call(bf16[4,512,256]{2,1,0:T(8,128)(2,1)} %get-tuple-element.52.refs_4_.refs_0_, bf16[4,512,256]{2,1,0:T(8,128)(2,1)} %copy-done.8, bf16[1,512,256]{2,1,0:T(8,128)(2,1)} %bitcast.23, bf16[1,512,256]{2,1,0:T(8,128)(2,1)} %bitcast.21, bf16[1,512,256]{2,1,0:T(8,128)(2,1)} %bitcast.22, ...), custom_call_target="tpu_custom_call", output_to_operand_aliasing={{}: (5, {})} | custom-call | flops 40000 | bytes 80000 | tf_op jit(solution)/shard_map/sum_gradient/pallas_call | solution.py:378
  (66 shorter events, 22.0 us)
Async XLA Ops:
  0.6 11.2 %collective-permute-start = (bf16[256,512]{1,0:T(8,128)(2,1)}, bf16[256,512]{1,0:T(8,128)(2,1)S(1)}, u32[]{:S(2)}, u32[]{:S(2)}) collective-permute-start(bf16[256,512]{1,0:T(8,128)(2,1)} %cot_ref.1), channel_id=1, source_target_pairs={{0,1},{1,0},{2,3},{3,2},{4,5},{5,4},{6,7},{7,6},{8,9},{9,8},{10,11... | collective-permute-start | bytes 786440 | tf_op jit(solution)/shard_map/ppermute | solution.py:469
  4.2 16.2 %all-to-all-start = ((f32[16,24,128]{2,1,0:T(8,128)}), f32[16,24,128]{2,1,0:T(8,128)S(1)}, u32[]{:S(2)}, u32[]{:S(2)}) async-start(f32[16,24,128]{2,1,0:T(8,128)} %pack_parameters.1), calls=%async_computation | async-start | bytes 393216 | tf_op jit(solution)/shard_map/all_to_all | solution.py:424
  14.6 32.7 %collective-permute-start.1 = (bf16[2,256,512]{2,1,0:T(8,128)(2,1)}, bf16[2,256,512]{2,1,0:T(8,128)(2,1)S(1)}, u32[]{:S(2)}, u32[]{:S(2)}) collective-permute-start(bf16[2,256,512]{2,1,0:T(8,128)(2,1)} %get-tuple-element.41.refs_0_.part0), channel_id=1, source_target_pairs={{0,2},{1,3},{2,4},{3,5},{4,6},{5,7},{6,0},{7,1},{8,10},{9,11},{10,... | collective-permute-start | bytes 1572872 | tf_op jit(solution)/shard_map/ppermute | solution.py:479
  16.1 31.3 %collective-permute-start.2 = (bf16[2,256,512]{2,1,0:T(8,128)(2,1)}, bf16[2,256,512]{2,1,0:T(8,128)(2,1)S(1)}, u32[]{:S(2)}, u32[]{:S(2)}) collective-permute-start(bf16[2,256,512]{2,1,0:T(8,128)(2,1)} %get-tuple-element.41.refs_0_.part0), channel_id=1, source_target_pairs={{0,4},{1,5},{2,6},{3,7},{4,0},{5,1},{6,2},{7,3},{8,12},{9,13},{10,... | collective-permute-start | bytes 1572872 | tf_op jit(solution)/shard_map/ppermute | solution.py:479
  18.8 28.5 %collective-permute-start.3 = (bf16[2,256,512]{2,1,0:T(8,128)(2,1)}, bf16[2,256,512]{2,1,0:T(8,128)(2,1)S(1)}, u32[]{:S(2)}, u32[]{:S(2)}) collective-permute-start(bf16[2,256,512]{2,1,0:T(8,128)(2,1)} %get-tuple-element.41.refs_0_.part0), channel_id=1, source_target_pairs={{0,6},{1,7},{2,0},{3,1},{4,2},{5,3},{6,4},{7,5},{8,14},{9,15},{10,... | collective-permute-start | bytes 1572872 | tf_op jit(solution)/shard_map/ppermute | solution.py:479
  22.6 19.5 %all-to-all-start.1 = ((bf16[16,16,8,128]{3,2,1,0:T(8,128)(2,1)}), bf16[16,16,8,128]{3,2,1,0:T(8,128)(2,1)S(1)}, u32[]{:S(2)}, u32[]{:S(2)}) async-start(bf16[16,16,8,128]{3,2,1,0:T(8,128)(2,1)} %get-tuple-element.37), calls=%async_computation.1 | async-start | bytes 1048576 | tf_op jit(solution)/shard_map/all_to_all | solution.py:424
  49.9 11.7 %collective-permute-start.5 = (bf16[8,256,256]{2,1,0:T(8,128)(2,1)S(1)}, bf16[8,256,256]{2,1,0:T(8,128)(2,1)S(1)}, u32[]{:S(2)}, u32[]{:S(2)}) collective-permute-start(bf16[8,256,256]{2,1,0:T(8,128)(2,1)S(1)} %get-tuple-element.45), channel_id=1, source_target_pairs={{0,8},{8,0},{16,24},{24,16},{32,40},{40,32},{48,56},{56,48},{64,72... | collective-permute-start | bytes 3145736 | tf_op jit(solution)/shard_map/ppermute | solution.py:513
  50.0 11.6 %collective-permute-start.4 = (bf16[256,1024]{1,0:T(8,128)(2,1)}, bf16[256,1024]{1,0:T(8,128)(2,1)S(1)}, u32[]{:S(2)}, u32[]{:S(2)}) collective-permute-start(bf16[256,1024]{1,0:T(8,128)(2,1)} %get-tuple-element.40.refs_4_.gated_ref), channel_id=1, source_target_pairs={{0,8},{8,0},{16,24},{24,16},{32,40},{40,32},{48,56},{56,48},{64,72... | collective-permute-start | bytes 1572872 | tf_op jit(solution)/shard_map/ppermute | solution.py:503
  56.9 31.4 %all-to-all-start.2 = ((bf16[4,2,256,512]{3,2,1,0:T(8,128)(2,1)}), bf16[4,2,256,512]{3,2,1,0:T(8,128)(2,1)}, u32[]{:S(2)}, u32[]{:S(2)}) async-start(bf16[4,2,256,512]{3,2,1,0:T(8,128)(2,1)} %bitcast.20), calls=%async_computation.2 | async-start | bytes 4194304 | tf_op jit(solution)/shard_map/all_to_all | solution.py:424
  68.1 27.5 %collective-permute-start.7 = (bf16[4,512,256]{2,1,0:T(8,128)(2,1)}, bf16[4,512,256]{2,1,0:T(8,128)(2,1)S(1)}, u32[]{:S(2)}, u32[]{:S(2)}) collective-permute-start(bf16[4,512,256]{2,1,0:T(8,128)(2,1)} %get-tuple-element.46.after_ref), channel_id=1, source_target_pairs={{0,64},{8,72},{16,80},{24,88},{32,96},{40,104},{48,112},{56,120},{... | collective-permute-start | bytes 3145736 | tf_op jit(solution)/shard_map/ppermute | solution.py:547
  68.7 25.0 %collective-permute-start.10 = (bf16[2,512,256]{2,1,0:T(8,128)(2,1)}, bf16[2,512,256]{2,1,0:T(8,128)(2,1)S(1)}, u32[]{:S(2)}, u32[]{:S(2)}) collective-permute-start(bf16[2,512,256]{2,1,0:T(8,128)(2,1)} %get-tuple-element.56), channel_id=1, source_target_pairs={{0,48},{8,56},{16,0},{24,8},{32,16},{40,24},{48,32},{56,40},{64,11... | collective-permute-start | bytes 1572872 | tf_op jit(solution)/shard_map/ppermute | solution.py:548
  69.6 26.0 %collective-permute-start.8 = (bf16[2,512,256]{2,1,0:T(8,128)(2,1)}, bf16[2,512,256]{2,1,0:T(8,128)(2,1)S(1)}, u32[]{:S(2)}, u32[]{:S(2)}) collective-permute-start(bf16[2,512,256]{2,1,0:T(8,128)(2,1)} %get-tuple-element.54), channel_id=1, source_target_pairs={{0,16},{8,24},{16,32},{24,40},{32,48},{40,56},{48,0},{56,8},{64,80... | collective-permute-start | bytes 1572872 | tf_op jit(solution)/shard_map/ppermute | solution.py:548
  70.7 24.9 %collective-permute-start.9 = (bf16[2,512,256]{2,1,0:T(8,128)(2,1)}, bf16[2,512,256]{2,1,0:T(8,128)(2,1)S(1)}, u32[]{:S(2)}, u32[]{:S(2)}) collective-permute-start(bf16[2,512,256]{2,1,0:T(8,128)(2,1)} %get-tuple-element.55), channel_id=1, source_target_pairs={{0,32},{8,40},{16,48},{24,56},{32,0},{40,8},{48,16},{56,24},{64,96... | collective-permute-start | bytes 1572872 | tf_op jit(solution)/shard_map/ppermute | solution.py:548
  88.3 26.0 %all-to-all-start.3 = ((bf16[16,224,128]{2,1,0:T(8,128)(2,1)}), bf16[16,224,128]{2,1,0:T(8,128)(2,1)S(1)}, u32[]{:S(2)}, u32[]{:S(2)}) async-start(bf16[16,224,128]{2,1,0:T(8,128)(2,1)} %get-tuple-element.47.refs_4_.refs_5_), calls=%async_computation.3 | async-start | bytes 1835008 | tf_op jit(solution)/shard_map/all_to_all | solution.py:424
  93.6 3.0 %copy-start = (bf16[256,512]{1,0:T(8,128)(2,1)}, bf16[256,512]{1,0:T(8,128)(2,1)S(1)}, u32[]{:S(2)}) copy-start(bf16[256,512]{1,0:T(8,128)(2,1)S(1)} %sum_output.2.refs_6_) | copy-start | bytes 786436
  93.6 15.4 %collective-permute-start.6 = (bf16[256,512]{1,0:T(8,128)(2,1)S(1)}, bf16[256,512]{1,0:T(8,128)(2,1)S(1)}, u32[]{:S(2)}, u32[]{:S(2)}) collective-permute-start(bf16[256,512]{1,0:T(8,128)(2,1)S(1)} %sum_output.2.refs_6_), channel_id=1, source_target_pairs={{0,1},{1,0},{2,3},{3,2},{4,5},{5,4},{6,7},{7,6},{8,9},{9,8},{10,11... | collective-permute-start | bytes 786440 | tf_op jit(solution)/shard_map/ppermute | solution.py:582
  93.7 2.8 %copy-start.9 = (bf16[2,512,256]{2,1,0:T(8,128)(2,1)}, bf16[2,512,256]{2,1,0:T(8,128)(2,1)S(1)}, u32[]{:S(2)}) copy-start(bf16[2,512,256]{2,1,0:T(8,128)(2,1)S(1)} %collective-permute-done.10.refs_3_) | copy-start | bytes 1572868
  95.6 1.3 %copy-start.8 = (bf16[4,512,256]{2,1,0:T(8,128)(2,1)}, bf16[4,512,256]{2,1,0:T(8,128)(2,1)S(1)}, u32[]{:S(2)}) copy-start(bf16[4,512,256]{2,1,0:T(8,128)(2,1)S(1)} %collective-permute-done.7.refs_5_.refs_1_) | copy-start | bytes 3145732
  99.1 24.1 %collective-permute-start.14 = (bf16[512,256]{1,0:T(8,128)(2,1)S(1)}, bf16[512,256]{1,0:T(8,128)(2,1)S(1)}, u32[]{:S(2)}, u32[]{:S(2)}) collective-permute-start(bf16[512,256]{1,0:T(8,128)(2,1)S(1)} %get-tuple-element.60), channel_id=1, source_target_pairs={{0,64},{8,72},{16,80},{24,88},{32,96},{40,104},{48,112},{56,120},{... | collective-permute-start | bytes 786440 | tf_op jit(solution)/shard_map/ppermute | solution.py:594
  102.1 24.0 %collective-permute-start.12 = (bf16[512,256]{1,0:T(8,128)(2,1)S(1)}, bf16[512,256]{1,0:T(8,128)(2,1)S(1)}, u32[]{:S(2)}, u32[]{:S(2)}) collective-permute-start(bf16[512,256]{1,0:T(8,128)(2,1)S(1)} %get-tuple-element.58), channel_id=1, source_target_pairs={{0,32},{8,40},{16,48},{24,56},{32,0},{40,8},{48,16},{56,24},{64,96... | collective-permute-start | bytes 786440 | tf_op jit(solution)/shard_map/ppermute | solution.py:595
  104.2 21.9 %collective-permute-start.13 = (bf16[512,256]{1,0:T(8,128)(2,1)S(1)}, bf16[512,256]{1,0:T(8,128)(2,1)S(1)}, u32[]{:S(2)}, u32[]{:S(2)}) collective-permute-start(bf16[512,256]{1,0:T(8,128)(2,1)S(1)} %get-tuple-element.59), channel_id=1, source_target_pairs={{0,48},{8,56},{16,0},{24,8},{32,16},{40,24},{48,32},{56,40},{64,11... | collective-permute-start | bytes 786440 | tf_op jit(solution)/shard_map/ppermute | solution.py:595
  105.4 20.7 %collective-permute-start.11 = (bf16[512,256]{1,0:T(8,128)(2,1)S(1)}, bf16[512,256]{1,0:T(8,128)(2,1)S(1)}, u32[]{:S(2)}, u32[]{:S(2)}) collective-permute-start(bf16[512,256]{1,0:T(8,128)(2,1)S(1)} %get-tuple-element.57), channel_id=1, source_target_pairs={{0,16},{8,24},{16,32},{24,40},{32,48},{40,56},{48,0},{56,8},{64,80... | collective-permute-start | bytes 786440 | tf_op jit(solution)/shard_map/ppermute | solution.py:595
  109.7 5.5 %copy-start.1 = (f32[64,16]{0,1:T(8,128)S(1)}, f32[64,16]{0,1:T(8,128)}, u32[]{:S(2)}) copy-start(f32[64,16]{0,1:T(8,128)} %param.14) | copy-start | bytes 12292
  109.7 5.5 %copy-start.2 = (f32[64,16]{0,1:T(8,128)S(1)}, f32[64,16]{0,1:T(8,128)}, u32[]{:S(2)}) copy-start(f32[64,16]{0,1:T(8,128)} %param.13) | copy-start | bytes 12292
  (12 other events, 10.0 us)

commit v4 on v3

--- a/solution.py
+++ b/solution.py
@@ -113,7 +113,7 @@
 
 
 def gather_kernel(core_ref, *refs):
-    parts, half_ref, sems = refs[:4], refs[5], refs[7]
+    parts, half_ref, sems = refs[:4], refs[5], refs[6]
     half = pl.ds(pl.multiple_of((1 - core_ref[0]) * 256, 256), 256)
     copies = [
         pltpu.make_async_copy(parts[i // 2].at[i % 2, :, half], half_ref.at[i], sems.at[i]) for i in range(8)
@@ -145,14 +145,35 @@
             sent_ref[j, m] = state
 
 
-def forward_kernel(own_ref, sent_ref, mixed_ref, query_ref, table, conv_ref, gated_ref, carry_ref, buffer):
+def forward_kernel(
+    own_ref, sent_ref, mixed_in, query_in, table_in, weight_in,
+    conv_out, gated_out, carry_out, gated_ref, weight_ref,
+    buffer, mixed_ref, query_ref, table, conv_ref, carry_ref, sems,
+):
     own = own_ref[0]
+    copies = [
+        pltpu.make_async_copy(source, target, sems.at[i])
+        for i, (source, target) in enumerate([(table_in, table), (mixed_in, mixed_ref), (query_in, query_ref)])
+    ]
+    weights = [
+        pltpu.make_async_copy(weight_in.at[:, 512 * i : 512 * (i + 1)], weight_ref.at[i], sems.at[6 + i])
+        for i in range(8)
+    ]
+    results = [
+        pltpu.make_async_copy(source, target, sems.at[3 + i])
+        for i, (source, target) in enumerate([(carry_ref, carry_out), (conv_ref, conv_out), (gated_ref, gated_out)])
+    ]
+    for copy in copies + weights:
+        copy.start()
+    copies[0].wait()
     for m in range(MODES):
         far = block_decay(table, m)
         carry = jnp.zeros((SUB, 128), F32)
         for j in range(BLOCKS - 1):
             carry = jnp.where(j < own, far * carry + sent_ref[j, m].astype(F32), carry)
         carry_ref[m] = carry
+    results[0].start()
+    copies[1].wait()
     decay = [step_decay(table, m) for m in range(MODES)]
     weight = [mode_weight(table, m) for m in range(MODES)]
     skip = skip_of(table)
@@ -167,25 +188,21 @@
         return held
 
     lax.fori_loop(0, ROWS // UNROLL, body, tuple(carry_ref[m] for m in range(MODES)))
+    copies[2].wait()
     for group in range(SUB):
         conv = buffer[group_rows(group), :].astype(BF16)
         conv_ref[:, lanes(group)] = conv
         gated_ref[:, lanes(group)] = (query_ref[:, lanes(group)].astype(F32) * conv.astype(F32)).astype(BF16)
-
-
-def output_kernel(gated_ref, weight_ref, after_ref, out_ref, gated, weight, blocks, sems):
-    copies = [
-        pltpu.make_async_copy(weight_ref.at[:, 512 * i : 512 * (i + 1)], weight.at[i], sems.at[i]) for i in range(8)
-    ]
-    results = [pltpu.make_async_copy(blocks.at[i], out_ref.at[i], sems.at[8 + i]) for i in range(8)]
-    first = pltpu.make_async_copy(gated_ref, gated, sems.at[16])
-    first.start()
-    for copy in copies:
-        copy.start()
-    first.wait()
+    results[1].start()
+    results[2].start()
+    for copy in results + weights:
+        copy.wait()
+
+
+def output_kernel(gated_ref, weight_ref, out_ref, blocks, sems):
+    results = [pltpu.make_async_copy(blocks.at[i], out_ref.at[i], sems.at[i]) for i in range(8)]
     for i in range(8):
-        copies[i].wait()
-        blocks[i] = jnp.dot(gated[...], weight[i], preferred_element_type=F32).astype(BF16)
+        blocks[i] = jnp.dot(gated_ref[...], weight_ref[i], preferred_element_type=F32).astype(BF16)
         results[i].start()
     for result in results:
         result.wait()
@@ -227,8 +244,9 @@
 
 
 def cotangent_kernel(
-    came_ref, part0, part1, part2, part3, weight_ref, query_ref, conv_ref, mixed_ref, carry_ref, table, after_ref,
-    dquery_ref, dconv_ref, sent_ref, total, terms, parts, weight, sems,
+    came_ref, part0, part1, part2, part3, weight_ref, query_in, conv_in, mixed_in, carry_in, table_in, after_ref,
+    dquery_out, dconv_out, sent_out,
+    total, terms, parts, weight, query_ref, conv_ref, mixed_ref, carry_ref, table, dquery_ref, dconv_ref, sent_ref, sems,
 ):
     copies = []
     for i in range(8):
@@ -236,7 +254,19 @@
         part = (part0, part1, part2, part3)[i // 2].at[i % 2]
         copies.append(pltpu.make_async_copy(weight_ref.at[:, columns], weight.at[i], sems.at[i]))
         copies.append(pltpu.make_async_copy(part, parts.at[i], sems.at[8 + i]))
-    for copy in copies:
+    later = [
+        pltpu.make_async_copy(source, target, sems.at[16 + i])
+        for i, (source, target) in enumerate(
+            [(query_in, query_ref), (conv_in, conv_ref), (mixed_in, mixed_ref), (carry_in, carry_ref), (table_in, table)]
+        )
+    ]
+    results = [
+        pltpu.make_async_copy(source, target, sems.at[21 + i])
+        for i, (source, target) in enumerate(
+            [(dquery_ref, dquery_out), (dconv_ref, dconv_out), (sent_ref, sent_out)]
+        )
+    ]
+    for copy in copies + later:
         copy.start()
     for i in range(8):
         copies[2 * i].wait()
@@ -246,11 +276,15 @@
             total[...] = product
         else:
             total[...] += product
+    for copy in later:
+        copy.wait()
     for group in range(SUB):
         cot = total[:, lanes(group)]
         dquery_ref[:, lanes(group)] = (cot * conv_ref[:, lanes(group)].astype(F32)).astype(BF16)
         dconv_ref[group_rows(group), :] = (cot * query_ref[:, lanes(group)].astype(F32)).astype(BF16).astype(F32)
 
+    results[0].start()
+    results[1].start()
     left = lax.broadcasted_iota(jnp.int32, (SUB, 128), 1) < 64
 
     def put(row, one, two):
@@ -299,16 +333,44 @@
         upper = term.astype(BF16)
         sent_ref[j, STATE : STATE + TERMS, :] = upper
         sent_ref[j, STATE + TERMS :, :] = (term - upper.astype(F32)).astype(BF16)
-
-
-def backward_kernel(own_ref, sent_ref, dconv_ref, key_ref, value_ref, table, dkey_ref, dvalue_ref, carry_ref, buffer):
+    results[2].start()
+    for result in results:
+        result.wait()
+
+
+def backward_kernel(
+    own_ref, sent_in, dconv_in, key_in, value_in, table_in,
+    dkey_out, dvalue_out,
+    sent_ref, dconv_ref, key_ref, value_ref, table, dkey_ref, dvalue_ref, carry_ref, buffer, sems,
+):
     own = own_ref[0]
+    copies = [
+        pltpu.make_async_copy(source, target, sems.at[i])
+        for i, (source, target) in enumerate(
+            [
+                (sent_in.at[:, :STATE], sent_ref),
+                (table_in, table),
+                (dconv_in, dconv_ref),
+                (key_in, key_ref),
+                (value_in, value_ref),
+            ]
+        )
+    ]
+    results = [
+        pltpu.make_async_copy(dkey_ref, dkey_out, sems.at[5]),
+        pltpu.make_async_copy(dvalue_ref, dvalue_out, sems.at[6]),
+    ]
+    for copy in copies:
+        copy.start()
+    copies[0].wait()
+    copies[1].wait()
     for m in range(MODES):
         far = block_decay(table, m)
         carry = jnp.zeros((SUB, 128), F32)
         for j in range(BLOCKS - 1, 0, -1):
             carry = jnp.where(j > own, far * carry + sent_ref[j, SUB * m : SUB * (m + 1), :].astype(F32), carry)
         carry_ref[m] = carry
+    copies[2].wait()
     decay = [step_decay(table, m) for m in range(MODES)]
     weight = [mode_weight(table, m) for m in range(MODES)]
     skip = skip_of(table)
@@ -323,10 +385,16 @@
         return held
 
     lax.fori_loop(0, ROWS // UNROLL, body, tuple(carry_ref[m] for m in range(MODES)))
+    copies[3].wait()
+    copies[4].wait()
     for group in range(SUB):
         grad = buffer[group_rows(group), :].astype(BF16).astype(F32)
         dkey_ref[:, lanes(group)] = (grad * value_ref[:, lanes(group)].astype(F32)).astype(BF16)
         dvalue_ref[:, lanes(group)] = (grad * key_ref[:, lanes(group)].astype(F32)).astype(BF16)
+    for result in results:
+        result.start()
+    for result in results:
+        result.wait()
 
 
 def add_kernel(*refs):
@@ -365,30 +433,23 @@
     )(place.reshape(1).astype(jnp.int32), *[far(array)] * 4, *[far(one) for one in more], far(after))
 
 
-def half_kernel(*refs):
-    out_ref = refs[-1]
-    total = refs[0][0].astype(F32)
-    for ref in refs[1 : 5]:
-        total += ref[0].astype(F32)
-    out_ref[...] = total
-
-
-def half_gradient(which, picked, after, result=None):
-    earlier = ([] if result is None else [result]) + after
-    return pl.pallas_call(
-        half_kernel,
-        grid=(1,),
-        out_shape=far_f32(2 * HALF, 256),
-        in_specs=[pl.BlockSpec((1, HALF, 256), lambda i: (0, 0, 0))] * 5
-        + [pl.BlockSpec(memory_space=pl.ANY)] * len(earlier),
-        out_specs=pl.BlockSpec((HALF, 256), lambda i: (which, 0)),
-        input_output_aliases={} if result is None else {5: 0},
-        name="sum_gradient",
-        **params_of(2_000_000, 4_000_000),
-    )(*[far(array) for array in picked], *[far(array) for array in earlier])
-
-
-def owner_kernel(parts_ref, rate_ref, residue_ref, dresidue_ref, drate_ref, dskip_ref):
+def gradient_kernel(*refs):
+    first, second, out_ref, held, sems = refs[:5], refs[5:10], refs[11], refs[12], refs[13]
+    copies = []
+    for i, ref in enumerate(first + second):
+        copies.append(pltpu.make_async_copy(ref.at[0], held.at[i], sems.at[i]))
+    for copy in copies:
+        copy.start()
+    for copy in copies:
+        copy.wait()
+    out_ref[:HALF] = sum(held[i].astype(F32) for i in range(5))
+    out_ref[HALF:] = sum(held[i].astype(F32) for i in range(5, 10))
+
+
+def owner_kernel(parts_in, rate_ref, residue_ref, dresidue_ref, drate_ref, dskip_ref, parts_ref, sem):
+    copy = pltpu.make_async_copy(parts_in.at[:, STATE:], parts_ref, sem)
+    copy.start()
+    copy.wait()
     rate = rate_ref[...]
     residue = residue_ref[...]
     near = jnp.exp(rate * (-1.0 / SEQ))
@@ -399,7 +460,7 @@
     skip = jnp.zeros((1, rate.shape[1]), F32)
     later = jnp.zeros_like(rate)
     for j in range(BLOCKS - 1, -1, -1):
-        upper, lower = parts_ref[j, STATE : STATE + TERMS, :], parts_ref[j, STATE + TERMS :, :]
+        upper, lower = parts_ref[j, :TERMS, :], parts_ref[j, TERMS:, :]
         terms = upper.astype(F32) + lower.astype(F32)
         sums, ends = terms[0:MODES], terms[MODES : 2 * MODES]
         first += sums[:, :64]
@@ -489,44 +550,52 @@
     )(mixed_near, packed)
     sent = exchange(sent, "ctx")
 
-    conv_out, gated, carry = pl.pallas_call(
+    anywhere = pl.BlockSpec(memory_space=pl.ANY)
+    conv_out, gated, carry, gated_near, weight_near = pl.pallas_call(
         forward_kernel,
-        grid=(1,),
-        out_shape=(far_bf16(ROWS, 1024), far_bf16(ROWS, 1024), far_f32(MODES, SUB, 128)),
-        in_specs=[smem, whole(), full(ROWS * SUB, 128), full(ROWS, 1024), full(TABLE, 128)],
-        out_specs=(full(ROWS, 1024), full(ROWS, 1024), full(MODES, SUB, 128)),
-        scratch_shapes=[pltpu.VMEM((ROWS * SUB, 128), F32)],
+        out_shape=(
+            far_bf16(ROWS, 1024),
+            far_bf16(ROWS, 1024),
+            far_f32(MODES, SUB, 128),
+            bf16(ROWS, 1024),
+            bf16(8, 1024, 512),
+        ),
+        in_specs=[smem, whole(), anywhere, anywhere, anywhere, anywhere],
+        out_specs=(anywhere, anywhere, anywhere, whole(), whole()),
+        scratch_shapes=[
+            pltpu.VMEM((ROWS * SUB, 128), F32),
+            pltpu.VMEM((ROWS * SUB, 128), F32),
+            pltpu.VMEM((ROWS, 1024), BF16),
+            pltpu.VMEM((TABLE, 128), F32),
+            pltpu.VMEM((ROWS, 1024), BF16),
+            pltpu.VMEM((MODES, SUB, 128), F32),
+            pltpu.SemaphoreType.DMA((14,)),
+        ],
         name="forward_conv",
         **params_of(5_000_000_000, 4_000_000),
-    )(own_array, sent, far(mixed), far(query), far(table))
+    )(own_array, sent, far(mixed), far(query), far(table), far(w_out))
 
     other_gated = lax.ppermute(gated, "ctx", core_swap)
-    half_cots, gathered = pl.pallas_call(
+    partial_out = pl.pallas_call(
+        output_kernel,
+        out_shape=far_bf16(8, ROWS, 512),
+        in_specs=[whole()] * 2,
+        out_specs=anywhere,
+        scratch_shapes=[pltpu.VMEM((8, ROWS, 512), BF16), pltpu.SemaphoreType.DMA((8,))],
+        name="output_projection",
+        **params_of(2_147_483_648, 11_000_000),
+    )(gated_near, weight_near)
+
+    half_cots = pl.pallas_call(
         gather_kernel,
-        out_shape=(bf16(8, ROWS, 256), far_f32(8, 128)),
+        out_shape=bf16(8, ROWS, 256),
         in_specs=[smem] + [pl.BlockSpec(memory_space=pl.ANY)] * 5,
-        out_specs=(whole(), pl.BlockSpec(memory_space=pl.ANY)),
+        out_specs=whole(),
         scratch_shapes=[pltpu.SemaphoreType.DMA((8,))],
         name="gather_cotangent",
         **params_of(100_000, 6_000_000),
-    )(core_array, *[far(part) for part in cot_parts], far(gated))
+    )(core_array, *[far(part) for part in cot_parts], far(partial_out))
     other_cots = lax.ppermute(half_cots, "ctx", core_swap)
-
-    anywhere = pl.BlockSpec(memory_space=pl.ANY)
-    partial_out = pl.pallas_call(
-        output_kernel,
-        out_shape=far_bf16(8, ROWS, 512),
-        in_specs=[anywhere] * 3,
-        out_specs=anywhere,
-        scratch_shapes=[
-            pltpu.VMEM((ROWS, 1024), BF16),
-            pltpu.VMEM((8, 1024, 512), BF16),
-            pltpu.VMEM((8, ROWS, 512), BF16),
-            pltpu.SemaphoreType.DMA((17,)),
-        ],
-        name="output_projection",
-        **params_of(2_147_483_648, 11_000_000),
-    )(far(gated), far(w_out), gathered)
 
     *by_y, same_z, other_z = pl.pallas_call(
         weight_kernel,
@@ -552,25 +621,23 @@
 
     d_query, d_conv, payload = pl.pallas_call(
         cotangent_kernel,
-        grid=(1,),
-        out_shape=(bf16(ROWS, 1024), far_f32(ROWS * SUB, 128), far_bf16(BLOCKS, STATE + 2 * TERMS, 128)),
-        in_specs=[
-            smem,
-            *[anywhere] * 5,
-            full(ROWS, 1024),
-            full(ROWS, 1024),
-            full(ROWS * SUB, 128),
-            full(MODES, SUB, 128),
-            full(TABLE, 128),
-            anywhere,
-        ],
-        out_specs=(full(ROWS, 1024), full(ROWS * SUB, 128), full(BLOCKS, STATE + 2 * TERMS, 128)),
+        out_shape=(far_bf16(ROWS, 1024), far_f32(ROWS * SUB, 128), far_bf16(BLOCKS, STATE + 2 * TERMS, 128)),
+        in_specs=[smem] + [anywhere] * 11,
+        out_specs=(anywhere,) * 3,
         scratch_shapes=[
             pltpu.VMEM((ROWS, 1024), F32),
             pltpu.VMEM((BLOCKS * TERMS, 128), F32),
             pltpu.VMEM((8, ROWS, 512), BF16),
             pltpu.VMEM((8, 1024, 512), BF16),
-            pltpu.SemaphoreType.DMA((16,)),
+            pltpu.VMEM((ROWS, 1024), BF16),
+            pltpu.VMEM((ROWS, 1024), BF16),
+            pltpu.VMEM((ROWS * SUB, 128), F32),
+            pltpu.VMEM((MODES, SUB, 128), F32),
+            pltpu.VMEM((TABLE, 128), F32),
+            pltpu.VMEM((ROWS, 1024), BF16),
+            pltpu.VMEM((ROWS * SUB, 128), F32),
+            pltpu.VMEM((BLOCKS, STATE + 2 * TERMS, 128), BF16),
+            pltpu.SemaphoreType.DMA((24,)),
         ],
         name="cotangent_states",
         **params_of(14_000_000_000, 13_000_000),
@@ -596,34 +663,53 @@
 
     d_key, d_value = pl.pallas_call(
         backward_kernel,
-        grid=(1,),
-        out_shape=(bf16(ROWS, 1024), bf16(ROWS, 1024)),
-        in_specs=[
-            smem,
-            full(BLOCKS, STATE + 2 * TERMS, 128),
-            full(ROWS * SUB, 128),
-            full(ROWS, 1024),
-            full(ROWS, 1024),
-            full(TABLE, 128),
+        out_shape=(far_bf16(ROWS, 1024), far_bf16(ROWS, 1024)),
+        in_specs=[smem] + [anywhere] * 5,
+        out_specs=(anywhere,) * 2,
+        scratch_shapes=[
+            pltpu.VMEM((BLOCKS, STATE, 128), BF16),
+            pltpu.VMEM((ROWS * SUB, 128), F32),
+            pltpu.VMEM((ROWS, 1024), BF16),
+            pltpu.VMEM((ROWS, 1024), BF16),
+            pltpu.VMEM((TABLE, 128), F32),
+            pltpu.VMEM((ROWS, 1024), BF16),
+            pltpu.VMEM((ROWS, 1024), BF16),
+            pltpu.VMEM((MODES, SUB, 128), F32),
+            pltpu.VMEM((ROWS * SUB, 128), F32),
+            pltpu.SemaphoreType.DMA((7,)),
         ],
-        out_specs=(full(ROWS, 1024), full(ROWS, 1024)),
-        scratch_shapes=[pltpu.VMEM((MODES, SUB, 128), F32), pltpu.VMEM((ROWS * SUB, 128), F32)],
         name="backward_conv",
         **params_of(5_000_000_000, 4_000_000),
     )(own_array, far(received), far(d_conv), far(key_part), far(value_part), far(table))
 
-    d_weight = half_gradient(0, [by_y[0], *came_y, first_far[None]], [d_key])
-    d_weight = half_gradient(1, [same_z, came_z, *[part[None] for part in second_far]], [d_key], d_weight)
+    d_weight = pl.pallas_call(
+        gradient_kernel,
+        grid=(1,),
+        out_shape=f32(2 * HALF, 256),
+        in_specs=[anywhere] * 11,
+        out_specs=full(2 * HALF, 256),
+        scratch_shapes=[pltpu.VMEM((10, HALF, 256), BF16), pltpu.SemaphoreType.DMA((10,))],
+        name="sum_gradient",
+        **params_of(2_000_000, 4_000_000),
+    )(
+        *[far(part) for part in [by_y[0]] + came_y],
+        first_far[None],
+        far(same_z),
+        far(came_z),
+        *[part[None] for part in second_far],
+        far(d_key),
+    )
 
     d_residue, d_rate, d_skip = pl.pallas_call(
         owner_kernel,
         grid=(1,),
         out_shape=(f32(MODES, 64), f32(MODES, 64), f32(1, 64)),
-        in_specs=[full(BLOCKS, STATE + 2 * TERMS, 128), whole(), whole()],
-        out_specs=(whole(),) * 3,
+        in_specs=[anywhere, full(MODES, 64), full(MODES, 64)],
+        out_specs=(full(MODES, 64), full(MODES, 64), full(1, 64)),
+        scratch_shapes=[pltpu.VMEM((BLOCKS, 2 * TERMS, 128), BF16), pltpu.SemaphoreType.DMA],
         name="owner_sums",
         **params_of(1_000_000, 400_000),
-    )(far(received), rate.T, residue.T)
+    )(far(received), far(rate.T), far(residue.T))
     return (output, d_query, d_key, d_value, d_weight, d_residue.T, d_rate.T, d_skip[0])
 
 

time: 130 us -> 122 us (0.938)
  Pallas kernels: 57.5 us -> 52.3 us
  waiting for transfers between devices: 21.8 us -> 18.6 us
  local copies, waits for them, and re-layouts: 6.3 us -> 3.92 us
  starting transfers between devices: 42.5 us -> 44.1 us
    pallas_call x6 -> x5, Pallas kernels: 31.1 us -> 27.9 us  [the longest x1 13.5 us: local(): pl.pallas_call(cotangent_kernel, out_shape=(far_bf16(ROWS, 1024), far_f32...]
    pallas_call x1, Pallas kernels: 5.75 us -> 3.12 us  [local(): pl.pallas_call(output_kernel, out_shape=far_bf16(8, ROWS, 512), in_specs=...]
    all_to_all x4, waiting for transfers between devices: 17.1 us -> 14.7 us  [exchange(): lax.all_to_all(array, axis, split_axis=0, concat_axis=0, tiled=True, axis...]
    unnamed x34 -> x22, local copies, waits for them, and re-layouts: 6.3 us -> 3.92 us
  transfers between devices with their start and end apart: 19 -> 19, of which waited for: 6 -> 6; matrix products, arithmetic and copies ran while one was open for 0% -> 0% of each run, Pallas kernels for 42% -> 40%
where the time goes in v4:
time: 122 us; the launch traced here: 120 us
  Pallas kernels  52.3 us (43%)
  starting transfers between devices  44.1 us (36%)
  waiting for transfers between devices  18.6 us (15%)
  local copies, waits for them, and re-layouts  3.92 us (3%)
    all_to_all x4, starting transfers between devices, exchange(): lax.all_to_all(array, axis, split_axis=0, concat_axis=0, tiled=True, axis...  23.1 us
    all_to_all x4, waiting for transfers between devices, exchange(): lax.all_to_all(array, axis, split_axis=0, concat_axis=0, tiled=True, axis...  14.7 us
    pallas_call x1, Pallas kernels, local(): pl.pallas_call(cotangent_kernel, out_shape=(far_bf16(ROWS, 1024), far_f32...  13.5 us
    pallas_call x1, Pallas kernels, local(): pl.pallas_call(weight_kernel, out_shape=(far_bf16(2, HALF, 256),) * 4 + (...  6.52 us
    ppermute x3, starting transfers between devices, local(): lax.ppermute(cot_pair, 'tp', shift_x(k))  5.65 us
    pallas_call x1, Pallas kernels, local(): pl.pallas_call(backward_kernel, out_shape=(far_bf16(ROWS, 1024), far_bf16...  5.29 us
    pallas_call x1, Pallas kernels, local(): pl.pallas_call(forward_kernel, out_shape=(far_bf16(ROWS, 1024), far_bf16(...  5.05 us
    ppermute x3, starting transfers between devices, local(): lax.ppermute(second_far[k - 1], 'ctx', shift_y(k))  4.3 us
  transfers between devices with their start and end apart: 19, of which 6 were waited for; matrix products, arithmetic and copies ran while one was open for 0% of the time, Pallas kernels for 40%

profile of v4, /device:TPU:0, one launch (start us, length us, event | category | flops | bytes accessed | tf_op | source)
XLA Modules:
  0.0 120.0 jit_solution(18193882687500679446)
XLA Ops:
  0.6 2.1 %collective-permute-start = (bf16[256,512]{1,0:T(8,128)(2,1)}, bf16[256,512]{1,0:T(8,128)(2,1)S(1)}, u32[]{:S(2)}, u32[]{:S(2)}) collective-permute-start(bf16[256,512]{1,0:T(8,128)(2,1)} %cot_ref.1), channel_id=1, source_target_pairs={{0,1},{1,0},{2,3},{3,2},{4,5},{5,4},{6,7},{7,6},{8,9},{9,8},{10,11... | collective-permute-start | bytes 786440 | tf_op jit(solution)/shard_map/ppermute | solution.py:530
  4.2 7.6 %all-to-all-start = ((f32[16,24,128]{2,1,0:T(8,128)}), f32[16,24,128]{2,1,0:T(8,128)S(1)}, u32[]{:S(2)}, u32[]{:S(2)}) async-start(f32[16,24,128]{2,1,0:T(8,128)} %pack_parameters.1), calls=%async_computation | async-start | bytes 393216 | tf_op jit(solution)/shard_map/all_to_all | solution.py:485
  11.8 2.8 %mix_inputs.1 = (f32[2048,128]{1,0:T(8,128)S(1)}, f32[2048,128]{1,0:T(8,128)}, bf16[2,256,512]{2,1,0:T(8,128)(2,1)}) custom-call(bf16[256,1024]{1,0:T(8,128)(2,1)} %key_in.1, bf16[256,1024]{1,0:T(8,128)(2,1)} %value_in.1, bf16[256,512]{1,0:T(8,128)(2,1)} %cot_ref.1, bf16[256,512]{1,0:T(8,128)(2,1)S(1)} %collective-permute-done.near_cot_ref), custom_call_target="tpu_custom_call" | custom-call | flops 2000000 | bytes 60000 | tf_op jit(solution)/shard_map/mix_inputs/pallas_call | solution.py:531
  14.6 1.5 %collective-permute-start.1 = (bf16[2,256,512]{2,1,0:T(8,128)(2,1)}, bf16[2,256,512]{2,1,0:T(8,128)(2,1)S(1)}, u32[]{:S(2)}, u32[]{:S(2)}) collective-permute-start(bf16[2,256,512]{2,1,0:T(8,128)(2,1)} %get-tuple-element.42.refs_0_.part0), channel_id=1, source_target_pairs={{0,2},{1,3},{2,4},{3,5},{4,6},{5,7},{6,0},{7,1},{8,10},{9,11},{10,... | collective-permute-start | bytes 1572872 | tf_op jit(solution)/shard_map/ppermute | solution.py:540
  16.1 2.7 %collective-permute-start.2 = (bf16[2,256,512]{2,1,0:T(8,128)(2,1)}, bf16[2,256,512]{2,1,0:T(8,128)(2,1)S(1)}, u32[]{:S(2)}, u32[]{:S(2)}) collective-permute-start(bf16[2,256,512]{2,1,0:T(8,128)(2,1)} %get-tuple-element.42.refs_0_.part0), channel_id=1, source_target_pairs={{0,4},{1,5},{2,6},{3,7},{4,0},{5,1},{6,2},{7,3},{8,12},{9,13},{10,... | collective-permute-start | bytes 1572872 | tf_op jit(solution)/shard_map/ppermute | solution.py:540
  20.4 2.2 %forward_states.1 = (bf16[16,16,8,128]{3,2,1,0:T(8,128)(2,1)}, f32[384,128]{1,0:T(8,128)}) custom-call(f32[2048,128]{1,0:T(8,128)S(1)} %get-tuple-element.36.mixed_ref, f32[16,24,128]{2,1,0:T(8,128)S(1)} %all-to-all-done.packed_ref), custom_call_target="tpu_custom_call" | custom-call | flops 60000000 | bytes 80000 | tf_op jit(solution)/shard_map/forward_states/pallas_call | solution.py:542
  22.6 7.1 %all-to-all-start.1 = ((bf16[16,16,8,128]{3,2,1,0:T(8,128)(2,1)}), bf16[16,16,8,128]{3,2,1,0:T(8,128)(2,1)S(1)}, u32[]{:S(2)}, u32[]{:S(2)}) async-start(bf16[16,16,8,128]{3,2,1,0:T(8,128)(2,1)} %get-tuple-element.37), calls=%async_computation.1 | async-start | bytes 1048576 | tf_op jit(solution)/shard_map/all_to_all | solution.py:485
  29.7 12.4 %all-to-all-done.1.sent_ref = bf16[16,16,8,128]{3,2,1,0:T(8,128)(2,1)S(1)} async-done(((bf16[16,16,8,128]{3,2,1,0:T(8,128)(2,1)}), bf16[16,16,8,128]{3,2,1,0:T(8,128)(2,1)S(1)}, u32[]{:S(2)}, u32[]{:S(2)}) %all-to-all-start.1) | async-done | bytes 524320 | tf_op jit(solution)/shard_map/all_to_all | solution.py:485
  42.1 5.0 %forward_conv.1 = (bf16[256,1024]{1,0:T(8,128)(2,1)}, bf16[256,1024]{1,0:T(8,128)(2,1)}, f32[16,8,128]{2,1,0:T(8,128)}, bf16[256,1024]{1,0:T(8,128)(2,1)S(1)}, bf16[8,1024,512]{2,1,0:T(8,128)(2,1)S(1)}) custom-call(s32[1]{0:T(128)} %bitcast.1.own_ref, bf16[16,16,8,128]{3,2,1,0:T(8,128)(2,1)S(1)} %all-to-all-done.1.sent_ref, ...), custom_call_target="tpu_custom_call" | custom-call | flops 100000000 | bytes 80000 | tf_op jit(solution)/shard_map/forward_conv/pallas_call | solution.py:554
  47.1 3.1 %output_projection.1.refs_4_.refs_5_ = bf16[8,256,512]{2,1,0:T(8,128)(2,1)} custom-call(bf16[256,1024]{1,0:T(8,128)(2,1)S(1)} %get-tuple-element.40.gated_ref, bf16[8,1024,512]{2,1,0:T(8,128)(2,1)S(1)} %get-tuple-element.41.weight_ref), custom_call_target="tpu_custom_call" | custom-call | flops 42949672 | bytes 220000 | tf_op jit(solution)/shard_map/output_projection/pallas_call | solution.py:579
  53.4 4.4 %all-to-all-start.2 = ((bf16[4,2,256,512]{3,2,1,0:T(8,128)(2,1)}), bf16[4,2,256,512]{3,2,1,0:T(8,128)(2,1)}, u32[]{:S(2)}, u32[]{:S(2)}) async-start(bf16[4,2,256,512]{3,2,1,0:T(8,128)(2,1)} %bitcast.20), calls=%async_computation.2 | async-start | bytes 4194304 | tf_op jit(solution)/shard_map/all_to_all | solution.py:485
  58.0 6.5 %projection_gradient.1 = (bf16[2,512,256]{2,1,0:T(8,128)(2,1)}, bf16[2,512,256]{2,1,0:T(8,128)(2,1)}, bf16[2,512,256]{2,1,0:T(8,128)(2,1)}, bf16[2,512,256]{2,1,...) custom-call(s32[9]{0:T(128)S(1)} %pad_add_fusion.index_ref, ...), custom_call_target="tpu_custom_call" | custom-call | flops 42949672 | bytes 160000 | tf_op jit(solution)/shard_map/projection_gradient/pallas_call | solution.py:600
  65.4 2.1 %collective-permute-start.8 = (bf16[2,512,256]{2,1,0:T(8,128)(2,1)}, bf16[2,512,256]{2,1,0:T(8,128)(2,1)S(1)}, u32[]{:S(2)}, u32[]{:S(2)}) collective-permute-start(bf16[2,512,256]{2,1,0:T(8,128)(2,1)} %get-tuple-element.54), channel_id=1, source_target_pairs={{0,32},{8,40},{16,48},{24,56},{32,0},{40,8},{48,16},{56,24},{64,96... | collective-permute-start | bytes 1572872 | tf_op jit(solution)/shard_map/ppermute | solution.py:617
  69.0 13.5 %cotangent_states.1 = (bf16[256,1024]{1,0:T(8,128)(2,1)}, f32[2048,128]{1,0:T(8,128)}, bf16[16,224,128]{2,1,0:T(8,128)(2,1)}) custom-call(s32[8]{0:T(128)S(1)} %fusion.came_ref, bf16[2,256,512]{2,1,0:T(8,128)(2,1)} %get-tuple-element.42.refs_0_.part0, bf16[2,256,512]{2,1,0:T(8,128)(2,1)} %copy-done.2, bf16[2,256,512]{2,1,0:T(8,128)(2,1)} %copy-done.3, ...), custom_call_target="tpu_custom_call" | custom-call | flops 280000000 | bytes 260000 | tf_op jit(solution)/shard_map/cotangent_states/pallas_call | solution.py:622
  82.5 2.2 %all-to-all-done.2 = bf16[4,2,256,512]{3,2,1,0:T(8,128)(2,1)} async-done(((bf16[4,2,256,512]{3,2,1,0:T(8,128)(2,1)}), bf16[4,2,256,512]{3,2,1,0:T(8,128)(2,1)}, u32[]{:S(2)}, u32[]{:S(2)}) %all-to-all-start.2) | async-done | bytes 2097184 | tf_op jit(solution)/shard_map/all_to_all | solution.py:485
  84.8 3.9 %all-to-all-start.3 = ((bf16[16,224,128]{2,1,0:T(8,128)(2,1)}), bf16[16,224,128]{2,1,0:T(8,128)(2,1)S(1)}, u32[]{:S(2)}, u32[]{:S(2)}) async-start(bf16[16,224,128]{2,1,0:T(8,128)(2,1)} %get-tuple-element.47.refs_4_.refs_5_), calls=%async_computation.3 | async-start | bytes 1835008 | tf_op jit(solution)/shard_map/all_to_all | solution.py:485
  93.5 2.2 %sum_stage.1 = (bf16[512,256]{1,0:T(8,128)(2,1)S(1)}, bf16[512,256]{1,0:T(8,128)(2,1)S(1)}, bf16[512,256]{1,0:T(8,128)(2,1)S(1)}, bf16[512,256]{1,0:T(8,128)(2,1)S(1)}) custom-call(bf16[2,512,256]{2,1,0:T(8,128)(2,1)} %get-tuple-element.52.refs_0_, bf16[2,512,256]{2,1,0:T(8,128)(2,1)} %copy-done.7, bf16[2,512,256]{2,1,0:T(8,128)(2,1)} %copy-done.8, ...), custom_call_target="tpu_custom_call" | custom-call | flops 40000000000 | bytes 40000 | tf_op jit(solution)/shard_map/sum_stage/pallas_call | solution.py:652
  96.4 3.5 %collective-permute-start.13 = (bf16[512,256]{1,0:T(8,128)(2,1)S(1)}, bf16[512,256]{1,0:T(8,128)(2,1)S(1)}, u32[]{:S(2)}, u32[]{:S(2)}) collective-permute-start(bf16[512,256]{1,0:T(8,128)(2,1)S(1)} %get-tuple-element.59), channel_id=1, source_target_pairs={{0,32},{8,40},{16,48},{24,56},{32,0},{40,8},{48,16},{56,24},{64,96... | collective-permute-start | bytes 786440 | tf_op jit(solution)/shard_map/ppermute | solution.py:662
  99.9 3.9 %collective-permute-start.11 = (bf16[512,256]{1,0:T(8,128)(2,1)S(1)}, bf16[512,256]{1,0:T(8,128)(2,1)S(1)}, u32[]{:S(2)}, u32[]{:S(2)}) collective-permute-start(bf16[512,256]{1,0:T(8,128)(2,1)S(1)} %get-tuple-element.57), channel_id=1, source_target_pairs={{0,64},{8,72},{16,80},{24,88},{32,96},{40,104},{48,112},{56,120},{... | collective-permute-start | bytes 786440 | tf_op jit(solution)/shard_map/ppermute | solution.py:661
  103.8 1.7 %collective-permute-done.6.refs_4_ = bf16[256,512]{1,0:T(8,128)(2,1)S(1)} collective-permute-done((bf16[256,512]{1,0:T(8,128)(2,1)S(1)}, bf16[256,512]{1,0:T(8,128)(2,1)S(1)}, u32[]{:S(2)}, u32[]{:S(2)}) %collective-permute-start.6) | collective-permute-done | bytes 262176 | tf_op jit(solution)/shard_map/ppermute | solution.py:649
  106.2 2.1 %sum_output.3 = bf16[256,512]{1,0:T(8,128)(2,1)} custom-call(s32[1]{0:T(128)} %bitcast.place_ref, bf16[8,256,512]{2,1,0:T(8,128)(2,1)} %bitcast.6.refs_0_.refs_1_.refs_2_.refs_3_, bf16[8,256,512]{2,1,0:T(8,128)(2,1)} %bitcast.6.refs_0_.refs_1_.refs_2_.refs_3_, bf16[8,256,512]{2,1,0:T(8,128)(2,1)} %bitcast.6.refs_0_.refs_1_.refs_2_.refs_3_, ...), custom_call_target="tpu_custom_call" | custom-call | flops 20000 | bytes 40000 | tf_op jit(solution)/shard_map/sum_output/pallas_call | solution.py:422
  109.2 2.6 %owner_sums.1 = (f32[16,64]{1,0:T(8,128)}, f32[16,64]{1,0:T(8,128)}, f32[1,64]{1,0:T(1,128)}) custom-call(bf16[16,224,128]{2,1,0:T(8,128)(2,1)} %copy-done.1, f32[16,64]{1,0:T(8,128)} %bitcast.22, f32[16,64]{1,0:T(8,128)} %bitcast.24), custom_call_target="tpu_custom_call" | custom-call | flops 20000 | bytes 8000 | tf_op jit(solution)/shard_map/owner_sums/pallas_call | solution.py:703
  111.8 5.3 %backward_conv.1 = (bf16[256,1024]{1,0:T(8,128)(2,1)}, bf16[256,1024]{1,0:T(8,128)(2,1)}) custom-call(s32[1]{0:T(128)} %bitcast.1.own_ref, bf16[16,224,128]{2,1,0:T(8,128)(2,1)} %copy-done.1, f32[2048,128]{1,0:T(8,128)} %get-tuple-element.49.dconv_in, bf16[256,1024]{1,0:T(8,128)(2,1)} %key_in.1, bf16[256,1024]{1,0:T(8,128)(2,1)} %value_in.1, ...), custom_call_target="tpu_custom_call" | custom-call | flops 100000000 | bytes 80000 | tf_op jit(solution)/shard_map/backward_conv/pallas_call | solution.py:664
  117.2 2.7 %sum_gradient.1 = f32[1024,256]{1,0:T(8,128)} custom-call(bf16[2,512,256]{2,1,0:T(8,128)(2,1)} %get-tuple-element.52.refs_0_, bf16[2,512,256]{2,1,0:T(8,128)(2,1)} %copy-done.7, bf16[2,512,256]{2,1,0:T(8,128)(2,1)} %copy-done.8, bf16[2,512,256]{2,1,0:T(8,128)(2,1)} %copy-done.9, bf16[1,512,256]{2,1,0:T(8,128)(2,1)S(1)} %bitcast.19, ...), custom_call_target="tpu_custom_call" | custom-call | flops 40000 | bytes 80000 | tf_op jit(solution)/shard_map/sum_gradient/pallas_call | solution.py:685
  (53 shorter events, 15.6 us)
Async XLA Ops:
  0.6 11.2 %collective-permute-start = (bf16[256,512]{1,0:T(8,128)(2,1)}, bf16[256,512]{1,0:T(8,128)(2,1)S(1)}, u32[]{:S(2)}, u32[]{:S(2)}) collective-permute-start(bf16[256,512]{1,0:T(8,128)(2,1)} %cot_ref.1), channel_id=1, source_target_pairs={{0,1},{1,0},{2,3},{3,2},{4,5},{5,4},{6,7},{7,6},{8,9},{9,8},{10,11... | collective-permute-start | bytes 786440 | tf_op jit(solution)/shard_map/ppermute | solution.py:530
  4.2 16.2 %all-to-all-start = ((f32[16,24,128]{2,1,0:T(8,128)}), f32[16,24,128]{2,1,0:T(8,128)S(1)}, u32[]{:S(2)}, u32[]{:S(2)}) async-start(f32[16,24,128]{2,1,0:T(8,128)} %pack_parameters.1), calls=%async_computation | async-start | bytes 393216 | tf_op jit(solution)/shard_map/all_to_all | solution.py:485
  14.6 35.7 %collective-permute-start.1 = (bf16[2,256,512]{2,1,0:T(8,128)(2,1)}, bf16[2,256,512]{2,1,0:T(8,128)(2,1)S(1)}, u32[]{:S(2)}, u32[]{:S(2)}) collective-permute-start(bf16[2,256,512]{2,1,0:T(8,128)(2,1)} %get-tuple-element.42.refs_0_.part0), channel_id=1, source_target_pairs={{0,2},{1,3},{2,4},{3,5},{4,6},{5,7},{6,0},{7,1},{8,10},{9,11},{10,... | collective-permute-start | bytes 1572872 | tf_op jit(solution)/shard_map/ppermute | solution.py:540
  16.1 34.2 %collective-permute-start.2 = (bf16[2,256,512]{2,1,0:T(8,128)(2,1)}, bf16[2,256,512]{2,1,0:T(8,128)(2,1)S(1)}, u32[]{:S(2)}, u32[]{:S(2)}) collective-permute-start(bf16[2,256,512]{2,1,0:T(8,128)(2,1)} %get-tuple-element.42.refs_0_.part0), channel_id=1, source_target_pairs={{0,4},{1,5},{2,6},{3,7},{4,0},{5,1},{6,2},{7,3},{8,12},{9,13},{10,... | collective-permute-start | bytes 1572872 | tf_op jit(solution)/shard_map/ppermute | solution.py:540
  18.8 31.5 %collective-permute-start.3 = (bf16[2,256,512]{2,1,0:T(8,128)(2,1)}, bf16[2,256,512]{2,1,0:T(8,128)(2,1)S(1)}, u32[]{:S(2)}, u32[]{:S(2)}) collective-permute-start(bf16[2,256,512]{2,1,0:T(8,128)(2,1)} %get-tuple-element.42.refs_0_.part0), channel_id=1, source_target_pairs={{0,6},{1,7},{2,0},{3,1},{4,2},{5,3},{6,4},{7,5},{8,14},{9,15},{10,... | collective-permute-start | bytes 1572872 | tf_op jit(solution)/shard_map/ppermute | solution.py:540
  22.6 19.5 %all-to-all-start.1 = ((bf16[16,16,8,128]{3,2,1,0:T(8,128)(2,1)}), bf16[16,16,8,128]{3,2,1,0:T(8,128)(2,1)S(1)}, u32[]{:S(2)}, u32[]{:S(2)}) async-start(bf16[16,16,8,128]{3,2,1,0:T(8,128)(2,1)} %get-tuple-element.37), calls=%async_computation.1 | async-start | bytes 1048576 | tf_op jit(solution)/shard_map/all_to_all | solution.py:485
  47.1 5.7 %copy-start.6 = (bf16[256,1024]{1,0:T(8,128)(2,1)S(1)}, bf16[256,1024]{1,0:T(8,128)(2,1)}, u32[]{:S(2)}) copy-start(bf16[256,1024]{1,0:T(8,128)(2,1)} %get-tuple-element.45.gated_ref) | copy-start | bytes 1572868
  50.3 1.1 copy-start.3
  52.8 5.2 %collective-permute-start.5 = (bf16[8,256,256]{2,1,0:T(8,128)(2,1)S(1)}, bf16[8,256,256]{2,1,0:T(8,128)(2,1)S(1)}, u32[]{:S(2)}, u32[]{:S(2)}) collective-permute-start(bf16[8,256,256]{2,1,0:T(8,128)(2,1)S(1)} %gather_cotangent.1), channel_id=1, source_target_pairs={{0,8},{8,0},{16,24},{24,16},{32,40},{40,32},{48,56},{56,48},{64,72... | collective-permute-start | bytes 3145736 | tf_op jit(solution)/shard_map/ppermute | solution.py:598
  52.9 5.1 %collective-permute-start.4 = (bf16[256,1024]{1,0:T(8,128)(2,1)S(1)}, bf16[256,1024]{1,0:T(8,128)(2,1)S(1)}, u32[]{:S(2)}, u32[]{:S(2)}) collective-permute-start(bf16[256,1024]{1,0:T(8,128)(2,1)S(1)} %copy-done.6), channel_id=1, source_target_pairs={{0,8},{8,0},{16,24},{24,16},{32,40},{40,32},{48,56},{56,48},{64,72... | collective-permute-start | bytes 1572872 | tf_op jit(solution)/shard_map/ppermute | solution.py:578
  53.4 31.4 %all-to-all-start.2 = ((bf16[4,2,256,512]{3,2,1,0:T(8,128)(2,1)}), bf16[4,2,256,512]{3,2,1,0:T(8,128)(2,1)}, u32[]{:S(2)}, u32[]{:S(2)}) async-start(bf16[4,2,256,512]{3,2,1,0:T(8,128)(2,1)} %bitcast.20), calls=%async_computation.2 | async-start | bytes 4194304 | tf_op jit(solution)/shard_map/all_to_all | solution.py:485
  64.5 27.8 %collective-permute-start.10 = (bf16[4,512,256]{2,1,0:T(8,128)(2,1)}, bf16[4,512,256]{2,1,0:T(8,128)(2,1)S(1)}, u32[]{:S(2)}, u32[]{:S(2)}) collective-permute-start(bf16[4,512,256]{2,1,0:T(8,128)(2,1)} %get-tuple-element.46.after_ref), channel_id=1, source_target_pairs={{0,64},{8,72},{16,80},{24,88},{32,96},{40,104},{48,112},{56,120},{... | collective-permute-start | bytes 3145736 | tf_op jit(solution)/shard_map/ppermute | solution.py:616
  65.2 26.3 %collective-permute-start.7 = (bf16[2,512,256]{2,1,0:T(8,128)(2,1)}, bf16[2,512,256]{2,1,0:T(8,128)(2,1)S(1)}, u32[]{:S(2)}, u32[]{:S(2)}) collective-permute-start(bf16[2,512,256]{2,1,0:T(8,128)(2,1)} %get-tuple-element.53), channel_id=1, source_target_pairs={{0,16},{8,24},{16,32},{24,40},{32,48},{40,56},{48,0},{56,8},{64,80... | collective-permute-start | bytes 1572872 | tf_op jit(solution)/shard_map/ppermute | solution.py:617
  65.4 26.1 %collective-permute-start.8 = (bf16[2,512,256]{2,1,0:T(8,128)(2,1)}, bf16[2,512,256]{2,1,0:T(8,128)(2,1)S(1)}, u32[]{:S(2)}, u32[]{:S(2)}) collective-permute-start(bf16[2,512,256]{2,1,0:T(8,128)(2,1)} %get-tuple-element.54), channel_id=1, source_target_pairs={{0,32},{8,40},{16,48},{24,56},{32,0},{40,8},{48,16},{56,24},{64,96... | collective-permute-start | bytes 1572872 | tf_op jit(solution)/shard_map/ppermute | solution.py:617
  67.5 24.8 %collective-permute-start.9 = (bf16[2,512,256]{2,1,0:T(8,128)(2,1)}, bf16[2,512,256]{2,1,0:T(8,128)(2,1)S(1)}, u32[]{:S(2)}, u32[]{:S(2)}) collective-permute-start(bf16[2,512,256]{2,1,0:T(8,128)(2,1)} %get-tuple-element.55), channel_id=1, source_target_pairs={{0,48},{8,56},{16,0},{24,8},{32,16},{40,24},{48,32},{56,40},{64,11... | collective-permute-start | bytes 1572872 | tf_op jit(solution)/shard_map/ppermute | solution.py:617
  84.8 23.6 %all-to-all-start.3 = ((bf16[16,224,128]{2,1,0:T(8,128)(2,1)}), bf16[16,224,128]{2,1,0:T(8,128)(2,1)S(1)}, u32[]{:S(2)}, u32[]{:S(2)}) async-start(bf16[16,224,128]{2,1,0:T(8,128)(2,1)} %get-tuple-element.47.refs_4_.refs_5_), calls=%async_computation.3 | async-start | bytes 1835008 | tf_op jit(solution)/shard_map/all_to_all | solution.py:485
  90.0 3.4 %copy-start = (bf16[256,512]{1,0:T(8,128)(2,1)}, bf16[256,512]{1,0:T(8,128)(2,1)S(1)}, u32[]{:S(2)}) copy-start(bf16[256,512]{1,0:T(8,128)(2,1)S(1)} %sum_output.2.refs_6_) | copy-start | bytes 786436
  90.0 15.4 %collective-permute-start.6 = (bf16[256,512]{1,0:T(8,128)(2,1)S(1)}, bf16[256,512]{1,0:T(8,128)(2,1)S(1)}, u32[]{:S(2)}, u32[]{:S(2)}) collective-permute-start(bf16[256,512]{1,0:T(8,128)(2,1)S(1)} %sum_output.2.refs_6_), channel_id=1, source_target_pairs={{0,1},{1,0},{2,3},{3,2},{4,5},{5,4},{6,7},{7,6},{8,9},{9,8},{10,11... | collective-permute-start | bytes 786440 | tf_op jit(solution)/shard_map/ppermute | solution.py:649
  91.5 2.0 %copy-start.7 = (bf16[2,512,256]{2,1,0:T(8,128)(2,1)}, bf16[2,512,256]{2,1,0:T(8,128)(2,1)S(1)}, u32[]{:S(2)}) copy-start(bf16[2,512,256]{2,1,0:T(8,128)(2,1)S(1)} %collective-permute-done.7.refs_1_) | copy-start | bytes 1572868
  92.3 1.2 copy-start.5
  95.6 21.5 %collective-permute-start.12 = (bf16[512,256]{1,0:T(8,128)(2,1)S(1)}, bf16[512,256]{1,0:T(8,128)(2,1)S(1)}, u32[]{:S(2)}, u32[]{:S(2)}) collective-permute-start(bf16[512,256]{1,0:T(8,128)(2,1)S(1)} %get-tuple-element.58), channel_id=1, source_target_pairs={{0,16},{8,24},{16,32},{24,40},{32,48},{40,56},{48,0},{56,8},{64,80... | collective-permute-start | bytes 786440 | tf_op jit(solution)/shard_map/ppermute | solution.py:662
  96.4 20.8 %collective-permute-start.13 = (bf16[512,256]{1,0:T(8,128)(2,1)S(1)}, bf16[512,256]{1,0:T(8,128)(2,1)S(1)}, u32[]{:S(2)}, u32[]{:S(2)}) collective-permute-start(bf16[512,256]{1,0:T(8,128)(2,1)S(1)} %get-tuple-element.59), channel_id=1, source_target_pairs={{0,32},{8,40},{16,48},{24,56},{32,0},{40,8},{48,16},{56,24},{64,96... | collective-permute-start | bytes 786440 | tf_op jit(solution)/shard_map/ppermute | solution.py:662
  99.9 17.2 %collective-permute-start.14 = (bf16[512,256]{1,0:T(8,128)(2,1)S(1)}, bf16[512,256]{1,0:T(8,128)(2,1)S(1)}, u32[]{:S(2)}, u32[]{:S(2)}) collective-permute-start(bf16[512,256]{1,0:T(8,128)(2,1)S(1)} %get-tuple-element.60), channel_id=1, source_target_pairs={{0,48},{8,56},{16,0},{24,8},{32,16},{40,24},{48,32},{56,40},{64,11... | collective-permute-start | bytes 786440 | tf_op jit(solution)/shard_map/ppermute | solution.py:662
  99.9 17.2 %collective-permute-start.11 = (bf16[512,256]{1,0:T(8,128)(2,1)S(1)}, bf16[512,256]{1,0:T(8,128)(2,1)S(1)}, u32[]{:S(2)}, u32[]{:S(2)}) collective-permute-start(bf16[512,256]{1,0:T(8,128)(2,1)S(1)} %get-tuple-element.57), channel_id=1, source_target_pairs={{0,64},{8,72},{16,80},{24,88},{32,96},{40,104},{48,112},{56,120},{... | collective-permute-start | bytes 786440 | tf_op jit(solution)/shard_map/ppermute | solution.py:661
  (6 other events, 5.1 us)

commit v5 on v4

--- a/solution.py
+++ b/solution.py
@@ -112,18 +112,6 @@
     kept_ref[...] = mixed_ref[...]
 
 
-def gather_kernel(core_ref, *refs):
-    parts, half_ref, sems = refs[:4], refs[5], refs[6]
-    half = pl.ds(pl.multiple_of((1 - core_ref[0]) * 256, 256), 256)
-    copies = [
-        pltpu.make_async_copy(parts[i // 2].at[i % 2, :, half], half_ref.at[i], sems.at[i]) for i in range(8)
-    ]
-    for copy in copies:
-        copy.start()
-    for copy in copies:
-        copy.wait()
-
-
 def states_kernel(mixed_ref, packed_ref, sent_ref, table):
     left = lax.broadcasted_iota(jnp.int32, (PACK, 128), 1) < 64
     for group in range(SUB):
@@ -199,13 +187,20 @@
         copy.wait()
 
 
-def output_kernel(gated_ref, weight_ref, out_ref, blocks, sems):
+def output_kernel(core_ref, gated_ref, weight_ref, *refs):
+    parts, out_ref, half_ref, blocks, sems = refs[:4], refs[4], refs[5], refs[6], refs[7]
+    half = pl.ds(pl.multiple_of((1 - core_ref[0]) * 256, 256), 256)
+    copies = [
+        pltpu.make_async_copy(parts[i // 2].at[i % 2, :, half], half_ref.at[i], sems.at[8 + i]) for i in range(8)
+    ]
     results = [pltpu.make_async_copy(blocks.at[i], out_ref.at[i], sems.at[i]) for i in range(8)]
+    for copy in copies:
+        copy.start()
     for i in range(8):
         blocks[i] = jnp.dot(gated_ref[...], weight_ref[i], preferred_element_type=F32).astype(BF16)
         results[i].start()
-    for result in results:
-        result.wait()
+    for copy in copies + results:
+        copy.wait()
 
 
 def weight_kernel(index_ref, gated_ref, other_ref, *refs):
@@ -239,21 +234,22 @@
             results.append(pltpu.make_async_copy(chunks.at[i, :HALF], along_y[k].at[z], out_sems.at[8 + i]))
             results[-2].start()
             results[-1].start()
-    for result in results:
-        result.wait()
+    for copy in results:
+        copy.wait()
 
 
 def cotangent_kernel(
     came_ref, part0, part1, part2, part3, weight_ref, query_in, conv_in, mixed_in, carry_in, table_in, after_ref,
     dquery_out, dconv_out, sent_out,
-    total, terms, parts, weight, query_ref, conv_ref, mixed_ref, carry_ref, table, dquery_ref, dconv_ref, sent_ref, sems,
+    total, terms, parts, weight, query_ref, conv_ref, mixed_ref, carry_ref, table, dquery_ref, dconv_ref, sent_ref, back_ref, sems,
 ):
     copies = []
     for i in range(8):
         columns = pl.ds(pl.multiple_of(came_ref[i] * 512, 512), 512)
         part = (part0, part1, part2, part3)[i // 2].at[i % 2]
-        copies.append(pltpu.make_async_copy(weight_ref.at[:, columns], weight.at[i], sems.at[i]))
-        copies.append(pltpu.make_async_copy(part, parts.at[i], sems.at[8 + i]))
+        place = slice(512 * (i % 2), 512 * (i % 2 + 1))
+        copies.append(pltpu.make_async_copy(weight_ref.at[:, columns], weight.at[i // 2, :, place], sems.at[i]))
+        copies.append(pltpu.make_async_copy(part, parts.at[i // 2, :, place], sems.at[8 + i]))
     later = [
         pltpu.make_async_copy(source, target, sems.at[16 + i])
         for i, (source, target) in enumerate(
@@ -268,9 +264,9 @@
     ]
     for copy in copies + later:
         copy.start()
-    for i in range(8):
-        copies[2 * i].wait()
-        copies[2 * i + 1].wait()
+    for i in range(4):
+        for copy in copies[4 * i : 4 * i + 4]:
+            copy.wait()
         product = lax.dot_general(parts[i], weight[i], (((1,), (1,)), ((), ())), preferred_element_type=F32)
         if i == 0:
             total[...] = product
@@ -291,6 +287,21 @@
         terms[pl.ds(row, SUB, stride=2 * TERMS), :] = jnp.where(left, one, pltpu.roll(two, 64, 1))
         terms[pl.ds(TERMS + row, SUB, stride=2 * TERMS), :] = jnp.where(left, pltpu.roll(one, 64, 1), two)
 
+    all_decay = [step_decay(table, m) for m in range(MODES)]
+
+    def backward(i, back):
+        for u in range(UNROLL):
+            value = at(dconv_ref, ROWS - 1 - (i * UNROLL + u))
+            back = tuple(all_decay[m] * back[m] + value for m in range(MODES))
+        return back
+
+    back = lax.fori_loop(0, ROWS // UNROLL, backward, zeros(MODES))
+    for m in range(MODES):
+        back_ref[m] = back[m]
+    for m in range(0, MODES, 2):
+        state = jnp.concatenate([back[m], back[m + 1]]).astype(BF16)
+        for j in range(BLOCKS):
+            sent_ref[j, SUB * m : SUB * (m + 2), :] = state
     half = MODES // 2
     for first in (0, half):
         modes = range(first, first + half)
@@ -312,20 +323,9 @@
         start = (tuple(carry_ref[m] for m in modes), zeros(half), zeros(half), zeros(half), zeros(1)[0])
         held, moment, first_sum, second_sum, skip_sum = lax.fori_loop(0, ROWS // UNROLL, forward, start)
 
-        def backward(i, back):
-            for u in range(UNROLL):
-                value = at(dconv_ref, ROWS - 1 - (i * UNROLL + u))
-                back = tuple(decay[m] * back[m] + value for m in range(half))
-            return back
-
-        back = lax.fori_loop(0, ROWS // UNROLL, backward, zeros(half))
         for m in range(half):
             put(first + m, first_sum[m], second_sum[m])
-            put(MODES + first + m, moment[m], back[m])
-        for m in range(0, half, 2):
-            state = jnp.concatenate([back[m], back[m + 1]]).astype(BF16)
-            for j in range(BLOCKS):
-                sent_ref[j, SUB * (first + m) : SUB * (first + m + 2), :] = state
+            put(MODES + first + m, moment[m], back_ref[first + m])
     for row in range(2 * MODES, TERMS):
         put(row, skip_sum, skip_sum)
     for j in range(BLOCKS):
@@ -338,118 +338,7 @@
         result.wait()
 
 
-def backward_kernel(
-    own_ref, sent_in, dconv_in, key_in, value_in, table_in,
-    dkey_out, dvalue_out,
-    sent_ref, dconv_ref, key_ref, value_ref, table, dkey_ref, dvalue_ref, carry_ref, buffer, sems,
-):
-    own = own_ref[0]
-    copies = [
-        pltpu.make_async_copy(source, target, sems.at[i])
-        for i, (source, target) in enumerate(
-            [
-                (sent_in.at[:, :STATE], sent_ref),
-                (table_in, table),
-                (dconv_in, dconv_ref),
-                (key_in, key_ref),
-                (value_in, value_ref),
-            ]
-        )
-    ]
-    results = [
-        pltpu.make_async_copy(dkey_ref, dkey_out, sems.at[5]),
-        pltpu.make_async_copy(dvalue_ref, dvalue_out, sems.at[6]),
-    ]
-    for copy in copies:
-        copy.start()
-    copies[0].wait()
-    copies[1].wait()
-    for m in range(MODES):
-        far = block_decay(table, m)
-        carry = jnp.zeros((SUB, 128), F32)
-        for j in range(BLOCKS - 1, 0, -1):
-            carry = jnp.where(j > own, far * carry + sent_ref[j, SUB * m : SUB * (m + 1), :].astype(F32), carry)
-        carry_ref[m] = carry
-    copies[2].wait()
-    decay = [step_decay(table, m) for m in range(MODES)]
-    weight = [mode_weight(table, m) for m in range(MODES)]
-    skip = skip_of(table)
-
-    def body(i, held):
-        for u in range(UNROLL):
-            step = ROWS - 1 - (i * UNROLL + u)
-            value = at(dconv_ref, step)
-            held = tuple(decay[m] * held[m] + value for m in range(MODES))
-            total = tree_sum([weight[m] * held[m] for m in range(MODES)])
-            buffer[pl.ds(pl.multiple_of(step * SUB, SUB), SUB), :] = total + skip * value
-        return held
-
-    lax.fori_loop(0, ROWS // UNROLL, body, tuple(carry_ref[m] for m in range(MODES)))
-    copies[3].wait()
-    copies[4].wait()
-    for group in range(SUB):
-        grad = buffer[group_rows(group), :].astype(BF16).astype(F32)
-        dkey_ref[:, lanes(group)] = (grad * value_ref[:, lanes(group)].astype(F32)).astype(BF16)
-        dvalue_ref[:, lanes(group)] = (grad * key_ref[:, lanes(group)].astype(F32)).astype(BF16)
-    for result in results:
-        result.start()
-    for result in results:
-        result.wait()
-
-
-def add_kernel(*refs):
-    out_ref = refs[-1]
-    total = refs[0][...].astype(F32).reshape(out_ref.shape)
-    for ref in refs[1:-2]:
-        total += ref[...].astype(F32).reshape(out_ref.shape)
-    out_ref[...] = total.astype(out_ref.dtype)
-
-
-def stage_kernel(*refs):
-    first, same, other, outs = refs[:4], refs[4], refs[5], refs[7:]
-    outs[0][...] = sum(ref[0].astype(F32) for ref in first).astype(BF16)
-    for k in (1, 2, 3):
-        outs[k][...] = (same[k].astype(F32) + other[k].astype(F32)).astype(BF16)
-
-
-def add_placed_kernel(place_ref, *refs):
-    add_kernel(*refs)
-
-
-def add_placed(array, place, after, *more):
-    specs = [pl.BlockSpec((1, ROWS, 512), lambda i, at, k=k: (2 * k + at[0], 0, 0)) for k in range(4)]
-    specs += [pl.BlockSpec((ROWS, 512), lambda i, at: (0, 0))] * len(more)
-    return pl.pallas_call(
-        add_placed_kernel,
-        grid_spec=pltpu.PrefetchScalarGridSpec(
-            num_scalar_prefetch=1,
-            grid=(1,),
-            in_specs=specs + [pl.BlockSpec(memory_space=pl.ANY)],
-            out_specs=pl.BlockSpec((ROWS, 512), lambda i, at: (0, 0)),
-        ),
-        out_shape=bf16(ROWS, 512),
-        name="sum_output",
-        **params_of(1_000_000, 2_000_000),
-    )(place.reshape(1).astype(jnp.int32), *[far(array)] * 4, *[far(one) for one in more], far(after))
-
-
-def gradient_kernel(*refs):
-    first, second, out_ref, held, sems = refs[:5], refs[5:10], refs[11], refs[12], refs[13]
-    copies = []
-    for i, ref in enumerate(first + second):
-        copies.append(pltpu.make_async_copy(ref.at[0], held.at[i], sems.at[i]))
-    for copy in copies:
-        copy.start()
-    for copy in copies:
-        copy.wait()
-    out_ref[:HALF] = sum(held[i].astype(F32) for i in range(5))
-    out_ref[HALF:] = sum(held[i].astype(F32) for i in range(5, 10))
-
-
-def owner_kernel(parts_in, rate_ref, residue_ref, dresidue_ref, drate_ref, dskip_ref, parts_ref, sem):
-    copy = pltpu.make_async_copy(parts_in.at[:, STATE:], parts_ref, sem)
-    copy.start()
-    copy.wait()
+def owner_sums(parts_ref, rate_ref, residue_ref, dresidue_ref, drate_ref, dskip_ref):
     rate = rate_ref[...]
     residue = residue_ref[...]
     near = jnp.exp(rate * (-1.0 / SEQ))
@@ -473,6 +362,140 @@
     dskip_ref[...] = skip
 
 
+def backward_kernel(
+    own_ref, sent_in, dconv_in, key_in, value_in, table_in, rate_ref, residue_ref,
+    dkey_out, dvalue_out, dresidue_ref, drate_ref, dskip_ref,
+    sent_ref, dconv_ref, key_ref, value_ref, table, dkey_ref, dvalue_ref, carry_ref, buffer, sems,
+):
+    own = own_ref[0]
+    copies = [
+        pltpu.make_async_copy(source, target, sems.at[i])
+        for i, (source, target) in enumerate(
+            [
+                (sent_in, sent_ref),
+                (table_in, table),
+                (dconv_in, dconv_ref),
+                (key_in, key_ref),
+                (value_in, value_ref),
+            ]
+        )
+    ]
+    results = [
+        pltpu.make_async_copy(dkey_ref, dkey_out, sems.at[5]),
+        pltpu.make_async_copy(dvalue_ref, dvalue_out, sems.at[6]),
+    ]
+    for copy in copies:
+        copy.start()
+    copies[0].wait()
+    copies[1].wait()
+    for m in range(MODES):
+        far = block_decay(table, m)
+        carry = jnp.zeros((SUB, 128), F32)
+        for j in range(BLOCKS - 1, 0, -1):
+            carry = jnp.where(j > own, far * carry + sent_ref[j, SUB * m : SUB * (m + 1), :].astype(F32), carry)
+        carry_ref[m] = carry
+    copies[2].wait()
+    decay = [step_decay(table, m) for m in range(MODES)]
+    weight = [mode_weight(table, m) for m in range(MODES)]
+    skip = skip_of(table)
+
+    def body(i, held):
+        for u in range(UNROLL):
+            step = ROWS - 1 - (i * UNROLL + u)
+            value = at(dconv_ref, step)
+            held = tuple(decay[m] * held[m] + value for m in range(MODES))
+            total = tree_sum([weight[m] * held[m] for m in range(MODES)])
+            buffer[pl.ds(pl.multiple_of(step * SUB, SUB), SUB), :] = total + skip * value
+        return held
+
+    lax.fori_loop(0, ROWS // UNROLL, body, tuple(carry_ref[m] for m in range(MODES)))
+    copies[3].wait()
+    copies[4].wait()
+    for group in range(SUB):
+        grad = buffer[group_rows(group), :].astype(BF16).astype(F32)
+        dkey_ref[:, lanes(group)] = (grad * value_ref[:, lanes(group)].astype(F32)).astype(BF16)
+        dvalue_ref[:, lanes(group)] = (grad * key_ref[:, lanes(group)].astype(F32)).astype(BF16)
+    for result in results:
+        result.start()
+    owner_sums(sent_ref.at[:, STATE:], rate_ref, residue_ref, dresidue_ref, drate_ref, dskip_ref)
+    for result in results:
+        result.wait()
+
+
+def add_kernel(*refs):
+    out_ref = refs[-1]
+    total = refs[0][...].astype(F32).reshape(out_ref.shape)
+    for ref in refs[1:-2]:
+        total += ref[...].astype(F32).reshape(out_ref.shape)
+    out_ref[...] = total.astype(out_ref.dtype)
+
+
+def stage_kernel(*refs):
+    parts, outs, held, sems = refs[:6], refs[7:11], refs[11], refs[12]
+    copies = [pltpu.make_async_copy(parts[i].at[1], held.at[i], sems.at[i]) for i in range(4)]
+    for k in (1, 2, 3):
+        for i in (0, 1):
+            at = 2 * k + 2 + i
+            copies.append(pltpu.make_async_copy(parts[4 + i].at[k], held.at[at], sems.at[at]))
+    for copy in copies:
+        copy.start()
+    for copy in copies[:4]:
+        copy.wait()
+    outs[0][...] = sum(held[i].astype(F32) for i in range(4)).astype(BF16)
+    for k in (1, 2, 3):
+        copies[2 * k + 2].wait()
+        copies[2 * k + 3].wait()
+        outs[k][...] = (held[2 * k + 2].astype(F32) + held[2 * k + 3].astype(F32)).astype(BF16)
+
+
+def add_placed_kernel(place_ref, *refs):
+    add_kernel(*refs)
+
+
+def add_placed(array, place, after):
+    specs = [pl.BlockSpec((1, ROWS, 512), lambda i, at, k=k: (2 * k + at[0], 0, 0)) for k in range(4)]
+    return pl.pallas_call(
+        add_placed_kernel,
+        grid_spec=pltpu.PrefetchScalarGridSpec(
+            num_scalar_prefetch=1,
+            grid=(1,),
+            in_specs=specs + [pl.BlockSpec(memory_space=pl.ANY)],
+            out_specs=pl.BlockSpec((ROWS, 512), lambda i, at: (0, 0)),
+        ),
+        out_shape=bf16(ROWS, 512),
+        name="sum_output",
+        **params_of(1_000_000, 2_000_000),
+    )(place.reshape(1).astype(jnp.int32), *[far(array)] * 4, far(after))
+
+
+def last_kernel(place_ref, *refs):
+    parts, arrived_ref, last_ref = refs[:10], refs[10], refs[11]
+    weight_out, output_out = refs[13:15]
+    held, arrived, weight_ref, output_ref, sems = refs[15:]
+    copies = [pltpu.make_async_copy(parts[i].at[0], held.at[i], sems.at[i]) for i in range(10)]
+    for k in range(4):
+        copies.append(pltpu.make_async_copy(arrived_ref.at[2 * k + place_ref[0]], arrived.at[k], sems.at[10 + k]))
+    copies.append(pltpu.make_async_copy(last_ref, arrived.at[4], sems.at[14]))
+    results = [
+        pltpu.make_async_copy(weight_ref.at[:HALF], weight_out.at[:HALF], sems.at[15]),
+        pltpu.make_async_copy(weight_ref.at[HALF:], weight_out.at[HALF:], sems.at[16]),
+        pltpu.make_async_copy(output_ref, output_out, sems.at[17]),
+    ]
+    for copy in copies:
+        copy.start()
+    for half in (0, 1):
+        for copy in copies[5 * half : 5 * half + 5]:
+            copy.wait()
+        weight_ref[HALF * half : HALF * (half + 1)] = sum(held[5 * half + i].astype(F32) for i in range(5))
+        results[half].start()
+    for copy in copies[10:]:
+        copy.wait()
+    output_ref[...] = sum(arrived[k].astype(F32) for k in range(5)).astype(BF16)
+    results[2].start()
+    for copy in results:
+        copy.wait()
+
+
 def f32(*shape):
     return jax.ShapeDtypeStruct(shape, F32)
 
@@ -576,25 +599,15 @@
     )(own_array, sent, far(mixed), far(query), far(table), far(w_out))
 
     other_gated = lax.ppermute(gated, "ctx", core_swap)
-    partial_out = pl.pallas_call(
+    partial_out, half_cots = pl.pallas_call(
         output_kernel,
-        out_shape=far_bf16(8, ROWS, 512),
-        in_specs=[whole()] * 2,
-        out_specs=anywhere,
-        scratch_shapes=[pltpu.VMEM((8, ROWS, 512), BF16), pltpu.SemaphoreType.DMA((8,))],
+        out_shape=(far_bf16(8, ROWS, 512), bf16(8, ROWS, 256)),
+        in_specs=[smem, whole(), whole()] + [anywhere] * 4,
+        out_specs=(anywhere, whole()),
+        scratch_shapes=[pltpu.VMEM((8, ROWS, 512), BF16), pltpu.SemaphoreType.DMA((16,))],
         name="output_projection",
         **params_of(2_147_483_648, 11_000_000),
-    )(gated_near, weight_near)
-
-    half_cots = pl.pallas_call(
-        gather_kernel,
-        out_shape=bf16(8, ROWS, 256),
-        in_specs=[smem] + [pl.BlockSpec(memory_space=pl.ANY)] * 5,
-        out_specs=whole(),
-        scratch_shapes=[pltpu.SemaphoreType.DMA((8,))],
-        name="gather_cotangent",
-        **params_of(100_000, 6_000_000),
-    )(core_array, *[far(part) for part in cot_parts], far(partial_out))
+    )(core_array, gated_near, weight_near, far(cot_parts[0]), *cot_parts[1:])
     other_cots = lax.ppermute(half_cots, "ctx", core_swap)
 
     *by_y, same_z, other_z = pl.pallas_call(
@@ -627,8 +640,8 @@
         scratch_shapes=[
             pltpu.VMEM((ROWS, 1024), F32),
             pltpu.VMEM((BLOCKS * TERMS, 128), F32),
-            pltpu.VMEM((8, ROWS, 512), BF16),
-            pltpu.VMEM((8, 1024, 512), BF16),
+            pltpu.VMEM((4, ROWS, 1024), BF16),
+            pltpu.VMEM((4, 1024, 1024), BF16),
             pltpu.VMEM((ROWS, 1024), BF16),
             pltpu.VMEM((ROWS, 1024), BF16),
             pltpu.VMEM((ROWS * SUB, 128), F32),
@@ -637,6 +650,7 @@
             pltpu.VMEM((ROWS, 1024), BF16),
             pltpu.VMEM((ROWS * SUB, 128), F32),
             pltpu.VMEM((BLOCKS, STATE + 2 * TERMS, 128), BF16),
+            pltpu.VMEM((MODES, SUB, 128), F32),
             pltpu.SemaphoreType.DMA((24,)),
         ],
         name="cotangent_states",
@@ -647,27 +661,32 @@
     near_out = add_placed(arrived, 1 - place_z, payload)
     near_sum = near_out
     near_out = lax.ppermute(near_out, "tp", shift_x(0, 1))
-    output = add_placed(arrived, place_z, payload, near_out)
-
     first_far, *second_far = pl.pallas_call(
         stage_kernel,
-        grid=(1,),
         out_shape=(bf16(HALF, 256),) * 4,
-        in_specs=[pl.BlockSpec((1, HALF, 256), lambda i: (1, 0, 0))] * 4 + [full(4, HALF, 256)] * 2 + [anywhere],
-        out_specs=(full(HALF, 256),) * 4,
+        in_specs=[anywhere] * 7,
+        out_specs=(whole(),) * 4,
+        scratch_shapes=[pltpu.VMEM((10, HALF, 256), BF16), pltpu.SemaphoreType.DMA((10,))],
         name="sum_stage",
         **params_of(LONG, 2_000_000),
-    )(*[far(part) for part in [by_y[0]] + came_y], far(same_z), far(came_z), far(near_sum))
+    )(far(by_y[0]), *came_y, far(same_z), came_z, near_sum)
     first_far = lax.ppermute(first_far, "ctx", far_swap)
     second_far = [lax.ppermute(second_far[k - 1], "ctx", shift_y(k)) for k in (1, 2, 3)]
 
-    d_key, d_value = pl.pallas_call(
+    d_key, d_value, d_residue, d_rate, d_skip = pl.pallas_call(
         backward_kernel,
-        out_shape=(far_bf16(ROWS, 1024), far_bf16(ROWS, 1024)),
-        in_specs=[smem] + [anywhere] * 5,
-        out_specs=(anywhere,) * 2,
+        grid=(1,),
+        out_shape=(
+            far_bf16(ROWS, 1024),
+            far_bf16(ROWS, 1024),
+            f32(MODES, 64),
+            f32(MODES, 64),
+            f32(1, 64),
+        ),
+        in_specs=[smem] + [anywhere] * 5 + [full(MODES, 64)] * 2,
+        out_specs=(anywhere, anywhere, full(MODES, 64), full(MODES, 64), full(1, 64)),
         scratch_shapes=[
-            pltpu.VMEM((BLOCKS, STATE, 128), BF16),
+            pltpu.VMEM((BLOCKS, STATE + 2 * TERMS, 128), BF16),
             pltpu.VMEM((ROWS * SUB, 128), F32),
             pltpu.VMEM((ROWS, 1024), BF16),
             pltpu.VMEM((ROWS, 1024), BF16),
@@ -680,36 +699,44 @@
         ],
         name="backward_conv",
         **params_of(5_000_000_000, 4_000_000),
-    )(own_array, far(received), far(d_conv), far(key_part), far(value_part), far(table))
-
-    d_weight = pl.pallas_call(
-        gradient_kernel,
-        grid=(1,),
-        out_shape=f32(2 * HALF, 256),
-        in_specs=[anywhere] * 11,
-        out_specs=full(2 * HALF, 256),
-        scratch_shapes=[pltpu.VMEM((10, HALF, 256), BF16), pltpu.SemaphoreType.DMA((10,))],
-        name="sum_gradient",
+    )(
+        own_array,
+        received,
+        far(d_conv),
+        far(key_part),
+        far(value_part),
+        far(table),
+        far(rate.T),
+        far(residue.T),
+    )
+
+    d_weight, output = pl.pallas_call(
+        last_kernel,
+        out_shape=(far_f32(2 * HALF, 256), far_bf16(ROWS, 512)),
+        in_specs=[smem] + [anywhere] * 13,
+        out_specs=(anywhere,) * 2,
+        scratch_shapes=[
+            pltpu.VMEM((10, HALF, 256), BF16),
+            pltpu.VMEM((5, ROWS, 512), BF16),
+            pltpu.VMEM((2 * HALF, 256), F32),
+            pltpu.VMEM((ROWS, 512), BF16),
+            pltpu.SemaphoreType.DMA((18,)),
+        ],
+        name="last_sums",
         **params_of(2_000_000, 4_000_000),
     )(
-        *[far(part) for part in [by_y[0]] + came_y],
+        place_z.reshape(1).astype(jnp.int32),
+        far(by_y[0]),
+        *came_y,
         first_far[None],
         far(same_z),
-        far(came_z),
+        came_z,
         *[part[None] for part in second_far],
+        far(arrived),
+        near_out,
         far(d_key),
     )
 
-    d_residue, d_rate, d_skip = pl.pallas_call(
-        owner_kernel,
-        grid=(1,),
-        out_shape=(f32(MODES, 64), f32(MODES, 64), f32(1, 64)),
-        in_specs=[anywhere, full(MODES, 64), full(MODES, 64)],
-        out_specs=(full(MODES, 64), full(MODES, 64), full(1, 64)),
-        scratch_shapes=[pltpu.VMEM((BLOCKS, 2 * TERMS, 128), BF16), pltpu.SemaphoreType.DMA],
-        name="owner_sums",
-        **params_of(1_000_000, 400_000),
-    )(far(received), far(rate.T), far(residue.T))
     return (output, d_query, d_key, d_value, d_weight, d_residue.T, d_rate.T, d_skip[0])
 
 

time: 122 us -> 118 us (0.967)
  local copies, waits for them, and re-layouts: 3.92 us -> 0.01 us
  Pallas kernels: 52.3 us -> 50.2 us
    unnamed x22 -> x6, local copies, waits for them, and re-layouts: 3.92 us -> 0.01 us
    all_to_all x4, waiting for transfers between devices: 14.7 us -> 16.8 us  [exchange(): lax.all_to_all(array, axis, split_axis=0, concat_axis=0, tiled=True, axis...]
    ppermute x3, starting transfers between devices: 3.8 us -> 5.6 us  [local(): came_y = [lax.ppermute(by_y[k], 'ctx', shift_y(k)) for k in (1, 2, 3)]]
    ppermute x1, waiting for transfers between devices: 0.01 us -> 1.77 us  [local(): first_far = lax.ppermute(first_far, 'ctx', far_swap)]
    ppermute x1, waiting for transfers between devices: 1.71 us -> 0.01 us  [local(): near_out = lax.ppermute(near_out, 'tp', shift_x(0, 1))]
    pallas_call x2 -> x1, Pallas kernels: 3.46 us -> 2.03 us  [add_placed(): pl.pallas_call(add_placed_kernel, grid_spec=pltpu.PrefetchScalarGridSpec(...]
    ppermute x3, starting transfers between devices: 4.3 us -> 5.6 us  [local(): lax.ppermute(second_far[k - 1], 'ctx', shift_y(k))]
    pallas_call x6 -> x4, Pallas kernels: 17.2 us -> 16.5 us  [the longest x1 7.11 us: local(): pl.pallas_call(backward_kernel, grid=(1,), out_shape=(far_bf16(ROWS, 1024...]
  transfers between devices with their start and end apart: 19 -> 19, of which waited for: 6 -> 5; matrix products, arithmetic and copies ran while one was open for 0% -> 0% of each run, Pallas kernels for 40% -> 37%
where the time goes in v5:
time: 118 us; the launch traced here: 116 us
  Pallas kernels  50.2 us (43%)
  starting transfers between devices  45 us (38%)
  waiting for transfers between devices  19.8 us (17%)
    all_to_all x4, starting transfers between devices, exchange(): lax.all_to_all(array, axis, split_axis=0, concat_axis=0, tiled=True, axis...  22.5 us
    all_to_all x4, waiting for transfers between devices, exchange(): lax.all_to_all(array, axis, split_axis=0, concat_axis=0, tiled=True, axis...  16.8 us
    pallas_call x1, Pallas kernels, local(): pl.pallas_call(cotangent_kernel, out_shape=(far_bf16(ROWS, 1024), far_f32...  13.7 us
    pallas_call x1, Pallas kernels, local(): pl.pallas_call(backward_kernel, grid=(1,), out_shape=(far_bf16(ROWS, 1024...  7.11 us
    pallas_call x1, Pallas kernels, local(): pl.pallas_call(weight_kernel, out_shape=(far_bf16(2, HALF, 256),) * 4 + (...  6.53 us
    ppermute x3, starting transfers between devices, local(): came_y = [lax.ppermute(by_y[k], 'ctx', shift_y(k)) for k in (1, 2, 3)]  5.6 us
    ppermute x3, starting transfers between devices, local(): lax.ppermute(second_far[k - 1], 'ctx', shift_y(k))  5.6 us
    pallas_call x1, Pallas kernels, local(): pl.pallas_call(forward_kernel, out_shape=(far_bf16(ROWS, 1024), far_bf16(...  5.05 us
  transfers between devices with their start and end apart: 19, of which 5 were waited for; matrix products, arithmetic and copies ran while one was open for 0% of the time, Pallas kernels for 37%

profile of v5, /device:TPU:0, one launch (start us, length us, event | category | flops | bytes accessed | tf_op | source)
XLA Modules:
  0.0 116.3 jit_solution(2430248739345056347)
XLA Ops:
  0.6 2.1 %collective-permute-start = (bf16[256,512]{1,0:T(8,128)(2,1)}, bf16[256,512]{1,0:T(8,128)(2,1)S(1)}, u32[]{:S(2)}, u32[]{:S(2)}) collective-permute-start(bf16[256,512]{1,0:T(8,128)(2,1)} %cot_ref.1), channel_id=1, source_target_pairs={{0,1},{1,0},{2,3},{3,2},{4,5},{5,4},{6,7},{7,6},{8,9},{9,8},{10,11... | collective-permute-start | bytes 786440 | tf_op jit(solution)/shard_map/ppermute | solution.py:553
  2.7 1.5 %pack_parameters.1 = f32[16,24,128]{2,1,0:T(8,128)} custom-call(f32[16,64]{1,0:T(8,128)} %bitcast.17, f32[16,64]{1,0:T(8,128)} %bitcast.19, f32[1,64]{1,0:T(1,128)} %bitcast.21), custom_call_target="tpu_custom_call" | custom-call | flops 2000 | bytes 4000 | tf_op jit(solution)/shard_map/pack_parameters/pallas_call | solution.py:543
  4.2 7.6 %all-to-all-start = ((f32[16,24,128]{2,1,0:T(8,128)}), f32[16,24,128]{2,1,0:T(8,128)S(1)}, u32[]{:S(2)}, u32[]{:S(2)}) async-start(f32[16,24,128]{2,1,0:T(8,128)} %pack_parameters.1), calls=%async_computation | async-start | bytes 393216 | tf_op jit(solution)/shard_map/all_to_all | solution.py:508
  11.8 2.8 %mix_inputs.1 = (f32[2048,128]{1,0:T(8,128)S(1)}, f32[2048,128]{1,0:T(8,128)}, bf16[2,256,512]{2,1,0:T(8,128)(2,1)}) custom-call(bf16[256,1024]{1,0:T(8,128)(2,1)} %key_in.1, bf16[256,1024]{1,0:T(8,128)(2,1)} %value_in.1, bf16[256,512]{1,0:T(8,128)(2,1)} %cot_ref.1, bf16[256,512]{1,0:T(8,128)(2,1)S(1)} %collective-permute-done.near_cot_ref), custom_call_target="tpu_custom_call" | custom-call | flops 2000000 | bytes 60000 | tf_op jit(solution)/shard_map/mix_inputs/pallas_call | solution.py:554
  14.6 2.8 %collective-permute-start.4 = (bf16[2,256,512]{2,1,0:T(8,128)(2,1)}, bf16[2,256,512]{2,1,0:T(8,128)(2,1)S(1)}, u32[]{:S(2)}, u32[]{:S(2)}) collective-permute-start(bf16[2,256,512]{2,1,0:T(8,128)(2,1)} %get-tuple-element.45.refs_0_.part0), channel_id=1, source_target_pairs={{0,6},{1,7},{2,0},{3,1},{4,2},{5,3},{6,4},{7,5},{8,14},{9,15},{10,... | collective-permute-start | bytes 1572872 | tf_op jit(solution)/shard_map/ppermute | solution.py:563
  20.4 2.2 %forward_states.1 = (bf16[16,16,8,128]{3,2,1,0:T(8,128)(2,1)}, f32[384,128]{1,0:T(8,128)}) custom-call(f32[2048,128]{1,0:T(8,128)S(1)} %get-tuple-element.40.mixed_ref, f32[16,24,128]{2,1,0:T(8,128)S(1)} %all-to-all-done.packed_ref), custom_call_target="tpu_custom_call" | custom-call | flops 60000000 | bytes 80000 | tf_op jit(solution)/shard_map/forward_states/pallas_call | solution.py:565
  22.6 5.9 %all-to-all-start.1 = ((bf16[16,16,8,128]{3,2,1,0:T(8,128)(2,1)}), bf16[16,16,8,128]{3,2,1,0:T(8,128)(2,1)S(1)}, u32[]{:S(2)}, u32[]{:S(2)}) async-start(bf16[16,16,8,128]{3,2,1,0:T(8,128)(2,1)} %get-tuple-element.41), calls=%async_computation.1 | async-start | bytes 1048576 | tf_op jit(solution)/shard_map/all_to_all | solution.py:508
  28.5 12.4 %all-to-all-done.1.sent_ref = bf16[16,16,8,128]{3,2,1,0:T(8,128)(2,1)S(1)} async-done(((bf16[16,16,8,128]{3,2,1,0:T(8,128)(2,1)}), bf16[16,16,8,128]{3,2,1,0:T(8,128)(2,1)S(1)}, u32[]{:S(2)}, u32[]{:S(2)}) %all-to-all-start.1) | async-done | bytes 524320 | tf_op jit(solution)/shard_map/all_to_all | solution.py:508
  40.9 5.0 %forward_conv.1 = (bf16[256,1024]{1,0:T(8,128)(2,1)}, bf16[256,1024]{1,0:T(8,128)(2,1)}, f32[16,8,128]{2,1,0:T(8,128)}, bf16[256,1024]{1,0:T(8,128)(2,1)S(1)}, bf16[8,1024,512]{2,1,0:T(8,128)(2,1)S(1)}) custom-call(s32[1]{0:T(128)} %bitcast.2.own_ref, bf16[16,16,8,128]{3,2,1,0:T(8,128)(2,1)S(1)} %all-to-all-done.1.sent_ref, ...), custom_call_target="tpu_custom_call" | custom-call | flops 100000000 | bytes 80000 | tf_op jit(solution)/shard_map/forward_conv/pallas_call | solution.py:577
  46.0 4.3 %output_projection.1 = (bf16[8,256,512]{2,1,0:T(8,128)(2,1)}, bf16[8,256,256]{2,1,0:T(8,128)(2,1)}) custom-call(s32[1]{0:T(128)} %bitcast.1.core_ref, bf16[256,1024]{1,0:T(8,128)(2,1)S(1)} %get-tuple-element.46.gated_ref, bf16[8,1024,512]{2,1,0:T(8,128)(2,1)S(1)} %get-tuple-element.47.weight_ref, bf16[2,256,512]{2,1,0:T(8,128)(2,1)} %get-tuple-element.45.refs_0_.part0, ...), custom_call_target="tpu_custom_call" | custom-call | flops 42949672 | bytes 220000 | tf_op jit(solution)/shard_map/output_projection/pallas_call | solution.py:602
  50.9 4.4 %all-to-all-start.2 = ((bf16[4,2,256,512]{3,2,1,0:T(8,128)(2,1)}), bf16[4,2,256,512]{3,2,1,0:T(8,128)(2,1)}, u32[]{:S(2)}, u32[]{:S(2)}) async-start(bf16[4,2,256,512]{3,2,1,0:T(8,128)(2,1)} %bitcast.16), calls=%async_computation.2 | async-start | bytes 4194304 | tf_op jit(solution)/shard_map/all_to_all | solution.py:508
  55.5 6.5 %projection_gradient.1 = (bf16[2,512,256]{2,1,0:T(8,128)(2,1)}, bf16[2,512,256]{2,1,0:T(8,128)(2,1)}, bf16[2,512,256]{2,1,0:T(8,128)(2,1)}, bf16[2,512,256]{2,1,...) custom-call(s32[9]{0:T(128)S(1)} %pad_add_fusion.index_ref, ...), custom_call_target="tpu_custom_call" | custom-call | flops 42949672 | bytes 160000 | tf_op jit(solution)/shard_map/projection_gradient/pallas_call | solution.py:613
  62.1 1.5 %collective-permute-start.9 = (bf16[4,512,256]{2,1,0:T(8,128)(2,1)}, bf16[4,512,256]{2,1,0:T(8,128)(2,1)S(1)}, u32[]{:S(2)}, u32[]{:S(2)}) collective-permute-start(bf16[4,512,256]{2,1,0:T(8,128)(2,1)} %get-tuple-element.55.after_ref), channel_id=1, source_target_pairs={{0,64},{8,72},{16,80},{24,88},{32,96},{40,104},{48,112},{56,120},{... | collective-permute-start | bytes 3145736 | tf_op jit(solution)/shard_map/ppermute | solution.py:629
  65.1 2.7 %collective-permute-start.7 = (bf16[2,512,256]{2,1,0:T(8,128)(2,1)}, bf16[2,512,256]{2,1,0:T(8,128)(2,1)S(1)}, u32[]{:S(2)}, u32[]{:S(2)}) collective-permute-start(bf16[2,512,256]{2,1,0:T(8,128)(2,1)} %get-tuple-element.52), channel_id=1, source_target_pairs={{0,32},{8,40},{16,48},{24,56},{32,0},{40,8},{48,16},{56,24},{64,96... | collective-permute-start | bytes 1572872 | tf_op jit(solution)/shard_map/ppermute | solution.py:630
  69.2 13.7 %cotangent_states.1 = (bf16[256,1024]{1,0:T(8,128)(2,1)}, f32[2048,128]{1,0:T(8,128)}, bf16[16,224,128]{2,1,0:T(8,128)(2,1)}) custom-call(s32[8]{0:T(128)S(1)} %fusion.2.came_ref, bf16[2,256,512]{2,1,0:T(8,128)(2,1)} %get-tuple-element.45.refs_0_.part0, bf16[2,256,512]{2,1,0:T(8,128)(2,1)} %copy-done.2, bf16[2,256,512]{2,1,0:T(8,128)(2,1)} %copy-done.1, ...), custom_call_target="tpu_custom_call" | custom-call | flops 280000000 | bytes 260000 | tf_op jit(solution)/shard_map/cotangent_states/pallas_call | solution.py:635
  82.9 4.6 %all-to-all-start.3 = ((bf16[16,224,128]{2,1,0:T(8,128)(2,1)}), bf16[16,224,128]{2,1,0:T(8,128)(2,1)S(1)}, u32[]{:S(2)}, u32[]{:S(2)}) async-start(bf16[16,224,128]{2,1,0:T(8,128)(2,1)} %get-tuple-element.58.refs_4_), calls=%async_computation.3 | async-start | bytes 1835008 | tf_op jit(solution)/shard_map/all_to_all | solution.py:508
  87.5 2.0 %sum_output.1.refs_6_ = bf16[256,512]{1,0:T(8,128)(2,1)} custom-call(s32[1]{0:T(128)} %bitcast.6.place_ref, bf16[8,256,512]{2,1,0:T(8,128)(2,1)} %bitcast.8.refs_0_.refs_1_.refs_2_.refs_3_.refs_10_, bf16[8,256,512]{2,1,0:T(8,128)(2,1)} %bitcast.8.refs_0_.refs_1_.refs_2_.refs_3_.refs_10_, ...), custom_call_target="tpu_custom_call" | custom-call | flops 20000 | bytes 40000 | tf_op jit(solution)/shard_map/sum_output/pallas_call | solution.py:457
  90.8 2.3 %sum_stage.1 = (bf16[512,256]{1,0:T(8,128)(2,1)}, bf16[512,256]{1,0:T(8,128)(2,1)}, bf16[512,256]{1,0:T(8,128)(2,1)}, bf16[512,256]{1,0:T(8,128)(2,1)}) custom-call(bf16[2,512,256]{2,1,0:T(8,128)(2,1)} %get-tuple-element.50.refs_0_, bf16[2,512,256]{2,1,0:T(8,128)(2,1)S(1)} %collective-permute-done.6.refs_1_, ...), custom_call_target="tpu_custom_call" | custom-call | flops 40000000000 | bytes 40000 | tf_op jit(solution)/shard_map/sum_stage/pallas_call | solution.py:664
  93.1 2.7 %collective-permute-start.10 = (bf16[512,256]{1,0:T(8,128)(2,1)}, bf16[512,256]{1,0:T(8,128)(2,1)}, u32[]{:S(2)}, u32[]{:S(2)}) collective-permute-start(bf16[512,256]{1,0:T(8,128)(2,1)} %get-tuple-element.59), channel_id=1, source_target_pairs={{0,64},{8,72},{16,80},{24,88},{32,96},{40,104},{48,112},{56,120},{... | collective-permute-start | bytes 786440 | tf_op jit(solution)/shard_map/ppermute | solution.py:673
  97.2 2.7 %collective-permute-start.12 = (bf16[512,256]{1,0:T(8,128)(2,1)}, bf16[512,256]{1,0:T(8,128)(2,1)}, u32[]{:S(2)}, u32[]{:S(2)}) collective-permute-start(bf16[512,256]{1,0:T(8,128)(2,1)} %get-tuple-element.61), channel_id=1, source_target_pairs={{0,32},{8,40},{16,48},{24,56},{32,0},{40,8},{48,16},{56,24},{64,96... | collective-permute-start | bytes 786440 | tf_op jit(solution)/shard_map/ppermute | solution.py:674
  101.3 3.1 %all-to-all-done.3.sent_in = bf16[16,224,128]{2,1,0:T(8,128)(2,1)S(1)} async-done(((bf16[16,224,128]{2,1,0:T(8,128)(2,1)}), bf16[16,224,128]{2,1,0:T(8,128)(2,1)S(1)}, u32[]{:S(2)}, u32[]{:S(2)}) %all-to-all-start.3) | async-done | bytes 917536 | tf_op jit(solution)/shard_map/all_to_all | solution.py:508
  104.4 7.1 %backward_conv.1 = (bf16[256,1024]{1,0:T(8,128)(2,1)}, bf16[256,1024]{1,0:T(8,128)(2,1)}, f32[16,64]{1,0:T(8,128)}, f32[16,64]{1,0:T(8,128)}, f32[1,64]{1,0:T(1,128)}) custom-call(s32[1]{0:T(128)} %bitcast.2.own_ref, bf16[16,224,128]{2,1,0:T(8,128)(2,1)S(1)} %all-to-all-done.3.sent_in, f32[2048,128]{1,0:T(8,128)} %get-tuple-element.63.dconv_in, ...), custom_call_target="tpu_custom_call" | custom-call | flops 100000000 | bytes 80000 | tf_op jit(solution)/shard_map/backward_conv/pallas_call | solution.py:676
  111.5 1.8 %collective-permute-done.10 = bf16[512,256]{1,0:T(8,128)(2,1)} collective-permute-done((bf16[512,256]{1,0:T(8,128)(2,1)}, bf16[512,256]{1,0:T(8,128)(2,1)}, u32[]{:S(2)}, u32[]{:S(2)}) %collective-permute-start.10) | collective-permute-done | bytes 262176 | tf_op jit(solution)/shard_map/ppermute | solution.py:673
  113.3 2.8 %last_sums.1 = (f32[1024,256]{1,0:T(8,128)}, bf16[256,512]{1,0:T(8,128)(2,1)}) custom-call(s32[1]{0:T(128)} %bitcast.place_ref, bf16[2,512,256]{2,1,0:T(8,128)(2,1)} %get-tuple-element.50.refs_0_, bf16[2,512,256]{2,1,0:T(8,128)(2,1)S(1)} %collective-permute-done.6.refs_1_, bf16[2,512,256]{2,1,0:T(8,128)(2,1)S(1)} %collective-permute-done.7.refs_2_, ...), custom_call_target="tpu_custom_call" | custom-call | flops 40000 | bytes 80000 | tf_op jit(solution)/shard_map/last_sums/pallas_call | solution.py:713
  (34 shorter events, 10.9 us)
Async XLA Ops:
  0.6 11.2 %collective-permute-start = (bf16[256,512]{1,0:T(8,128)(2,1)}, bf16[256,512]{1,0:T(8,128)(2,1)S(1)}, u32[]{:S(2)}, u32[]{:S(2)}) collective-permute-start(bf16[256,512]{1,0:T(8,128)(2,1)} %cot_ref.1), channel_id=1, source_target_pairs={{0,1},{1,0},{2,3},{3,2},{4,5},{5,4},{6,7},{7,6},{8,9},{9,8},{10,11... | collective-permute-start | bytes 786440 | tf_op jit(solution)/shard_map/ppermute | solution.py:553
  4.2 16.2 %all-to-all-start = ((f32[16,24,128]{2,1,0:T(8,128)}), f32[16,24,128]{2,1,0:T(8,128)S(1)}, u32[]{:S(2)}, u32[]{:S(2)}) async-start(f32[16,24,128]{2,1,0:T(8,128)} %pack_parameters.1), calls=%async_computation | async-start | bytes 393216 | tf_op jit(solution)/shard_map/all_to_all | solution.py:508
  14.6 31.3 %collective-permute-start.4 = (bf16[2,256,512]{2,1,0:T(8,128)(2,1)}, bf16[2,256,512]{2,1,0:T(8,128)(2,1)S(1)}, u32[]{:S(2)}, u32[]{:S(2)}) collective-permute-start(bf16[2,256,512]{2,1,0:T(8,128)(2,1)} %get-tuple-element.45.refs_0_.part0), channel_id=1, source_target_pairs={{0,6},{1,7},{2,0},{3,1},{4,2},{5,3},{6,4},{7,5},{8,14},{9,15},{10,... | collective-permute-start | bytes 1572872 | tf_op jit(solution)/shard_map/ppermute | solution.py:563
  17.4 28.6 %collective-permute-start.3 = (bf16[2,256,512]{2,1,0:T(8,128)(2,1)}, bf16[2,256,512]{2,1,0:T(8,128)(2,1)S(1)}, u32[]{:S(2)}, u32[]{:S(2)}) collective-permute-start(bf16[2,256,512]{2,1,0:T(8,128)(2,1)} %get-tuple-element.45.refs_0_.part0), channel_id=1, source_target_pairs={{0,4},{1,5},{2,6},{3,7},{4,0},{5,1},{6,2},{7,3},{8,12},{9,13},{10,... | collective-permute-start | bytes 1572872 | tf_op jit(solution)/shard_map/ppermute | solution.py:563
  18.2 27.8 %collective-permute-start.2 = (bf16[2,256,512]{2,1,0:T(8,128)(2,1)}, bf16[2,256,512]{2,1,0:T(8,128)(2,1)S(1)}, u32[]{:S(2)}, u32[]{:S(2)}) collective-permute-start(bf16[2,256,512]{2,1,0:T(8,128)(2,1)} %get-tuple-element.45.refs_0_.part0), channel_id=1, source_target_pairs={{0,2},{1,3},{2,4},{3,5},{4,6},{5,7},{6,0},{7,1},{8,10},{9,11},{10,... | collective-permute-start | bytes 1572872 | tf_op jit(solution)/shard_map/ppermute | solution.py:563
  22.6 18.3 %all-to-all-start.1 = ((bf16[16,16,8,128]{3,2,1,0:T(8,128)(2,1)}), bf16[16,16,8,128]{3,2,1,0:T(8,128)(2,1)S(1)}, u32[]{:S(2)}, u32[]{:S(2)}) async-start(bf16[16,16,8,128]{3,2,1,0:T(8,128)(2,1)} %get-tuple-element.41), calls=%async_computation.1 | async-start | bytes 1048576 | tf_op jit(solution)/shard_map/all_to_all | solution.py:508
  45.9 9.6 %copy-start = (bf16[2,256,512]{2,1,0:T(8,128)(2,1)}, bf16[2,256,512]{2,1,0:T(8,128)(2,1)S(1)}, u32[]{:S(2)}) copy-start(bf16[2,256,512]{2,1,0:T(8,128)(2,1)S(1)} %collective-permute-done.4.refs_3_.part3) | copy-start | bytes 1572868
  46.0 9.6 %copy-start.1 = (bf16[2,256,512]{2,1,0:T(8,128)(2,1)}, bf16[2,256,512]{2,1,0:T(8,128)(2,1)S(1)}, u32[]{:S(2)}) copy-start(bf16[2,256,512]{2,1,0:T(8,128)(2,1)S(1)} %collective-permute-done.3.refs_2_.part2) | copy-start | bytes 1572868
  46.0 9.5 %copy-start.2 = (bf16[2,256,512]{2,1,0:T(8,128)(2,1)}, bf16[2,256,512]{2,1,0:T(8,128)(2,1)S(1)}, u32[]{:S(2)}) copy-start(bf16[2,256,512]{2,1,0:T(8,128)(2,1)S(1)} %collective-permute-done.2.refs_1_.part1) | copy-start | bytes 1572868
  50.3 5.2 %collective-permute-start.5 = (bf16[8,256,256]{2,1,0:T(8,128)(2,1)}, bf16[8,256,256]{2,1,0:T(8,128)(2,1)S(1)}, u32[]{:S(2)}, u32[]{:S(2)}) collective-permute-start(bf16[8,256,256]{2,1,0:T(8,128)(2,1)} %get-tuple-element.48), channel_id=1, source_target_pairs={{0,8},{8,0},{16,24},{24,16},{32,40},{40,32},{48,56},{56,48},{64,72... | collective-permute-start | bytes 3145736 | tf_op jit(solution)/shard_map/ppermute | solution.py:611
  50.4 5.1 %collective-permute-start.1 = (bf16[256,1024]{1,0:T(8,128)(2,1)}, bf16[256,1024]{1,0:T(8,128)(2,1)S(1)}, u32[]{:S(2)}, u32[]{:S(2)}) collective-permute-start(bf16[256,1024]{1,0:T(8,128)(2,1)} %get-tuple-element.44.gated_ref), channel_id=1, source_target_pairs={{0,8},{8,0},{16,24},{24,16},{32,40},{40,32},{48,56},{56,48},{64,72... | collective-permute-start | bytes 1572872 | tf_op jit(solution)/shard_map/ppermute | solution.py:601
  50.9 32.0 %all-to-all-start.2 = ((bf16[4,2,256,512]{3,2,1,0:T(8,128)(2,1)}), bf16[4,2,256,512]{3,2,1,0:T(8,128)(2,1)}, u32[]{:S(2)}, u32[]{:S(2)}) async-start(bf16[4,2,256,512]{3,2,1,0:T(8,128)(2,1)} %bitcast.16), calls=%async_computation.2 | async-start | bytes 4194304 | tf_op jit(solution)/shard_map/all_to_all | solution.py:508
  62.1 28.8 %collective-permute-start.9 = (bf16[4,512,256]{2,1,0:T(8,128)(2,1)}, bf16[4,512,256]{2,1,0:T(8,128)(2,1)S(1)}, u32[]{:S(2)}, u32[]{:S(2)}) collective-permute-start(bf16[4,512,256]{2,1,0:T(8,128)(2,1)} %get-tuple-element.55.after_ref), channel_id=1, source_target_pairs={{0,64},{8,72},{16,80},{24,88},{32,96},{40,104},{48,112},{56,120},{... | collective-permute-start | bytes 3145736 | tf_op jit(solution)/shard_map/ppermute | solution.py:629
  63.6 25.9 %collective-permute-start.6 = (bf16[2,512,256]{2,1,0:T(8,128)(2,1)}, bf16[2,512,256]{2,1,0:T(8,128)(2,1)S(1)}, u32[]{:S(2)}, u32[]{:S(2)}) collective-permute-start(bf16[2,512,256]{2,1,0:T(8,128)(2,1)} %get-tuple-element.51), channel_id=1, source_target_pairs={{0,16},{8,24},{16,32},{24,40},{32,48},{40,56},{48,0},{56,8},{64,80... | collective-permute-start | bytes 1572872 | tf_op jit(solution)/shard_map/ppermute | solution.py:630
  65.1 25.7 %collective-permute-start.7 = (bf16[2,512,256]{2,1,0:T(8,128)(2,1)}, bf16[2,512,256]{2,1,0:T(8,128)(2,1)S(1)}, u32[]{:S(2)}, u32[]{:S(2)}) collective-permute-start(bf16[2,512,256]{2,1,0:T(8,128)(2,1)} %get-tuple-element.52), channel_id=1, source_target_pairs={{0,32},{8,40},{16,48},{24,56},{32,0},{40,8},{48,16},{56,24},{64,96... | collective-permute-start | bytes 1572872 | tf_op jit(solution)/shard_map/ppermute | solution.py:630
  67.7 23.1 %collective-permute-start.8 = (bf16[2,512,256]{2,1,0:T(8,128)(2,1)}, bf16[2,512,256]{2,1,0:T(8,128)(2,1)S(1)}, u32[]{:S(2)}, u32[]{:S(2)}) collective-permute-start(bf16[2,512,256]{2,1,0:T(8,128)(2,1)} %get-tuple-element.53), channel_id=1, source_target_pairs={{0,48},{8,56},{16,0},{24,8},{32,16},{40,24},{48,32},{56,40},{64,11... | collective-permute-start | bytes 1572872 | tf_op jit(solution)/shard_map/ppermute | solution.py:630
  82.9 21.5 %all-to-all-start.3 = ((bf16[16,224,128]{2,1,0:T(8,128)(2,1)}), bf16[16,224,128]{2,1,0:T(8,128)(2,1)S(1)}, u32[]{:S(2)}, u32[]{:S(2)}) async-start(bf16[16,224,128]{2,1,0:T(8,128)(2,1)} %get-tuple-element.58.refs_4_), calls=%async_computation.3 | async-start | bytes 1835008 | tf_op jit(solution)/shard_map/all_to_all | solution.py:508
  89.5 22.0 %collective-permute-start.14 = (bf16[256,512]{1,0:T(8,128)(2,1)}, bf16[256,512]{1,0:T(8,128)(2,1)}, u32[]{:S(2)}, u32[]{:S(2)}) collective-permute-start(bf16[256,512]{1,0:T(8,128)(2,1)} %sum_output.1.refs_6_), channel_id=1, source_target_pairs={{0,1},{1,0},{2,3},{3,2},{4,5},{5,4},{6,7},{7,6},{8,9},{9,8},{10,11... | collective-permute-start | bytes 786440 | tf_op jit(solution)/shard_map/ppermute | solution.py:663
  93.1 20.2 %collective-permute-start.10 = (bf16[512,256]{1,0:T(8,128)(2,1)}, bf16[512,256]{1,0:T(8,128)(2,1)}, u32[]{:S(2)}, u32[]{:S(2)}) collective-permute-start(bf16[512,256]{1,0:T(8,128)(2,1)} %get-tuple-element.59), channel_id=1, source_target_pairs={{0,64},{8,72},{16,80},{24,88},{32,96},{40,104},{48,112},{56,120},{... | collective-permute-start | bytes 786440 | tf_op jit(solution)/shard_map/ppermute | solution.py:673
  95.7 17.6 %collective-permute-start.11 = (bf16[512,256]{1,0:T(8,128)(2,1)}, bf16[512,256]{1,0:T(8,128)(2,1)}, u32[]{:S(2)}, u32[]{:S(2)}) collective-permute-start(bf16[512,256]{1,0:T(8,128)(2,1)} %get-tuple-element.60), channel_id=1, source_target_pairs={{0,16},{8,24},{16,32},{24,40},{32,48},{40,56},{48,0},{56,8},{64,80... | collective-permute-start | bytes 786440 | tf_op jit(solution)/shard_map/ppermute | solution.py:674
  97.2 16.1 %collective-permute-start.12 = (bf16[512,256]{1,0:T(8,128)(2,1)}, bf16[512,256]{1,0:T(8,128)(2,1)}, u32[]{:S(2)}, u32[]{:S(2)}) collective-permute-start(bf16[512,256]{1,0:T(8,128)(2,1)} %get-tuple-element.61), channel_id=1, source_target_pairs={{0,32},{8,40},{16,48},{24,56},{32,0},{40,8},{48,16},{56,24},{64,96... | collective-permute-start | bytes 786440 | tf_op jit(solution)/shard_map/ppermute | solution.py:674
  99.9 13.4 %collective-permute-start.13 = (bf16[512,256]{1,0:T(8,128)(2,1)}, bf16[512,256]{1,0:T(8,128)(2,1)}, u32[]{:S(2)}, u32[]{:S(2)}) collective-permute-start(bf16[512,256]{1,0:T(8,128)(2,1)} %get-tuple-element.62), channel_id=1, source_target_pairs={{0,48},{8,56},{16,0},{24,8},{32,16},{40,24},{48,32},{56,40},{64,11... | collective-permute-start | bytes 786440 | tf_op jit(solution)/shard_map/ppermute | solution.py:674

commit v6 on v5

--- a/solution.py
+++ b/solution.py
@@ -187,42 +187,34 @@
         copy.wait()
 
 
-def output_kernel(core_ref, gated_ref, weight_ref, *refs):
-    parts, out_ref, half_ref, blocks, sems = refs[:4], refs[4], refs[5], refs[6], refs[7]
-    half = pl.ds(pl.multiple_of((1 - core_ref[0]) * 256, 256), 256)
-    copies = [
-        pltpu.make_async_copy(parts[i // 2].at[i % 2, :, half], half_ref.at[i], sems.at[8 + i]) for i in range(8)
-    ]
+def output_kernel(gated_ref, weight_ref, out_ref, blocks, sems):
     results = [pltpu.make_async_copy(blocks.at[i], out_ref.at[i], sems.at[i]) for i in range(8)]
-    for copy in copies:
-        copy.start()
     for i in range(8):
         blocks[i] = jnp.dot(gated_ref[...], weight_ref[i], preferred_element_type=F32).astype(BF16)
         results[i].start()
-    for copy in copies + results:
-        copy.wait()
+    for result in results:
+        result.wait()
 
 
 def weight_kernel(index_ref, gated_ref, other_ref, *refs):
-    cot_refs, other_cot_ref = refs[:4], refs[4]
-    along_y, along_z = refs[6:10], refs[10:12]
-    gated, turned, cots, chunks, sems, out_sems = refs[12:]
+    cot_refs, other_refs = refs[:4], refs[4:8]
+    along_y, along_z = refs[9:13], refs[13:15]
+    gated, turned, cots, chunks, sems, out_sems = refs[15:]
     half = pl.ds(pl.multiple_of(index_ref[8] * 256, 256), 256)
     copies = [
-        pltpu.make_async_copy(gated_ref, gated.at[0], sems.at[16]),
-        pltpu.make_async_copy(other_ref, gated.at[1], sems.at[17]),
+        pltpu.make_async_copy(gated_ref, gated, sems.at[8]),
     ]
     for i in range(8):
         own = cot_refs[i // 2].at[i % 2, :, half]
+        other = other_refs[i // 2].at[i % 2, :, half]
         copies.append(pltpu.make_async_copy(own, cots.at[i, :ROWS], sems.at[i]))
-        copies.append(pltpu.make_async_copy(other_cot_ref.at[i], cots.at[i, ROWS:], sems.at[8 + i]))
+        copies.append(pltpu.make_async_copy(other, cots.at[i, ROWS:], sems.at[9 + i]))
     for copy in copies:
         copy.start()
+    turned[:, ROWS:] = other_ref[...].T
     copies[0].wait()
-    turned[:, :ROWS] = gated[0].T
-    copies[1].wait()
-    turned[:, ROWS:] = gated[1].T
-    for copy in copies[2:]:
+    turned[:, :ROWS] = gated[...].T
+    for copy in copies[1:]:
         copy.wait()
     results = []
     for z in (1, 0):
@@ -330,9 +322,7 @@
         put(row, skip_sum, skip_sum)
     for j in range(BLOCKS):
         term = terms[TERMS * j : TERMS * (j + 1), :]
-        upper = term.astype(BF16)
-        sent_ref[j, STATE : STATE + TERMS, :] = upper
-        sent_ref[j, STATE + TERMS :, :] = (term - upper.astype(F32)).astype(BF16)
+        sent_ref[j, STATE:, :] = term.astype(BF16)
     results[2].start()
     for result in results:
         result.wait()
@@ -349,8 +339,7 @@
     skip = jnp.zeros((1, rate.shape[1]), F32)
     later = jnp.zeros_like(rate)
     for j in range(BLOCKS - 1, -1, -1):
-        upper, lower = parts_ref[j, :TERMS, :], parts_ref[j, TERMS:, :]
-        terms = upper.astype(F32) + lower.astype(F32)
+        terms = parts_ref[j].astype(F32)
         sums, ends = terms[0:MODES], terms[MODES : 2 * MODES]
         first += sums[:, :64]
         second += sums[:, 64:] + near * later * ends[:, :64]
@@ -363,38 +352,40 @@
 
 
 def backward_kernel(
-    own_ref, sent_in, dconv_in, key_in, value_in, table_in, rate_ref, residue_ref,
-    dkey_out, dvalue_out, dresidue_ref, drate_ref, dskip_ref,
-    sent_ref, dconv_ref, key_ref, value_ref, table, dkey_ref, dvalue_ref, carry_ref, buffer, sems,
+    own_ref, sent_ref, dconv_in, key_in, value_in, table_in, first_in, same_in, arrived_in,
+    came1, came2, came3, came_z, rate_ref, residue_ref,
+    dkey_out, dvalue_out, gradient_ref, output_ref, dresidue_ref, drate_ref, dskip_ref,
+    dconv_ref, key_ref, value_ref, table, dkey_ref, dvalue_ref, carry_ref, buffer, blocks, arrived, sems,
 ):
     own = own_ref[0]
     copies = [
         pltpu.make_async_copy(source, target, sems.at[i])
         for i, (source, target) in enumerate(
             [
-                (sent_in, sent_ref),
                 (table_in, table),
                 (dconv_in, dconv_ref),
                 (key_in, key_ref),
                 (value_in, value_ref),
+                (first_in.at[0], blocks.at[0]),
+                (same_in.at[0], blocks.at[1]),
             ]
+            + [(arrived_in.at[2 * k + own_ref[1]], arrived.at[k]) for k in range(4)]
         )
     ]
     results = [
-        pltpu.make_async_copy(dkey_ref, dkey_out, sems.at[5]),
-        pltpu.make_async_copy(dvalue_ref, dvalue_out, sems.at[6]),
+        pltpu.make_async_copy(dkey_ref, dkey_out, sems.at[10]),
+        pltpu.make_async_copy(dvalue_ref, dvalue_out, sems.at[11]),
     ]
     for copy in copies:
         copy.start()
     copies[0].wait()
-    copies[1].wait()
     for m in range(MODES):
         far = block_decay(table, m)
         carry = jnp.zeros((SUB, 128), F32)
         for j in range(BLOCKS - 1, 0, -1):
             carry = jnp.where(j > own, far * carry + sent_ref[j, SUB * m : SUB * (m + 1), :].astype(F32), carry)
         carry_ref[m] = carry
-    copies[2].wait()
+    copies[1].wait()
     decay = [step_decay(table, m) for m in range(MODES)]
     weight = [mode_weight(table, m) for m in range(MODES)]
     skip = skip_of(table)
@@ -409,14 +400,19 @@
         return held
 
     lax.fori_loop(0, ROWS // UNROLL, body, tuple(carry_ref[m] for m in range(MODES)))
+    copies[2].wait()
     copies[3].wait()
-    copies[4].wait()
     for group in range(SUB):
         grad = buffer[group_rows(group), :].astype(BF16).astype(F32)
         dkey_ref[:, lanes(group)] = (grad * value_ref[:, lanes(group)].astype(F32)).astype(BF16)
         dvalue_ref[:, lanes(group)] = (grad * key_ref[:, lanes(group)].astype(F32)).astype(BF16)
     for result in results:
         result.start()
+    for copy in copies[4:]:
+        copy.wait()
+    gradient_ref[:HALF] = blocks[0].astype(F32) + sum(part[0].astype(F32) for part in (came1, came2, came3))
+    gradient_ref[HALF:] = blocks[1].astype(F32) + came_z[0].astype(F32)
+    output_ref[...] = sum(arrived[k].astype(F32) for k in range(4))
     owner_sums(sent_ref.at[:, STATE:], rate_ref, residue_ref, dresidue_ref, drate_ref, dskip_ref)
     for result in results:
         result.wait()
@@ -430,67 +426,47 @@
     out_ref[...] = total.astype(out_ref.dtype)
 
 
-def stage_kernel(*refs):
-    parts, outs, held, sems = refs[:6], refs[7:11], refs[11], refs[12]
-    copies = [pltpu.make_async_copy(parts[i].at[1], held.at[i], sems.at[i]) for i in range(4)]
+def stage_kernel(own_ref, *refs):
+    came_y, came_z, outs = refs[:3], refs[3], refs[4:8]
+    outs[0][...] = (own_ref[0].astype(F32) + sum(part[1].astype(F32) for part in came_y)).astype(BF16)
     for k in (1, 2, 3):
-        for i in (0, 1):
-            at = 2 * k + 2 + i
-            copies.append(pltpu.make_async_copy(parts[4 + i].at[k], held.at[at], sems.at[at]))
+        outs[k][...] = (own_ref[k].astype(F32) + came_z[k].astype(F32)).astype(BF16)
+
+
+def add_placed_kernel(place_ref, arrived_ref, first_ref, same_ref, after_ref, out_ref, own_ref, held, sems):
+    copies = [pltpu.make_async_copy(arrived_ref.at[2 * k + place_ref[0]], held.at[k], sems.at[k]) for k in range(4)]
+    copies.append(pltpu.make_async_copy(first_ref.at[1], own_ref.at[0], sems.at[4]))
+    copies += [pltpu.make_async_copy(same_ref.at[k], own_ref.at[k], sems.at[4 + k]) for k in (1, 2, 3)]
     for copy in copies:
         copy.start()
     for copy in copies[:4]:
         copy.wait()
-    outs[0][...] = sum(held[i].astype(F32) for i in range(4)).astype(BF16)
-    for k in (1, 2, 3):
-        copies[2 * k + 2].wait()
-        copies[2 * k + 3].wait()
-        outs[k][...] = (held[2 * k + 2].astype(F32) + held[2 * k + 3].astype(F32)).astype(BF16)
-
-
-def add_placed_kernel(place_ref, *refs):
-    add_kernel(*refs)
-
-
-def add_placed(array, place, after):
-    specs = [pl.BlockSpec((1, ROWS, 512), lambda i, at, k=k: (2 * k + at[0], 0, 0)) for k in range(4)]
-    return pl.pallas_call(
-        add_placed_kernel,
-        grid_spec=pltpu.PrefetchScalarGridSpec(
-            num_scalar_prefetch=1,
-            grid=(1,),
-            in_specs=specs + [pl.BlockSpec(memory_space=pl.ANY)],
-            out_specs=pl.BlockSpec((ROWS, 512), lambda i, at: (0, 0)),
-        ),
-        out_shape=bf16(ROWS, 512),
-        name="sum_output",
-        **params_of(1_000_000, 2_000_000),
-    )(place.reshape(1).astype(jnp.int32), *[far(array)] * 4, far(after))
-
-
-def last_kernel(place_ref, *refs):
-    parts, arrived_ref, last_ref = refs[:10], refs[10], refs[11]
-    weight_out, output_out = refs[13:15]
-    held, arrived, weight_ref, output_ref, sems = refs[15:]
-    copies = [pltpu.make_async_copy(parts[i].at[0], held.at[i], sems.at[i]) for i in range(10)]
-    for k in range(4):
-        copies.append(pltpu.make_async_copy(arrived_ref.at[2 * k + place_ref[0]], arrived.at[k], sems.at[10 + k]))
-    copies.append(pltpu.make_async_copy(last_ref, arrived.at[4], sems.at[14]))
+    out_ref[...] = sum(held[k].astype(F32) for k in range(4)).astype(BF16)
+    for copy in copies[4:]:
+        copy.wait()
+
+
+def last_kernel(gradient_ref, out_sum_ref, *refs):
+    parts, last_in, weight_out, output_out = refs[:4], refs[4], refs[5], refs[6]
+    held, last, weight_ref, output_ref, sems = refs[7:]
+    copies = [pltpu.make_async_copy(parts[i], held.at[i], sems.at[i]) for i in range(4)]
+    copies.append(pltpu.make_async_copy(last_in, last, sems.at[4]))
     results = [
-        pltpu.make_async_copy(weight_ref.at[:HALF], weight_out.at[:HALF], sems.at[15]),
-        pltpu.make_async_copy(weight_ref.at[HALF:], weight_out.at[HALF:], sems.at[16]),
-        pltpu.make_async_copy(output_ref, output_out, sems.at[17]),
+        pltpu.make_async_copy(weight_ref.at[:HALF], weight_out.at[:HALF], sems.at[5]),
+        pltpu.make_async_copy(weight_ref.at[HALF:], weight_out.at[HALF:], sems.at[6]),
+        pltpu.make_async_copy(output_ref, output_out, sems.at[7]),
     ]
     for copy in copies:
         copy.start()
-    for half in (0, 1):
-        for copy in copies[5 * half : 5 * half + 5]:
-            copy.wait()
-        weight_ref[HALF * half : HALF * (half + 1)] = sum(held[5 * half + i].astype(F32) for i in range(5))
-        results[half].start()
-    for copy in copies[10:]:
-        copy.wait()
-    output_ref[...] = sum(arrived[k].astype(F32) for k in range(5)).astype(BF16)
+    copies[0].wait()
+    weight_ref[:HALF] = gradient_ref[:HALF] + held[0].astype(F32)
+    results[0].start()
+    for copy in copies[1:4]:
+        copy.wait()
+    weight_ref[HALF:] = gradient_ref[HALF:] + sum(held[i].astype(F32) for i in (1, 2, 3))
+    results[1].start()
+    copies[4].wait()
+    output_ref[...] = (out_sum_ref[...] + last[...].astype(F32)).astype(BF16)
     results[2].start()
     for copy in results:
         copy.wait()
@@ -599,33 +575,33 @@
     )(own_array, sent, far(mixed), far(query), far(table), far(w_out))
 
     other_gated = lax.ppermute(gated, "ctx", core_swap)
-    partial_out, half_cots = pl.pallas_call(
+    partial_out = pl.pallas_call(
         output_kernel,
-        out_shape=(far_bf16(8, ROWS, 512), bf16(8, ROWS, 256)),
-        in_specs=[smem, whole(), whole()] + [anywhere] * 4,
-        out_specs=(anywhere, whole()),
-        scratch_shapes=[pltpu.VMEM((8, ROWS, 512), BF16), pltpu.SemaphoreType.DMA((16,))],
+        out_shape=far_bf16(8, ROWS, 512),
+        in_specs=[whole(), whole()],
+        out_specs=anywhere,
+        scratch_shapes=[pltpu.VMEM((8, ROWS, 512), BF16), pltpu.SemaphoreType.DMA((8,))],
         name="output_projection",
         **params_of(2_147_483_648, 11_000_000),
-    )(core_array, gated_near, weight_near, far(cot_parts[0]), *cot_parts[1:])
-    other_cots = lax.ppermute(half_cots, "ctx", core_swap)
+    )(gated_near, weight_near)
+    other_parts = [lax.ppermute(part, "ctx", core_swap) for part in cot_parts]
 
     *by_y, same_z, other_z = pl.pallas_call(
         weight_kernel,
         out_shape=(far_bf16(2, HALF, 256),) * 4 + (far_bf16(4, HALF, 256),) * 2,
-        in_specs=[smem] + [anywhere] * 8,
+        in_specs=[smem, anywhere, whole()] + [anywhere] * 9,
         out_specs=(anywhere,) * 6,
         scratch_shapes=[
-            pltpu.VMEM((2, ROWS, 1024), BF16),
+            pltpu.VMEM((ROWS, 1024), BF16),
             pltpu.VMEM((1024, 2 * ROWS), BF16),
             pltpu.VMEM((8, 2 * ROWS, 256), BF16),
             pltpu.VMEM((8, 1024, 256), BF16),
-            pltpu.SemaphoreType.DMA((18,)),
+            pltpu.SemaphoreType.DMA((17,)),
             pltpu.SemaphoreType.DMA((16,)),
         ],
         name="projection_gradient",
         **params_of(2_147_483_648, 8_000_000),
-    )(jnp.concatenate([index, core_array]), far(gated), other_gated, *[far(part) for part in cot_parts], other_cots, far(partial_out))
+    )(jnp.concatenate([index, core_array]), far(gated), other_gated, *[far(part) for part in cot_parts], *other_parts, far(partial_out))
     came_z = lax.ppermute(other_z, "ctx", far_swap)
     came_y = [lax.ppermute(by_y[k], "ctx", shift_y(k)) for k in (1, 2, 3)]
 
@@ -634,7 +610,7 @@
 
     d_query, d_conv, payload = pl.pallas_call(
         cotangent_kernel,
-        out_shape=(far_bf16(ROWS, 1024), far_f32(ROWS * SUB, 128), far_bf16(BLOCKS, STATE + 2 * TERMS, 128)),
+        out_shape=(far_bf16(ROWS, 1024), far_f32(ROWS * SUB, 128), far_bf16(BLOCKS, STATE + TERMS, 128)),
         in_specs=[smem] + [anywhere] * 11,
         out_specs=(anywhere,) * 3,
         scratch_shapes=[
@@ -649,7 +625,7 @@
             pltpu.VMEM((TABLE, 128), F32),
             pltpu.VMEM((ROWS, 1024), BF16),
             pltpu.VMEM((ROWS * SUB, 128), F32),
-            pltpu.VMEM((BLOCKS, STATE + 2 * TERMS, 128), BF16),
+            pltpu.VMEM((BLOCKS, STATE + TERMS, 128), BF16),
             pltpu.VMEM((MODES, SUB, 128), F32),
             pltpu.SemaphoreType.DMA((24,)),
         ],
@@ -658,35 +634,49 @@
     )(came, *[far(part) for part in cot_parts], far(w_out), far(query), far(conv_out), far(mixed), far(carry), far(table), far(other_z))
     received = exchange(payload, "ctx")
 
-    near_out = add_placed(arrived, 1 - place_z, payload)
-    near_sum = near_out
-    near_out = lax.ppermute(near_out, "tp", shift_x(0, 1))
+    near_sum, own_blocks = pl.pallas_call(
+        add_placed_kernel,
+        out_shape=(bf16(ROWS, 512), bf16(4, HALF, 256)),
+        in_specs=[smem] + [anywhere] * 4,
+        out_specs=(whole(), whole()),
+        scratch_shapes=[pltpu.VMEM((4, ROWS, 512), BF16), pltpu.SemaphoreType.DMA((8,))],
+        name="sum_output",
+        **params_of(1_000_000, 2_000_000),
+    )(
+        (1 - place_z).reshape(1).astype(jnp.int32),
+        far(arrived),
+        far(by_y[0]),
+        far(same_z),
+        far(payload),
+    )
+    near_out = lax.ppermute(near_sum, "tp", shift_x(0, 1))
+
     first_far, *second_far = pl.pallas_call(
         stage_kernel,
         out_shape=(bf16(HALF, 256),) * 4,
-        in_specs=[anywhere] * 7,
+        in_specs=[whole()] * 5,
         out_specs=(whole(),) * 4,
-        scratch_shapes=[pltpu.VMEM((10, HALF, 256), BF16), pltpu.SemaphoreType.DMA((10,))],
         name="sum_stage",
         **params_of(LONG, 2_000_000),
-    )(far(by_y[0]), *came_y, far(same_z), came_z, near_sum)
+    )(own_blocks, *came_y, came_z)
     first_far = lax.ppermute(first_far, "ctx", far_swap)
     second_far = [lax.ppermute(second_far[k - 1], "ctx", shift_y(k)) for k in (1, 2, 3)]
 
-    d_key, d_value, d_residue, d_rate, d_skip = pl.pallas_call(
+    d_key, d_value, gradient, out_sum, d_residue, d_rate, d_skip = pl.pallas_call(
         backward_kernel,
         grid=(1,),
         out_shape=(
             far_bf16(ROWS, 1024),
             far_bf16(ROWS, 1024),
+            f32(2 * HALF, 256),
+            f32(ROWS, 512),
             f32(MODES, 64),
             f32(MODES, 64),
             f32(1, 64),
         ),
-        in_specs=[smem] + [anywhere] * 5 + [full(MODES, 64)] * 2,
-        out_specs=(anywhere, anywhere, full(MODES, 64), full(MODES, 64), full(1, 64)),
+        in_specs=[smem, whole()] + [anywhere] * 7 + [whole()] * 4 + [full(MODES, 64)] * 2,
+        out_specs=(anywhere, anywhere, whole(), whole(), full(MODES, 64), full(MODES, 64), full(1, 64)),
         scratch_shapes=[
-            pltpu.VMEM((BLOCKS, STATE + 2 * TERMS, 128), BF16),
             pltpu.VMEM((ROWS * SUB, 128), F32),
             pltpu.VMEM((ROWS, 1024), BF16),
             pltpu.VMEM((ROWS, 1024), BF16),
@@ -695,17 +685,24 @@
             pltpu.VMEM((ROWS, 1024), BF16),
             pltpu.VMEM((MODES, SUB, 128), F32),
             pltpu.VMEM((ROWS * SUB, 128), F32),
-            pltpu.SemaphoreType.DMA((7,)),
+            pltpu.VMEM((2, HALF, 256), BF16),
+            pltpu.VMEM((4, ROWS, 512), BF16),
+            pltpu.SemaphoreType.DMA((12,)),
         ],
         name="backward_conv",
         **params_of(5_000_000_000, 4_000_000),
     )(
-        own_array,
+        jnp.stack([own, place_z]).astype(jnp.int32),
         received,
         far(d_conv),
         far(key_part),
         far(value_part),
         far(table),
+        far(by_y[0]),
+        far(same_z),
+        far(arrived),
+        *came_y,
+        came_z,
         far(rate.T),
         far(residue.T),
     )
@@ -713,29 +710,18 @@
     d_weight, output = pl.pallas_call(
         last_kernel,
         out_shape=(far_f32(2 * HALF, 256), far_bf16(ROWS, 512)),
-        in_specs=[smem] + [anywhere] * 13,
+        in_specs=[whole(), whole()] + [anywhere] * 5,
         out_specs=(anywhere,) * 2,
         scratch_shapes=[
-            pltpu.VMEM((10, HALF, 256), BF16),
-            pltpu.VMEM((5, ROWS, 512), BF16),
+            pltpu.VMEM((4, HALF, 256), BF16),
+            pltpu.VMEM((ROWS, 512), BF16),
             pltpu.VMEM((2 * HALF, 256), F32),
             pltpu.VMEM((ROWS, 512), BF16),
-            pltpu.SemaphoreType.DMA((18,)),
+            pltpu.SemaphoreType.DMA((8,)),
         ],
         name="last_sums",
         **params_of(2_000_000, 4_000_000),
-    )(
-        place_z.reshape(1).astype(jnp.int32),
-        far(by_y[0]),
-        *came_y,
-        first_far[None],
-        far(same_z),
-        came_z,
-        *[part[None] for part in second_far],
-        far(arrived),
-        near_out,
-        far(d_key),
-    )
+    )(gradient, out_sum, first_far, *second_far, near_out)
 
     return (output, d_query, d_key, d_value, d_weight, d_residue.T, d_rate.T, d_skip[0])
 

time: 118 us -> 114 us (0.966)
  Pallas kernels: 50.2 us -> 46 us
    ppermute x3, starting transfers between devices: 5.6 us -> 3.31 us  [local(): came_y = [lax.ppermute(by_y[k], 'ctx', shift_y(k)) for k in (1, 2, 3)]]
    ppermute x2 -> x5, starting transfers between devices: 0.09 us -> 1.48 us  [the longest x4 1.4 us: local(): other_parts = [lax.ppermute(part, 'ctx', core_swap) for part in cot_parts]]
    ppermute x3, starting transfers between devices: 4.44 us -> 5.65 us  [local(): lax.ppermute(cot_pair, 'tp', shift_x(k))]
  transfers between devices with their start and end apart: 19 -> 22, of which waited for: 5 -> 6; matrix products, arithmetic and copies ran while one was open for 0% -> 0% of each run, Pallas kernels for 37% -> 39%
where the time goes in v6:
time: 114 us; the launch traced here: 112 us
  Pallas kernels  46 us (40%)
  starting transfers between devices  45.1 us (40%)
  waiting for transfers between devices  20 us (18%)
    all_to_all x4, starting transfers between devices, exchange(): lax.all_to_all(array, axis, split_axis=0, concat_axis=0, tiled=True, axis...  22.7 us
    all_to_all x4, waiting for transfers between devices, exchange(): lax.all_to_all(array, axis, split_axis=0, concat_axis=0, tiled=True, axis...  17.4 us
    pallas_call x1, Pallas kernels, local(): pl.pallas_call(cotangent_kernel, out_shape=(far_bf16(ROWS, 1024), far_f32...  13.5 us
    pallas_call x1, Pallas kernels, local(): pl.pallas_call(backward_kernel, grid=(1,), out_shape=(far_bf16(ROWS, 1024...  6.53 us
    pallas_call x1, Pallas kernels, local(): pl.pallas_call(weight_kernel, out_shape=(far_bf16(2, HALF, 256),) * 4 + (...  5.7 us
    ppermute x3, starting transfers between devices, local(): lax.ppermute(cot_pair, 'tp', shift_x(k))  5.65 us
    ppermute x3, starting transfers between devices, local(): lax.ppermute(second_far[k - 1], 'ctx', shift_y(k))  5.63 us
    pallas_call x1, Pallas kernels, local(): pl.pallas_call(forward_kernel, out_shape=(far_bf16(ROWS, 1024), far_bf16(...  5.05 us
  transfers between devices with their start and end apart: 22, of which 6 were waited for; matrix products, arithmetic and copies ran while one was open for 0% of the time, Pallas kernels for 39%

profile of v6, /device:TPU:0, one launch (start us, length us, event | category | flops | bytes accessed | tf_op | source)
XLA Modules:
  0.0 112.4 jit_solution(11026124570431200374)
XLA Ops:
  0.6 2.1 %collective-permute-start = (bf16[256,512]{1,0:T(8,128)(2,1)}, bf16[256,512]{1,0:T(8,128)(2,1)S(1)}, u32[]{:S(2)}, u32[]{:S(2)}) collective-permute-start(bf16[256,512]{1,0:T(8,128)(2,1)} %cot_ref.1), channel_id=1, source_target_pairs={{0,1},{1,0},{2,3},{3,2},{4,5},{5,4},{6,7},{7,6},{8,9},{9,8},{10,11... | collective-permute-start | bytes 786440 | tf_op jit(solution)/shard_map/ppermute | solution.py:529
  4.2 7.6 %all-to-all-start = ((f32[16,24,128]{2,1,0:T(8,128)}), f32[16,24,128]{2,1,0:T(8,128)S(1)}, u32[]{:S(2)}, u32[]{:S(2)}) async-start(f32[16,24,128]{2,1,0:T(8,128)} %pack_parameters.1), calls=%async_computation | async-start | bytes 393216 | tf_op jit(solution)/shard_map/all_to_all | solution.py:484
  11.8 2.8 %mix_inputs.1 = (f32[2048,128]{1,0:T(8,128)S(1)}, f32[2048,128]{1,0:T(8,128)}, bf16[2,256,512]{2,1,0:T(8,128)(2,1)}) custom-call(bf16[256,1024]{1,0:T(8,128)(2,1)} %key_in.1, bf16[256,1024]{1,0:T(8,128)(2,1)} %value_in.1, bf16[256,512]{1,0:T(8,128)(2,1)} %cot_ref.1, bf16[256,512]{1,0:T(8,128)(2,1)S(1)} %collective-permute-done.near_cot_ref), custom_call_target="tpu_custom_call" | custom-call | flops 2000000 | bytes 60000 | tf_op jit(solution)/shard_map/mix_inputs/pallas_call | solution.py:530
  14.6 1.5 %collective-permute-start.1 = (bf16[2,256,512]{2,1,0:T(8,128)(2,1)}, bf16[2,256,512]{2,1,0:T(8,128)(2,1)S(1)}, u32[]{:S(2)}, u32[]{:S(2)}) collective-permute-start(bf16[2,256,512]{2,1,0:T(8,128)(2,1)} %get-tuple-element.42.refs_0_.part0), channel_id=1, source_target_pairs={{0,2},{1,3},{2,4},{3,5},{4,6},{5,7},{6,0},{7,1},{8,10},{9,11},{10,... | collective-permute-start | bytes 1572872 | tf_op jit(solution)/shard_map/ppermute | solution.py:539
  16.1 2.7 %collective-permute-start.2 = (bf16[2,256,512]{2,1,0:T(8,128)(2,1)}, bf16[2,256,512]{2,1,0:T(8,128)(2,1)}, u32[]{:S(2)}, u32[]{:S(2)}) collective-permute-start(bf16[2,256,512]{2,1,0:T(8,128)(2,1)} %get-tuple-element.42.refs_0_.part0), channel_id=1, source_target_pairs={{0,4},{1,5},{2,6},{3,7},{4,0},{5,1},{6,2},{7,3},{8,12},{9,13},{10,... | collective-permute-start | bytes 1572872 | tf_op jit(solution)/shard_map/ppermute | solution.py:539
  20.4 2.2 %forward_states.1 = (bf16[16,16,8,128]{3,2,1,0:T(8,128)(2,1)}, f32[384,128]{1,0:T(8,128)}) custom-call(f32[2048,128]{1,0:T(8,128)S(1)} %get-tuple-element.43.mixed_ref, f32[16,24,128]{2,1,0:T(8,128)S(1)} %all-to-all-done.packed_ref), custom_call_target="tpu_custom_call" | custom-call | flops 60000000 | bytes 80000 | tf_op jit(solution)/shard_map/forward_states/pallas_call | solution.py:541
  22.6 7.1 %all-to-all-start.1 = ((bf16[16,16,8,128]{3,2,1,0:T(8,128)(2,1)}), bf16[16,16,8,128]{3,2,1,0:T(8,128)(2,1)S(1)}, u32[]{:S(2)}, u32[]{:S(2)}) async-start(bf16[16,16,8,128]{3,2,1,0:T(8,128)(2,1)} %get-tuple-element.44), calls=%async_computation.1 | async-start | bytes 1048576 | tf_op jit(solution)/shard_map/all_to_all | solution.py:484
  30.1 12.0 %all-to-all-done.1.sent_ref = bf16[16,16,8,128]{3,2,1,0:T(8,128)(2,1)S(1)} async-done(((bf16[16,16,8,128]{3,2,1,0:T(8,128)(2,1)}), bf16[16,16,8,128]{3,2,1,0:T(8,128)(2,1)S(1)}, u32[]{:S(2)}, u32[]{:S(2)}) %all-to-all-start.1) | async-done | bytes 524320 | tf_op jit(solution)/shard_map/all_to_all | solution.py:484
  42.1 5.0 %forward_conv.1 = (bf16[256,1024]{1,0:T(8,128)(2,1)}, bf16[256,1024]{1,0:T(8,128)(2,1)}, f32[16,8,128]{2,1,0:T(8,128)}, bf16[256,1024]{1,0:T(8,128)(2,1)S(1)}, bf16[8,1024,512]{2,1,0:T(8,128)(2,1)S(1)}) custom-call(s32[1]{0:T(128)} %bitcast.own_ref, bf16[16,16,8,128]{3,2,1,0:T(8,128)(2,1)S(1)} %all-to-all-done.1.sent_ref, ...), custom_call_target="tpu_custom_call" | custom-call | flops 100000000 | bytes 80000 | tf_op jit(solution)/shard_map/forward_conv/pallas_call | solution.py:553
  48.2 3.1 %output_projection.1.refs_8_ = bf16[8,256,512]{2,1,0:T(8,128)(2,1)} custom-call(bf16[256,1024]{1,0:T(8,128)(2,1)S(1)} %get-tuple-element.50.gated_ref, bf16[8,1024,512]{2,1,0:T(8,128)(2,1)S(1)} %get-tuple-element.51.weight_ref), custom_call_target="tpu_custom_call" | custom-call | flops 42949672 | bytes 220000 | tf_op jit(solution)/shard_map/output_projection/pallas_call | solution.py:578
  51.4 4.4 %all-to-all-start.3 = ((bf16[4,2,256,512]{3,2,1,0:T(8,128)(2,1)}), bf16[4,2,256,512]{3,2,1,0:T(8,128)(2,1)}, u32[]{:S(2)}, u32[]{:S(2)}) async-start(bf16[4,2,256,512]{3,2,1,0:T(8,128)(2,1)} %bitcast.12), calls=%async_computation.3 | async-start | bytes 4194304 | tf_op jit(solution)/shard_map/all_to_all | solution.py:484
  56.0 5.7 %projection_gradient.1 = (bf16[2,512,256]{2,1,0:T(8,128)(2,1)}, bf16[2,512,256]{2,1,0:T(8,128)(2,1)}, bf16[2,512,256]{2,1,0:T(8,128)(2,1)}, bf16[2,512,256]{2,1,...) custom-call(s32[9]{0:T(128)S(1)} %pad_add_fusion.1.index_ref, ...), custom_call_target="tpu_custom_call" | custom-call | flops 42949672 | bytes 160000 | tf_op jit(solution)/shard_map/projection_gradient/pallas_call | solution.py:589
  63.7 1.7 %collective-permute-start.11 = (bf16[2,512,256]{2,1,0:T(8,128)(2,1)}, bf16[2,512,256]{2,1,0:T(8,128)(2,1)S(1)}, u32[]{:S(2)}, u32[]{:S(2)}) collective-permute-start(bf16[2,512,256]{2,1,0:T(8,128)(2,1)} %get-tuple-element.59), channel_id=1, source_target_pairs={{0,48},{8,56},{16,0},{24,8},{32,16},{40,24},{48,32},{56,40},{64,11... | collective-permute-start | bytes 1572872 | tf_op jit(solution)/shard_map/ppermute | solution.py:606
  65.7 13.5 %cotangent_states.1 = (bf16[256,1024]{1,0:T(8,128)(2,1)}, f32[2048,128]{1,0:T(8,128)}, bf16[16,176,128]{2,1,0:T(8,128)(2,1)}) custom-call(s32[8]{0:T(128)S(1)} %fusion.came_ref, bf16[2,256,512]{2,1,0:T(8,128)(2,1)} %get-tuple-element.42.refs_0_.part0, bf16[2,256,512]{2,1,0:T(8,128)(2,1)} %copy-done, ...), custom_call_target="tpu_custom_call" | custom-call | flops 280000000 | bytes 260000 | tf_op jit(solution)/shard_map/cotangent_states/pallas_call | solution.py:611
  79.2 3.5 %all-to-all-done.3 = bf16[4,2,256,512]{3,2,1,0:T(8,128)(2,1)} async-done(((bf16[4,2,256,512]{3,2,1,0:T(8,128)(2,1)}), bf16[4,2,256,512]{3,2,1,0:T(8,128)(2,1)}, u32[]{:S(2)}, u32[]{:S(2)}) %all-to-all-start.3) | async-done | bytes 2097184 | tf_op jit(solution)/shard_map/all_to_all | solution.py:484
  82.8 3.6 %all-to-all-start.2 = ((bf16[16,176,128]{2,1,0:T(8,128)(2,1)}), bf16[16,176,128]{2,1,0:T(8,128)(2,1)S(1)}, u32[]{:S(2)}, u32[]{:S(2)}) async-start(bf16[16,176,128]{2,1,0:T(8,128)(2,1)} %get-tuple-element.53.after_ref), calls=%async_computation.2 | async-start | bytes 1441792 | tf_op jit(solution)/shard_map/all_to_all | solution.py:484
  86.4 2.3 %sum_output.1 = (bf16[256,512]{1,0:T(8,128)(2,1)}, bf16[4,512,256]{2,1,0:T(8,128)(2,1)S(1)}) custom-call(s32[1]{0:T(128)} %bitcast.8.place_ref, bf16[8,256,512]{2,1,0:T(8,128)(2,1)} %bitcast.7.arrived_in.arrived_ref, bf16[2,512,256]{2,1,0:T(8,128)(2,1)} %get-tuple-element.55.first_in.first_ref, bf16[4,512,256]{2,1,0:T(8,128)(2,1)} %get-tuple-element.56.same_in.same_ref, ...), custom_call_target="tpu_custom_call" | custom-call | flops 20000 | bytes 40000 | tf_op jit(solution)/shard_map/sum_output/pallas_call | solution.py:637
  90.2 3.5 %collective-permute-start.13 = (bf16[512,256]{1,0:T(8,128)(2,1)}, bf16[512,256]{1,0:T(8,128)(2,1)}, u32[]{:S(2)}, u32[]{:S(2)}) collective-permute-start(bf16[512,256]{1,0:T(8,128)(2,1)} %get-tuple-element.63), channel_id=1, source_target_pairs={{0,64},{8,72},{16,80},{24,88},{32,96},{40,104},{48,112},{56,120},{... | collective-permute-start | bytes 786440 | tf_op jit(solution)/shard_map/ppermute | solution.py:662
  93.6 1.5 %collective-permute-start.14 = (bf16[512,256]{1,0:T(8,128)(2,1)}, bf16[512,256]{1,0:T(8,128)(2,1)}, u32[]{:S(2)}, u32[]{:S(2)}) collective-permute-start(bf16[512,256]{1,0:T(8,128)(2,1)} %get-tuple-element.64), channel_id=1, source_target_pairs={{0,16},{8,24},{16,32},{24,40},{32,48},{40,56},{48,0},{56,8},{64,80... | collective-permute-start | bytes 786440 | tf_op jit(solution)/shard_map/ppermute | solution.py:663
  95.1 2.7 %collective-permute-start.15 = (bf16[512,256]{1,0:T(8,128)(2,1)}, bf16[512,256]{1,0:T(8,128)(2,1)}, u32[]{:S(2)}, u32[]{:S(2)}) collective-permute-start(bf16[512,256]{1,0:T(8,128)(2,1)} %get-tuple-element.65), channel_id=1, source_target_pairs={{0,32},{8,40},{16,48},{24,56},{32,0},{40,8},{48,16},{56,24},{64,96... | collective-permute-start | bytes 786440 | tf_op jit(solution)/shard_map/ppermute | solution.py:663
  99.3 1.8 %all-to-all-done.2.sent_ref = bf16[16,176,128]{2,1,0:T(8,128)(2,1)S(1)} async-done(((bf16[16,176,128]{2,1,0:T(8,128)(2,1)}), bf16[16,176,128]{2,1,0:T(8,128)(2,1)S(1)}, u32[]{:S(2)}, u32[]{:S(2)}) %all-to-all-start.2) | async-done | bytes 720928 | tf_op jit(solution)/shard_map/all_to_all | solution.py:484
  101.1 6.5 %backward_conv.1 = (bf16[256,1024]{1,0:T(8,128)(2,1)}, bf16[256,1024]{1,0:T(8,128)(2,1)}, f32[1024,256]{1,0:T(8,128)S(1)}, f32[256,512]{1,0:T(8,128)S(1)}, f32[1...) custom-call(s32[2]{0:T(128)S(1)} %pad_add_fusion.own_ref, bf16[16,176,128]{2,1,0:T(8,128)(2,1)S(1)} %all-to-all-done.2.sent_ref, ...), custom_call_target="tpu_custom_call" | custom-call | flops 100000000 | bytes 80000 | tf_op jit(solution)/shard_map/backward_conv/pallas_call | solution.py:665
  107.7 2.3 %collective-permute-done.13.refs_0_ = bf16[512,256]{1,0:T(8,128)(2,1)} collective-permute-done((bf16[512,256]{1,0:T(8,128)(2,1)}, bf16[512,256]{1,0:T(8,128)(2,1)}, u32[]{:S(2)}, u32[]{:S(2)}) %collective-permute-start.13) | collective-permute-done | bytes 262176 | tf_op jit(solution)/shard_map/ppermute | solution.py:662
  110.0 2.2 %last_sums.1 = (f32[1024,256]{1,0:T(8,128)}, bf16[256,512]{1,0:T(8,128)(2,1)}) custom-call(f32[1024,256]{1,0:T(8,128)S(1)} %get-tuple-element.60.gradient_ref, f32[256,512]{1,0:T(8,128)S(1)} %get-tuple-element.61.out_sum_ref, bf16[512,256]{1,0:T(8,128)(2,1)} %collective-permute-done.13.refs_0_, bf16[512,256]{1,0:T(8,128)(2,1)} %collective-permute-done.14.refs_1_, ...), custom_call_target="tpu_custom_call" | custom-call | flops 40000 | bytes 80000 | tf_op jit(solution)/shard_map/last_sums/pallas_call | solution.py:710
  (37 shorter events, 9.9 us)
Async XLA Ops:
  0.6 11.2 %collective-permute-start = (bf16[256,512]{1,0:T(8,128)(2,1)}, bf16[256,512]{1,0:T(8,128)(2,1)S(1)}, u32[]{:S(2)}, u32[]{:S(2)}) collective-permute-start(bf16[256,512]{1,0:T(8,128)(2,1)} %cot_ref.1), channel_id=1, source_target_pairs={{0,1},{1,0},{2,3},{3,2},{4,5},{5,4},{6,7},{7,6},{8,9},{9,8},{10,11... | collective-permute-start | bytes 786440 | tf_op jit(solution)/shard_map/ppermute | solution.py:529
  4.2 16.2 %all-to-all-start = ((f32[16,24,128]{2,1,0:T(8,128)}), f32[16,24,128]{2,1,0:T(8,128)S(1)}, u32[]{:S(2)}, u32[]{:S(2)}) async-start(f32[16,24,128]{2,1,0:T(8,128)} %pack_parameters.1), calls=%async_computation | async-start | bytes 393216 | tf_op jit(solution)/shard_map/all_to_all | solution.py:484
  14.6 32.6 %collective-permute-start.1 = (bf16[2,256,512]{2,1,0:T(8,128)(2,1)}, bf16[2,256,512]{2,1,0:T(8,128)(2,1)S(1)}, u32[]{:S(2)}, u32[]{:S(2)}) collective-permute-start(bf16[2,256,512]{2,1,0:T(8,128)(2,1)} %get-tuple-element.42.refs_0_.part0), channel_id=1, source_target_pairs={{0,2},{1,3},{2,4},{3,5},{4,6},{5,7},{6,0},{7,1},{8,10},{9,11},{10,... | collective-permute-start | bytes 1572872 | tf_op jit(solution)/shard_map/ppermute | solution.py:539
  16.1 31.6 %collective-permute-start.2 = (bf16[2,256,512]{2,1,0:T(8,128)(2,1)}, bf16[2,256,512]{2,1,0:T(8,128)(2,1)}, u32[]{:S(2)}, u32[]{:S(2)}) collective-permute-start(bf16[2,256,512]{2,1,0:T(8,128)(2,1)} %get-tuple-element.42.refs_0_.part0), channel_id=1, source_target_pairs={{0,4},{1,5},{2,6},{3,7},{4,0},{5,1},{6,2},{7,3},{8,12},{9,13},{10,... | collective-permute-start | bytes 1572872 | tf_op jit(solution)/shard_map/ppermute | solution.py:539
  18.8 29.0 %collective-permute-start.3 = (bf16[2,256,512]{2,1,0:T(8,128)(2,1)}, bf16[2,256,512]{2,1,0:T(8,128)(2,1)}, u32[]{:S(2)}, u32[]{:S(2)}) collective-permute-start(bf16[2,256,512]{2,1,0:T(8,128)(2,1)} %get-tuple-element.42.refs_0_.part0), channel_id=1, source_target_pairs={{0,6},{1,7},{2,0},{3,1},{4,2},{5,3},{6,4},{7,5},{8,14},{9,15},{10,... | collective-permute-start | bytes 1572872 | tf_op jit(solution)/shard_map/ppermute | solution.py:539
  22.6 19.5 %all-to-all-start.1 = ((bf16[16,16,8,128]{3,2,1,0:T(8,128)(2,1)}), bf16[16,16,8,128]{3,2,1,0:T(8,128)(2,1)S(1)}, u32[]{:S(2)}, u32[]{:S(2)}) async-start(bf16[16,16,8,128]{3,2,1,0:T(8,128)(2,1)} %get-tuple-element.44), calls=%async_computation.1 | async-start | bytes 1048576 | tf_op jit(solution)/shard_map/all_to_all | solution.py:484
  29.7 26.3 %collective-permute-start.5 = (bf16[2,256,512]{2,1,0:T(8,128)(2,1)}, bf16[2,256,512]{2,1,0:T(8,128)(2,1)S(1)}, u32[]{:S(2)}, u32[]{:S(2)}) collective-permute-start(bf16[2,256,512]{2,1,0:T(8,128)(2,1)} %get-tuple-element.42.refs_0_.part0), channel_id=1, source_target_pairs={{0,8},{8,0},{16,24},{24,16},{32,40},{40,32},{48,56},{56,48},{64,72... | collective-permute-start | bytes 1572872 | tf_op jit(solution)/shard_map/ppermute | solution.py:587
  47.1 8.9 %collective-permute-start.4 = (bf16[256,1024]{1,0:T(8,128)(2,1)}, bf16[256,1024]{1,0:T(8,128)(2,1)S(1)}, u32[]{:S(2)}, u32[]{:S(2)}) collective-permute-start(bf16[256,1024]{1,0:T(8,128)(2,1)} %get-tuple-element.49.gated_ref), channel_id=1, source_target_pairs={{0,8},{8,0},{16,24},{24,16},{32,40},{40,32},{48,56},{56,48},{64,72... | collective-permute-start | bytes 1572872 | tf_op jit(solution)/shard_map/ppermute | solution.py:577
  47.2 8.8 %copy-start = (bf16[2,256,512]{2,1,0:T(8,128)(2,1)}, bf16[2,256,512]{2,1,0:T(8,128)(2,1)S(1)}, u32[]{:S(2)}) copy-start(bf16[2,256,512]{2,1,0:T(8,128)(2,1)S(1)} %collective-permute-done.1.refs_1_.part1) | copy-start | bytes 1572868
  47.2 8.8 %collective-permute-start.6 = (bf16[2,256,512]{2,1,0:T(8,128)(2,1)S(1)}, bf16[2,256,512]{2,1,0:T(8,128)(2,1)S(1)}, u32[]{:S(2)}, u32[]{:S(2)}) collective-permute-start(bf16[2,256,512]{2,1,0:T(8,128)(2,1)S(1)} %collective-permute-done.1.refs_1_.part1), channel_id=1, source_target_pairs={{0,8},{8,0},{16,24},{24,16},{32,40},{40,32},{48,56},{56,48},{64,72... | collective-permute-start | bytes 1572872 | tf_op jit(solution)/shard_map/ppermute | solution.py:587
  47.7 8.3 %collective-permute-start.7 = (bf16[2,256,512]{2,1,0:T(8,128)(2,1)}, bf16[2,256,512]{2,1,0:T(8,128)(2,1)S(1)}, u32[]{:S(2)}, u32[]{:S(2)}) collective-permute-start(bf16[2,256,512]{2,1,0:T(8,128)(2,1)} %collective-permute-done.2.refs_2_.part2), channel_id=1, source_target_pairs={{0,8},{8,0},{16,24},{24,16},{32,40},{40,32},{48,56},{56,48},{64,72... | collective-permute-start | bytes 1572872 | tf_op jit(solution)/shard_map/ppermute | solution.py:587
  47.8 8.2 %collective-permute-start.8 = (bf16[2,256,512]{2,1,0:T(8,128)(2,1)}, bf16[2,256,512]{2,1,0:T(8,128)(2,1)S(1)}, u32[]{:S(2)}, u32[]{:S(2)}) collective-permute-start(bf16[2,256,512]{2,1,0:T(8,128)(2,1)} %collective-permute-done.3.refs_3_.part3), channel_id=1, source_target_pairs={{0,8},{8,0},{16,24},{24,16},{32,40},{40,32},{48,56},{56,48},{64,72... | collective-permute-start | bytes 1572872 | tf_op jit(solution)/shard_map/ppermute | solution.py:587
  51.4 31.4 %all-to-all-start.3 = ((bf16[4,2,256,512]{3,2,1,0:T(8,128)(2,1)}), bf16[4,2,256,512]{3,2,1,0:T(8,128)(2,1)}, u32[]{:S(2)}, u32[]{:S(2)}) async-start(bf16[4,2,256,512]{3,2,1,0:T(8,128)(2,1)} %bitcast.12), calls=%async_computation.3 | async-start | bytes 4194304 | tf_op jit(solution)/shard_map/all_to_all | solution.py:484
  61.8 27.3 %collective-permute-start.12 = (bf16[4,512,256]{2,1,0:T(8,128)(2,1)}, bf16[4,512,256]{2,1,0:T(8,128)(2,1)S(1)}, u32[]{:S(2)}, u32[]{:S(2)}) collective-permute-start(bf16[4,512,256]{2,1,0:T(8,128)(2,1)} %get-tuple-element.52.after_ref), channel_id=1, source_target_pairs={{0,64},{8,72},{16,80},{24,88},{32,96},{40,104},{48,112},{56,120},{... | collective-permute-start | bytes 3145736 | tf_op jit(solution)/shard_map/ppermute | solution.py:605
  62.4 26.4 %collective-permute-start.10 = (bf16[2,512,256]{2,1,0:T(8,128)(2,1)}, bf16[2,512,256]{2,1,0:T(8,128)(2,1)S(1)}, u32[]{:S(2)}, u32[]{:S(2)}) collective-permute-start(bf16[2,512,256]{2,1,0:T(8,128)(2,1)} %get-tuple-element.58), channel_id=1, source_target_pairs={{0,32},{8,40},{16,48},{24,56},{32,0},{40,8},{48,16},{56,24},{64,96... | collective-permute-start | bytes 1572872 | tf_op jit(solution)/shard_map/ppermute | solution.py:606
  63.7 25.1 %collective-permute-start.11 = (bf16[2,512,256]{2,1,0:T(8,128)(2,1)}, bf16[2,512,256]{2,1,0:T(8,128)(2,1)S(1)}, u32[]{:S(2)}, u32[]{:S(2)}) collective-permute-start(bf16[2,512,256]{2,1,0:T(8,128)(2,1)} %get-tuple-element.59), channel_id=1, source_target_pairs={{0,48},{8,56},{16,0},{24,8},{32,16},{40,24},{48,32},{56,40},{64,11... | collective-permute-start | bytes 1572872 | tf_op jit(solution)/shard_map/ppermute | solution.py:606
  65.4 23.7 %collective-permute-start.9 = (bf16[2,512,256]{2,1,0:T(8,128)(2,1)}, bf16[2,512,256]{2,1,0:T(8,128)(2,1)S(1)}, u32[]{:S(2)}, u32[]{:S(2)}) collective-permute-start(bf16[2,512,256]{2,1,0:T(8,128)(2,1)} %get-tuple-element.57), channel_id=1, source_target_pairs={{0,16},{8,24},{16,32},{24,40},{32,48},{40,56},{48,0},{56,8},{64,80... | collective-permute-start | bytes 1572872 | tf_op jit(solution)/shard_map/ppermute | solution.py:606
  82.8 18.4 %all-to-all-start.2 = ((bf16[16,176,128]{2,1,0:T(8,128)(2,1)}), bf16[16,176,128]{2,1,0:T(8,128)(2,1)S(1)}, u32[]{:S(2)}, u32[]{:S(2)}) async-start(bf16[16,176,128]{2,1,0:T(8,128)(2,1)} %get-tuple-element.53.after_ref), calls=%async_computation.2 | async-start | bytes 1441792 | tf_op jit(solution)/shard_map/all_to_all | solution.py:484
  88.7 19.0 %collective-permute-start.17 = (bf16[256,512]{1,0:T(8,128)(2,1)}, bf16[256,512]{1,0:T(8,128)(2,1)}, u32[]{:S(2)}, u32[]{:S(2)}) collective-permute-start(bf16[256,512]{1,0:T(8,128)(2,1)} %get-tuple-element.67), channel_id=1, source_target_pairs={{0,1},{1,0},{2,3},{3,2},{4,5},{5,4},{6,7},{7,6},{8,9},{9,8},{10,11... | collective-permute-start | bytes 786440 | tf_op jit(solution)/shard_map/ppermute | solution.py:652
  90.2 19.8 %collective-permute-start.13 = (bf16[512,256]{1,0:T(8,128)(2,1)}, bf16[512,256]{1,0:T(8,128)(2,1)}, u32[]{:S(2)}, u32[]{:S(2)}) collective-permute-start(bf16[512,256]{1,0:T(8,128)(2,1)} %get-tuple-element.63), channel_id=1, source_target_pairs={{0,64},{8,72},{16,80},{24,88},{32,96},{40,104},{48,112},{56,120},{... | collective-permute-start | bytes 786440 | tf_op jit(solution)/shard_map/ppermute | solution.py:662
  93.6 16.4 %collective-permute-start.14 = (bf16[512,256]{1,0:T(8,128)(2,1)}, bf16[512,256]{1,0:T(8,128)(2,1)}, u32[]{:S(2)}, u32[]{:S(2)}) collective-permute-start(bf16[512,256]{1,0:T(8,128)(2,1)} %get-tuple-element.64), channel_id=1, source_target_pairs={{0,16},{8,24},{16,32},{24,40},{32,48},{40,56},{48,0},{56,8},{64,80... | collective-permute-start | bytes 786440 | tf_op jit(solution)/shard_map/ppermute | solution.py:663
  95.1 14.9 %collective-permute-start.15 = (bf16[512,256]{1,0:T(8,128)(2,1)}, bf16[512,256]{1,0:T(8,128)(2,1)}, u32[]{:S(2)}, u32[]{:S(2)}) collective-permute-start(bf16[512,256]{1,0:T(8,128)(2,1)} %get-tuple-element.65), channel_id=1, source_target_pairs={{0,32},{8,40},{16,48},{24,56},{32,0},{40,8},{48,16},{56,24},{64,96... | collective-permute-start | bytes 786440 | tf_op jit(solution)/shard_map/ppermute | solution.py:663
  97.8 12.2 %collective-permute-start.16 = (bf16[512,256]{1,0:T(8,128)(2,1)}, bf16[512,256]{1,0:T(8,128)(2,1)}, u32[]{:S(2)}, u32[]{:S(2)}) collective-permute-start(bf16[512,256]{1,0:T(8,128)(2,1)} %get-tuple-element.66), channel_id=1, source_target_pairs={{0,48},{8,56},{16,0},{24,8},{32,16},{40,24},{48,32},{56,40},{64,11... | collective-permute-start | bytes 786440 | tf_op jit(solution)/shard_map/ppermute | solution.py:663

commit v7 on v6

--- a/solution.py
+++ b/solution.py
@@ -19,7 +19,7 @@
 PACK = 24
 TABLE = 2 * PACK * SUB
 STATE = MODES * SUB
-TERMS = 48
+TERMS = 32
 VMEM = 32 * 1024 * 1024
 LONG = 2_000_000_000_000
 SHORT = 50
@@ -103,13 +103,31 @@
         out_ref[j, MODES:] = jnp.broadcast_to(last, (PACK - MODES, 128))
 
 
-def mix_kernel(key_ref, value_ref, cot_ref, near_cot_ref, mixed_ref, kept_ref, pair_ref):
-    pair_ref[0] = cot_ref[...]
-    pair_ref[1] = near_cot_ref[...]
+def mix_kernel(
+    key_in, value_in, cot_in, near_cot_in, mixed_ref, mixed_out, pair_out, key_ref, value_ref, cot_ref, sems
+):
+    copies = [
+        pltpu.make_async_copy(key_in, key_ref, sems.at[0]),
+        pltpu.make_async_copy(value_in, value_ref, sems.at[1]),
+        pltpu.make_async_copy(near_cot_in, pair_out.at[1], sems.at[2]),
+        pltpu.make_async_copy(cot_in, cot_ref, sems.at[3]),
+    ]
+    results = [
+        pltpu.make_async_copy(mixed_ref, mixed_out, sems.at[4]),
+        pltpu.make_async_copy(cot_ref, pair_out.at[0], sems.at[5]),
+    ]
+    for copy in copies:
+        copy.start()
+    copies[0].wait()
+    copies[1].wait()
     for group in range(SUB):
         product = key_ref[:, lanes(group)].astype(F32) * value_ref[:, lanes(group)].astype(F32)
         mixed_ref[group_rows(group), :] = product.astype(BF16).astype(F32)
-    kept_ref[...] = mixed_ref[...]
+    results[0].start()
+    copies[3].wait()
+    results[1].start()
+    for copy in copies[2:3] + results:
+        copy.wait()
 
 
 def states_kernel(mixed_ref, packed_ref, sent_ref, table):
@@ -233,7 +251,7 @@
 def cotangent_kernel(
     came_ref, part0, part1, part2, part3, weight_ref, query_in, conv_in, mixed_in, carry_in, table_in, after_ref,
     dquery_out, dconv_out, sent_out,
-    total, terms, parts, weight, query_ref, conv_ref, mixed_ref, carry_ref, table, dquery_ref, dconv_ref, sent_ref, back_ref, sems,
+    total, terms, parts, weight, query_ref, conv_ref, mixed_ref, carry_ref, table, dquery_ref, dconv_ref, sent_ref, moments, sems,
 ):
     copies = []
     for i in range(8):
@@ -288,8 +306,6 @@
         return back
 
     back = lax.fori_loop(0, ROWS // UNROLL, backward, zeros(MODES))
-    for m in range(MODES):
-        back_ref[m] = back[m]
     for m in range(0, MODES, 2):
         state = jnp.concatenate([back[m], back[m + 1]]).astype(BF16)
         for j in range(BLOCKS):
@@ -317,8 +333,10 @@
 
         for m in range(half):
             put(first + m, first_sum[m], second_sum[m])
-            put(MODES + first + m, moment[m], back_ref[first + m])
-    for row in range(2 * MODES, TERMS):
+            moments[first + m] = moment[m]
+    for m in range(half):
+        put(MODES + m, moments[m], moments[half + m])
+    for row in range(MODES + half, TERMS):
         put(row, skip_sum, skip_sum)
     for j in range(BLOCKS):
         term = terms[TERMS * j : TERMS * (j + 1), :]
@@ -328,23 +346,29 @@
         result.wait()
 
 
-def owner_sums(parts_ref, rate_ref, residue_ref, dresidue_ref, drate_ref, dskip_ref):
+def owner_sums(parts_ref, place_ref, rate_ref, residue_ref, dresidue_ref, drate_ref, dskip_ref, states):
     rate = rate_ref[...]
     residue = residue_ref[...]
     near = jnp.exp(rate * (-1.0 / SEQ))
     far = jnp.exp(rate * (-float(ROWS) / SEQ))
     scale = jnp.sqrt(rate * (2.0 / SEQ))
+    half = MODES // 2
     first = jnp.zeros_like(rate)
     second = jnp.zeros_like(rate)
     skip = jnp.zeros((1, rate.shape[1]), F32)
     later = jnp.zeros_like(rate)
+    for j in range(BLOCKS):
+        states[STATE * j : STATE * (j + 1), :] = parts_ref[j, :STATE, :].astype(F32)
     for j in range(BLOCKS - 1, -1, -1):
-        terms = parts_ref[j].astype(F32)
-        sums, ends = terms[0:MODES], terms[MODES : 2 * MODES]
+        terms = parts_ref[j, STATE:, :].astype(F32)
+        sums, ends = terms[0:MODES], terms[MODES : MODES + half]
+        ends = jnp.concatenate([ends[:, :64], ends[:, 64:]])
+        back = states[pl.ds(STATE * j + place_ref[2], MODES, stride=SUB), :]
+        back = jnp.where(place_ref[3] == 0, back, pltpu.roll(back, 64, 1))[:, :64]
         first += sums[:, :64]
-        second += sums[:, 64:] + near * later * ends[:, :64]
-        later = far * later + ends[:, 64:]
-        skip += terms[2 * MODES : 2 * MODES + 1, :64]
+        second += sums[:, 64:] + near * later * ends
+        later = far * later + back
+        skip += terms[MODES + half : MODES + half + 1, :64]
     proj = scale * first
     dresidue_ref[...] = proj
     drate_ref[...] = residue * (0.5 * proj / rate - scale * second * (1.0 / SEQ))
@@ -355,7 +379,7 @@
     own_ref, sent_ref, dconv_in, key_in, value_in, table_in, first_in, same_in, arrived_in,
     came1, came2, came3, came_z, rate_ref, residue_ref,
     dkey_out, dvalue_out, gradient_ref, output_ref, dresidue_ref, drate_ref, dskip_ref,
-    dconv_ref, key_ref, value_ref, table, dkey_ref, dvalue_ref, carry_ref, buffer, blocks, arrived, sems,
+    dconv_ref, key_ref, value_ref, table, dkey_ref, dvalue_ref, carry_ref, buffer, blocks, arrived, states, sems,
 ):
     own = own_ref[0]
     copies = [
@@ -413,7 +437,7 @@
     gradient_ref[:HALF] = blocks[0].astype(F32) + sum(part[0].astype(F32) for part in (came1, came2, came3))
     gradient_ref[HALF:] = blocks[1].astype(F32) + came_z[0].astype(F32)
     output_ref[...] = sum(arrived[k].astype(F32) for k in range(4))
-    owner_sums(sent_ref.at[:, STATE:], rate_ref, residue_ref, dresidue_ref, drate_ref, dskip_ref)
+    owner_sums(sent_ref, own_ref, rate_ref, residue_ref, dresidue_ref, drate_ref, dskip_ref, states)
     for result in results:
         result.wait()
 
@@ -529,10 +553,15 @@
     near_cot = lax.ppermute(out_cotangent, "tp", shift_x(0, 1))
     mixed_near, mixed, cot_pair = pl.pallas_call(
         mix_kernel,
-        grid=(1,),
         out_shape=(f32(ROWS * SUB, 128), far_f32(ROWS * SUB, 128), far_bf16(2, ROWS, 512)),
-        in_specs=[full(ROWS, 1024)] * 2 + [full(ROWS, 512)] * 2,
-        out_specs=(whole(), full(ROWS * SUB, 128), full(2, ROWS, 512)),
+        in_specs=[pl.BlockSpec(memory_space=pl.ANY)] * 4,
+        out_specs=(whole(), pl.BlockSpec(memory_space=pl.ANY), pl.BlockSpec(memory_space=pl.ANY)),
+        scratch_shapes=[
+            pltpu.VMEM((ROWS, 1024), BF16),
+            pltpu.VMEM((ROWS, 1024), BF16),
+            pltpu.VMEM((ROWS, 512), BF16),
+            pltpu.SemaphoreType.DMA((6,)),
+        ],
         name="mix_inputs",
         **params_of(100_000_000, 3_000_000),
     )(far(key_part), far(value_part), far(out_cotangent), near_cot)
@@ -687,12 +716,13 @@
             pltpu.VMEM((ROWS * SUB, 128), F32),
             pltpu.VMEM((2, HALF, 256), BF16),
             pltpu.VMEM((4, ROWS, 512), BF16),
+            pltpu.VMEM((BLOCKS * STATE, 128), F32),
             pltpu.SemaphoreType.DMA((12,)),
         ],
         name="backward_conv",
         **params_of(5_000_000_000, 4_000_000),
     )(
-        jnp.stack([own, place_z]).astype(jnp.int32),
+        jnp.stack([own, place_z, own // 2, core]).astype(jnp.int32),
         received,
         far(d_conv),
         far(key_part),

time: 114 us -> 114 us (level)
  no operation moved by 1% of the time
where the time goes in v7:
time: 114 us; the launch traced here: 112 us
  Pallas kernels  45.9 us (40%)
  starting transfers between devices  45.1 us (40%)
  waiting for transfers between devices  19.6 us (17%)
    all_to_all x4, starting transfers between devices, exchange(): lax.all_to_all(array, axis, split_axis=0, concat_axis=0, tiled=True, axis...  22.7 us
    all_to_all x4, waiting for transfers between devices, exchange(): lax.all_to_all(array, axis, split_axis=0, concat_axis=0, tiled=True, axis...  16.8 us
    pallas_call x1, Pallas kernels, local(): pl.pallas_call(cotangent_kernel, out_shape=(far_bf16(ROWS, 1024), far_f32...  13.5 us
    pallas_call x1, Pallas kernels, local(): pl.pallas_call(backward_kernel, grid=(1,), out_shape=(far_bf16(ROWS, 1024...  6.61 us
    ppermute x3, starting transfers between devices, local(): lax.ppermute(cot_pair, 'tp', shift_x(k))  5.72 us
    pallas_call x1, Pallas kernels, local(): pl.pallas_call(weight_kernel, out_shape=(far_bf16(2, HALF, 256),) * 4 + (...  5.71 us
    ppermute x3, starting transfers between devices, local(): lax.ppermute(second_far[k - 1], 'ctx', shift_y(k))  5.63 us
    pallas_call x1, Pallas kernels, local(): pl.pallas_call(forward_kernel, out_shape=(far_bf16(ROWS, 1024), far_bf16(...  5.05 us
  transfers between devices with their start and end apart: 22, of which 6 were waited for; matrix products, arithmetic and copies ran while one was open for 0% of the time, Pallas kernels for 39%

profile of v7, /device:TPU:0, one launch (start us, length us, event | category | flops | bytes accessed | tf_op | source)
XLA Modules:
  0.0 111.9 jit_solution(14561441061577275427)
XLA Ops:
  0.6 2.1 %collective-permute-start = (bf16[256,512]{1,0:T(8,128)(2,1)}, bf16[256,512]{1,0:T(8,128)(2,1)S(1)}, u32[]{:S(2)}, u32[]{:S(2)}) collective-permute-start(bf16[256,512]{1,0:T(8,128)(2,1)} %cot_in.1), channel_id=1, source_target_pairs={{0,1},{1,0},{2,3},{3,2},{4,5},{5,4},{6,7},{7,6},{8,9},{9,8},{10,11... | collective-permute-start | bytes 786440 | tf_op jit(solution)/shard_map/ppermute | solution.py:553
  2.7 1.5 %pack_parameters.1 = f32[16,24,128]{2,1,0:T(8,128)} custom-call(f32[16,64]{1,0:T(8,128)} %bitcast.14, f32[16,64]{1,0:T(8,128)} %bitcast.16, f32[1,64]{1,0:T(1,128)} %bitcast.18), custom_call_target="tpu_custom_call" | custom-call | flops 2000 | bytes 4000 | tf_op jit(solution)/shard_map/pack_parameters/pallas_call | solution.py:543
  4.2 7.6 %all-to-all-start = ((f32[16,24,128]{2,1,0:T(8,128)}), f32[16,24,128]{2,1,0:T(8,128)S(1)}, u32[]{:S(2)}, u32[]{:S(2)}) async-start(f32[16,24,128]{2,1,0:T(8,128)} %pack_parameters.1), calls=%async_computation | async-start | bytes 393216 | tf_op jit(solution)/shard_map/all_to_all | solution.py:508
  11.8 2.7 %mix_inputs.1 = (f32[2048,128]{1,0:T(8,128)S(1)}, f32[2048,128]{1,0:T(8,128)}, bf16[2,256,512]{2,1,0:T(8,128)(2,1)}) custom-call(bf16[256,1024]{1,0:T(8,128)(2,1)} %key_in.3, bf16[256,1024]{1,0:T(8,128)(2,1)} %value_in.3, bf16[256,512]{1,0:T(8,128)(2,1)} %cot_in.1, bf16[256,512]{1,0:T(8,128)(2,1)S(1)} %collective-permute-done.near_cot_in), custom_call_target="tpu_custom_call" | custom-call | flops 2000000 | bytes 60000 | tf_op jit(solution)/shard_map/mix_inputs/pallas_call | solution.py:554
  14.5 1.6 %collective-permute-start.1 = (bf16[2,256,512]{2,1,0:T(8,128)(2,1)}, bf16[2,256,512]{2,1,0:T(8,128)(2,1)S(1)}, u32[]{:S(2)}, u32[]{:S(2)}) collective-permute-start(bf16[2,256,512]{2,1,0:T(8,128)(2,1)} %get-tuple-element.42.refs_0_.part0), channel_id=1, source_target_pairs={{0,2},{1,3},{2,4},{3,5},{4,6},{5,7},{6,0},{7,1},{8,10},{9,11},{10,... | collective-permute-start | bytes 1572872 | tf_op jit(solution)/shard_map/ppermute | solution.py:568
  16.1 2.7 %collective-permute-start.2 = (bf16[2,256,512]{2,1,0:T(8,128)(2,1)}, bf16[2,256,512]{2,1,0:T(8,128)(2,1)}, u32[]{:S(2)}, u32[]{:S(2)}) collective-permute-start(bf16[2,256,512]{2,1,0:T(8,128)(2,1)} %get-tuple-element.42.refs_0_.part0), channel_id=1, source_target_pairs={{0,4},{1,5},{2,6},{3,7},{4,0},{5,1},{6,2},{7,3},{8,12},{9,13},{10,... | collective-permute-start | bytes 1572872 | tf_op jit(solution)/shard_map/ppermute | solution.py:568
  20.4 2.2 %forward_states.1 = (bf16[16,16,8,128]{3,2,1,0:T(8,128)(2,1)}, f32[384,128]{1,0:T(8,128)}) custom-call(f32[2048,128]{1,0:T(8,128)S(1)} %get-tuple-element.43.mixed_ref, f32[16,24,128]{2,1,0:T(8,128)S(1)} %all-to-all-done.packed_ref), custom_call_target="tpu_custom_call" | custom-call | flops 60000000 | bytes 80000 | tf_op jit(solution)/shard_map/forward_states/pallas_call | solution.py:570
  22.6 7.1 %all-to-all-start.1 = ((bf16[16,16,8,128]{3,2,1,0:T(8,128)(2,1)}), bf16[16,16,8,128]{3,2,1,0:T(8,128)(2,1)S(1)}, u32[]{:S(2)}, u32[]{:S(2)}) async-start(bf16[16,16,8,128]{3,2,1,0:T(8,128)(2,1)} %get-tuple-element.44), calls=%async_computation.1 | async-start | bytes 1048576 | tf_op jit(solution)/shard_map/all_to_all | solution.py:508
  30.1 12.0 %all-to-all-done.1.sent_ref = bf16[16,16,8,128]{3,2,1,0:T(8,128)(2,1)S(1)} async-done(((bf16[16,16,8,128]{3,2,1,0:T(8,128)(2,1)}), bf16[16,16,8,128]{3,2,1,0:T(8,128)(2,1)S(1)}, u32[]{:S(2)}, u32[]{:S(2)}) %all-to-all-start.1) | async-done | bytes 524320 | tf_op jit(solution)/shard_map/all_to_all | solution.py:508
  42.0 5.0 %forward_conv.1 = (bf16[256,1024]{1,0:T(8,128)(2,1)}, bf16[256,1024]{1,0:T(8,128)(2,1)}, f32[16,8,128]{2,1,0:T(8,128)}, bf16[256,1024]{1,0:T(8,128)(2,1)S(1)}, bf16[8,1024,512]{2,1,0:T(8,128)(2,1)S(1)}) custom-call(s32[1]{0:T(128)} %bitcast.own_ref, bf16[16,16,8,128]{3,2,1,0:T(8,128)(2,1)S(1)} %all-to-all-done.1.sent_ref, ...), custom_call_target="tpu_custom_call" | custom-call | flops 100000000 | bytes 80000 | tf_op jit(solution)/shard_map/forward_conv/pallas_call | solution.py:582
  48.2 3.1 %output_projection.1.refs_8_ = bf16[8,256,512]{2,1,0:T(8,128)(2,1)} custom-call(bf16[256,1024]{1,0:T(8,128)(2,1)S(1)} %get-tuple-element.50.gated_ref, bf16[8,1024,512]{2,1,0:T(8,128)(2,1)S(1)} %get-tuple-element.51.weight_ref), custom_call_target="tpu_custom_call" | custom-call | flops 42949672 | bytes 220000 | tf_op jit(solution)/shard_map/output_projection/pallas_call | solution.py:607
  51.3 4.4 %all-to-all-start.3 = ((bf16[4,2,256,512]{3,2,1,0:T(8,128)(2,1)}), bf16[4,2,256,512]{3,2,1,0:T(8,128)(2,1)}, u32[]{:S(2)}, u32[]{:S(2)}) async-start(bf16[4,2,256,512]{3,2,1,0:T(8,128)(2,1)} %bitcast.13), calls=%async_computation.3 | async-start | bytes 4194304 | tf_op jit(solution)/shard_map/all_to_all | solution.py:508
  56.0 5.7 %projection_gradient.1 = (bf16[2,512,256]{2,1,0:T(8,128)(2,1)}, bf16[2,512,256]{2,1,0:T(8,128)(2,1)}, bf16[2,512,256]{2,1,0:T(8,128)(2,1)}, bf16[2,512,256]{2,1,...) custom-call(s32[9]{0:T(128)S(1)} %pad_add_fusion.1.index_ref, ...), custom_call_target="tpu_custom_call" | custom-call | flops 42949672 | bytes 160000 | tf_op jit(solution)/shard_map/projection_gradient/pallas_call | solution.py:618
  63.6 1.7 %collective-permute-start.11 = (bf16[2,512,256]{2,1,0:T(8,128)(2,1)}, bf16[2,512,256]{2,1,0:T(8,128)(2,1)S(1)}, u32[]{:S(2)}, u32[]{:S(2)}) collective-permute-start(bf16[2,512,256]{2,1,0:T(8,128)(2,1)} %get-tuple-element.59), channel_id=1, source_target_pairs={{0,48},{8,56},{16,0},{24,8},{32,16},{40,24},{48,32},{56,40},{64,11... | collective-permute-start | bytes 1572872 | tf_op jit(solution)/shard_map/ppermute | solution.py:635
  65.7 13.5 %cotangent_states.1 = (bf16[256,1024]{1,0:T(8,128)(2,1)}, f32[2048,128]{1,0:T(8,128)}, bf16[16,160,128]{2,1,0:T(8,128)(2,1)}) custom-call(s32[8]{0:T(128)S(1)} %fusion.came_ref, bf16[2,256,512]{2,1,0:T(8,128)(2,1)} %get-tuple-element.42.refs_0_.part0, bf16[2,256,512]{2,1,0:T(8,128)(2,1)} %copy-done, ...), custom_call_target="tpu_custom_call" | custom-call | flops 280000000 | bytes 260000 | tf_op jit(solution)/shard_map/cotangent_states/pallas_call | solution.py:640
  79.1 3.6 %all-to-all-done.3 = bf16[4,2,256,512]{3,2,1,0:T(8,128)(2,1)} async-done(((bf16[4,2,256,512]{3,2,1,0:T(8,128)(2,1)}), bf16[4,2,256,512]{3,2,1,0:T(8,128)(2,1)}, u32[]{:S(2)}, u32[]{:S(2)}) %all-to-all-start.3) | async-done | bytes 2097184 | tf_op jit(solution)/shard_map/all_to_all | solution.py:508
  82.7 3.6 %all-to-all-start.2 = ((bf16[16,160,128]{2,1,0:T(8,128)(2,1)}), bf16[16,160,128]{2,1,0:T(8,128)(2,1)S(1)}, u32[]{:S(2)}, u32[]{:S(2)}) async-start(bf16[16,160,128]{2,1,0:T(8,128)(2,1)} %get-tuple-element.53.after_ref), calls=%async_computation.2 | async-start | bytes 1310720 | tf_op jit(solution)/shard_map/all_to_all | solution.py:508
  86.3 2.3 %sum_output.1 = (bf16[256,512]{1,0:T(8,128)(2,1)}, bf16[4,512,256]{2,1,0:T(8,128)(2,1)S(1)}) custom-call(s32[1]{0:T(128)} %bitcast.9.place_ref, bf16[8,256,512]{2,1,0:T(8,128)(2,1)} %bitcast.8.arrived_in.arrived_ref, bf16[2,512,256]{2,1,0:T(8,128)(2,1)} %get-tuple-element.55.first_in.first_ref, bf16[4,512,256]{2,1,0:T(8,128)(2,1)} %get-tuple-element.56.same_in.same_ref, ...), custom_call_target="tpu_custom_call" | custom-call | flops 20000 | bytes 40000 | tf_op jit(solution)/shard_map/sum_output/pallas_call | solution.py:666
  90.1 3.5 %collective-permute-start.13 = (bf16[512,256]{1,0:T(8,128)(2,1)}, bf16[512,256]{1,0:T(8,128)(2,1)}, u32[]{:S(2)}, u32[]{:S(2)}) collective-permute-start(bf16[512,256]{1,0:T(8,128)(2,1)} %get-tuple-element.63), channel_id=1, source_target_pairs={{0,64},{8,72},{16,80},{24,88},{32,96},{40,104},{48,112},{56,120},{... | collective-permute-start | bytes 786440 | tf_op jit(solution)/shard_map/ppermute | solution.py:691
  93.6 1.5 %collective-permute-start.14 = (bf16[512,256]{1,0:T(8,128)(2,1)}, bf16[512,256]{1,0:T(8,128)(2,1)}, u32[]{:S(2)}, u32[]{:S(2)}) collective-permute-start(bf16[512,256]{1,0:T(8,128)(2,1)} %get-tuple-element.64), channel_id=1, source_target_pairs={{0,16},{8,24},{16,32},{24,40},{32,48},{40,56},{48,0},{56,8},{64,80... | collective-permute-start | bytes 786440 | tf_op jit(solution)/shard_map/ppermute | solution.py:692
  95.1 2.7 %collective-permute-start.15 = (bf16[512,256]{1,0:T(8,128)(2,1)}, bf16[512,256]{1,0:T(8,128)(2,1)}, u32[]{:S(2)}, u32[]{:S(2)}) collective-permute-start(bf16[512,256]{1,0:T(8,128)(2,1)} %get-tuple-element.65), channel_id=1, source_target_pairs={{0,32},{8,40},{16,48},{24,56},{32,0},{40,8},{48,16},{56,24},{64,96... | collective-permute-start | bytes 786440 | tf_op jit(solution)/shard_map/ppermute | solution.py:692
  100.4 6.6 %backward_conv.1 = (bf16[256,1024]{1,0:T(8,128)(2,1)}, bf16[256,1024]{1,0:T(8,128)(2,1)}, f32[1024,256]{1,0:T(8,128)S(1)}, f32[256,512]{1,0:T(8,128)S(1)}, f32[1...) custom-call(s32[4]{0:T(128)S(1)} %pad_add_fusion.own_ref, bf16[16,160,128]{2,1,0:T(8,128)(2,1)S(1)} %all-to-all-done.2.sent_ref, ...), custom_call_target="tpu_custom_call" | custom-call | flops 100000000 | bytes 80000 | tf_op jit(solution)/shard_map/backward_conv/pallas_call | solution.py:694
  107.0 2.4 %collective-permute-done.13.refs_0_ = bf16[512,256]{1,0:T(8,128)(2,1)} collective-permute-done((bf16[512,256]{1,0:T(8,128)(2,1)}, bf16[512,256]{1,0:T(8,128)(2,1)}, u32[]{:S(2)}, u32[]{:S(2)}) %collective-permute-start.13) | collective-permute-done | bytes 262176 | tf_op jit(solution)/shard_map/ppermute | solution.py:691
  109.5 2.2 %last_sums.1 = (f32[1024,256]{1,0:T(8,128)}, bf16[256,512]{1,0:T(8,128)(2,1)}) custom-call(f32[1024,256]{1,0:T(8,128)S(1)} %get-tuple-element.60.gradient_ref, f32[256,512]{1,0:T(8,128)S(1)} %get-tuple-element.61.out_sum_ref, bf16[512,256]{1,0:T(8,128)(2,1)} %collective-permute-done.13.refs_0_, bf16[512,256]{1,0:T(8,128)(2,1)} %collective-permute-done.14.refs_1_, ...), custom_call_target="tpu_custom_call" | custom-call | flops 40000 | bytes 80000 | tf_op jit(solution)/shard_map/last_sums/pallas_call | solution.py:740
  (37 shorter events, 9.6 us)
Async XLA Ops:
  0.6 11.2 %collective-permute-start = (bf16[256,512]{1,0:T(8,128)(2,1)}, bf16[256,512]{1,0:T(8,128)(2,1)S(1)}, u32[]{:S(2)}, u32[]{:S(2)}) collective-permute-start(bf16[256,512]{1,0:T(8,128)(2,1)} %cot_in.1), channel_id=1, source_target_pairs={{0,1},{1,0},{2,3},{3,2},{4,5},{5,4},{6,7},{7,6},{8,9},{9,8},{10,11... | collective-permute-start | bytes 786440 | tf_op jit(solution)/shard_map/ppermute | solution.py:553
  4.2 16.2 %all-to-all-start = ((f32[16,24,128]{2,1,0:T(8,128)}), f32[16,24,128]{2,1,0:T(8,128)S(1)}, u32[]{:S(2)}, u32[]{:S(2)}) async-start(f32[16,24,128]{2,1,0:T(8,128)} %pack_parameters.1), calls=%async_computation | async-start | bytes 393216 | tf_op jit(solution)/shard_map/all_to_all | solution.py:508
  14.5 32.7 %collective-permute-start.1 = (bf16[2,256,512]{2,1,0:T(8,128)(2,1)}, bf16[2,256,512]{2,1,0:T(8,128)(2,1)S(1)}, u32[]{:S(2)}, u32[]{:S(2)}) collective-permute-start(bf16[2,256,512]{2,1,0:T(8,128)(2,1)} %get-tuple-element.42.refs_0_.part0), channel_id=1, source_target_pairs={{0,2},{1,3},{2,4},{3,5},{4,6},{5,7},{6,0},{7,1},{8,10},{9,11},{10,... | collective-permute-start | bytes 1572872 | tf_op jit(solution)/shard_map/ppermute | solution.py:568
  16.1 31.6 %collective-permute-start.2 = (bf16[2,256,512]{2,1,0:T(8,128)(2,1)}, bf16[2,256,512]{2,1,0:T(8,128)(2,1)}, u32[]{:S(2)}, u32[]{:S(2)}) collective-permute-start(bf16[2,256,512]{2,1,0:T(8,128)(2,1)} %get-tuple-element.42.refs_0_.part0), channel_id=1, source_target_pairs={{0,4},{1,5},{2,6},{3,7},{4,0},{5,1},{6,2},{7,3},{8,12},{9,13},{10,... | collective-permute-start | bytes 1572872 | tf_op jit(solution)/shard_map/ppermute | solution.py:568
  18.8 29.0 %collective-permute-start.3 = (bf16[2,256,512]{2,1,0:T(8,128)(2,1)}, bf16[2,256,512]{2,1,0:T(8,128)(2,1)}, u32[]{:S(2)}, u32[]{:S(2)}) collective-permute-start(bf16[2,256,512]{2,1,0:T(8,128)(2,1)} %get-tuple-element.42.refs_0_.part0), channel_id=1, source_target_pairs={{0,6},{1,7},{2,0},{3,1},{4,2},{5,3},{6,4},{7,5},{8,14},{9,15},{10,... | collective-permute-start | bytes 1572872 | tf_op jit(solution)/shard_map/ppermute | solution.py:568
  22.6 19.4 %all-to-all-start.1 = ((bf16[16,16,8,128]{3,2,1,0:T(8,128)(2,1)}), bf16[16,16,8,128]{3,2,1,0:T(8,128)(2,1)S(1)}, u32[]{:S(2)}, u32[]{:S(2)}) async-start(bf16[16,16,8,128]{3,2,1,0:T(8,128)(2,1)} %get-tuple-element.44), calls=%async_computation.1 | async-start | bytes 1048576 | tf_op jit(solution)/shard_map/all_to_all | solution.py:508
  29.7 26.3 %collective-permute-start.5 = (bf16[2,256,512]{2,1,0:T(8,128)(2,1)}, bf16[2,256,512]{2,1,0:T(8,128)(2,1)S(1)}, u32[]{:S(2)}, u32[]{:S(2)}) collective-permute-start(bf16[2,256,512]{2,1,0:T(8,128)(2,1)} %get-tuple-element.42.refs_0_.part0), channel_id=1, source_target_pairs={{0,8},{8,0},{16,24},{24,16},{32,40},{40,32},{48,56},{56,48},{64,72... | collective-permute-start | bytes 1572872 | tf_op jit(solution)/shard_map/ppermute | solution.py:616
  47.1 8.9 %collective-permute-start.4 = (bf16[256,1024]{1,0:T(8,128)(2,1)}, bf16[256,1024]{1,0:T(8,128)(2,1)S(1)}, u32[]{:S(2)}, u32[]{:S(2)}) collective-permute-start(bf16[256,1024]{1,0:T(8,128)(2,1)} %get-tuple-element.49.gated_ref), channel_id=1, source_target_pairs={{0,8},{8,0},{16,24},{24,16},{32,40},{40,32},{48,56},{56,48},{64,72... | collective-permute-start | bytes 1572872 | tf_op jit(solution)/shard_map/ppermute | solution.py:606
  47.2 8.8 %copy-start = (bf16[2,256,512]{2,1,0:T(8,128)(2,1)}, bf16[2,256,512]{2,1,0:T(8,128)(2,1)S(1)}, u32[]{:S(2)}) copy-start(bf16[2,256,512]{2,1,0:T(8,128)(2,1)S(1)} %collective-permute-done.1.refs_1_.part1) | copy-start | bytes 1572868
  47.2 8.8 %collective-permute-start.6 = (bf16[2,256,512]{2,1,0:T(8,128)(2,1)S(1)}, bf16[2,256,512]{2,1,0:T(8,128)(2,1)S(1)}, u32[]{:S(2)}, u32[]{:S(2)}) collective-permute-start(bf16[2,256,512]{2,1,0:T(8,128)(2,1)S(1)} %collective-permute-done.1.refs_1_.part1), channel_id=1, source_target_pairs={{0,8},{8,0},{16,24},{24,16},{32,40},{40,32},{48,56},{56,48},{64,72... | collective-permute-start | bytes 1572872 | tf_op jit(solution)/shard_map/ppermute | solution.py:616
  47.7 8.3 %collective-permute-start.7 = (bf16[2,256,512]{2,1,0:T(8,128)(2,1)}, bf16[2,256,512]{2,1,0:T(8,128)(2,1)S(1)}, u32[]{:S(2)}, u32[]{:S(2)}) collective-permute-start(bf16[2,256,512]{2,1,0:T(8,128)(2,1)} %collective-permute-done.2.refs_2_.part2), channel_id=1, source_target_pairs={{0,8},{8,0},{16,24},{24,16},{32,40},{40,32},{48,56},{56,48},{64,72... | collective-permute-start | bytes 1572872 | tf_op jit(solution)/shard_map/ppermute | solution.py:616
  47.8 8.2 %collective-permute-start.8 = (bf16[2,256,512]{2,1,0:T(8,128)(2,1)}, bf16[2,256,512]{2,1,0:T(8,128)(2,1)S(1)}, u32[]{:S(2)}, u32[]{:S(2)}) collective-permute-start(bf16[2,256,512]{2,1,0:T(8,128)(2,1)} %collective-permute-done.3.refs_3_.part3), channel_id=1, source_target_pairs={{0,8},{8,0},{16,24},{24,16},{32,40},{40,32},{48,56},{56,48},{64,72... | collective-permute-start | bytes 1572872 | tf_op jit(solution)/shard_map/ppermute | solution.py:616
  51.3 31.4 %all-to-all-start.3 = ((bf16[4,2,256,512]{3,2,1,0:T(8,128)(2,1)}), bf16[4,2,256,512]{3,2,1,0:T(8,128)(2,1)}, u32[]{:S(2)}, u32[]{:S(2)}) async-start(bf16[4,2,256,512]{3,2,1,0:T(8,128)(2,1)} %bitcast.13), calls=%async_computation.3 | async-start | bytes 4194304 | tf_op jit(solution)/shard_map/all_to_all | solution.py:508
  61.7 27.3 %collective-permute-start.12 = (bf16[4,512,256]{2,1,0:T(8,128)(2,1)}, bf16[4,512,256]{2,1,0:T(8,128)(2,1)S(1)}, u32[]{:S(2)}, u32[]{:S(2)}) collective-permute-start(bf16[4,512,256]{2,1,0:T(8,128)(2,1)} %get-tuple-element.52.after_ref), channel_id=1, source_target_pairs={{0,64},{8,72},{16,80},{24,88},{32,96},{40,104},{48,112},{56,120},{... | collective-permute-start | bytes 3145736 | tf_op jit(solution)/shard_map/ppermute | solution.py:634
  62.4 26.4 %collective-permute-start.10 = (bf16[2,512,256]{2,1,0:T(8,128)(2,1)}, bf16[2,512,256]{2,1,0:T(8,128)(2,1)S(1)}, u32[]{:S(2)}, u32[]{:S(2)}) collective-permute-start(bf16[2,512,256]{2,1,0:T(8,128)(2,1)} %get-tuple-element.58), channel_id=1, source_target_pairs={{0,32},{8,40},{16,48},{24,56},{32,0},{40,8},{48,16},{56,24},{64,96... | collective-permute-start | bytes 1572872 | tf_op jit(solution)/shard_map/ppermute | solution.py:635
  63.6 25.1 %collective-permute-start.11 = (bf16[2,512,256]{2,1,0:T(8,128)(2,1)}, bf16[2,512,256]{2,1,0:T(8,128)(2,1)S(1)}, u32[]{:S(2)}, u32[]{:S(2)}) collective-permute-start(bf16[2,512,256]{2,1,0:T(8,128)(2,1)} %get-tuple-element.59), channel_id=1, source_target_pairs={{0,48},{8,56},{16,0},{24,8},{32,16},{40,24},{48,32},{56,40},{64,11... | collective-permute-start | bytes 1572872 | tf_op jit(solution)/shard_map/ppermute | solution.py:635
  65.4 23.7 %collective-permute-start.9 = (bf16[2,512,256]{2,1,0:T(8,128)(2,1)}, bf16[2,512,256]{2,1,0:T(8,128)(2,1)S(1)}, u32[]{:S(2)}, u32[]{:S(2)}) collective-permute-start(bf16[2,512,256]{2,1,0:T(8,128)(2,1)} %get-tuple-element.57), channel_id=1, source_target_pairs={{0,16},{8,24},{16,32},{24,40},{32,48},{40,56},{48,0},{56,8},{64,80... | collective-permute-start | bytes 1572872 | tf_op jit(solution)/shard_map/ppermute | solution.py:635
  82.7 17.6 %all-to-all-start.2 = ((bf16[16,160,128]{2,1,0:T(8,128)(2,1)}), bf16[16,160,128]{2,1,0:T(8,128)(2,1)S(1)}, u32[]{:S(2)}, u32[]{:S(2)}) async-start(bf16[16,160,128]{2,1,0:T(8,128)(2,1)} %get-tuple-element.53.after_ref), calls=%async_computation.2 | async-start | bytes 1310720 | tf_op jit(solution)/shard_map/all_to_all | solution.py:508
  88.6 18.4 %collective-permute-start.17 = (bf16[256,512]{1,0:T(8,128)(2,1)}, bf16[256,512]{1,0:T(8,128)(2,1)S(1)}, u32[]{:S(2)}, u32[]{:S(2)}) collective-permute-start(bf16[256,512]{1,0:T(8,128)(2,1)} %get-tuple-element.67), channel_id=1, source_target_pairs={{0,1},{1,0},{2,3},{3,2},{4,5},{5,4},{6,7},{7,6},{8,9},{9,8},{10,11... | collective-permute-start | bytes 786440 | tf_op jit(solution)/shard_map/ppermute | solution.py:681
  90.1 19.3 %collective-permute-start.13 = (bf16[512,256]{1,0:T(8,128)(2,1)}, bf16[512,256]{1,0:T(8,128)(2,1)}, u32[]{:S(2)}, u32[]{:S(2)}) collective-permute-start(bf16[512,256]{1,0:T(8,128)(2,1)} %get-tuple-element.63), channel_id=1, source_target_pairs={{0,64},{8,72},{16,80},{24,88},{32,96},{40,104},{48,112},{56,120},{... | collective-permute-start | bytes 786440 | tf_op jit(solution)/shard_map/ppermute | solution.py:691
  93.6 15.8 %collective-permute-start.14 = (bf16[512,256]{1,0:T(8,128)(2,1)}, bf16[512,256]{1,0:T(8,128)(2,1)}, u32[]{:S(2)}, u32[]{:S(2)}) collective-permute-start(bf16[512,256]{1,0:T(8,128)(2,1)} %get-tuple-element.64), channel_id=1, source_target_pairs={{0,16},{8,24},{16,32},{24,40},{32,48},{40,56},{48,0},{56,8},{64,80... | collective-permute-start | bytes 786440 | tf_op jit(solution)/shard_map/ppermute | solution.py:692
  95.1 14.4 %collective-permute-start.15 = (bf16[512,256]{1,0:T(8,128)(2,1)}, bf16[512,256]{1,0:T(8,128)(2,1)}, u32[]{:S(2)}, u32[]{:S(2)}) collective-permute-start(bf16[512,256]{1,0:T(8,128)(2,1)} %get-tuple-element.65), channel_id=1, source_target_pairs={{0,32},{8,40},{16,48},{24,56},{32,0},{40,8},{48,16},{56,24},{64,96... | collective-permute-start | bytes 786440 | tf_op jit(solution)/shard_map/ppermute | solution.py:692
  97.8 11.7 %collective-permute-start.16 = (bf16[512,256]{1,0:T(8,128)(2,1)}, bf16[512,256]{1,0:T(8,128)(2,1)}, u32[]{:S(2)}, u32[]{:S(2)}) collective-permute-start(bf16[512,256]{1,0:T(8,128)(2,1)} %get-tuple-element.66), channel_id=1, source_target_pairs={{0,48},{8,56},{16,0},{24,8},{32,16},{40,24},{48,32},{56,40},{64,11... | collective-permute-start | bytes 786440 | tf_op jit(solution)/shard_map/ppermute | solution.py:692

commit v8 on v7

--- a/solution.py
+++ b/solution.py
@@ -15,7 +15,7 @@
 SUB = 8
 BLOCKS = 16
 HALF = 512
-UNROLL = 8
+UNROLL = 16
 PACK = 24
 TABLE = 2 * PACK * SUB
 STATE = MODES * SUB
@@ -145,10 +145,10 @@
         return held
 
     held = lax.fori_loop(0, ROWS // UNROLL, body, zeros(MODES))
-    for m in range(MODES):
-        state = held[m].astype(BF16)
+    for m in range(0, MODES, 2):
+        state = jnp.concatenate([held[m], held[m + 1]]).astype(BF16)
         for j in range(BLOCKS):
-            sent_ref[j, m] = state
+            sent_ref[j, SUB * m : SUB * (m + 2), :] = state
 
 
 def forward_kernel(
@@ -172,12 +172,14 @@
     for copy in copies + weights:
         copy.start()
     copies[0].wait()
-    for m in range(MODES):
-        far = block_decay(table, m)
-        carry = jnp.zeros((SUB, 128), F32)
+    for m in range(0, MODES, 2):
+        decays = jnp.concatenate([block_decay(table, m), block_decay(table, m + 1)])
+        carry = jnp.zeros((2 * SUB, 128), F32)
         for j in range(BLOCKS - 1):
-            carry = jnp.where(j < own, far * carry + sent_ref[j, m].astype(F32), carry)
-        carry_ref[m] = carry
+            state = sent_ref[j, SUB * m : SUB * (m + 2), :].astype(F32)
+            carry = jnp.where(j < own, decays * carry + state, carry)
+        carry_ref[m] = carry[:SUB]
+        carry_ref[m + 1] = carry[SUB:]
     results[0].start()
     copies[1].wait()
     decay = [step_decay(table, m) for m in range(MODES)]
@@ -403,12 +405,14 @@
     for copy in copies:
         copy.start()
     copies[0].wait()
-    for m in range(MODES):
-        far = block_decay(table, m)
-        carry = jnp.zeros((SUB, 128), F32)
+    for m in range(0, MODES, 2):
+        decays = jnp.concatenate([block_decay(table, m), block_decay(table, m + 1)])
+        carry = jnp.zeros((2 * SUB, 128), F32)
         for j in range(BLOCKS - 1, 0, -1):
-            carry = jnp.where(j > own, far * carry + sent_ref[j, SUB * m : SUB * (m + 1), :].astype(F32), carry)
-        carry_ref[m] = carry
+            state = sent_ref[j, SUB * m : SUB * (m + 2), :].astype(F32)
+            carry = jnp.where(j > own, decays * carry + state, carry)
+        carry_ref[m] = carry[:SUB]
+        carry_ref[m + 1] = carry[SUB:]
     copies[1].wait()
     decay = [step_decay(table, m) for m in range(MODES)]
     weight = [mode_weight(table, m) for m in range(MODES)]
@@ -570,9 +574,9 @@
     sent, table = pl.pallas_call(
         states_kernel,
         grid=(1,),
-        out_shape=(far_bf16(BLOCKS, MODES, SUB, 128), far_f32(TABLE, 128)),
+        out_shape=(far_bf16(BLOCKS, STATE, 128), far_f32(TABLE, 128)),
         in_specs=[whole()] * 2,
-        out_specs=(full(BLOCKS, MODES, SUB, 128), full(TABLE, 128)),
+        out_specs=(full(BLOCKS, STATE, 128), full(TABLE, 128)),
         name="forward_states",
         **params_of(3_000_000_000, 4_000_000),
     )(mixed_near, packed)

time: 114 us -> 113 us (level)
  no operation moved by 1% of the time
where the time goes in v8:
time: 113 us; the launch traced here: 112 us
  Pallas kernels  45.3 us (40%)
  starting transfers between devices  45.1 us (40%)
  waiting for transfers between devices  20 us (18%)
    all_to_all x4, starting transfers between devices, exchange(): lax.all_to_all(array, axis, split_axis=0, concat_axis=0, tiled=True, axis...  22.7 us
    all_to_all x4, waiting for transfers between devices, exchange(): lax.all_to_all(array, axis, split_axis=0, concat_axis=0, tiled=True, axis...  17.1 us
    pallas_call x1, Pallas kernels, local(): pl.pallas_call(cotangent_kernel, out_shape=(far_bf16(ROWS, 1024), far_f32...  13.1 us
    pallas_call x1, Pallas kernels, local(): pl.pallas_call(backward_kernel, grid=(1,), out_shape=(far_bf16(ROWS, 1024...  6.52 us
    ppermute x3, starting transfers between devices, local(): lax.ppermute(cot_pair, 'tp', shift_x(k))  5.72 us
    pallas_call x1, Pallas kernels, local(): pl.pallas_call(weight_kernel, out_shape=(far_bf16(2, HALF, 256),) * 4 + (...  5.71 us
    ppermute x3, starting transfers between devices, local(): lax.ppermute(second_far[k - 1], 'ctx', shift_y(k))  5.63 us
    pallas_call x1, Pallas kernels, local(): pl.pallas_call(forward_kernel, out_shape=(far_bf16(ROWS, 1024), far_bf16(...  4.98 us
  transfers between devices with their start and end apart: 22, of which 6 were waited for; matrix products, arithmetic and copies ran while one was open for 0% of the time, Pallas kernels for 39%

profile of v8, /device:TPU:0, one launch (start us, length us, event | category | flops | bytes accessed | tf_op | source)
XLA Modules:
  0.0 111.7 jit_solution(4213663173798354289)
XLA Ops:
  0.6 2.1 %collective-permute-start = (bf16[256,512]{1,0:T(8,128)(2,1)}, bf16[256,512]{1,0:T(8,128)(2,1)S(1)}, u32[]{:S(2)}, u32[]{:S(2)}) collective-permute-start(bf16[256,512]{1,0:T(8,128)(2,1)} %cot_in.1), channel_id=1, source_target_pairs={{0,1},{1,0},{2,3},{3,2},{4,5},{5,4},{6,7},{7,6},{8,9},{9,8},{10,11... | collective-permute-start | bytes 786440 | tf_op jit(solution)/shard_map/ppermute | solution.py:557
  2.7 1.5 %pack_parameters.1 = f32[16,24,128]{2,1,0:T(8,128)} custom-call(f32[16,64]{1,0:T(8,128)} %bitcast.14, f32[16,64]{1,0:T(8,128)} %bitcast.16, f32[1,64]{1,0:T(1,128)} %bitcast.18), custom_call_target="tpu_custom_call" | custom-call | flops 2000 | bytes 4000 | tf_op jit(solution)/shard_map/pack_parameters/pallas_call | solution.py:547
  4.2 7.6 %all-to-all-start = ((f32[16,24,128]{2,1,0:T(8,128)}), f32[16,24,128]{2,1,0:T(8,128)S(1)}, u32[]{:S(2)}, u32[]{:S(2)}) async-start(f32[16,24,128]{2,1,0:T(8,128)} %pack_parameters.1), calls=%async_computation | async-start | bytes 393216 | tf_op jit(solution)/shard_map/all_to_all | solution.py:512
  11.8 2.7 %mix_inputs.1 = (f32[2048,128]{1,0:T(8,128)S(1)}, f32[2048,128]{1,0:T(8,128)}, bf16[2,256,512]{2,1,0:T(8,128)(2,1)}) custom-call(bf16[256,1024]{1,0:T(8,128)(2,1)} %key_in.3, bf16[256,1024]{1,0:T(8,128)(2,1)} %value_in.3, bf16[256,512]{1,0:T(8,128)(2,1)} %cot_in.1, bf16[256,512]{1,0:T(8,128)(2,1)S(1)} %collective-permute-done.near_cot_in), custom_call_target="tpu_custom_call" | custom-call | flops 2000000 | bytes 60000 | tf_op jit(solution)/shard_map/mix_inputs/pallas_call | solution.py:558
  14.5 1.6 %collective-permute-start.1 = (bf16[2,256,512]{2,1,0:T(8,128)(2,1)}, bf16[2,256,512]{2,1,0:T(8,128)(2,1)S(1)}, u32[]{:S(2)}, u32[]{:S(2)}) collective-permute-start(bf16[2,256,512]{2,1,0:T(8,128)(2,1)} %get-tuple-element.42.refs_0_.part0), channel_id=1, source_target_pairs={{0,2},{1,3},{2,4},{3,5},{4,6},{5,7},{6,0},{7,1},{8,10},{9,11},{10,... | collective-permute-start | bytes 1572872 | tf_op jit(solution)/shard_map/ppermute | solution.py:572
  16.1 2.7 %collective-permute-start.2 = (bf16[2,256,512]{2,1,0:T(8,128)(2,1)}, bf16[2,256,512]{2,1,0:T(8,128)(2,1)}, u32[]{:S(2)}, u32[]{:S(2)}) collective-permute-start(bf16[2,256,512]{2,1,0:T(8,128)(2,1)} %get-tuple-element.42.refs_0_.part0), channel_id=1, source_target_pairs={{0,4},{1,5},{2,6},{3,7},{4,0},{5,1},{6,2},{7,3},{8,12},{9,13},{10,... | collective-permute-start | bytes 1572872 | tf_op jit(solution)/shard_map/ppermute | solution.py:572
  20.4 2.1 %forward_states.1 = (bf16[16,128,128]{2,1,0:T(8,128)(2,1)}, f32[384,128]{1,0:T(8,128)}) custom-call(f32[2048,128]{1,0:T(8,128)S(1)} %get-tuple-element.43.mixed_ref, f32[16,24,128]{2,1,0:T(8,128)S(1)} %all-to-all-done.packed_ref), custom_call_target="tpu_custom_call" | custom-call | flops 60000000 | bytes 80000 | tf_op jit(solution)/shard_map/forward_states/pallas_call | solution.py:574
  22.5 7.1 %all-to-all-start.1 = ((bf16[16,128,128]{2,1,0:T(8,128)(2,1)}), bf16[16,128,128]{2,1,0:T(8,128)(2,1)S(1)}, u32[]{:S(2)}, u32[]{:S(2)}) async-start(bf16[16,128,128]{2,1,0:T(8,128)(2,1)} %get-tuple-element.44), calls=%async_computation.1 | async-start | bytes 1048576 | tf_op jit(solution)/shard_map/all_to_all | solution.py:512
  30.0 12.0 %all-to-all-done.1.sent_ref = bf16[16,128,128]{2,1,0:T(8,128)(2,1)S(1)} async-done(((bf16[16,128,128]{2,1,0:T(8,128)(2,1)}), bf16[16,128,128]{2,1,0:T(8,128)(2,1)S(1)}, u32[]{:S(2)}, u32[]{:S(2)}) %all-to-all-start.1) | async-done | bytes 524320 | tf_op jit(solution)/shard_map/all_to_all | solution.py:512
  41.9 5.0 %forward_conv.1 = (bf16[256,1024]{1,0:T(8,128)(2,1)}, bf16[256,1024]{1,0:T(8,128)(2,1)}, f32[16,8,128]{2,1,0:T(8,128)}, bf16[256,1024]{1,0:T(8,128)(2,1)S(1)}, bf16[8,1024,512]{2,1,0:T(8,128)(2,1)S(1)}) custom-call(s32[1]{0:T(128)} %bitcast.own_ref, bf16[16,128,128]{2,1,0:T(8,128)(2,1)S(1)} %all-to-all-done.1.sent_ref, ...), custom_call_target="tpu_custom_call" | custom-call | flops 100000000 | bytes 80000 | tf_op jit(solution)/shard_map/forward_conv/pallas_call | solution.py:586
  48.0 3.1 %output_projection.1.refs_8_ = bf16[8,256,512]{2,1,0:T(8,128)(2,1)} custom-call(bf16[256,1024]{1,0:T(8,128)(2,1)S(1)} %get-tuple-element.50.gated_ref, bf16[8,1024,512]{2,1,0:T(8,128)(2,1)S(1)} %get-tuple-element.51.weight_ref), custom_call_target="tpu_custom_call" | custom-call | flops 42949672 | bytes 220000 | tf_op jit(solution)/shard_map/output_projection/pallas_call | solution.py:611
  51.1 4.4 %all-to-all-start.3 = ((bf16[4,2,256,512]{3,2,1,0:T(8,128)(2,1)}), bf16[4,2,256,512]{3,2,1,0:T(8,128)(2,1)}, u32[]{:S(2)}, u32[]{:S(2)}) async-start(bf16[4,2,256,512]{3,2,1,0:T(8,128)(2,1)} %bitcast.13), calls=%async_computation.3 | async-start | bytes 4194304 | tf_op jit(solution)/shard_map/all_to_all | solution.py:512
  55.8 5.7 %projection_gradient.1 = (bf16[2,512,256]{2,1,0:T(8,128)(2,1)}, bf16[2,512,256]{2,1,0:T(8,128)(2,1)}, bf16[2,512,256]{2,1,0:T(8,128)(2,1)}, bf16[2,512,256]{2,1,...) custom-call(s32[9]{0:T(128)S(1)} %pad_add_fusion.1.index_ref, ...), custom_call_target="tpu_custom_call" | custom-call | flops 42949672 | bytes 160000 | tf_op jit(solution)/shard_map/projection_gradient/pallas_call | solution.py:622
  63.5 1.7 %collective-permute-start.11 = (bf16[2,512,256]{2,1,0:T(8,128)(2,1)}, bf16[2,512,256]{2,1,0:T(8,128)(2,1)S(1)}, u32[]{:S(2)}, u32[]{:S(2)}) collective-permute-start(bf16[2,512,256]{2,1,0:T(8,128)(2,1)} %get-tuple-element.59), channel_id=1, source_target_pairs={{0,48},{8,56},{16,0},{24,8},{32,16},{40,24},{48,32},{56,40},{64,11... | collective-permute-start | bytes 1572872 | tf_op jit(solution)/shard_map/ppermute | solution.py:639
  65.5 13.1 %cotangent_states.1 = (bf16[256,1024]{1,0:T(8,128)(2,1)}, f32[2048,128]{1,0:T(8,128)}, bf16[16,160,128]{2,1,0:T(8,128)(2,1)}) custom-call(s32[8]{0:T(128)S(1)} %fusion.came_ref, bf16[2,256,512]{2,1,0:T(8,128)(2,1)} %get-tuple-element.42.refs_0_.part0, bf16[2,256,512]{2,1,0:T(8,128)(2,1)} %copy-done, ...), custom_call_target="tpu_custom_call" | custom-call | flops 280000000 | bytes 260000 | tf_op jit(solution)/shard_map/cotangent_states/pallas_call | solution.py:644
  78.6 3.9 %all-to-all-done.3 = bf16[4,2,256,512]{3,2,1,0:T(8,128)(2,1)} async-done(((bf16[4,2,256,512]{3,2,1,0:T(8,128)(2,1)}), bf16[4,2,256,512]{3,2,1,0:T(8,128)(2,1)}, u32[]{:S(2)}, u32[]{:S(2)}) %all-to-all-start.3) | async-done | bytes 2097184 | tf_op jit(solution)/shard_map/all_to_all | solution.py:512
  82.5 3.6 %all-to-all-start.2 = ((bf16[16,160,128]{2,1,0:T(8,128)(2,1)}), bf16[16,160,128]{2,1,0:T(8,128)(2,1)S(1)}, u32[]{:S(2)}, u32[]{:S(2)}) async-start(bf16[16,160,128]{2,1,0:T(8,128)(2,1)} %get-tuple-element.53.after_ref), calls=%async_computation.2 | async-start | bytes 1310720 | tf_op jit(solution)/shard_map/all_to_all | solution.py:512
  86.1 2.3 %sum_output.1 = (bf16[256,512]{1,0:T(8,128)(2,1)}, bf16[4,512,256]{2,1,0:T(8,128)(2,1)S(1)}) custom-call(s32[1]{0:T(128)} %bitcast.9.place_ref, bf16[8,256,512]{2,1,0:T(8,128)(2,1)} %bitcast.8.arrived_in.arrived_ref, bf16[2,512,256]{2,1,0:T(8,128)(2,1)} %get-tuple-element.55.first_in.first_ref, bf16[4,512,256]{2,1,0:T(8,128)(2,1)} %get-tuple-element.56.same_in.same_ref, ...), custom_call_target="tpu_custom_call" | custom-call | flops 20000 | bytes 40000 | tf_op jit(solution)/shard_map/sum_output/pallas_call | solution.py:670
  89.9 3.5 %collective-permute-start.13 = (bf16[512,256]{1,0:T(8,128)(2,1)}, bf16[512,256]{1,0:T(8,128)(2,1)}, u32[]{:S(2)}, u32[]{:S(2)}) collective-permute-start(bf16[512,256]{1,0:T(8,128)(2,1)} %get-tuple-element.63), channel_id=1, source_target_pairs={{0,64},{8,72},{16,80},{24,88},{32,96},{40,104},{48,112},{56,120},{... | collective-permute-start | bytes 786440 | tf_op jit(solution)/shard_map/ppermute | solution.py:695
  93.4 1.5 %collective-permute-start.14 = (bf16[512,256]{1,0:T(8,128)(2,1)}, bf16[512,256]{1,0:T(8,128)(2,1)}, u32[]{:S(2)}, u32[]{:S(2)}) collective-permute-start(bf16[512,256]{1,0:T(8,128)(2,1)} %get-tuple-element.64), channel_id=1, source_target_pairs={{0,16},{8,24},{16,32},{24,40},{32,48},{40,56},{48,0},{56,8},{64,80... | collective-permute-start | bytes 786440 | tf_op jit(solution)/shard_map/ppermute | solution.py:696
  94.9 2.7 %collective-permute-start.15 = (bf16[512,256]{1,0:T(8,128)(2,1)}, bf16[512,256]{1,0:T(8,128)(2,1)}, u32[]{:S(2)}, u32[]{:S(2)}) collective-permute-start(bf16[512,256]{1,0:T(8,128)(2,1)} %get-tuple-element.65), channel_id=1, source_target_pairs={{0,32},{8,40},{16,48},{24,56},{32,0},{40,8},{48,16},{56,24},{64,96... | collective-permute-start | bytes 786440 | tf_op jit(solution)/shard_map/ppermute | solution.py:696
  100.2 6.5 %backward_conv.1 = (bf16[256,1024]{1,0:T(8,128)(2,1)}, bf16[256,1024]{1,0:T(8,128)(2,1)}, f32[1024,256]{1,0:T(8,128)S(1)}, f32[256,512]{1,0:T(8,128)S(1)}, f32[1...) custom-call(s32[4]{0:T(128)S(1)} %pad_add_fusion.own_ref, bf16[16,160,128]{2,1,0:T(8,128)(2,1)S(1)} %all-to-all-done.2.sent_ref, ...), custom_call_target="tpu_custom_call" | custom-call | flops 100000000 | bytes 80000 | tf_op jit(solution)/shard_map/backward_conv/pallas_call | solution.py:698
  106.7 2.5 %collective-permute-done.13.refs_0_ = bf16[512,256]{1,0:T(8,128)(2,1)} collective-permute-done((bf16[512,256]{1,0:T(8,128)(2,1)}, bf16[512,256]{1,0:T(8,128)(2,1)}, u32[]{:S(2)}, u32[]{:S(2)}) %collective-permute-start.13) | collective-permute-done | bytes 262176 | tf_op jit(solution)/shard_map/ppermute | solution.py:695
  109.3 2.2 %last_sums.1 = (f32[1024,256]{1,0:T(8,128)}, bf16[256,512]{1,0:T(8,128)(2,1)}) custom-call(f32[1024,256]{1,0:T(8,128)S(1)} %get-tuple-element.60.gradient_ref, f32[256,512]{1,0:T(8,128)S(1)} %get-tuple-element.61.out_sum_ref, bf16[512,256]{1,0:T(8,128)(2,1)} %collective-permute-done.13.refs_0_, bf16[512,256]{1,0:T(8,128)(2,1)} %collective-permute-done.14.refs_1_, ...), custom_call_target="tpu_custom_call" | custom-call | flops 40000 | bytes 80000 | tf_op jit(solution)/shard_map/last_sums/pallas_call | solution.py:744
  (37 shorter events, 9.6 us)
Async XLA Ops:
  0.6 11.2 %collective-permute-start = (bf16[256,512]{1,0:T(8,128)(2,1)}, bf16[256,512]{1,0:T(8,128)(2,1)S(1)}, u32[]{:S(2)}, u32[]{:S(2)}) collective-permute-start(bf16[256,512]{1,0:T(8,128)(2,1)} %cot_in.1), channel_id=1, source_target_pairs={{0,1},{1,0},{2,3},{3,2},{4,5},{5,4},{6,7},{7,6},{8,9},{9,8},{10,11... | collective-permute-start | bytes 786440 | tf_op jit(solution)/shard_map/ppermute | solution.py:557
  4.2 16.2 %all-to-all-start = ((f32[16,24,128]{2,1,0:T(8,128)}), f32[16,24,128]{2,1,0:T(8,128)S(1)}, u32[]{:S(2)}, u32[]{:S(2)}) async-start(f32[16,24,128]{2,1,0:T(8,128)} %pack_parameters.1), calls=%async_computation | async-start | bytes 393216 | tf_op jit(solution)/shard_map/all_to_all | solution.py:512
  14.5 32.5 %collective-permute-start.1 = (bf16[2,256,512]{2,1,0:T(8,128)(2,1)}, bf16[2,256,512]{2,1,0:T(8,128)(2,1)S(1)}, u32[]{:S(2)}, u32[]{:S(2)}) collective-permute-start(bf16[2,256,512]{2,1,0:T(8,128)(2,1)} %get-tuple-element.42.refs_0_.part0), channel_id=1, source_target_pairs={{0,2},{1,3},{2,4},{3,5},{4,6},{5,7},{6,0},{7,1},{8,10},{9,11},{10,... | collective-permute-start | bytes 1572872 | tf_op jit(solution)/shard_map/ppermute | solution.py:572
  16.1 31.4 %collective-permute-start.2 = (bf16[2,256,512]{2,1,0:T(8,128)(2,1)}, bf16[2,256,512]{2,1,0:T(8,128)(2,1)}, u32[]{:S(2)}, u32[]{:S(2)}) collective-permute-start(bf16[2,256,512]{2,1,0:T(8,128)(2,1)} %get-tuple-element.42.refs_0_.part0), channel_id=1, source_target_pairs={{0,4},{1,5},{2,6},{3,7},{4,0},{5,1},{6,2},{7,3},{8,12},{9,13},{10,... | collective-permute-start | bytes 1572872 | tf_op jit(solution)/shard_map/ppermute | solution.py:572
  18.8 28.8 %collective-permute-start.3 = (bf16[2,256,512]{2,1,0:T(8,128)(2,1)}, bf16[2,256,512]{2,1,0:T(8,128)(2,1)}, u32[]{:S(2)}, u32[]{:S(2)}) collective-permute-start(bf16[2,256,512]{2,1,0:T(8,128)(2,1)} %get-tuple-element.42.refs_0_.part0), channel_id=1, source_target_pairs={{0,6},{1,7},{2,0},{3,1},{4,2},{5,3},{6,4},{7,5},{8,14},{9,15},{10,... | collective-permute-start | bytes 1572872 | tf_op jit(solution)/shard_map/ppermute | solution.py:572
  22.5 19.4 %all-to-all-start.1 = ((bf16[16,128,128]{2,1,0:T(8,128)(2,1)}), bf16[16,128,128]{2,1,0:T(8,128)(2,1)S(1)}, u32[]{:S(2)}, u32[]{:S(2)}) async-start(bf16[16,128,128]{2,1,0:T(8,128)(2,1)} %get-tuple-element.44), calls=%async_computation.1 | async-start | bytes 1048576 | tf_op jit(solution)/shard_map/all_to_all | solution.py:512
  29.6 26.2 %collective-permute-start.5 = (bf16[2,256,512]{2,1,0:T(8,128)(2,1)}, bf16[2,256,512]{2,1,0:T(8,128)(2,1)S(1)}, u32[]{:S(2)}, u32[]{:S(2)}) collective-permute-start(bf16[2,256,512]{2,1,0:T(8,128)(2,1)} %get-tuple-element.42.refs_0_.part0), channel_id=1, source_target_pairs={{0,8},{8,0},{16,24},{24,16},{32,40},{40,32},{48,56},{56,48},{64,72... | collective-permute-start | bytes 1572872 | tf_op jit(solution)/shard_map/ppermute | solution.py:620
  46.9 8.9 %collective-permute-start.4 = (bf16[256,1024]{1,0:T(8,128)(2,1)}, bf16[256,1024]{1,0:T(8,128)(2,1)S(1)}, u32[]{:S(2)}, u32[]{:S(2)}) collective-permute-start(bf16[256,1024]{1,0:T(8,128)(2,1)} %get-tuple-element.49.gated_ref), channel_id=1, source_target_pairs={{0,8},{8,0},{16,24},{24,16},{32,40},{40,32},{48,56},{56,48},{64,72... | collective-permute-start | bytes 1572872 | tf_op jit(solution)/shard_map/ppermute | solution.py:610
  47.0 8.8 %copy-start = (bf16[2,256,512]{2,1,0:T(8,128)(2,1)}, bf16[2,256,512]{2,1,0:T(8,128)(2,1)S(1)}, u32[]{:S(2)}) copy-start(bf16[2,256,512]{2,1,0:T(8,128)(2,1)S(1)} %collective-permute-done.1.refs_1_.part1) | copy-start | bytes 1572868
  47.0 8.8 %collective-permute-start.6 = (bf16[2,256,512]{2,1,0:T(8,128)(2,1)S(1)}, bf16[2,256,512]{2,1,0:T(8,128)(2,1)S(1)}, u32[]{:S(2)}, u32[]{:S(2)}) collective-permute-start(bf16[2,256,512]{2,1,0:T(8,128)(2,1)S(1)} %collective-permute-done.1.refs_1_.part1), channel_id=1, source_target_pairs={{0,8},{8,0},{16,24},{24,16},{32,40},{40,32},{48,56},{56,48},{64,72... | collective-permute-start | bytes 1572872 | tf_op jit(solution)/shard_map/ppermute | solution.py:620
  47.5 8.3 %collective-permute-start.7 = (bf16[2,256,512]{2,1,0:T(8,128)(2,1)}, bf16[2,256,512]{2,1,0:T(8,128)(2,1)S(1)}, u32[]{:S(2)}, u32[]{:S(2)}) collective-permute-start(bf16[2,256,512]{2,1,0:T(8,128)(2,1)} %collective-permute-done.2.refs_2_.part2), channel_id=1, source_target_pairs={{0,8},{8,0},{16,24},{24,16},{32,40},{40,32},{48,56},{56,48},{64,72... | collective-permute-start | bytes 1572872 | tf_op jit(solution)/shard_map/ppermute | solution.py:620
  47.6 8.2 %collective-permute-start.8 = (bf16[2,256,512]{2,1,0:T(8,128)(2,1)}, bf16[2,256,512]{2,1,0:T(8,128)(2,1)S(1)}, u32[]{:S(2)}, u32[]{:S(2)}) collective-permute-start(bf16[2,256,512]{2,1,0:T(8,128)(2,1)} %collective-permute-done.3.refs_3_.part3), channel_id=1, source_target_pairs={{0,8},{8,0},{16,24},{24,16},{32,40},{40,32},{48,56},{56,48},{64,72... | collective-permute-start | bytes 1572872 | tf_op jit(solution)/shard_map/ppermute | solution.py:620
  51.1 31.4 %all-to-all-start.3 = ((bf16[4,2,256,512]{3,2,1,0:T(8,128)(2,1)}), bf16[4,2,256,512]{3,2,1,0:T(8,128)(2,1)}, u32[]{:S(2)}, u32[]{:S(2)}) async-start(bf16[4,2,256,512]{3,2,1,0:T(8,128)(2,1)} %bitcast.13), calls=%async_computation.3 | async-start | bytes 4194304 | tf_op jit(solution)/shard_map/all_to_all | solution.py:512
  61.5 27.3 %collective-permute-start.12 = (bf16[4,512,256]{2,1,0:T(8,128)(2,1)}, bf16[4,512,256]{2,1,0:T(8,128)(2,1)S(1)}, u32[]{:S(2)}, u32[]{:S(2)}) collective-permute-start(bf16[4,512,256]{2,1,0:T(8,128)(2,1)} %get-tuple-element.52.after_ref), channel_id=1, source_target_pairs={{0,64},{8,72},{16,80},{24,88},{32,96},{40,104},{48,112},{56,120},{... | collective-permute-start | bytes 3145736 | tf_op jit(solution)/shard_map/ppermute | solution.py:638
  62.2 26.4 %collective-permute-start.10 = (bf16[2,512,256]{2,1,0:T(8,128)(2,1)}, bf16[2,512,256]{2,1,0:T(8,128)(2,1)S(1)}, u32[]{:S(2)}, u32[]{:S(2)}) collective-permute-start(bf16[2,512,256]{2,1,0:T(8,128)(2,1)} %get-tuple-element.58), channel_id=1, source_target_pairs={{0,32},{8,40},{16,48},{24,56},{32,0},{40,8},{48,16},{56,24},{64,96... | collective-permute-start | bytes 1572872 | tf_op jit(solution)/shard_map/ppermute | solution.py:639
  63.5 25.1 %collective-permute-start.11 = (bf16[2,512,256]{2,1,0:T(8,128)(2,1)}, bf16[2,512,256]{2,1,0:T(8,128)(2,1)S(1)}, u32[]{:S(2)}, u32[]{:S(2)}) collective-permute-start(bf16[2,512,256]{2,1,0:T(8,128)(2,1)} %get-tuple-element.59), channel_id=1, source_target_pairs={{0,48},{8,56},{16,0},{24,8},{32,16},{40,24},{48,32},{56,40},{64,11... | collective-permute-start | bytes 1572872 | tf_op jit(solution)/shard_map/ppermute | solution.py:639
  65.2 23.7 %collective-permute-start.9 = (bf16[2,512,256]{2,1,0:T(8,128)(2,1)}, bf16[2,512,256]{2,1,0:T(8,128)(2,1)S(1)}, u32[]{:S(2)}, u32[]{:S(2)}) collective-permute-start(bf16[2,512,256]{2,1,0:T(8,128)(2,1)} %get-tuple-element.57), channel_id=1, source_target_pairs={{0,16},{8,24},{16,32},{24,40},{32,48},{40,56},{48,0},{56,8},{64,80... | collective-permute-start | bytes 1572872 | tf_op jit(solution)/shard_map/ppermute | solution.py:639
  82.5 17.6 %all-to-all-start.2 = ((bf16[16,160,128]{2,1,0:T(8,128)(2,1)}), bf16[16,160,128]{2,1,0:T(8,128)(2,1)S(1)}, u32[]{:S(2)}, u32[]{:S(2)}) async-start(bf16[16,160,128]{2,1,0:T(8,128)(2,1)} %get-tuple-element.53.after_ref), calls=%async_computation.2 | async-start | bytes 1310720 | tf_op jit(solution)/shard_map/all_to_all | solution.py:512
  88.4 18.3 %collective-permute-start.17 = (bf16[256,512]{1,0:T(8,128)(2,1)}, bf16[256,512]{1,0:T(8,128)(2,1)S(1)}, u32[]{:S(2)}, u32[]{:S(2)}) collective-permute-start(bf16[256,512]{1,0:T(8,128)(2,1)} %get-tuple-element.67), channel_id=1, source_target_pairs={{0,1},{1,0},{2,3},{3,2},{4,5},{5,4},{6,7},{7,6},{8,9},{9,8},{10,11... | collective-permute-start | bytes 786440 | tf_op jit(solution)/shard_map/ppermute | solution.py:685
  89.9 19.3 %collective-permute-start.13 = (bf16[512,256]{1,0:T(8,128)(2,1)}, bf16[512,256]{1,0:T(8,128)(2,1)}, u32[]{:S(2)}, u32[]{:S(2)}) collective-permute-start(bf16[512,256]{1,0:T(8,128)(2,1)} %get-tuple-element.63), channel_id=1, source_target_pairs={{0,64},{8,72},{16,80},{24,88},{32,96},{40,104},{48,112},{56,120},{... | collective-permute-start | bytes 786440 | tf_op jit(solution)/shard_map/ppermute | solution.py:695
  93.4 15.8 %collective-permute-start.14 = (bf16[512,256]{1,0:T(8,128)(2,1)}, bf16[512,256]{1,0:T(8,128)(2,1)}, u32[]{:S(2)}, u32[]{:S(2)}) collective-permute-start(bf16[512,256]{1,0:T(8,128)(2,1)} %get-tuple-element.64), channel_id=1, source_target_pairs={{0,16},{8,24},{16,32},{24,40},{32,48},{40,56},{48,0},{56,8},{64,80... | collective-permute-start | bytes 786440 | tf_op jit(solution)/shard_map/ppermute | solution.py:696
  94.9 14.4 %collective-permute-start.15 = (bf16[512,256]{1,0:T(8,128)(2,1)}, bf16[512,256]{1,0:T(8,128)(2,1)}, u32[]{:S(2)}, u32[]{:S(2)}) collective-permute-start(bf16[512,256]{1,0:T(8,128)(2,1)} %get-tuple-element.65), channel_id=1, source_target_pairs={{0,32},{8,40},{16,48},{24,56},{32,0},{40,8},{48,16},{56,24},{64,96... | collective-permute-start | bytes 786440 | tf_op jit(solution)/shard_map/ppermute | solution.py:696
  97.6 11.7 %collective-permute-start.16 = (bf16[512,256]{1,0:T(8,128)(2,1)}, bf16[512,256]{1,0:T(8,128)(2,1)}, u32[]{:S(2)}, u32[]{:S(2)}) collective-permute-start(bf16[512,256]{1,0:T(8,128)(2,1)} %get-tuple-element.66), channel_id=1, source_target_pairs={{0,48},{8,56},{16,0},{24,8},{32,16},{40,24},{48,32},{56,40},{64,11... | collective-permute-start | bytes 786440 | tf_op jit(solution)/shard_map/ppermute | solution.py:696

commit v9 on v8

--- a/solution.py
+++ b/solution.py
@@ -226,11 +226,11 @@
     ]
     for i in range(8):
         own = cot_refs[i // 2].at[i % 2, :, half]
-        other = other_refs[i // 2].at[i % 2, :, half]
         copies.append(pltpu.make_async_copy(own, cots.at[i, :ROWS], sems.at[i]))
-        copies.append(pltpu.make_async_copy(other, cots.at[i, ROWS:], sems.at[9 + i]))
     for copy in copies:
         copy.start()
+    for i in range(8):
+        cots[i, ROWS:] = other_refs[i // 2][i % 2, :, half]
     turned[:, ROWS:] = other_ref[...].T
     copies[0].wait()
     turned[:, :ROWS] = gated[...].T
@@ -622,14 +622,14 @@
     *by_y, same_z, other_z = pl.pallas_call(
         weight_kernel,
         out_shape=(far_bf16(2, HALF, 256),) * 4 + (far_bf16(4, HALF, 256),) * 2,
-        in_specs=[smem, anywhere, whole()] + [anywhere] * 9,
+        in_specs=[smem, anywhere, whole()] + [anywhere] * 4 + [whole()] * 4 + [anywhere],
         out_specs=(anywhere,) * 6,
         scratch_shapes=[
             pltpu.VMEM((ROWS, 1024), BF16),
             pltpu.VMEM((1024, 2 * ROWS), BF16),
             pltpu.VMEM((8, 2 * ROWS, 256), BF16),
             pltpu.VMEM((8, 1024, 256), BF16),
-            pltpu.SemaphoreType.DMA((17,)),
+            pltpu.SemaphoreType.DMA((9,)),
             pltpu.SemaphoreType.DMA((16,)),
         ],
         name="projection_gradient",

time: 113 us -> 113 us (level)
  no operation moved by 1% of the time
where the time goes in v9:
time: 113 us; the launch traced here: 112 us
  Pallas kernels  45.2 us (40%)
  starting transfers between devices  45.1 us (40%)
  waiting for transfers between devices  20 us (18%)
    all_to_all x4, starting transfers between devices, exchange(): lax.all_to_all(array, axis, split_axis=0, concat_axis=0, tiled=True, axis...  22.7 us
    all_to_all x4, waiting for transfers between devices, exchange(): lax.all_to_all(array, axis, split_axis=0, concat_axis=0, tiled=True, axis...  17.2 us
    pallas_call x1, Pallas kernels, local(): pl.pallas_call(cotangent_kernel, out_shape=(far_bf16(ROWS, 1024), far_f32...  13.1 us
    pallas_call x1, Pallas kernels, local(): pl.pallas_call(backward_kernel, grid=(1,), out_shape=(far_bf16(ROWS, 1024...  6.52 us
    ppermute x3, starting transfers between devices, local(): lax.ppermute(cot_pair, 'tp', shift_x(k))  5.72 us
    pallas_call x1, Pallas kernels, local(): pl.pallas_call(weight_kernel, out_shape=(far_bf16(2, HALF, 256),) * 4 + (...  5.66 us
    ppermute x3, starting transfers between devices, local(): lax.ppermute(second_far[k - 1], 'ctx', shift_y(k))  5.63 us
    pallas_call x1, Pallas kernels, local(): pl.pallas_call(forward_kernel, out_shape=(far_bf16(ROWS, 1024), far_bf16(...  4.98 us
  transfers between devices with their start and end apart: 22, of which 6 were waited for; matrix products, arithmetic and copies ran while one was open for 0% of the time, Pallas kernels for 39%

profile of v9, /device:TPU:0, one launch (start us, length us, event | category | flops | bytes accessed | tf_op | source)
XLA Modules:
  0.0 111.7 jit_solution(16005183897502290193)
XLA Ops:
  0.6 2.1 %collective-permute-start = (bf16[256,512]{1,0:T(8,128)(2,1)}, bf16[256,512]{1,0:T(8,128)(2,1)S(1)}, u32[]{:S(2)}, u32[]{:S(2)}) collective-permute-start(bf16[256,512]{1,0:T(8,128)(2,1)} %cot_in.1), channel_id=1, source_target_pairs={{0,1},{1,0},{2,3},{3,2},{4,5},{5,4},{6,7},{7,6},{8,9},{9,8},{10,11... | collective-permute-start | bytes 786440 | tf_op jit(solution)/shard_map/ppermute | solution.py:557
  2.7 1.5 %pack_parameters.1 = f32[16,24,128]{2,1,0:T(8,128)} custom-call(f32[16,64]{1,0:T(8,128)} %bitcast.14, f32[16,64]{1,0:T(8,128)} %bitcast.16, f32[1,64]{1,0:T(1,128)} %bitcast.18), custom_call_target="tpu_custom_call" | custom-call | flops 2000 | bytes 4000 | tf_op jit(solution)/shard_map/pack_parameters/pallas_call | solution.py:547
  4.2 7.6 %all-to-all-start = ((f32[16,24,128]{2,1,0:T(8,128)}), f32[16,24,128]{2,1,0:T(8,128)S(1)}, u32[]{:S(2)}, u32[]{:S(2)}) async-start(f32[16,24,128]{2,1,0:T(8,128)} %pack_parameters.1), calls=%async_computation | async-start | bytes 393216 | tf_op jit(solution)/shard_map/all_to_all | solution.py:512
  11.8 2.7 %mix_inputs.1 = (f32[2048,128]{1,0:T(8,128)S(1)}, f32[2048,128]{1,0:T(8,128)}, bf16[2,256,512]{2,1,0:T(8,128)(2,1)}) custom-call(bf16[256,1024]{1,0:T(8,128)(2,1)} %key_in.3, bf16[256,1024]{1,0:T(8,128)(2,1)} %value_in.3, bf16[256,512]{1,0:T(8,128)(2,1)} %cot_in.1, bf16[256,512]{1,0:T(8,128)(2,1)S(1)} %collective-permute-done.near_cot_in), custom_call_target="tpu_custom_call" | custom-call | flops 2000000 | bytes 60000 | tf_op jit(solution)/shard_map/mix_inputs/pallas_call | solution.py:558
  14.5 1.6 %collective-permute-start.1 = (bf16[2,256,512]{2,1,0:T(8,128)(2,1)}, bf16[2,256,512]{2,1,0:T(8,128)(2,1)S(1)}, u32[]{:S(2)}, u32[]{:S(2)}) collective-permute-start(bf16[2,256,512]{2,1,0:T(8,128)(2,1)} %get-tuple-element.42.refs_0_.part0), channel_id=1, source_target_pairs={{0,2},{1,3},{2,4},{3,5},{4,6},{5,7},{6,0},{7,1},{8,10},{9,11},{10,... | collective-permute-start | bytes 1572872 | tf_op jit(solution)/shard_map/ppermute | solution.py:572
  16.1 2.7 %collective-permute-start.2 = (bf16[2,256,512]{2,1,0:T(8,128)(2,1)}, bf16[2,256,512]{2,1,0:T(8,128)(2,1)}, u32[]{:S(2)}, u32[]{:S(2)}) collective-permute-start(bf16[2,256,512]{2,1,0:T(8,128)(2,1)} %get-tuple-element.42.refs_0_.part0), channel_id=1, source_target_pairs={{0,4},{1,5},{2,6},{3,7},{4,0},{5,1},{6,2},{7,3},{8,12},{9,13},{10,... | collective-permute-start | bytes 1572872 | tf_op jit(solution)/shard_map/ppermute | solution.py:572
  20.4 2.1 %forward_states.1 = (bf16[16,128,128]{2,1,0:T(8,128)(2,1)}, f32[384,128]{1,0:T(8,128)}) custom-call(f32[2048,128]{1,0:T(8,128)S(1)} %get-tuple-element.43.mixed_ref, f32[16,24,128]{2,1,0:T(8,128)S(1)} %all-to-all-done.packed_ref), custom_call_target="tpu_custom_call" | custom-call | flops 60000000 | bytes 80000 | tf_op jit(solution)/shard_map/forward_states/pallas_call | solution.py:574
  22.5 7.1 %all-to-all-start.1 = ((bf16[16,128,128]{2,1,0:T(8,128)(2,1)}), bf16[16,128,128]{2,1,0:T(8,128)(2,1)S(1)}, u32[]{:S(2)}, u32[]{:S(2)}) async-start(bf16[16,128,128]{2,1,0:T(8,128)(2,1)} %get-tuple-element.44), calls=%async_computation.1 | async-start | bytes 1048576 | tf_op jit(solution)/shard_map/all_to_all | solution.py:512
  30.0 12.0 %all-to-all-done.1.sent_ref = bf16[16,128,128]{2,1,0:T(8,128)(2,1)S(1)} async-done(((bf16[16,128,128]{2,1,0:T(8,128)(2,1)}), bf16[16,128,128]{2,1,0:T(8,128)(2,1)S(1)}, u32[]{:S(2)}, u32[]{:S(2)}) %all-to-all-start.1) | async-done | bytes 524320 | tf_op jit(solution)/shard_map/all_to_all | solution.py:512
  41.9 5.0 %forward_conv.1 = (bf16[256,1024]{1,0:T(8,128)(2,1)}, bf16[256,1024]{1,0:T(8,128)(2,1)}, f32[16,8,128]{2,1,0:T(8,128)}, bf16[256,1024]{1,0:T(8,128)(2,1)S(1)}, bf16[8,1024,512]{2,1,0:T(8,128)(2,1)S(1)}) custom-call(s32[1]{0:T(128)} %bitcast.own_ref, bf16[16,128,128]{2,1,0:T(8,128)(2,1)S(1)} %all-to-all-done.1.sent_ref, ...), custom_call_target="tpu_custom_call" | custom-call | flops 100000000 | bytes 80000 | tf_op jit(solution)/shard_map/forward_conv/pallas_call | solution.py:586
  48.0 3.1 %output_projection.1.refs_8_ = bf16[8,256,512]{2,1,0:T(8,128)(2,1)} custom-call(bf16[256,1024]{1,0:T(8,128)(2,1)S(1)} %get-tuple-element.50.gated_ref, bf16[8,1024,512]{2,1,0:T(8,128)(2,1)S(1)} %get-tuple-element.51.weight_ref), custom_call_target="tpu_custom_call" | custom-call | flops 42949672 | bytes 220000 | tf_op jit(solution)/shard_map/output_projection/pallas_call | solution.py:611
  51.1 4.4 %all-to-all-start.3 = ((bf16[4,2,256,512]{3,2,1,0:T(8,128)(2,1)}), bf16[4,2,256,512]{3,2,1,0:T(8,128)(2,1)}, u32[]{:S(2)}, u32[]{:S(2)}) async-start(bf16[4,2,256,512]{3,2,1,0:T(8,128)(2,1)} %bitcast.13), calls=%async_computation.3 | async-start | bytes 4194304 | tf_op jit(solution)/shard_map/all_to_all | solution.py:512
  55.8 5.7 %projection_gradient.1 = (bf16[2,512,256]{2,1,0:T(8,128)(2,1)}, bf16[2,512,256]{2,1,0:T(8,128)(2,1)}, bf16[2,512,256]{2,1,0:T(8,128)(2,1)}, bf16[2,512,256]{2,1,...) custom-call(s32[9]{0:T(128)S(1)} %pad_add_fusion.1.index_ref, ...), custom_call_target="tpu_custom_call" | custom-call | flops 42949672 | bytes 160000 | tf_op jit(solution)/shard_map/projection_gradient/pallas_call | solution.py:622
  63.4 1.7 %collective-permute-start.11 = (bf16[2,512,256]{2,1,0:T(8,128)(2,1)}, bf16[2,512,256]{2,1,0:T(8,128)(2,1)S(1)}, u32[]{:S(2)}, u32[]{:S(2)}) collective-permute-start(bf16[2,512,256]{2,1,0:T(8,128)(2,1)} %get-tuple-element.59), channel_id=1, source_target_pairs={{0,48},{8,56},{16,0},{24,8},{32,16},{40,24},{48,32},{56,40},{64,11... | collective-permute-start | bytes 1572872 | tf_op jit(solution)/shard_map/ppermute | solution.py:639
  65.4 13.1 %cotangent_states.1 = (bf16[256,1024]{1,0:T(8,128)(2,1)}, f32[2048,128]{1,0:T(8,128)}, bf16[16,160,128]{2,1,0:T(8,128)(2,1)}) custom-call(s32[8]{0:T(128)S(1)} %fusion.came_ref, bf16[2,256,512]{2,1,0:T(8,128)(2,1)} %get-tuple-element.42.refs_0_.part0, bf16[2,256,512]{2,1,0:T(8,128)(2,1)} %copy-done, ...), custom_call_target="tpu_custom_call" | custom-call | flops 280000000 | bytes 260000 | tf_op jit(solution)/shard_map/cotangent_states/pallas_call | solution.py:644
  78.5 4.0 %all-to-all-done.3 = bf16[4,2,256,512]{3,2,1,0:T(8,128)(2,1)} async-done(((bf16[4,2,256,512]{3,2,1,0:T(8,128)(2,1)}), bf16[4,2,256,512]{3,2,1,0:T(8,128)(2,1)}, u32[]{:S(2)}, u32[]{:S(2)}) %all-to-all-start.3) | async-done | bytes 2097184 | tf_op jit(solution)/shard_map/all_to_all | solution.py:512
  82.5 3.6 %all-to-all-start.2 = ((bf16[16,160,128]{2,1,0:T(8,128)(2,1)}), bf16[16,160,128]{2,1,0:T(8,128)(2,1)S(1)}, u32[]{:S(2)}, u32[]{:S(2)}) async-start(bf16[16,160,128]{2,1,0:T(8,128)(2,1)} %get-tuple-element.53.after_ref), calls=%async_computation.2 | async-start | bytes 1310720 | tf_op jit(solution)/shard_map/all_to_all | solution.py:512
  86.1 2.3 %sum_output.1 = (bf16[256,512]{1,0:T(8,128)(2,1)}, bf16[4,512,256]{2,1,0:T(8,128)(2,1)S(1)}) custom-call(s32[1]{0:T(128)} %bitcast.9.place_ref, bf16[8,256,512]{2,1,0:T(8,128)(2,1)} %bitcast.8.arrived_in.arrived_ref, bf16[2,512,256]{2,1,0:T(8,128)(2,1)} %get-tuple-element.55.first_in.first_ref, bf16[4,512,256]{2,1,0:T(8,128)(2,1)} %get-tuple-element.56.same_in.same_ref, ...), custom_call_target="tpu_custom_call" | custom-call | flops 20000 | bytes 40000 | tf_op jit(solution)/shard_map/sum_output/pallas_call | solution.py:670
  89.9 3.5 %collective-permute-start.13 = (bf16[512,256]{1,0:T(8,128)(2,1)}, bf16[512,256]{1,0:T(8,128)(2,1)}, u32[]{:S(2)}, u32[]{:S(2)}) collective-permute-start(bf16[512,256]{1,0:T(8,128)(2,1)} %get-tuple-element.63), channel_id=1, source_target_pairs={{0,64},{8,72},{16,80},{24,88},{32,96},{40,104},{48,112},{56,120},{... | collective-permute-start | bytes 786440 | tf_op jit(solution)/shard_map/ppermute | solution.py:695
  93.4 1.5 %collective-permute-start.14 = (bf16[512,256]{1,0:T(8,128)(2,1)}, bf16[512,256]{1,0:T(8,128)(2,1)}, u32[]{:S(2)}, u32[]{:S(2)}) collective-permute-start(bf16[512,256]{1,0:T(8,128)(2,1)} %get-tuple-element.64), channel_id=1, source_target_pairs={{0,16},{8,24},{16,32},{24,40},{32,48},{40,56},{48,0},{56,8},{64,80... | collective-permute-start | bytes 786440 | tf_op jit(solution)/shard_map/ppermute | solution.py:696
  94.9 2.7 %collective-permute-start.15 = (bf16[512,256]{1,0:T(8,128)(2,1)}, bf16[512,256]{1,0:T(8,128)(2,1)}, u32[]{:S(2)}, u32[]{:S(2)}) collective-permute-start(bf16[512,256]{1,0:T(8,128)(2,1)} %get-tuple-element.65), channel_id=1, source_target_pairs={{0,32},{8,40},{16,48},{24,56},{32,0},{40,8},{48,16},{56,24},{64,96... | collective-permute-start | bytes 786440 | tf_op jit(solution)/shard_map/ppermute | solution.py:696
  100.2 6.5 %backward_conv.1 = (bf16[256,1024]{1,0:T(8,128)(2,1)}, bf16[256,1024]{1,0:T(8,128)(2,1)}, f32[1024,256]{1,0:T(8,128)S(1)}, f32[256,512]{1,0:T(8,128)S(1)}, f32[1...) custom-call(s32[4]{0:T(128)S(1)} %pad_add_fusion.own_ref, bf16[16,160,128]{2,1,0:T(8,128)(2,1)S(1)} %all-to-all-done.2.sent_ref, ...), custom_call_target="tpu_custom_call" | custom-call | flops 100000000 | bytes 80000 | tf_op jit(solution)/shard_map/backward_conv/pallas_call | solution.py:698
  106.7 2.5 %collective-permute-done.13.refs_0_ = bf16[512,256]{1,0:T(8,128)(2,1)} collective-permute-done((bf16[512,256]{1,0:T(8,128)(2,1)}, bf16[512,256]{1,0:T(8,128)(2,1)}, u32[]{:S(2)}, u32[]{:S(2)}) %collective-permute-start.13) | collective-permute-done | bytes 262176 | tf_op jit(solution)/shard_map/ppermute | solution.py:695
  109.3 2.2 %last_sums.1 = (f32[1024,256]{1,0:T(8,128)}, bf16[256,512]{1,0:T(8,128)(2,1)}) custom-call(f32[1024,256]{1,0:T(8,128)S(1)} %get-tuple-element.60.gradient_ref, f32[256,512]{1,0:T(8,128)S(1)} %get-tuple-element.61.out_sum_ref, bf16[512,256]{1,0:T(8,128)(2,1)} %collective-permute-done.13.refs_0_, bf16[512,256]{1,0:T(8,128)(2,1)} %collective-permute-done.14.refs_1_, ...), custom_call_target="tpu_custom_call" | custom-call | flops 40000 | bytes 80000 | tf_op jit(solution)/shard_map/last_sums/pallas_call | solution.py:744
  (37 shorter events, 9.5 us)
Async XLA Ops:
  0.6 11.2 %collective-permute-start = (bf16[256,512]{1,0:T(8,128)(2,1)}, bf16[256,512]{1,0:T(8,128)(2,1)S(1)}, u32[]{:S(2)}, u32[]{:S(2)}) collective-permute-start(bf16[256,512]{1,0:T(8,128)(2,1)} %cot_in.1), channel_id=1, source_target_pairs={{0,1},{1,0},{2,3},{3,2},{4,5},{5,4},{6,7},{7,6},{8,9},{9,8},{10,11... | collective-permute-start | bytes 786440 | tf_op jit(solution)/shard_map/ppermute | solution.py:557
  4.2 16.2 %all-to-all-start = ((f32[16,24,128]{2,1,0:T(8,128)}), f32[16,24,128]{2,1,0:T(8,128)S(1)}, u32[]{:S(2)}, u32[]{:S(2)}) async-start(f32[16,24,128]{2,1,0:T(8,128)} %pack_parameters.1), calls=%async_computation | async-start | bytes 393216 | tf_op jit(solution)/shard_map/all_to_all | solution.py:512
  14.5 32.5 %collective-permute-start.1 = (bf16[2,256,512]{2,1,0:T(8,128)(2,1)}, bf16[2,256,512]{2,1,0:T(8,128)(2,1)S(1)}, u32[]{:S(2)}, u32[]{:S(2)}) collective-permute-start(bf16[2,256,512]{2,1,0:T(8,128)(2,1)} %get-tuple-element.42.refs_0_.part0), channel_id=1, source_target_pairs={{0,2},{1,3},{2,4},{3,5},{4,6},{5,7},{6,0},{7,1},{8,10},{9,11},{10,... | collective-permute-start | bytes 1572872 | tf_op jit(solution)/shard_map/ppermute | solution.py:572
  16.1 31.4 %collective-permute-start.2 = (bf16[2,256,512]{2,1,0:T(8,128)(2,1)}, bf16[2,256,512]{2,1,0:T(8,128)(2,1)}, u32[]{:S(2)}, u32[]{:S(2)}) collective-permute-start(bf16[2,256,512]{2,1,0:T(8,128)(2,1)} %get-tuple-element.42.refs_0_.part0), channel_id=1, source_target_pairs={{0,4},{1,5},{2,6},{3,7},{4,0},{5,1},{6,2},{7,3},{8,12},{9,13},{10,... | collective-permute-start | bytes 1572872 | tf_op jit(solution)/shard_map/ppermute | solution.py:572
  18.8 28.8 %collective-permute-start.3 = (bf16[2,256,512]{2,1,0:T(8,128)(2,1)}, bf16[2,256,512]{2,1,0:T(8,128)(2,1)}, u32[]{:S(2)}, u32[]{:S(2)}) collective-permute-start(bf16[2,256,512]{2,1,0:T(8,128)(2,1)} %get-tuple-element.42.refs_0_.part0), channel_id=1, source_target_pairs={{0,6},{1,7},{2,0},{3,1},{4,2},{5,3},{6,4},{7,5},{8,14},{9,15},{10,... | collective-permute-start | bytes 1572872 | tf_op jit(solution)/shard_map/ppermute | solution.py:572
  22.5 19.4 %all-to-all-start.1 = ((bf16[16,128,128]{2,1,0:T(8,128)(2,1)}), bf16[16,128,128]{2,1,0:T(8,128)(2,1)S(1)}, u32[]{:S(2)}, u32[]{:S(2)}) async-start(bf16[16,128,128]{2,1,0:T(8,128)(2,1)} %get-tuple-element.44), calls=%async_computation.1 | async-start | bytes 1048576 | tf_op jit(solution)/shard_map/all_to_all | solution.py:512
  29.6 26.2 %collective-permute-start.5 = (bf16[2,256,512]{2,1,0:T(8,128)(2,1)}, bf16[2,256,512]{2,1,0:T(8,128)(2,1)S(1)}, u32[]{:S(2)}, u32[]{:S(2)}) collective-permute-start(bf16[2,256,512]{2,1,0:T(8,128)(2,1)} %get-tuple-element.42.refs_0_.part0), channel_id=1, source_target_pairs={{0,8},{8,0},{16,24},{24,16},{32,40},{40,32},{48,56},{56,48},{64,72... | collective-permute-start | bytes 1572872 | tf_op jit(solution)/shard_map/ppermute | solution.py:620
  46.9 8.9 %collective-permute-start.4 = (bf16[256,1024]{1,0:T(8,128)(2,1)}, bf16[256,1024]{1,0:T(8,128)(2,1)S(1)}, u32[]{:S(2)}, u32[]{:S(2)}) collective-permute-start(bf16[256,1024]{1,0:T(8,128)(2,1)} %get-tuple-element.49.gated_ref), channel_id=1, source_target_pairs={{0,8},{8,0},{16,24},{24,16},{32,40},{40,32},{48,56},{56,48},{64,72... | collective-permute-start | bytes 1572872 | tf_op jit(solution)/shard_map/ppermute | solution.py:610
  47.0 8.8 %copy-start = (bf16[2,256,512]{2,1,0:T(8,128)(2,1)}, bf16[2,256,512]{2,1,0:T(8,128)(2,1)S(1)}, u32[]{:S(2)}) copy-start(bf16[2,256,512]{2,1,0:T(8,128)(2,1)S(1)} %collective-permute-done.1.refs_1_.part1) | copy-start | bytes 1572868
  47.0 8.8 %collective-permute-start.6 = (bf16[2,256,512]{2,1,0:T(8,128)(2,1)S(1)}, bf16[2,256,512]{2,1,0:T(8,128)(2,1)S(1)}, u32[]{:S(2)}, u32[]{:S(2)}) collective-permute-start(bf16[2,256,512]{2,1,0:T(8,128)(2,1)S(1)} %collective-permute-done.1.refs_1_.part1), channel_id=1, source_target_pairs={{0,8},{8,0},{16,24},{24,16},{32,40},{40,32},{48,56},{56,48},{64,72... | collective-permute-start | bytes 1572872 | tf_op jit(solution)/shard_map/ppermute | solution.py:620
  47.5 8.3 %collective-permute-start.7 = (bf16[2,256,512]{2,1,0:T(8,128)(2,1)}, bf16[2,256,512]{2,1,0:T(8,128)(2,1)S(1)}, u32[]{:S(2)}, u32[]{:S(2)}) collective-permute-start(bf16[2,256,512]{2,1,0:T(8,128)(2,1)} %collective-permute-done.2.refs_2_.part2), channel_id=1, source_target_pairs={{0,8},{8,0},{16,24},{24,16},{32,40},{40,32},{48,56},{56,48},{64,72... | collective-permute-start | bytes 1572872 | tf_op jit(solution)/shard_map/ppermute | solution.py:620
  47.6 8.2 %collective-permute-start.8 = (bf16[2,256,512]{2,1,0:T(8,128)(2,1)}, bf16[2,256,512]{2,1,0:T(8,128)(2,1)S(1)}, u32[]{:S(2)}, u32[]{:S(2)}) collective-permute-start(bf16[2,256,512]{2,1,0:T(8,128)(2,1)} %collective-permute-done.3.refs_3_.part3), channel_id=1, source_target_pairs={{0,8},{8,0},{16,24},{24,16},{32,40},{40,32},{48,56},{56,48},{64,72... | collective-permute-start | bytes 1572872 | tf_op jit(solution)/shard_map/ppermute | solution.py:620
  51.1 31.4 %all-to-all-start.3 = ((bf16[4,2,256,512]{3,2,1,0:T(8,128)(2,1)}), bf16[4,2,256,512]{3,2,1,0:T(8,128)(2,1)}, u32[]{:S(2)}, u32[]{:S(2)}) async-start(bf16[4,2,256,512]{3,2,1,0:T(8,128)(2,1)} %bitcast.13), calls=%async_computation.3 | async-start | bytes 4194304 | tf_op jit(solution)/shard_map/all_to_all | solution.py:512
  61.5 27.3 %collective-permute-start.12 = (bf16[4,512,256]{2,1,0:T(8,128)(2,1)}, bf16[4,512,256]{2,1,0:T(8,128)(2,1)S(1)}, u32[]{:S(2)}, u32[]{:S(2)}) collective-permute-start(bf16[4,512,256]{2,1,0:T(8,128)(2,1)} %get-tuple-element.52.after_ref), channel_id=1, source_target_pairs={{0,64},{8,72},{16,80},{24,88},{32,96},{40,104},{48,112},{56,120},{... | collective-permute-start | bytes 3145736 | tf_op jit(solution)/shard_map/ppermute | solution.py:638
  62.1 26.4 %collective-permute-start.10 = (bf16[2,512,256]{2,1,0:T(8,128)(2,1)}, bf16[2,512,256]{2,1,0:T(8,128)(2,1)S(1)}, u32[]{:S(2)}, u32[]{:S(2)}) collective-permute-start(bf16[2,512,256]{2,1,0:T(8,128)(2,1)} %get-tuple-element.58), channel_id=1, source_target_pairs={{0,32},{8,40},{16,48},{24,56},{32,0},{40,8},{48,16},{56,24},{64,96... | collective-permute-start | bytes 1572872 | tf_op jit(solution)/shard_map/ppermute | solution.py:639
  63.4 25.1 %collective-permute-start.11 = (bf16[2,512,256]{2,1,0:T(8,128)(2,1)}, bf16[2,512,256]{2,1,0:T(8,128)(2,1)S(1)}, u32[]{:S(2)}, u32[]{:S(2)}) collective-permute-start(bf16[2,512,256]{2,1,0:T(8,128)(2,1)} %get-tuple-element.59), channel_id=1, source_target_pairs={{0,48},{8,56},{16,0},{24,8},{32,16},{40,24},{48,32},{56,40},{64,11... | collective-permute-start | bytes 1572872 | tf_op jit(solution)/shard_map/ppermute | solution.py:639
  65.1 23.7 %collective-permute-start.9 = (bf16[2,512,256]{2,1,0:T(8,128)(2,1)}, bf16[2,512,256]{2,1,0:T(8,128)(2,1)S(1)}, u32[]{:S(2)}, u32[]{:S(2)}) collective-permute-start(bf16[2,512,256]{2,1,0:T(8,128)(2,1)} %get-tuple-element.57), channel_id=1, source_target_pairs={{0,16},{8,24},{16,32},{24,40},{32,48},{40,56},{48,0},{56,8},{64,80... | collective-permute-start | bytes 1572872 | tf_op jit(solution)/shard_map/ppermute | solution.py:639
  82.5 17.6 %all-to-all-start.2 = ((bf16[16,160,128]{2,1,0:T(8,128)(2,1)}), bf16[16,160,128]{2,1,0:T(8,128)(2,1)S(1)}, u32[]{:S(2)}, u32[]{:S(2)}) async-start(bf16[16,160,128]{2,1,0:T(8,128)(2,1)} %get-tuple-element.53.after_ref), calls=%async_computation.2 | async-start | bytes 1310720 | tf_op jit(solution)/shard_map/all_to_all | solution.py:512
  88.4 18.3 %collective-permute-start.17 = (bf16[256,512]{1,0:T(8,128)(2,1)}, bf16[256,512]{1,0:T(8,128)(2,1)S(1)}, u32[]{:S(2)}, u32[]{:S(2)}) collective-permute-start(bf16[256,512]{1,0:T(8,128)(2,1)} %get-tuple-element.67), channel_id=1, source_target_pairs={{0,1},{1,0},{2,3},{3,2},{4,5},{5,4},{6,7},{7,6},{8,9},{9,8},{10,11... | collective-permute-start | bytes 786440 | tf_op jit(solution)/shard_map/ppermute | solution.py:685
  89.9 19.3 %collective-permute-start.13 = (bf16[512,256]{1,0:T(8,128)(2,1)}, bf16[512,256]{1,0:T(8,128)(2,1)}, u32[]{:S(2)}, u32[]{:S(2)}) collective-permute-start(bf16[512,256]{1,0:T(8,128)(2,1)} %get-tuple-element.63), channel_id=1, source_target_pairs={{0,64},{8,72},{16,80},{24,88},{32,96},{40,104},{48,112},{56,120},{... | collective-permute-start | bytes 786440 | tf_op jit(solution)/shard_map/ppermute | solution.py:695
  93.4 15.8 %collective-permute-start.14 = (bf16[512,256]{1,0:T(8,128)(2,1)}, bf16[512,256]{1,0:T(8,128)(2,1)}, u32[]{:S(2)}, u32[]{:S(2)}) collective-permute-start(bf16[512,256]{1,0:T(8,128)(2,1)} %get-tuple-element.64), channel_id=1, source_target_pairs={{0,16},{8,24},{16,32},{24,40},{32,48},{40,56},{48,0},{56,8},{64,80... | collective-permute-start | bytes 786440 | tf_op jit(solution)/shard_map/ppermute | solution.py:696
  94.9 14.4 %collective-permute-start.15 = (bf16[512,256]{1,0:T(8,128)(2,1)}, bf16[512,256]{1,0:T(8,128)(2,1)}, u32[]{:S(2)}, u32[]{:S(2)}) collective-permute-start(bf16[512,256]{1,0:T(8,128)(2,1)} %get-tuple-element.65), channel_id=1, source_target_pairs={{0,32},{8,40},{16,48},{24,56},{32,0},{40,8},{48,16},{56,24},{64,96... | collective-permute-start | bytes 786440 | tf_op jit(solution)/shard_map/ppermute | solution.py:696
  97.6 11.7 %collective-permute-start.16 = (bf16[512,256]{1,0:T(8,128)(2,1)}, bf16[512,256]{1,0:T(8,128)(2,1)}, u32[]{:S(2)}, u32[]{:S(2)}) collective-permute-start(bf16[512,256]{1,0:T(8,128)(2,1)} %get-tuple-element.66), channel_id=1, source_target_pairs={{0,48},{8,56},{16,0},{24,8},{32,16},{40,24},{48,32},{56,40},{64,11... | collective-permute-start | bytes 786440 | tf_op jit(solution)/shard_map/ppermute | solution.py:696
